TPU v7x, 256 devices: a whole 4x4x8 slice. The times are simulated.
256 devices in a mesh: ctx: 32 (over z, x), head: 8 (over y, core).
Axes of the slice: x: 4, y: 4, z: 8, core: 2. Of those that a mesh axis runs over, the one named last changes fastest.
Arguments:
- queries: bfloat16 [65536, 1024], P('ctx', 'head'), may hold values from -8 to 8
- block_picks: int32 [128, 8, 4], P('ctx', 'head'), may hold values from 0 to 255, as said below
- span_keys: bfloat16 [65536, 256], P('ctx'), may hold values from -8 to 8
- span_values: bfloat16 [65536, 256], P('ctx'), may hold values from -3.5 to 3.5
- cache_keys: bfloat16 [131072, 256], P('ctx'), may hold values from -4 to 4
- cache_values: bfloat16 [131072, 256], P('ctx'), may hold values from -3.5 to 3.5
- out_weight: bfloat16 [1024, 2048], P('head'), may hold values from -0.1875 to 0.1875
Outputs:
- attention: bfloat16 [65536, 1024], P('ctx', 'head')
- projected: bfloat16 [65536, 2048], P(('ctx', 'head'))
Inputs may be any that keep to these rules, and one draw needn't show every extreme that they name: `block_picks`: the 4 picks of one query block and query head are distinct. Cache block b is held by ctx index b // 8. For each query head, at most 2 of the picks of the 4 query blocks of one ctx index lie in the blocks of any one ctx index; for each query head there is a ctx index into whose blocks exactly 2 picks fall from every ctx index.
All inputs are finite; a program needn't handle non-finite values.
Results may differ from a plain program's by a relative error of at most 0.017.
Values may be sent and summed in bfloat16 or wider, within the bound.
No kernel may reach another device: no remote copies, remote signals or barrier semaphores. Data moves between devices by JAX's collectives and lax.ppermute only.
A program may use at most 128 MiB of HBM per device.

v0:
```python
import math

import jax
import jax.numpy as jnp
from jax import lax
from jax.sharding import PartitionSpec as P

HD = 128
GROUP = 4
KVH = 2
BLK = 512
SEL = 4


NEG_FILL = -1e30


def partial_softmax(query_tile, key_block, value_block, allowed):
    inverse = 1.0 / math.sqrt(query_tile.shape[-1])
    scores = (
        jnp.einsum("qd,kd->qk", query_tile, key_block, preferred_element_type=jnp.float32) * inverse
    )
    scores = jnp.where(allowed, scores, NEG_FILL)
    highest = jnp.max(scores, axis=1)
    weights = jnp.where(allowed, jnp.exp(scores - highest[:, None]), 0.0)
    totals = jnp.sum(weights, axis=1)
    block_out = jnp.dot(
        weights.astype(jnp.bfloat16), value_block, preferred_element_type=jnp.float32
    )
    return (block_out.astype(jnp.bfloat16), highest, totals)


def merge_partials(block_out, highest, totals):
    overall_top = jnp.max(highest, axis=0)
    factor = jnp.exp(highest - overall_top[None, :])
    denominator = jnp.sum(factor * totals, axis=0)
    numerator = jnp.sum(factor[:, :, None] * block_out.astype(jnp.float32), axis=0)
    return (numerator / denominator[:, None]).astype(jnp.bfloat16)


def in_groups(function, operands):
    total_items = operands[0].shape[0]
    group_size = min(8, total_items)
    groups = -(-total_items // group_size)
    shaped = []
    for operand in operands:
        shaped.append(operand.reshape((groups, group_size) + operand.shape[1:]))
    results = lax.map(lambda members: jax.vmap(function)(*members), tuple(shaped))
    return tuple(
        (
            result.reshape((groups * group_size,) + result.shape[2:])[:total_items]
            for result in results
        )
    )


def body(queries, block_picks, span_keys, span_values, cache_keys, cache_values, out_weight):
    owners_total = lax.axis_size("ctx")
    heads_total = lax.axis_size("head")
    head_index = lax.axis_index("head")
    tok_rows = queries.shape[0]
    heads_here = queries.shape[1] // HD
    qblocks_here = tok_rows // BLK
    blocks_here = cache_keys.shape[0] // BLK
    capacity = max(2, (qblocks_here * SEL + owners_total - 1) // owners_total)
    slots_each = heads_here * capacity
    slots_total = owners_total * slots_each
    picks_total = qblocks_here * heads_here * SEL
    query_view = queries.reshape(qblocks_here, BLK, heads_here, HD)
    key_view = cache_keys.reshape(blocks_here, BLK, KVH, HD)
    value_view = cache_values.reshape(blocks_here, BLK, KVH, HD)
    picks_flat = block_picks.reshape(picks_total)
    pick_order = jnp.arange(picks_total, dtype=jnp.int32)
    owner_of = picks_flat // blocks_here
    local_of = picks_flat % blocks_here
    head_of = pick_order // SEL % heads_here
    qblock_of = pick_order // (SEL * heads_here)
    kv_of = (head_index * heads_here + head_of) // GROUP
    same_slot = (
        (owner_of[:, None] == owner_of[None, :])
        & (head_of[:, None] == head_of[None, :])
        & (pick_order[None, :] < pick_order[:, None])
    )
    rank_of = jnp.sum(same_slot.astype(jnp.int32), axis=1)
    slot_of = owner_of * slots_each + head_of * capacity + rank_of
    matches = slot_of[None, :] == jnp.arange(slots_total, dtype=jnp.int32)[:, None]
    filled = jnp.any(matches, axis=1)
    source = jnp.sum(jnp.where(matches, pick_order[None, :], 0), axis=1)
    send_ids = jnp.where(filled, local_of[source] * KVH + kv_of[source], -1).reshape(
        owners_total, slots_each
    )
    send_tiles = query_view[qblock_of[source], :, head_of[source], :]
    send_tiles = jnp.where(filled[:, None, None], send_tiles, jnp.zeros((), queries.dtype))
    send_tiles = send_tiles.reshape(owners_total, slots_each, BLK, HD)
    arrived_tiles = lax.all_to_all(send_tiles, "ctx", split_axis=0, concat_axis=0, tiled=True)
    arrived_ids = lax.all_to_all(send_ids, "ctx", split_axis=0, concat_axis=0, tiled=True)
    senders = arrived_ids.shape[0]
    item_count = arrived_ids.shape[1]
    flat_ids = jnp.maximum(arrived_ids.reshape(senders * item_count), 0)
    flat_tiles = arrived_tiles.reshape(senders * item_count, BLK, HD)

    def one_slot(query_tile, slot_id):
        return partial_softmax(
            query_tile,
            key_view[slot_id // KVH, :, slot_id % KVH, :],
            value_view[slot_id // KVH, :, slot_id % KVH, :],
            True,
        )

    block_out, highest, totals = in_groups(one_slot, (flat_tiles, flat_ids))
    block_out, highest, totals = (
        lax.all_to_all(
            block_out.reshape(senders, item_count, BLK, HD),
            "ctx",
            split_axis=0,
            concat_axis=0,
            tiled=True,
        ),
        lax.all_to_all(
            highest.reshape(senders, item_count, BLK),
            "ctx",
            split_axis=0,
            concat_axis=0,
            tiled=True,
        ),
        lax.all_to_all(
            totals.reshape(senders, item_count, BLK), "ctx", split_axis=0, concat_axis=0, tiled=True
        ),
    )
    far_out = block_out.reshape(slots_total, BLK, HD)[slot_of]
    far_top = highest.reshape(slots_total, BLK)[slot_of]
    far_totals = totals.reshape(slots_total, BLK)[slot_of]
    unit_total = qblocks_here * heads_here
    unit_order = jnp.arange(unit_total, dtype=jnp.int32)
    unit_qblock = unit_order // heads_here
    unit_head = unit_order % heads_here
    unit_kv = (head_index * heads_here + unit_head) // GROUP
    span_key_view = span_keys.reshape(qblocks_here, BLK, KVH, HD)
    span_value_view = span_values.reshape(qblocks_here, BLK, KVH, HD)
    own_queries = query_view[unit_qblock, :, unit_head, :]
    own_keys = span_key_view[unit_qblock, :, unit_kv, :]
    own_values = span_value_view[unit_qblock, :, unit_kv, :]
    causal = jnp.arange(BLK)[:, None] >= jnp.arange(BLK)[None, :]

    def own_block(query_tile, key_tile, value_tile):
        return partial_softmax(query_tile, key_tile, value_tile, causal)

    near_out, near_top, near_totals = in_groups(own_block, (own_queries, own_keys, own_values))
    all_out = jnp.concatenate(
        [far_out.reshape(unit_total, SEL, BLK, HD), near_out[:, None]], axis=1
    )
    all_top = jnp.concatenate([far_top.reshape(unit_total, SEL, BLK), near_top[:, None]], axis=1)
    all_totals = jnp.concatenate(
        [far_totals.reshape(unit_total, SEL, BLK), near_totals[:, None]], axis=1
    )
    merged = jax.vmap(merge_partials)(all_out, all_top, all_totals)
    attention = (
        merged.reshape(qblocks_here, heads_here, BLK, HD)
        .transpose(0, 2, 1, 3)
        .reshape(tok_rows, heads_here * HD)
    )
    share_rows = tok_rows // heads_total
    part_rows = lax.slice_in_dim(attention, 0, lax.axis_size("head") * share_rows, axis=0)
    projected = lax.psum_scatter(
        jnp.dot(part_rows, out_weight, preferred_element_type=jnp.float32).astype(jnp.bfloat16),
        "head",
        scatter_dimension=0,
        tiled=True,
    )
    return (attention, projected)


def solution(mesh):
    placed = (
        P("ctx", "head"),
        P("ctx", "head", None),
        P("ctx", None),
        P("ctx", None),
        P("ctx", None),
        P("ctx", None),
        P("head", None),
    )
    return jax.shard_map(
        body,
        mesh=mesh,
        in_specs=placed,
        out_specs=(P("ctx", "head"), P(("ctx", "head"), None)),
        check_vma=False,
    )
```

profile of v0, /device:TPU:1, one launch (start us, length us, event | category | flops | bytes accessed | tf_op | source)
XLA Modules:
  0.0 662.2 jit_solution(2218580328556657618)
XLA Ops:
  11.9 11.9 %all-to-all-start.1 = ((s32[32,1,2]{2,1,0:T(1,128)}), s32[32,1,2]{2,1,0:T(1,128)S(1)}, u32[]{:S(2)}, u32[]{:S(2)}) async-start(s32[32,1,2]{2,1,0:T(1,128)} %bitcast.14), calls=%async_computation.1 | async-start | bytes 32768 | tf_op jit(solution)/shard_map/all_to_all | solution.py:96
  25.4 5.3 gather_fusion.4
  30.8 7.2 %broadcast_select_fusion = bf16[32,2,512,128]{3,2,1,0:T(8,128)(2,1)} fusion(bf16[32,2,512,128]{3,2,1,0:T(8,128)(2,1)} %bitcast.83, pred[32,2]{1,0:T(8,128)(4,1)S(1)} %broadcast_in_dim.120), kind=kLoop, calls=%fused_computation.45 | loop fusion | flops 4194304 | bytes 16777280 | tf_op jit(solution)/shard_map/jit(_where)/select_n | solution.py:93
  38.0 9.4 %all-to-all-start = ((bf16[32,2,512,128]{3,2,1,0:T(8,128)(2,1)}), bf16[32,2,512,128]{3,2,1,0:T(8,128)(2,1)}, u32[]{:S(2)}, u32[]{:S(2)}) async-start(bf16[32,2,512,128]{3,2,1,0:T(8,128)(2,1)} %broadcast_select_fusion), calls=%async_computation | async-start | bytes 16777216 | tf_op jit(solution)/shard_map/all_to_all | solution.py:95
  50.0 3.8 copy.56
  56.3 3.8 copy.57
  60.3 178.3 %all-to-all-done = bf16[32,2,512,128]{3,2,1,0:T(8,128)(2,1)} async-done(((bf16[32,2,512,128]{3,2,1,0:T(8,128)(2,1)}), bf16[32,2,512,128]{3,2,1,0:T(8,128)(2,1)}, u32[]{:S(2)}, u32[]{:S(2)}) %all-to-all-start) | async-done | bytes 8388640 | tf_op jit(solution)/shard_map/all_to_all | solution.py:95
  238.6 132.2 %while.4 = (s32[]{:T(128)}, bf16[8,8,512,128]{3,2,1,0:T(8,128)(2,1)}, f32[8,8,512]{2,1,0:T(8,128)S(1)}, f32[8,8,512]{2,1,0:T(8,128)S(1)}, bf16[8,8,512,128]{3,2,...) while((s32[]{:T(128)}, ...), condition=%wide.region_6.7_spmd, body=%wide.region_3.6_spmd.sunk | while | flops 1091035392 | bytes 67241408 | solution.py:48
  248.8 6.3 fusion.72
  265.3 6.4 fusion.72
  281.9 6.3 fusion.72
  298.4 6.3 fusion.72
  314.9 6.3 fusion.72
  331.4 6.3 fusion.72
  347.9 6.3 fusion.72
  364.5 6.3 fusion.72
  371.5 6.2 all-to-all-start.2
  377.8 9.3 %all-to-all-done.2 = f32[32,2,512]{2,1,0:T(2,128)S(1)} async-done(((f32[32,2,512]{2,1,0:T(2,128)}), f32[32,2,512]{2,1,0:T(2,128)S(1)}, u32[]{:S(2)}, u32[]{:S(2)}) %all-to-all-start.2) | async-done | bytes 131104 | tf_op jit(solution)/shard_map/all_to_all | solution.py:119
  387.0 13.1 %all_to_all.26 = f32[32,2,512]{2,1,0:T(2,128)} all-to-all(f32[32,2,512]{2,1,0:T(2,128)S(1)} %reshape_reshape.15), channel_id=1, replica_groups=mesh['ctx'=32,'head'=8] {'ctx'}, dimensions={0} | all-to-all | bytes 262144 | tf_op jit(solution)/shard_map/all_to_all | solution.py:126
  400.1 5.1 all-to-all-start.3
  418.4 166.1 %all-to-all-done.3 = bf16[32,2,512,128]{3,2,1,0:T(8,128)(2,1)} async-done(((bf16[32,2,512,128]{3,2,1,0:T(8,128)(2,1)}), bf16[32,2,512,128]{3,2,1,0:T(8,128)(2,1)}, u32[]{:S(2)}, u32[]{:S(2)}) %all-to-all-start.3) | async-done | bytes 8388640 | tf_op jit(solution)/shard_map/all_to_all | solution.py:112
  584.5 4.5 gather_fusion.10
  591.0 5.6 convolution_convert_fusion
  596.6 58.8 %reduce-scatter.2.cloned.1.call-done = bf16[256,2048]{1,0:T(8,128)(2,1)} async-done(((bf16[2048,2048]{1,0:T(8,128)(2,1)}), bf16[256,2048]{1,0:T(8,128)(2,1)}) %reduce-scatter.2.cloned.1.call-update) | async-done | bytes 1048592 | tf_op jit(solution)/shard_map/reduce_scatter | solution.py:164
  (147 shorter events, 108.7 us)
Async XLA Ops:
  7.2 18.3 %copy-start = (bf16[2048,128]{1,0:T(8,128)(2,1)S(1)}, bf16[2048,128]{1,0:T(8,128)(2,1)}, u32[]{:S(2)}) copy-start(bf16[2048,128]{1,0:T(8,128)(2,1)} %param.9) | copy-start | bytes 1572868
  11.9 26.1 %all-to-all-start.1 = ((s32[32,1,2]{2,1,0:T(1,128)}), s32[32,1,2]{2,1,0:T(1,128)S(1)}, u32[]{:S(2)}, u32[]{:S(2)}) async-start(s32[32,1,2]{2,1,0:T(1,128)} %bitcast.14), calls=%async_computation.1 | async-start | bytes 32768 | tf_op jit(solution)/shard_map/all_to_all | solution.py:96
  38.0 200.6 %all-to-all-start = ((bf16[32,2,512,128]{3,2,1,0:T(8,128)(2,1)}), bf16[32,2,512,128]{3,2,1,0:T(8,128)(2,1)}, u32[]{:S(2)}, u32[]{:S(2)}) async-start(bf16[32,2,512,128]{3,2,1,0:T(8,128)(2,1)} %broadcast_select_fusion), calls=%async_computation | async-start | bytes 16777216 | tf_op jit(solution)/shard_map/all_to_all | solution.py:95
  243.3 3.2 copy-start.1
  259.9 3.2 copy-start.1
  276.4 3.2 copy-start.1
  292.9 3.2 copy-start.1
  309.4 3.2 copy-start.1
  326.0 3.2 copy-start.1
  342.5 3.2 copy-start.1
  359.0 3.2 copy-start.1
  371.5 15.5 %all-to-all-start.2 = ((f32[32,2,512]{2,1,0:T(2,128)}), f32[32,2,512]{2,1,0:T(2,128)S(1)}, u32[]{:S(2)}, u32[]{:S(2)}) async-start(f32[32,2,512]{2,1,0:T(2,128)} %reshape_reshape.13), calls=%async_computation.2 | async-start | bytes 262144 | tf_op jit(solution)/shard_map/all_to_all | solution.py:119
  400.1 5.3 copy-start.9
  400.1 5.4 copy-start.4
  400.1 184.4 %all-to-all-start.3 = ((bf16[32,2,512,128]{3,2,1,0:T(8,128)(2,1)}), bf16[32,2,512,128]{3,2,1,0:T(8,128)(2,1)}, u32[]{:S(2)}, u32[]{:S(2)}) async-start(bf16[32,2,512,128]{3,2,1,0:T(8,128)(2,1)} %bitcast.85), calls=%async_computation.3 | async-start | bytes 16777216 | tf_op jit(solution)/shard_map/all_to_all | solution.py:112
  405.2 250.2 %reduce-scatter.2.cloned.1.call-start = ((), (), s32[]{:S(2)}) async-start(), calls=%async_computation.6 | async-start | bytes 9437184 | tf_op jit(solution)/shard_map/reduce_scatter | solution.py:164
  407.4 4.5 copy-start.5
  408.3 2.0 copy-start.2
  413.0 4.7 copy-start.10
  413.1 4.5 copy-start.6
  413.1 5.3 copy-start.8
  588.9 2.1 copy-start.7
  591.0 5.6 copy-start.3
Sparse Core Ops, SparseCore 0:
  596.7 58.5 reduce-scatter.1
where the time goes:
time: 664 us; the launch traced here: 662 us
  waiting for transfers between devices  412 us (62%)
  local copies, waits for them, and re-layouts  84.6 us (13%)
  matrix products  81.1 us (12%)
  starting transfers between devices  32.7 us (5%)
  other arithmetic  23.6 us (4%)
  between operations  14.5 us (2%)
  blocking collectives  13.1 us (2%)
    all_to_all x1, waiting for transfers between devices, body(): lax.all_to_all(send_tiles, 'ctx', split_axis=0, concat_axis=0, tiled=True)  178 us
    all_to_all x1, waiting for transfers between devices, body(): lax.all_to_all(block_out.reshape(senders, item_count, BLK, HD), 'ctx', sp...  166 us
    reduce_scatter x1, waiting for transfers between devices, body(): lax.psum_scatter(jnp.dot(part_rows, out_weight, preferred_element_type=jn...  58.8 us
    dot_general x9, matrix products, partial_softmax(): jnp.dot(weights.astype(jnp.bfloat16), value_block, preferred_element_type...  54.4 us
    dot_general x9, matrix products, partial_softmax(): jnp.einsum('qd,kd->qk', query_tile, key_block, preferred_element_type=jnp...  21.1 us
    gather x8, local copies, waits for them, and re-layouts, one_slot(): key_view[slot_id // KVH, :, slot_id % KVH, :]  17.7 us
    gather x8, local copies, waits for them, and re-layouts, one_slot(): value_view[slot_id // KVH, :, slot_id % KVH, :]  17.7 us
    while x16, local copies, waits for them, and re-layouts  14.5 us
  transfers between devices with their start and end apart: 5, of which 4 were waited for; matrix products, arithmetic and copies ran while one was open for 6% of the time, Pallas kernels for 0%

commit v1 on v0

v1 whole, which is shorter than its diff:
```python
import functools
import math

import jax
import jax.numpy as jnp
from jax import lax
from jax.experimental import pallas as pl
from jax.experimental.pallas import tpu as pltpu
from jax.sharding import PartitionSpec as P

HD = 128
GROUP = 4
BLK = 512
SEL = 4
QB = 4
HEADS = 8
CHUNKS = 2
PAY = HD + 16
SCALE = math.log2(math.e) / math.sqrt(HD)
NEG = -1e30
F32 = jnp.float32
BF16 = jnp.bfloat16


def dot_nt(a, b):
    return lax.dot_general(a, b, (((1,), (1,)), ((), ())), preferred_element_type=F32)


def dot_tn(a, b):
    return lax.dot_general(a, b, (((0,), (0,)), ((), ())), preferred_element_type=F32)


def rounded_top(raw):
    return (raw * SCALE).astype(BF16).astype(F32)


def near_kernel(kv_ref, q_ref, k_ref, v_ref, acc_ref, m_ref, l_ref):
    scores = dot_nt(k_ref[...], q_ref[...])
    keys = lax.broadcasted_iota(jnp.int32, (BLK, BLK), 0)
    rows = lax.broadcasted_iota(jnp.int32, (BLK, BLK), 1)
    scores = jnp.where(keys <= rows, scores, NEG)
    top = rounded_top(jnp.max(scores, axis=0, keepdims=True))
    weights = jnp.exp2(scores * SCALE - top)
    m_ref[0] = top
    l_ref[0] = jnp.sum(weights, axis=0, keepdims=True)
    acc_ref[0] = dot_tn(v_ref[...], weights.astype(BF16))


def near(queries, span_keys, span_values, kv):
    grid_spec = pltpu.PrefetchScalarGridSpec(
        num_scalar_prefetch=1,
        grid=(QB,),
        in_specs=[
            pl.BlockSpec((BLK, HD), lambda i, kv: (i, 0)),
            pl.BlockSpec((BLK, HD), lambda i, kv: (i, kv[0])),
            pl.BlockSpec((BLK, HD), lambda i, kv: (i, kv[0])),
        ],
        out_specs=[
            pl.BlockSpec((1, HD, BLK), lambda i, kv: (i, 0, 0)),
            pl.BlockSpec((1, 1, BLK), lambda i, kv: (i, 0, 0)),
            pl.BlockSpec((1, 1, BLK), lambda i, kv: (i, 0, 0)),
        ],
    )
    return pl.pallas_call(
        near_kernel,
        grid_spec=grid_spec,
        out_shape=[
            jax.ShapeDtypeStruct((QB, HD, BLK), F32),
            jax.ShapeDtypeStruct((QB, 1, BLK), F32),
            jax.ShapeDtypeStruct((QB, 1, BLK), F32),
        ],
        cost_estimate=pl.CostEstimate(
            flops=QB * 4 * BLK * BLK * HD, bytes_accessed=4 << 20, transcendentals=QB * BLK * BLK
        ),
        name="near",
    )(kv, queries, span_keys, span_values)


def far_kernel(picks_ref, pos_ref, q_ref, *refs, first, last):
    kv_refs = refs[:SEL]
    refs = refs[SEL:]
    if not first:
        acc_in, m_in, l_in = refs[:3]
        refs = refs[3:]
    keys = jnp.concatenate([ref[0, 0] for ref in kv_refs], axis=0)
    values = jnp.concatenate([ref[0, 1] for ref in kv_refs], axis=0)
    scores = dot_nt(keys, q_ref[0])
    top = rounded_top(jnp.max(scores, axis=0, keepdims=True))
    if not first:
        top = jnp.maximum(top, m_in[0])
    weights = jnp.exp2(scores * SCALE - top)
    total = jnp.sum(weights, axis=0, keepdims=True)
    out = dot_tn(values, weights.astype(BF16))
    if not first:
        factor = jnp.exp2(m_in[0] - top)
        total = total + factor * l_in[0]
        out = out + factor * acc_in[0]
    if last:
        pack_state(refs[0], out, top, total)
    else:
        refs[0][0] = out
        refs[1][0] = top
        refs[2][0] = total


def pack_state(ref, out, top, total):
    ref[0, :HD, :] = out.astype(BF16)
    high = total.astype(BF16)
    low = (total - high.astype(F32)).astype(BF16)
    ref[0, HD:, :] = jnp.concatenate(
        [top.astype(BF16), high, low, jnp.zeros((PAY - HD - 3, BLK), BF16)], axis=0
    )


def unpack_state(ref):
    tail = ref[0, HD:, :].astype(F32)
    return ref[0, :HD, :].astype(F32), tail[0:1], tail[1:2] + tail[2:3]


def far(queries, gathered, picks, pos, state, last):
    rows = gathered.shape[2]
    units = GROUP * QB
    first = state is None

    def pick_spec(i):
        return pl.BlockSpec(
            (1, 2, rows, HD),
            lambda u, picks, pos: (picks[((u // QB) ^ pos[0]) * QB * SEL + (u % QB) * SEL + i], 0, 0, 0),
        )

    state_specs = [
        pl.BlockSpec((1, HD, BLK), lambda u, picks, pos: (u, 0, 0)),
        pl.BlockSpec((1, 1, BLK), lambda u, picks, pos: (u, 0, 0)),
        pl.BlockSpec((1, 1, BLK), lambda u, picks, pos: (u, 0, 0)),
    ]
    state_shapes = [
        jax.ShapeDtypeStruct((units, HD, BLK), F32),
        jax.ShapeDtypeStruct((units, 1, BLK), F32),
        jax.ShapeDtypeStruct((units, 1, BLK), F32),
    ]
    if last:
        out_specs = [pl.BlockSpec((1, PAY, BLK), lambda u, picks, pos: (u, 0, 0))]
        out_shapes = [jax.ShapeDtypeStruct((units, PAY, BLK), BF16)]
    else:
        out_specs, out_shapes = state_specs, state_shapes
    grid_spec = pltpu.PrefetchScalarGridSpec(
        num_scalar_prefetch=2,
        grid=(units,),
        in_specs=[
            pl.BlockSpec((1, BLK, HD), lambda u, picks, pos: ((u // QB) ^ pos[0], u % QB, 0))
        ]
        + [pick_spec(i) for i in range(SEL)]
        + ([] if first else state_specs),
        out_specs=out_specs,
    )
    result = pl.pallas_call(
        functools.partial(far_kernel, first=first, last=last),
        grid_spec=grid_spec,
        out_shape=out_shapes,
        cost_estimate=pl.CostEstimate(
            flops=units * 4 * BLK * SEL * rows * HD,
            bytes_accessed=8 << 20,
            transcendentals=units * BLK * SEL * rows,
        ),
        name="far",
    )(picks, pos, queries, *([gathered] * SEL), *(() if first else state))
    return result[0] if last else result


def merge_two_kernel(a_ref, b_ref, out_ref):
    acc_a, m_a, l_a = unpack_state(a_ref)
    acc_b, m_b, l_b = unpack_state(b_ref)
    top = jnp.maximum(m_a, m_b)
    f_a = jnp.exp2(m_a - top)
    f_b = jnp.exp2(m_b - top)
    pack_state(out_ref, f_a * acc_a + f_b * acc_b, top, f_a * l_a + f_b * l_b)


def merge_two(mine, mine_base, other, other_base):
    return pl.pallas_call(
        merge_two_kernel,
        grid=(QB,),
        in_specs=[
            pl.BlockSpec((1, PAY, BLK), lambda i: (mine_base + i, 0, 0)),
            pl.BlockSpec((1, PAY, BLK), lambda i: (other_base + i, 0, 0)),
        ],
        out_specs=pl.BlockSpec((1, PAY, BLK), lambda i: (i, 0, 0)),
        out_shape=jax.ShapeDtypeStruct((QB, PAY, BLK), BF16),
        name="merge_two",
    )(mine, other)


def merge_all_kernel(a_ref, b_ref, c_ref, acc_ref, m_ref, l_ref, out_ref):
    states = [unpack_state(a_ref), unpack_state(b_ref), unpack_state(c_ref)]
    states.append((acc_ref[0], m_ref[0], l_ref[0]))
    top = functools.reduce(jnp.maximum, [m for _, m, _ in states])
    factors = [jnp.exp2(m - top) for _, m, _ in states]
    total = sum(f * l for f, (_, _, l) in zip(factors, states))
    out = sum(f * acc for f, (acc, _, _) in zip(factors, states))
    out_ref[...] = (out / total).T.astype(BF16)


def merge_all(mine, core_part, chip_part, near_state):
    return pl.pallas_call(
        merge_all_kernel,
        grid=(QB,),
        in_specs=[
            pl.BlockSpec((1, PAY, BLK), lambda i: (i, 0, 0)),
            pl.BlockSpec((1, PAY, BLK), lambda i: (i, 0, 0)),
            pl.BlockSpec((1, PAY, BLK), lambda i: (i, 0, 0)),
            pl.BlockSpec((1, HD, BLK), lambda i: (i, 0, 0)),
            pl.BlockSpec((1, 1, BLK), lambda i: (i, 0, 0)),
            pl.BlockSpec((1, 1, BLK), lambda i: (i, 0, 0)),
        ],
        out_specs=pl.BlockSpec((BLK, HD), lambda i: (i, 0)),
        out_shape=jax.ShapeDtypeStruct((QB * BLK, HD), BF16),
        name="merge_all",
    )(mine, core_part, chip_part, *near_state)


def project_kernel(a_ref, w_ref, out_ref):
    rows = jnp.concatenate([a_ref[i] for i in range(HEADS)], axis=1)
    out_ref[...] = jnp.dot(rows, w_ref[...], preferred_element_type=F32).astype(BF16)


def project(parts, weight):
    rows = parts.shape[1]
    width = weight.shape[1]
    tile = 512
    return pl.pallas_call(
        project_kernel,
        grid=(width // tile,),
        in_specs=[
            pl.BlockSpec((HEADS, rows, HD), lambda i: (0, 0, 0)),
            pl.BlockSpec((HEADS * HD, tile), lambda i: (0, i)),
        ],
        out_specs=pl.BlockSpec((rows, tile), lambda i: (0, i)),
        out_shape=jax.ShapeDtypeStruct((rows, width), BF16),
        name="project",
    )(parts, weight)


def body(queries, block_picks, span_keys, span_values, cache_keys, cache_values, out_weight):
    head = lax.axis_index("head")
    part = head % GROUP
    kv = head // GROUP
    blocks = cache_keys.shape[0] // BLK
    share = BLK // GROUP
    rows = share // CHUNKS
    groups = [list(range(g, g + GROUP)) for g in range(0, HEADS, GROUP)]

    def cut(cache, chunk):
        view = cache.reshape(blocks, BLK, cache.shape[1])
        return lax.dynamic_slice(
            view, (0, part * share + chunk * rows, kv * HD), (blocks, rows, HD)
        )

    group_queries = lax.all_gather(queries, "head", axis_index_groups=groups)
    group_picks = lax.all_gather(block_picks, "head", axis_index_groups=groups).reshape(-1)
    gathered = []
    for chunk in range(CHUNKS):
        piece = jnp.stack([cut(cache_keys, chunk), cut(cache_values, chunk)], axis=1)
        gathered.append(lax.all_gather(piece, "ctx", axis=0, tiled=True))
    weight = lax.all_gather(out_weight, "head", axis=0, tiled=True)

    near_state = near(queries, span_keys, span_values, kv[None])
    state = None
    for chunk in range(CHUNKS):
        state = far(
            group_queries, gathered[chunk], group_picks, part[None], state, chunk == CHUNKS - 1
        )

    core_perm = [(h, h ^ 1) for h in range(HEADS)]
    chip_perm = [(h, h ^ 2) for h in range(HEADS)]
    for_chip = lax.ppermute(state[3 * QB :], "head", core_perm)
    for_core = lax.ppermute(state[QB : 2 * QB], "head", core_perm)
    chip_part = lax.ppermute(merge_two(state, 2 * QB, for_chip, 0), "head", chip_perm)
    attention = merge_all(state, for_core, chip_part, near_state)

    share_rows = attention.shape[0] // HEADS
    parts = lax.all_to_all(
        attention.reshape(HEADS, share_rows, HD), "head", split_axis=0, concat_axis=0, tiled=True
    )
    return attention, project(parts, weight)


def solution(mesh):
    placed = (
        P("ctx", "head"),
        P("ctx", "head", None),
        P("ctx", None),
        P("ctx", None),
        P("ctx", None),
        P("ctx", None),
        P("head", None),
    )
    return jax.shard_map(
        body,
        mesh=mesh,
        in_specs=placed,
        out_specs=(P("ctx", "head"), P(("ctx", "head"), None)),
        check_vma=False,
    )
```

time: 664 us -> 322 us (0.48)
  waiting for transfers between devices: 412 us -> 236 us
  matrix products: 81.1 us -> 0 us
  local copies, waits for them, and re-layouts: 84.6 us -> 6.06 us
  Pallas kernels: 0 us -> 47.2 us
  starting transfers between devices: 32.7 us -> 7.28 us
  other arithmetic: 23.6 us -> 2.11 us
    all_to_all x4 -> x1, waiting for transfers between devices: 354 us -> 9.48 us  [body(): lax.all_to_all(attention.reshape(HEADS, share_rows, HD), 'head', split_ax...]
    all_gather x0 -> x4, waiting for transfers between devices: none -> 210 us  [the longest x2 185 us: body(): gathered.append(lax.all_gather(piece, 'ctx', axis=0, tiled=True))]
    dot_general x19 -> x0, matrix products: 81.1 us -> none  [the longest x9 54.4 us: partial_softmax(): jnp.dot(weights.astype(jnp.bfloat16), value_block, preferred_element_type...]
    reduce_scatter x1 -> x0, waiting for transfers between devices: 58.8 us -> none  [body(): lax.psum_scatter(jnp.dot(part_rows, out_weight, preferred_element_type=jn...]
    gather x27 -> x0, local copies, waits for them, and re-layouts: 51.3 us -> none  [the longest x8 17.7 us: one_slot(): key_view[slot_id // KVH, :, slot_id % KVH, :]]
    pallas_call x0 -> x6, Pallas kernels: none -> 47.2 us  [the longest x2 30.1 us: far(): pl.pallas_call(functools.partial(far_kernel, first=first, last=last), gri...]
    all_to_all x4 -> x1, starting transfers between devices: 32.5 us -> 4.64 us  [body(): lax.all_to_all(attention.reshape(HEADS, share_rows, HD), 'head', split_ax...]
    while x18 -> x0, local copies, waits for them, and re-layouts: 22.1 us -> none
  transfers between devices with their start and end apart: 5 -> 8, of which waited for: 4 -> 6; matrix products, arithmetic and copies ran while one was open for 6% -> 2% of each run, Pallas kernels for 0% -> 13%
where the time goes in v1:
time: 322 us; the launch traced here: 321 us
  waiting for transfers between devices  236 us (73%)
  Pallas kernels  47.2 us (15%)
  between operations  13.9 us (4%)
  blocking collectives  8.2 us (3%)
  starting transfers between devices  7.28 us (2%)
  local copies, waits for them, and re-layouts  6.06 us (2%)
    all_gather x2, waiting for transfers between devices, body(): gathered.append(lax.all_gather(piece, 'ctx', axis=0, tiled=True))  185 us
    pallas_call x2, Pallas kernels, far(): pl.pallas_call(functools.partial(far_kernel, first=first, last=last), gri...  30.1 us
    all_gather x1, waiting for transfers between devices, body(): group_queries = lax.all_gather(queries, 'head', axis_index_groups=groups)  24.5 us
    ppermute x1, waiting for transfers between devices, body(): lax.ppermute(merge_two(state, 2 * QB, for_chip, 0), 'head', chip_perm)  14.4 us
    all_to_all x1, waiting for transfers between devices, body(): lax.all_to_all(attention.reshape(HEADS, share_rows, HD), 'head', split_ax...  9.48 us
    all_gather x1, blocking collectives, body(): lax.all_gather(block_picks, 'head', axis_index_groups=groups).reshape(-1)  8.2 us
  transfers between devices with their start and end apart: 8, of which 6 were waited for; matrix products, arithmetic and copies ran while one was open for 2% of the time, Pallas kernels for 13%

profile of v1, /device:TPU:1, one launch (start us, length us, event | category | flops | bytes accessed | tf_op | source)
XLA Modules:
  0.0 321.1 jit_solution(6748775270098794565)
XLA Ops:
  7.2 0.7 all-gather.13.cloned.1.call-update
  8.0 1.1 dynamic-slice_bitcast_fusion
  9.1 0.7 pad_maximum_fusion.1
  9.9 0.7 pad_maximum_fusion
  11.3 8.2 %all-gather = s32[16,1,4]{2,1,0:T(1,128)S(1)} all-gather(s32[4,1,4]{2,1,0:T(1,128)S(1)} %copy-done.4), channel_id=2, replica_groups={{0,1,2,3},{4,5,6,7},{8,9,10,11},{12,13,14,15},{16,17,18,19},{20,21,22,2..., dimensions={0}, use_global_device_ids=true | all-gather | bytes 320 | tf_op jit(solution)/shard_map/all_gather | solution.py:259
  21.3 24.5 %all-gather.13.cloned.1.call-done = bf16[8192,128]{1,0:T(8,128)(2,1)} async-done(((bf16[2048,128]{1,0:T(8,128)(2,1)}), bf16[8192,128]{1,0:T(8,128)(2,1)}) %all-gather.13.cloned.1.call-update) | async-done | bytes 2097168 | tf_op jit(solution)/shard_map/all_gather | solution.py:258
  45.7 101.6 %all-gather.9.cloned.1.call-done.refs_0_.refs_1_.refs_2_.refs_3_ = bf16[256,2,64,128]{3,2,1,0:T(8,128)(2,1)} async-done(((bf16[8,2,64,128]{3,2,1,0:T(8,128)(2,1)}), bf16[256,2,64,128]{3,2,1,0:T(8,128)(2,1)}) %all-gather.9.cloned.1.call-update) | async-done | bytes 8388624 | tf_op jit(solution)/shard_map/all_gather | solution.py:263
  147.3 14.8 %far.2 = (f32[16,128,512]{2,1,0:T(8,128)}, f32[16,1,512]{2,1,0:T(1,128)}, f32[16,1,512]{2,1,0:T(1,128)}) custom-call(s32[64]{0:T(128)} %reshape.18.picks_ref, s32[1]{0:T(128)} %bitcast.pos_ref, bf16[4,2048,128]{2,1,0:T(8,128)(2,1)} %bitcast.14, bf16[256,2,64,128]{3,2,1,0:T(8,128)(2,1)} %all-gather.9.cloned.1.call-done.refs_0_.refs_1_.refs_2_.refs_3_, ...), custom_call_target="tpu_custom_call" | custom-call | flops 1073741824 | bytes 8388608 | tf_op jit(solution)/shard_map/far/pallas_call | solution.py:156
  162.1 83.8 %all-gather.7.cloned.1.call-done.refs_0_.refs_1_.refs_2_.refs_3_ = bf16[256,2,64,128]{3,2,1,0:T(8,128)(2,1)} async-done(((bf16[8,2,64,128]{3,2,1,0:T(8,128)(2,1)}), bf16[256,2,64,128]{3,2,1,0:T(8,128)(2,1)}) %all-gather.7.cloned.1.call-update) | async-done | bytes 8388624 | tf_op jit(solution)/shard_map/all_gather | solution.py:263
  245.9 15.3 %far.3.a_ref = bf16[16,144,512]{2,1,0:T(8,128)(2,1)} custom-call(s32[64]{0:T(128)} %reshape.18.picks_ref, s32[1]{0:T(128)} %bitcast.pos_ref, bf16[4,2048,128]{2,1,0:T(8,128)(2,1)} %bitcast.15, bf16[256,2,64,128]{3,2,1,0:T(8,128)(2,1)} %all-gather.7.cloned.1.call-done.refs_0_.refs_1_.refs_2_.refs_3_, ...), custom_call_target="tpu_custom_call" | custom-call | flops 1073741824 | bytes 8388608 | tf_op jit(solution)/shard_map/far/pallas_call | solution.py:156
  261.2 1.3 fusion
  262.6 1.2 collective-permute-start.1
  263.9 1.5 collective-permute-done.1.b_ref
  265.4 0.8 copy-done.3
  266.2 3.5 %merge_two.1 = bf16[4,144,512]{2,1,0:T(8,128)(2,1)} custom-call(bf16[16,144,512]{2,1,0:T(8,128)(2,1)} %far.3.a_ref, bf16[4,144,512]{2,1,0:T(8,128)(2,1)} %copy-done.3), custom_call_target="tpu_custom_call" | custom-call | tf_op jit(solution)/shard_map/merge_two/pallas_call | solution.py:180
  269.7 1.2 collective-permute-start.2
  270.9 4.7 %near.1 = (f32[4,128,512]{2,1,0:T(8,128)}, f32[4,1,512]{2,1,0:T(1,128)}, f32[4,1,512]{2,1,0:T(1,128)}) custom-call(s32[1]{0:T(128)} %bitcast.8.kv_ref, bf16[2048,128]{1,0:T(8,128)(2,1)} %q_ref.1, bf16[2048,256]{1,0:T(8,128)(2,1)} %k_ref.1, bf16[2048,256]{1,0:T(8,128)(2,1)} %v_ref.1), custom_call_target="tpu_custom_call" | custom-call | flops 536870912 | bytes 4194304 | tf_op jit(solution)/shard_map/near/pallas_call | solution.py:64
  275.6 14.4 %collective-permute-done.2.c_ref = bf16[4,144,512]{2,1,0:T(8,128)(2,1)S(1)} collective-permute-done((bf16[4,144,512]{2,1,0:T(8,128)(2,1)}, bf16[4,144,512]{2,1,0:T(8,128)(2,1)S(1)}, u32[]{:S(2)}, u32[]{:S(2)}) %collective-permute-start.2) | collective-permute-done | bytes 589856 | tf_op jit(solution)/shard_map/ppermute | solution.py:277
  289.9 0.8 copy-done.2
  290.8 4.0 %merge_all.1 = bf16[2048,128]{1,0:T(8,128)(2,1)} custom-call(bf16[16,144,512]{2,1,0:T(8,128)(2,1)} %far.3.a_ref, bf16[4,144,512]{2,1,0:T(8,128)(2,1)} %copy-done.1, bf16[4,144,512]{2,1,0:T(8,128)(2,1)} %copy-done.2, f32[4,128,512]{2,1,0:T(8,128)} %get-tuple-element.11.acc_ref, f32[4,1,512]{2,1,0:T(1,128)} %get-tuple-element.12.m_ref, ...), custom_call_target="tpu_custom_call" | custom-call | tf_op jit(solution)/shard_map/merge_all/pallas_call | solution.py:204
  294.7 4.6 %all-to-all-start = ((bf16[8,256,128]{2,1,0:T(8,128)(2,1)}), bf16[8,256,128]{2,1,0:T(8,128)(2,1)S(1)}, u32[]{:S(2)}, u32[]{:S(2)}) async-start(bf16[8,256,128]{2,1,0:T(8,128)(2,1)} %bitcast.16), calls=%async_computation | async-start | bytes 1048576 | tf_op jit(solution)/shard_map/all_to_all | solution.py:281
  299.4 9.5 %all-to-all-done.a_ref = bf16[8,256,128]{2,1,0:T(8,128)(2,1)S(1)} async-done(((bf16[8,256,128]{2,1,0:T(8,128)(2,1)}), bf16[8,256,128]{2,1,0:T(8,128)(2,1)S(1)}, u32[]{:S(2)}, u32[]{:S(2)}) %all-to-all-start) | async-done | bytes 524320 | tf_op jit(solution)/shard_map/all_to_all | solution.py:281
  308.9 0.8 copy-done
  309.7 4.9 %project.1 = bf16[256,2048]{1,0:T(8,128)(2,1)} custom-call(bf16[8,256,128]{2,1,0:T(8,128)(2,1)} %copy-done, bf16[1024,2048]{1,0:T(8,128)(2,1)} %all-gather.11.cloned.1.call-done.w_ref), custom_call_target="tpu_custom_call" | custom-call | tf_op jit(solution)/shard_map/project/pallas_call | solution.py:230
  (20 shorter events, 2.6 us)
Async XLA Ops:
  7.2 4.1 %copy-start.4 = (s32[4,1,4]{2,1,0:T(1,128)S(1)}, s32[4,1,4]{2,1,0:T(1,128)}, u32[]{:S(2)}) copy-start(s32[4,1,4]{2,1,0:T(1,128)} %param.8) | copy-start | bytes 196
  7.2 38.6 %all-gather.13.cloned.1.call-start = ((), (), s32[]{:S(2)}) async-start(), calls=%async_computation.4 | async-start | bytes 2621440 | tf_op jit(solution)/shard_map/all_gather | solution.py:258
  7.9 139.4 %all-gather.9.cloned.1.call-start = ((), (), s32[]{:S(2)}) async-start(), calls=%async_computation.2 | async-start | bytes 8650752 | tf_op jit(solution)/shard_map/all_gather | solution.py:263
  9.9 236.0 %all-gather.7.cloned.1.call-start = ((), (), s32[]{:S(2)}) async-start(), calls=%async_computation.1 | async-start | bytes 8650752 | tf_op jit(solution)/shard_map/all_gather | solution.py:263
  10.7 288.7 %all-gather.11.cloned.1.call-start = ((), (), s32[]{:S(2)}) async-start(), calls=%async_computation.3 | async-start | bytes 4718592 | tf_op jit(solution)/shard_map/all_gather | solution.py:264
  262.6 2.8 collective-permute-start.1
  263.8 11.8 %collective-permute-start = (bf16[4,144,512]{2,1,0:T(8,128)(2,1)S(1)}, bf16[4,144,512]{2,1,0:T(8,128)(2,1)S(1)}, u32[]{:S(2)}, u32[]{:S(2)}) collective-permute-start(bf16[4,144,512]{2,1,0:T(8,128)(2,1)S(1)} %get-tuple-element.15), channel_id=1, source_target_pairs={{0,1},{1,0},{2,3},{3,2},{4,5},{5,4},{6,7},{7,6},{8,9},{9,8},{10,11... | collective-permute-start | bytes 1769480 | tf_op jit(solution)/shard_map/ppermute | solution.py:276
  265.4 0.8 copy-start.3
  269.7 20.3 %collective-permute-start.2 = (bf16[4,144,512]{2,1,0:T(8,128)(2,1)}, bf16[4,144,512]{2,1,0:T(8,128)(2,1)S(1)}, u32[]{:S(2)}, u32[]{:S(2)}) collective-permute-start(bf16[4,144,512]{2,1,0:T(8,128)(2,1)} %merge_two.1), channel_id=1, source_target_pairs={{0,2},{1,3},{2,0},{3,1},{4,6},{5,7},{6,4},{7,5},{8,10},{9,11},{10,... | collective-permute-start | bytes 1769480 | tf_op jit(solution)/shard_map/ppermute | solution.py:277
  275.6 14.4 %copy-start.1 = (bf16[4,144,512]{2,1,0:T(8,128)(2,1)}, bf16[4,144,512]{2,1,0:T(8,128)(2,1)S(1)}, u32[]{:S(2)}) copy-start(bf16[4,144,512]{2,1,0:T(8,128)(2,1)S(1)} %collective-permute-done.b_ref) | copy-start | bytes 1769476
  289.9 0.8 copy-start.2
  294.7 14.1 %all-to-all-start = ((bf16[8,256,128]{2,1,0:T(8,128)(2,1)}), bf16[8,256,128]{2,1,0:T(8,128)(2,1)S(1)}, u32[]{:S(2)}, u32[]{:S(2)}) async-start(bf16[8,256,128]{2,1,0:T(8,128)(2,1)} %bitcast.16), calls=%async_computation | async-start | bytes 1048576 | tf_op jit(solution)/shard_map/all_to_all | solution.py:281
  308.9 0.8 copy-start
Sparse Core Ops, SparseCore 0:
  9.8 35.8 all-gather.12
  48.9 98.3 all-gather.8
  150.5 95.4 all-gather.6
  247.6 36.6 all-gather.10

commit v2 on v1

v2 whole, which is shorter than its diff:
```python
import functools
import math

import jax
import jax.numpy as jnp
from jax import lax
from jax.experimental import pallas as pl
from jax.experimental.pallas import tpu as pltpu
from jax.sharding import PartitionSpec as P

HD = 128
GROUP = 4
BLK = 512
SEL = 4
QB = 4
BLOCKS = 8
NX = 4
NZ = 8
TAIL = 16
SCALE = math.log2(math.e) / math.sqrt(HD)
NEG = -1e30
F32 = jnp.float32
BF16 = jnp.bfloat16
SPLIT = (8, 4, 4)
VMEM_BYTES = 48 << 20


def dot_nt(a, b):
    return lax.dot_general(a, b, (((1,), (1,)), ((), ())), preferred_element_type=F32)


def dot_tn(a, b):
    return lax.dot_general(a, b, (((0,), (0,)), ((), ())), preferred_element_type=F32)


def rounded_top(raw):
    return (raw * SCALE).astype(BF16).astype(F32)


def near_kernel(kv_ref, q_ref, k_ref, v_ref, acc_ref, m_ref, l_ref):
    scores = dot_nt(k_ref[...], q_ref[...])
    keys = lax.broadcasted_iota(jnp.int32, (BLK, BLK), 0)
    rows = lax.broadcasted_iota(jnp.int32, (BLK, BLK), 1)
    scores = jnp.where(keys <= rows, scores, NEG)
    top = rounded_top(jnp.max(scores, axis=0, keepdims=True))
    weights = jnp.exp2(scores * SCALE - top)
    m_ref[0] = top
    l_ref[0] = jnp.sum(weights, axis=0, keepdims=True)
    acc_ref[0] = dot_tn(v_ref[...], weights.astype(BF16))


def state_shapes():
    return [
        jax.ShapeDtypeStruct((QB, HD, BLK), F32),
        jax.ShapeDtypeStruct((QB, 1, BLK), F32),
        jax.ShapeDtypeStruct((QB, 1, BLK), F32),
    ]


def near(queries, span_keys, span_values, kv):
    grid_spec = pltpu.PrefetchScalarGridSpec(
        num_scalar_prefetch=1,
        grid=(QB,),
        in_specs=[
            pl.BlockSpec((BLK, HD), lambda i, kv: (i, 0)),
            pl.BlockSpec((BLK, HD), lambda i, kv: (i, kv[0])),
            pl.BlockSpec((BLK, HD), lambda i, kv: (i, kv[0])),
        ],
        out_specs=[
            pl.BlockSpec((1, HD, BLK), lambda i, kv: (i, 0, 0)),
            pl.BlockSpec((1, 1, BLK), lambda i, kv: (i, 0, 0)),
            pl.BlockSpec((1, 1, BLK), lambda i, kv: (i, 0, 0)),
        ],
    )
    return pl.pallas_call(
        near_kernel,
        grid_spec=grid_spec,
        out_shape=state_shapes(),
        cost_estimate=pl.CostEstimate(
            flops=QB * 4 * BLK * BLK * HD, bytes_accessed=4 << 20, transcendentals=QB * BLK * BLK
        ),
        name="near",
    )(kv, queries, span_keys, span_values)


def pack_state(ref, i, out, top, total):
    ref[i, :HD, :] = out.astype(BF16)
    high = total.astype(BF16)
    low = (total - high.astype(F32)).astype(BF16)
    ref[i, HD:, :] = jnp.concatenate(
        [top.astype(BF16), high, low, jnp.zeros((TAIL - 3, out.shape[1]), BF16)], axis=0
    )


def unpack_state(ref, i):
    tail = ref[i, HD:, :].astype(F32)
    return ref[i, :HD, :].astype(F32), tail[0:1], tail[1:2] + tail[2:3]


def far_kernel(where_ref, *refs, counts):
    q_refs, refs = refs[:2], refs[2:]
    sources = []
    for count in counts:
        sources.append(refs[:count])
        refs = refs[count:]
    out_refs, refs = refs[:2], refs[2:]
    buffers, sems = refs[:-1], refs[-1]
    parts = len(counts)

    def fetch(pick, carry):
        for part in range(parts):
            array = where_ref[pick, 2 * part]
            index = where_ref[pick, 2 * part + 1]
            for number, source in enumerate(sources[part]):

                def start(source=source, part=part, index=index):
                    pltpu.make_async_copy(
                        source.at[index], buffers[part].at[pick], sems.at[pick // SEL, part]
                    ).start()

                if counts[part] == 1:
                    start()
                else:
                    pl.when(array == number)(start)
        return carry

    lax.fori_loop(0, 2 * QB * SEL, fetch, 0)

    def unit(row, q_ref, out_ref, i):
        for part in range(parts):
            held = buffers[part].at[pl.ds(row * SEL, SEL)]
            pltpu.make_async_copy(held, held, sems.at[row, part]).wait()

        def joined(which):
            return jnp.concatenate(
                [buffers[part][row * SEL + j, which] for part in range(parts) for j in range(SEL)],
                axis=0,
            )

        scores = dot_nt(joined(0), q_ref[pl.ds(i * BLK, BLK), :])
        top = rounded_top(jnp.max(scores, axis=0, keepdims=True))
        weights = jnp.exp2(scores * SCALE - top)
        total = jnp.sum(weights, axis=0, keepdims=True)
        pack_state(out_ref, i, dot_tn(joined(1), weights.astype(BF16)), top, total)

    for half in range(2):

        def pair(step, carry, half=half):
            for k in range(2):
                i = 2 * step + k
                unit(half * QB + i, q_refs[half], out_refs[half], i)
            return carry

        lax.fori_loop(0, QB // 2, pair, 0)


def far(where, queries, parts):
    pay = HD + TAIL
    vmem = pl.BlockSpec(memory_space=pltpu.VMEM)
    arrays = [array for part in parts for array in part]
    return pl.pallas_call(
        functools.partial(far_kernel, counts=tuple(len(part) for part in parts)),
        in_specs=[pl.BlockSpec(memory_space=pltpu.SMEM)]
        + [vmem] * 2
        + [pl.BlockSpec(memory_space=pl.ANY)] * len(arrays),
        out_specs=[vmem] * 2,
        out_shape=[jax.ShapeDtypeStruct((QB, pay, BLK), BF16)] * 2,
        scratch_shapes=[
            pltpu.VMEM((2 * QB * SEL,) + part[0].shape[1:], BF16) for part in parts
        ]
        + [pltpu.SemaphoreType.DMA((2 * QB, len(parts)))],
        compiler_params=pltpu.CompilerParams(vmem_limit_bytes=VMEM_BYTES),
        cost_estimate=pl.CostEstimate(
            flops=2 * QB * 4 * BLK * BLK * HD,
            bytes_accessed=5 << 20,
            transcendentals=2 * QB * BLK * BLK,
        ),
        name="far",
    )(where, *queries, *arrays)


def merge_two_kernel(a_ref, b_ref, *out_refs):
    per = QB // len(out_refs)
    for i in range(QB):
        acc_a, m_a, l_a = unpack_state(a_ref, i)
        acc_b, m_b, l_b = unpack_state(b_ref, i)
        top = jnp.maximum(m_a, m_b)
        f_a = jnp.exp2(m_a - top)
        f_b = jnp.exp2(m_b - top)
        pack_state(
            out_refs[i // per], i % per, f_a * acc_a + f_b * acc_b, top, f_a * l_a + f_b * l_b
        )


def merge_two(mine, other, pieces):
    vmem = pl.BlockSpec(memory_space=pltpu.VMEM)
    shape = (QB // pieces,) + mine.shape[1:]
    return pl.pallas_call(
        merge_two_kernel,
        in_specs=[vmem] * 2,
        out_specs=[vmem] * pieces,
        out_shape=[jax.ShapeDtypeStruct(shape, BF16)] * pieces,
        name="merge_two",
    )(mine, other)


def merge_here_kernel(a_ref, b_ref, acc_ref, m_ref, l_ref, acc_out, m_out, l_out):
    for i in range(QB):
        states = [unpack_state(a_ref, i), unpack_state(b_ref, i)]
        states.append((acc_ref[i], m_ref[i], l_ref[i]))
        top = functools.reduce(jnp.maximum, [m for _, m, _ in states])
        factors = [jnp.exp2(m - top) for _, m, _ in states]
        m_out[i] = top
        l_out[i] = sum(f * l for f, (_, _, l) in zip(factors, states))
        acc_out[i] = sum(f * acc for f, (acc, _, _) in zip(factors, states))


def merge_here(mine, core_part, near_state):
    vmem = pl.BlockSpec(memory_space=pltpu.VMEM)
    return pl.pallas_call(
        merge_here_kernel,
        in_specs=[vmem] * 5,
        out_specs=[vmem] * 3,
        out_shape=state_shapes(),
        name="merge_here",
    )(mine, core_part, *near_state)


def merge_last_kernel(acc_ref, m_ref, l_ref, *refs):
    chip_refs, out_ref = refs[:-1], refs[-1]
    per = QB // len(chip_refs)
    for i in range(QB):
        acc, m, l = unpack_state(chip_refs[i // per], i % per)
        top = jnp.maximum(m, m_ref[i])
        f_far = jnp.exp2(m - top)
        f_here = jnp.exp2(m_ref[i] - top)
        total = f_far * l + f_here * l_ref[i]
        out = (f_far * acc + f_here * acc_ref[i]) / total
        out_ref[i * BLK : (i + 1) * BLK, :] = out.T.astype(BF16)


def merge_last(here, chip_parts):
    vmem = pl.BlockSpec(memory_space=pltpu.VMEM)
    return pl.pallas_call(
        merge_last_kernel,
        in_specs=[vmem] * (3 + len(chip_parts)),
        out_specs=vmem,
        out_shape=jax.ShapeDtypeStruct((QB * BLK, HD), BF16),
        name="merge_last",
    )(*here, *chip_parts)


def project_kernel(head_ref, a_ref, *refs):
    w_refs, out_ref = refs[:-1], refs[-1]
    rows = jnp.concatenate([a_ref[head_ref[0] ^ i] for i in range(len(w_refs))], axis=1)
    weight = jnp.concatenate([w_ref[...] for w_ref in w_refs], axis=0)
    out_ref[...] = jnp.dot(rows, weight, preferred_element_type=F32).astype(BF16)


def project(head, parts, weights):
    heads, rows, _ = parts.shape
    width = weights[0].shape[1]
    tile = 512
    grid_spec = pltpu.PrefetchScalarGridSpec(
        num_scalar_prefetch=1,
        grid=(width // tile,),
        in_specs=[pl.BlockSpec((heads, rows, HD), lambda i, head: (0, 0, 0))]
        + [pl.BlockSpec((HD, tile), lambda i, head: (0, i))] * heads,
        out_specs=pl.BlockSpec((rows, tile), lambda i, head: (0, i)),
    )
    return pl.pallas_call(
        project_kernel,
        grid_spec=grid_spec,
        out_shape=jax.ShapeDtypeStruct((rows, width), BF16),
        name="project",
    )(head, parts, *weights)


def shift(array, dz, dx):
    pairs = []
    for z in range(NZ):
        for x in range(NX):
            pairs.append((z * NX + x, (z + dz) % NZ * NX + (x + dx) % NX))
    return lax.ppermute(array, "ctx", pairs)


def swap(array, bits):
    return lax.ppermute(array, "head", [(h, h ^ bits) for h in range(lax.axis_size("head"))])


def ring_four(piece):
    half = piece.shape[0] // 2
    below = shift(piece, 0, 1)
    above = shift(piece, 0, -1)
    return [piece, below, above, shift(below[:half], 0, 1), shift(above[half:], 0, -1)]


def ring_eight(piece):
    half = piece.shape[0] // 2
    result = [piece]
    below = above = piece
    for _ in range(3):
        below = shift(below, 1, 0)
        above = shift(above, -1, 0)
        result += [below, above]
    return result + [shift(below[:half], 1, 0), shift(above[half:], -1, 0)]


def body(queries, block_picks, span_keys, span_values, cache_keys, cache_values, out_weight):
    heads = lax.axis_size("head")
    head = lax.axis_index("head")
    ctx = lax.axis_index("ctx")
    part = head % GROUP
    kv = head // GROUP
    share = BLK // GROUP

    def cut(cache, first, rows):
        view = cache.reshape(BLOCKS, BLK, cache.shape[1])
        return lax.dynamic_slice(view, (0, part * share + first, kv * HD), (BLOCKS, rows, HD))

    pieces = []
    first = 0
    for sixteenths in SPLIT:
        rows = share * sixteenths // 16
        pieces.append(
            jnp.stack([cut(cache_keys, first, rows), cut(cache_values, first, rows)], axis=1)
        )
        first += rows
    gathered = lax.all_gather(pieces[0], "ctx", axis=0, tiled=True)
    by_x = jnp.concatenate(ring_four(pieces[1]), axis=0)
    by_z = jnp.concatenate(ring_eight(pieces[2]), axis=0)
    ring_a = ring_eight(by_x)
    ring_b = ring_four(by_z)
    ring_a = [jnp.concatenate(ring_a[:5], axis=0)] + ring_a[5:]

    swapped = swap(queries, 2)
    group_queries = [queries, swap(queries, 1), swapped, swap(swapped, 1)]
    group_picks = jnp.stack([block_picks] + [swap(block_picks, r) for r in range(1, GROUP)])
    picks = group_picks.reshape(GROUP, QB * SEL)
    owner, local = picks // BLOCKS, picks % BLOCKS
    dz = (owner // NX - ctx // NX) % NZ
    dx = (owner % NX - ctx % NX) % NX
    order_x = jnp.where(dx == 0, 0, jnp.where(dx == 3, 1, jnp.where(dx == 1, 2, 3)))
    order_z = jnp.where(dz == 0, 0, jnp.where(dz > NZ // 2, 2 * (NZ - dz) - 1, 2 * dz))
    order_z = jnp.where(dz == NZ // 2, NZ - 1, order_z)
    place_a = order_x * BLOCKS + local
    width_a = NX * BLOCKS
    upper_a = place_a >= width_a // 2
    array_a = jnp.where(
        order_z < 5, 0, jnp.where(order_z < 7, order_z - 4, jnp.where(upper_a, 4, 3))
    )
    index_a = jnp.where(
        order_z < 5,
        order_z * width_a + place_a,
        jnp.where((order_z == 7) & upper_a, place_a - width_a // 2, place_a),
    )
    place_b = order_z * BLOCKS + local
    width_b = NZ * BLOCKS
    upper_b = place_b >= width_b // 2
    array_b = jnp.where(order_x < 3, order_x, jnp.where(upper_b, 4, 3))
    index_b = jnp.where((order_x == 3) & upper_b, place_b - width_b // 2, place_b)
    where = jnp.stack(
        [jnp.zeros_like(picks), picks, array_a, index_a, array_b, index_b], axis=-1
    ).astype(jnp.int32)

    weights = [out_weight] + [None] * (heads - 1)
    for bits in range(2, heads, 2):
        weights[bits] = swap(out_weight, bits)
    for bits in range(0, heads, 2):
        weights[bits + 1] = swap(weights[bits], 1)

    near_state = near(queries, span_keys, span_values, kv[None])

    def far_of(first, second):
        return far(
            jnp.concatenate([where[first], where[second]], axis=0),
            [group_queries[first], group_queries[second]],
            [[gathered], ring_a, ring_b],
        )

    far_corner, far_chip = far_of(3, 2)
    for_chip = merge_two(far_chip, swap(far_corner, 1), QB)
    chip_parts = [swap(piece, 2) for piece in for_chip]
    far_core, far_own = far_of(1, 0)
    here = merge_here(far_own, swap(far_core, 1), near_state)
    attention = merge_last(here, chip_parts)

    share_rows = attention.shape[0] // heads
    parts = lax.all_to_all(
        attention.reshape(heads, share_rows, HD), "head", split_axis=0, concat_axis=0, tiled=True
    )
    return attention, project(head[None], parts, weights)


def solution(mesh):
    placed = (
        P("ctx", "head"),
        P("ctx", "head", None),
        P("ctx", None),
        P("ctx", None),
        P("ctx", None),
        P("ctx", None),
        P("head", None),
    )
    return jax.shard_map(
        body,
        mesh=mesh,
        in_specs=placed,
        out_specs=(P("ctx", "head"), P(("ctx", "head"), None)),
        check_vma=False,
    )
```

time: 322 us -> 223 us (0.69)
  waiting for transfers between devices: 236 us -> 70.9 us
  starting transfers between devices: 7.28 us -> 71.5 us
  local copies, waits for them, and re-layouts: 6.06 us -> 24.1 us
  Pallas kernels: 47.2 us -> 36.6 us
  blocking collectives: 8.2 us -> 0 us
    all_gather x4 -> x1, waiting for transfers between devices: 210 us -> 4.2 us  [body(): gathered = lax.all_gather(pieces[0], 'ctx', axis=0, tiled=True)]
    ppermute x3 -> x43, starting transfers between devices: 2.47 us -> 67.2 us  [the longest x24 37.5 us: shift(): return lax.ppermute(array, 'ctx', pairs)]
    ppermute x3 -> x43, waiting for transfers between devices: 15.9 us -> 57.3 us  [the longest x24 47.5 us: shift(): return lax.ppermute(array, 'ctx', pairs)]
    unnamed x10 -> x57, local copies, waits for them, and re-layouts: 2.44 us -> 16.2 us
    pallas_call x6 -> x7, Pallas kernels: 47.2 us -> 36.6 us  [the longest x2 19 us: far(): pl.pallas_call(functools.partial(far_kernel, counts=tuple((len(part) for...]
    all_gather x1 -> x0, blocking collectives: 8.2 us -> none  [body(): lax.all_gather(block_picks, 'head', axis_index_groups=groups).reshape(-1)]
  transfers between devices with their start and end apart: 8 -> 45, of which waited for: 6 -> 12; matrix products, arithmetic and copies ran while one was open for 2% -> 9% of each run, Pallas kernels for 13% -> 14%
where the time goes in v2:
time: 223 us; the launch traced here: 222 us
  starting transfers between devices  71.5 us (32%)
  waiting for transfers between devices  70.9 us (32%)
  Pallas kernels  36.6 us (16%)
  local copies, waits for them, and re-layouts  24.1 us (11%)
  between operations  14.5 us (7%)
  other arithmetic  4.41 us (2%)
    ppermute x24, waiting for transfers between devices, shift(): return lax.ppermute(array, 'ctx', pairs)  47.5 us
    ppermute x24, starting transfers between devices, shift(): return lax.ppermute(array, 'ctx', pairs)  37.5 us
    ppermute x19, starting transfers between devices, swap(): lax.ppermute(array, 'head', [(h, h ^ bits) for h in range(lax.axis_size('...  29.7 us
    pallas_call x2, Pallas kernels, far(): pl.pallas_call(functools.partial(far_kernel, counts=tuple((len(part) for...  19 us
    unnamed x57, local copies, waits for them, and re-layouts  16.2 us
    ppermute x19, waiting for transfers between devices, swap(): lax.ppermute(array, 'head', [(h, h ^ bits) for h in range(lax.axis_size('...  9.76 us
    all_to_all x1, waiting for transfers between devices, body(): lax.all_to_all(attention.reshape(heads, share_rows, HD), 'head', split_ax...  9.41 us
    pallas_call x1, Pallas kernels, project(): pl.pallas_call(project_kernel, grid_spec=grid_spec, out_shape=jax.ShapeDt...  5.22 us
  transfers between devices with their start and end apart: 45, of which 12 were waited for; matrix products, arithmetic and copies ran while one was open for 9% of the time, Pallas kernels for 14%

profile of v2, /device:TPU:1, one launch (start us, length us, event | category | flops | bytes accessed | tf_op | source)
XLA Modules:
  0.0 221.9 jit_solution(2994709844395537276)
XLA Ops:
  12.6 4.0 %collective-permute-start.17 = (bf16[8,2,32,128]{3,2,1,0:T(8,128)(2,1)S(1)}, bf16[8,2,32,128]{3,2,1,0:T(8,128)(2,1)S(1)}, u32[]{:S(2)}, u32[]{:S(2)}) collective-permute-start(bf16[8,2,32,128]{3,2,1,0:T(8,128)(2,1)S(1)} %get-tuple-element.39), channel_id=1, source_target_pairs={{0,224},{8,232},{16,240},{24,248},{32,0},{40,8},{48,16},{56,24},{6... | collective-permute-start | bytes 393224 | tf_op jit(solution)/shard_map/ppermute | solution.py:284
  28.6 2.7 %collective-permute-start.7 = (bf16[4,2,32,128]{3,2,1,0:T(8,128)(2,1)S(1)}, bf16[4,2,32,128]{3,2,1,0:T(8,128)(2,1)S(1)}, u32[]{:S(2)}, u32[]{:S(2)}) collective-permute-start(bf16[4,2,32,128]{3,2,1,0:T(8,128)(2,1)S(1)} %slice.51), channel_id=1, source_target_pairs={{0,24},{8,0},{16,8},{24,16},{32,56},{40,32},{48,40},{56,48},{64,88... | collective-permute-start | bytes 196616 | tf_op jit(solution)/shard_map/ppermute | solution.py:284
  31.3 2.7 %collective-permute-start.19 = (bf16[8,2,32,128]{3,2,1,0:T(8,128)(2,1)S(1)}, bf16[8,2,32,128]{3,2,1,0:T(8,128)(2,1)S(1)}, u32[]{:S(2)}, u32[]{:S(2)}) collective-permute-start(bf16[8,2,32,128]{3,2,1,0:T(8,128)(2,1)S(1)} %collective-permute-done.17), channel_id=1, source_target_pairs={{0,224},{8,232},{16,240},{24,248},{32,0},{40,8},{48,16},{56,24},{6... | collective-permute-start | bytes 393224 | tf_op jit(solution)/shard_map/ppermute | solution.py:284
  36.9 2.7 %collective-permute-start.9 = (bf16[32,2,32,128]{3,2,1,0:T(8,128)(2,1)}, bf16[32,2,32,128]{3,2,1,0:T(8,128)(2,1)S(1)}, u32[]{:S(2)}, u32[]{:S(2)}) collective-permute-start(bf16[32,2,32,128]{3,2,1,0:T(8,128)(2,1)} %get-tuple-element.48), channel_id=1, source_target_pairs={{0,224},{8,232},{16,240},{24,248},{32,0},{40,8},{48,16},{56,24},{6... | collective-permute-start | bytes 1572872 | tf_op jit(solution)/shard_map/ppermute | solution.py:284
  39.6 2.7 %collective-permute-start.21 = (bf16[8,2,32,128]{3,2,1,0:T(8,128)(2,1)S(1)}, bf16[8,2,32,128]{3,2,1,0:T(8,128)(2,1)S(1)}, u32[]{:S(2)}, u32[]{:S(2)}) collective-permute-start(bf16[8,2,32,128]{3,2,1,0:T(8,128)(2,1)S(1)} %collective-permute-done.19), channel_id=1, source_target_pairs={{0,224},{8,232},{16,240},{24,248},{32,0},{40,8},{48,16},{56,24},{6... | collective-permute-start | bytes 393224 | tf_op jit(solution)/shard_map/ppermute | solution.py:284
  42.3 18.7 %collective-permute-done.20 = bf16[8,2,32,128]{3,2,1,0:T(8,128)(2,1)S(1)} collective-permute-done((bf16[8,2,32,128]{3,2,1,0:T(8,128)(2,1)S(1)}, bf16[8,2,32,128]{3,2,1,0:T(8,128)(2,1)S(1)}, u32[]{:S(2)}, u32[]{:S(2)}) %collective-permute-start.20) | collective-permute-done | bytes 131104 | tf_op jit(solution)/shard_map/ppermute | solution.py:284
  61.0 2.7 %collective-permute-start.23 = (bf16[4,2,32,128]{3,2,1,0:T(8,128)(2,1)S(1)}, bf16[4,2,32,128]{3,2,1,0:T(8,128)(2,1)S(1)}, u32[]{:S(2)}, u32[]{:S(2)}) collective-permute-start(bf16[4,2,32,128]{3,2,1,0:T(8,128)(2,1)S(1)} %slice.55), channel_id=1, source_target_pairs={{0,224},{8,232},{16,240},{24,248},{32,0},{40,8},{48,16},{56,24},{6... | collective-permute-start | bytes 196616 | tf_op jit(solution)/shard_map/ppermute | solution.py:284
  72.1 7.1 %collective-permute-done.29.refs_1_ = bf16[2048,128]{1,0:T(8,128)(2,1)} collective-permute-done((bf16[2048,128]{1,0:T(8,128)(2,1)S(1)}, bf16[2048,128]{1,0:T(8,128)(2,1)}, u32[]{:S(2)}, u32[]{:S(2)}) %collective-permute-start.29) | collective-permute-done | bytes 524320 | tf_op jit(solution)/shard_map/ppermute | solution.py:288
  79.2 3.5 %collective-permute-start.30 = (bf16[2048,128]{1,0:T(8,128)(2,1)}, bf16[2048,128]{1,0:T(8,128)(2,1)}, u32[]{:S(2)}, u32[]{:S(2)}) collective-permute-start(bf16[2048,128]{1,0:T(8,128)(2,1)} %collective-permute-done.29.refs_1_), channel_id=1, source_target_pairs={{0,1},{1,0},{2,3},{3,2},{4,5},{5,4},{6,7},{7,6},{8,9},{9,8},{10,11... | collective-permute-start | bytes 1572872 | tf_op jit(solution)/shard_map/ppermute | solution.py:288
  82.7 8.5 %collective-permute-done.10 = bf16[32,2,32,128]{3,2,1,0:T(8,128)(2,1)} collective-permute-done((bf16[32,2,32,128]{3,2,1,0:T(8,128)(2,1)}, bf16[32,2,32,128]{3,2,1,0:T(8,128)(2,1)}, u32[]{:S(2)}, u32[]{:S(2)}) %collective-permute-start.10) | collective-permute-done | bytes 524320 | tf_op jit(solution)/shard_map/ppermute | solution.py:284
  91.2 2.7 %collective-permute-start.13 = (bf16[32,2,32,128]{3,2,1,0:T(8,128)(2,1)}, bf16[32,2,32,128]{3,2,1,0:T(8,128)(2,1)S(1)}, u32[]{:S(2)}, u32[]{:S(2)}) collective-permute-start(bf16[32,2,32,128]{3,2,1,0:T(8,128)(2,1)} %collective-permute-done.11), channel_id=1, source_target_pairs={{0,224},{8,232},{16,240},{24,248},{32,0},{40,8},{48,16},{56,24},{6... | collective-permute-start | bytes 1572872 | tf_op jit(solution)/shard_map/ppermute | solution.py:284
  93.9 16.5 %collective-permute-done.24.refs_9_ = bf16[64,2,32,128]{3,2,1,0:T(8,128)(2,1)S(1)} collective-permute-done((bf16[64,2,32,128]{3,2,1,0:T(8,128)(2,1)S(1)}, bf16[64,2,32,128]{3,2,1,0:T(8,128)(2,1)S(1)}, u32[]{:S(2)}, u32[]{:S(2)}) %collective-permute-start.24) | collective-permute-done | bytes 1048608 | tf_op jit(solution)/shard_map/ppermute | solution.py:284
  114.1 3.5 %collective-permute-start.27 = (bf16[32,2,32,128]{3,2,1,0:T(8,128)(2,1)}, bf16[32,2,32,128]{3,2,1,0:T(8,128)(2,1)S(1)}, u32[]{:S(2)}, u32[]{:S(2)}) collective-permute-start(bf16[32,2,32,128]{3,2,1,0:T(8,128)(2,1)} %slice.57), channel_id=1, source_target_pairs={{0,24},{8,0},{16,8},{24,16},{32,56},{40,32},{48,40},{56,48},{64,88... | collective-permute-start | bytes 1572872 | tf_op jit(solution)/shard_map/ppermute | solution.py:284
  119.7 4.6 %collective-permute-start.3 = (bf16[2048,128]{1,0:T(8,128)(2,1)}, bf16[2048,128]{1,0:T(8,128)(2,1)}, u32[]{:S(2)}, u32[]{:S(2)}) collective-permute-start(bf16[2048,128]{1,0:T(8,128)(2,1)} %q_ref.1), channel_id=1, source_target_pairs={{0,1},{1,0},{2,3},{3,2},{4,5},{5,4},{6,7},{7,6},{8,9},{9,8},{10,11... | collective-permute-start | bytes 1572872 | tf_op jit(solution)/shard_map/ppermute | solution.py:288
  124.4 2.8 %collective-permute-start.15 = (bf16[16,2,32,128]{3,2,1,0:T(8,128)(2,1)S(1)}, bf16[16,2,32,128]{3,2,1,0:T(8,128)(2,1)S(1)}, u32[]{:S(2)}, u32[]{:S(2)}) collective-permute-start(bf16[16,2,32,128]{3,2,1,0:T(8,128)(2,1)S(1)} %slice.53), channel_id=1, source_target_pairs={{0,224},{8,232},{16,240},{24,248},{32,0},{40,8},{48,16},{56,24},{6... | collective-permute-start | bytes 786440 | tf_op jit(solution)/shard_map/ppermute | solution.py:284
  135.1 3.5 %collective-permute-start.39 = (bf16[128,2048]{1,0:T(8,128)(2,1)}, bf16[128,2048]{1,0:T(8,128)(2,1)}, u32[]{:S(2)}, u32[]{:S(2)}) collective-permute-start(bf16[128,2048]{1,0:T(8,128)(2,1)} %refs_0_.1), channel_id=1, source_target_pairs={{0,4},{1,5},{2,6},{3,7},{4,0},{5,1},{6,2},{7,3},{8,12},{9,13},{10,... | collective-permute-start | bytes 1572872 | tf_op jit(solution)/shard_map/ppermute | solution.py:288
  139.7 4.2 %all-gather.2.cloned.1.call-done.refs_2_ = bf16[256,2,64,128]{3,2,1,0:T(8,128)(2,1)} async-done(((bf16[8,2,64,128]{3,2,1,0:T(8,128)(2,1)}), bf16[256,2,64,128]{3,2,1,0:T(8,128)(2,1)}) %all-gather.2.cloned.1.call-update) | async-done | bytes 8388624 | tf_op jit(solution)/shard_map/all_gather | solution.py:329
  144.9 9.6 %far.3 = (bf16[4,144,512]{2,1,0:T(8,128)(2,1)}, bf16[4,144,512]{2,1,0:T(8,128)(2,1)S(1)}) custom-call(s32[32,6]{1,0:T(8,128)S(1)} %copy.14.where_ref, bf16[2048,128]{1,0:T(8,128)(2,1)} %collective-permute-done.30.refs_0_, bf16[2048,128]{1,0:T(8,128)(2,1)} %collective-permute-done.29.refs_1_, bf16[256,2,64,128]{3,2,1,0:T(8,128)(2,1)} %all-gather.2.cloned.1.call-done.refs_2_, ...), custom_call_target="tpu_custom_call" | custom-call | flops 1073741824 | bytes 5242880 | tf_op jit(solution)/shard_map/far/pallas_call | solution.py:161
  158.3 9.4 %far.2 = (bf16[4,144,512]{2,1,0:T(8,128)(2,1)}, bf16[4,144,512]{2,1,0:T(8,128)(2,1)S(1)}) custom-call(s32[32,6]{1,0:T(8,128)S(1)} %copy.13.where_ref, bf16[2048,128]{1,0:T(8,128)(2,1)} %collective-permute-done.3.refs_0_, bf16[2048,128]{1,0:T(8,128)(2,1)S(1)} %copy-done.1, bf16[256,2,64,128]{3,2,1,0:T(8,128)(2,1)} %all-gather.2.cloned.1.call-done.refs_2_, ...), custom_call_target="tpu_custom_call" | custom-call | flops 1073741824 | bytes 5242880 | tf_op jit(solution)/shard_map/far/pallas_call | solution.py:161
  184.5 4.7 %near.1 = (f32[4,128,512]{2,1,0:T(8,128)}, f32[4,1,512]{2,1,0:T(1,128)}, f32[4,1,512]{2,1,0:T(1,128)}) custom-call(s32[1]{0:T(128)} %bitcast.10.kv_ref, bf16[2048,128]{1,0:T(8,128)(2,1)} %q_ref.1, bf16[2048,256]{1,0:T(8,128)(2,1)} %k_ref.1, bf16[2048,256]{1,0:T(8,128)(2,1)} %v_ref.1), custom_call_target="tpu_custom_call" | custom-call | flops 536870912 | bytes 4194304 | tf_op jit(solution)/shard_map/near/pallas_call | solution.py:75
  189.1 2.9 %merge_here.1 = (f32[4,128,512]{2,1,0:T(8,128)}, f32[4,1,512]{2,1,0:T(1,128)}, f32[4,1,512]{2,1,0:T(1,128)}) custom-call(bf16[4,144,512]{2,1,0:T(8,128)(2,1)} %copy-done.6, bf16[4,144,512]{2,1,0:T(8,128)(2,1)} %copy-done.9, f32[4,128,512]{2,1,0:T(8,128)} %get-tuple-element.18.acc_ref, f32[4,1,512]{2,1,0:T(1,128)} %get-tuple-element.19.m_ref, ...), custom_call_target="tpu_custom_call" | custom-call | tf_op jit(solution)/shard_map/merge_here/pallas_call | solution.py:220
  195.3 4.3 %all-to-all-start = ((bf16[8,256,128]{2,1,0:T(8,128)(2,1)}), bf16[8,256,128]{2,1,0:T(8,128)(2,1)S(1)}, u32[]{:S(2)}, u32[]{:S(2)}) async-start(bf16[8,256,128]{2,1,0:T(8,128)(2,1)} %bitcast.25), calls=%async_computation | async-start | bytes 1048576 | tf_op jit(solution)/shard_map/all_to_all | solution.py:389
  199.6 9.4 %all-to-all-done.a_ref = bf16[8,256,128]{2,1,0:T(8,128)(2,1)S(1)} async-done(((bf16[8,256,128]{2,1,0:T(8,128)(2,1)}), bf16[8,256,128]{2,1,0:T(8,128)(2,1)S(1)}, u32[]{:S(2)}, u32[]{:S(2)}) %all-to-all-start) | async-done | bytes 524320 | tf_op jit(solution)/shard_map/all_to_all | solution.py:389
  209.9 5.2 %project.1 = bf16[256,2048]{1,0:T(8,128)(2,1)} custom-call(s32[1]{0:T(128)} %bitcast.13.head_ref, bf16[8,256,128]{2,1,0:T(8,128)(2,1)} %copy-done.8, bf16[128,2048]{1,0:T(8,128)(2,1)} %refs_0_.1, bf16[128,2048]{1,0:T(8,128)(2,1)} %copy-done.10, bf16[128,2048]{1,0:T(8,128)(2,1)} %collective-permute-done.37.refs_2_, bf16[128,2048]{1,0:T(8,128)(2,1)} %copy-done.11, ...), custom_call_target="tpu_custom_call" | custom-call | tf_op jit(solution)/shard_map/project/pallas_call | solution.py:271
  (166 shorter events, 69.0 us)
Async XLA Ops:
  7.2 136.7 %all-gather.2.cloned.1.call-start = ((), (), s32[]{:S(2)}) async-start(), calls=%async_computation.1 | async-start | bytes 8650752 | tf_op jit(solution)/shard_map/all_gather | solution.py:329
  10.1 21.3 %collective-permute-start.16 = (bf16[8,2,32,128]{3,2,1,0:T(8,128)(2,1)S(1)}, bf16[8,2,32,128]{3,2,1,0:T(8,128)(2,1)S(1)}, u32[]{:S(2)}, u32[]{:S(2)}) collective-permute-start(bf16[8,2,32,128]{3,2,1,0:T(8,128)(2,1)S(1)} %get-tuple-element.39), channel_id=1, source_target_pairs={{0,32},{8,40},{16,48},{24,56},{32,64},{40,72},{48,80},{56,88},{64,... | collective-permute-start | bytes 393224 | tf_op jit(solution)/shard_map/ppermute | solution.py:284
  25.4 42.8 %collective-permute-start.2 = (s32[4,1,4]{2,1,0:T(1,128)S(1)}, s32[4,1,4]{2,1,0:T(1,128)S(1)}, u32[]{:S(2)}, u32[]{:S(2)}) collective-permute-start(s32[4,1,4]{2,1,0:T(1,128)S(1)} %copy-done.19), channel_id=1, source_target_pairs={{0,3},{1,2},{2,1},{3,0},{4,7},{5,6},{6,5},{7,4},{8,11},{9,10},{10,... | collective-permute-start | bytes 200 | tf_op jit(solution)/shard_map/ppermute | solution.py:288
  36.9 32.2 %collective-permute-start.8 = (bf16[32,2,32,128]{3,2,1,0:T(8,128)(2,1)}, bf16[32,2,32,128]{3,2,1,0:T(8,128)(2,1)}, u32[]{:S(2)}, u32[]{:S(2)}) collective-permute-start(bf16[32,2,32,128]{3,2,1,0:T(8,128)(2,1)} %get-tuple-element.48), channel_id=1, source_target_pairs={{0,32},{8,40},{16,48},{24,56},{32,64},{40,72},{48,80},{56,88},{64,... | collective-permute-start | bytes 1572872 | tf_op jit(solution)/shard_map/ppermute | solution.py:284
  36.9 32.4 %collective-permute-start.9 = (bf16[32,2,32,128]{3,2,1,0:T(8,128)(2,1)}, bf16[32,2,32,128]{3,2,1,0:T(8,128)(2,1)S(1)}, u32[]{:S(2)}, u32[]{:S(2)}) collective-permute-start(bf16[32,2,32,128]{3,2,1,0:T(8,128)(2,1)} %get-tuple-element.48), channel_id=1, source_target_pairs={{0,224},{8,232},{16,240},{24,248},{32,0},{40,8},{48,16},{56,24},{6... | collective-permute-start | bytes 1572872 | tf_op jit(solution)/shard_map/ppermute | solution.py:284
  39.6 21.4 %collective-permute-start.20 = (bf16[8,2,32,128]{3,2,1,0:T(8,128)(2,1)S(1)}, bf16[8,2,32,128]{3,2,1,0:T(8,128)(2,1)S(1)}, u32[]{:S(2)}, u32[]{:S(2)}) collective-permute-start(bf16[8,2,32,128]{3,2,1,0:T(8,128)(2,1)S(1)} %collective-permute-done.18), channel_id=1, source_target_pairs={{0,32},{8,40},{16,48},{24,56},{32,64},{40,72},{48,80},{56,88},{64,... | collective-permute-start | bytes 393224 | tf_op jit(solution)/shard_map/ppermute | solution.py:284
  39.6 21.4 %collective-permute-start.21 = (bf16[8,2,32,128]{3,2,1,0:T(8,128)(2,1)S(1)}, bf16[8,2,32,128]{3,2,1,0:T(8,128)(2,1)S(1)}, u32[]{:S(2)}, u32[]{:S(2)}) collective-permute-start(bf16[8,2,32,128]{3,2,1,0:T(8,128)(2,1)S(1)} %collective-permute-done.19), channel_id=1, source_target_pairs={{0,224},{8,232},{16,240},{24,248},{32,0},{40,8},{48,16},{56,24},{6... | collective-permute-start | bytes 393224 | tf_op jit(solution)/shard_map/ppermute | solution.py:284
  65.4 45.0 %collective-permute-start.24 = (bf16[64,2,32,128]{3,2,1,0:T(8,128)(2,1)S(1)}, bf16[64,2,32,128]{3,2,1,0:T(8,128)(2,1)S(1)}, u32[]{:S(2)}, u32[]{:S(2)}) collective-permute-start(bf16[64,2,32,128]{3,2,1,0:T(8,128)(2,1)S(1)} %constant_dynamic-update-slice_fusion.18.refs_8_), channel_id=1, source_target_pairs={{0,8},{8,16},{16,24},{24,0},{32,40},{40,48},{48,56},{56,32},{64,72... | collective-permute-start | bytes 3145736 | tf_op jit(solution)/shard_map/ppermute | solution.py:284
  65.5 46.8 %collective-permute-start.25 = (bf16[64,2,32,128]{3,2,1,0:T(8,128)(2,1)S(1)}, bf16[64,2,32,128]{3,2,1,0:T(8,128)(2,1)}, u32[]{:S(2)}, u32[]{:S(2)}) collective-permute-start(bf16[64,2,32,128]{3,2,1,0:T(8,128)(2,1)S(1)} %constant_dynamic-update-slice_fusion.18.refs_8_), channel_id=1, source_target_pairs={{0,24},{8,0},{16,8},{24,16},{32,56},{40,32},{48,40},{56,48},{64,88... | collective-permute-start | bytes 3145736 | tf_op jit(solution)/shard_map/ppermute | solution.py:284
  69.1 22.0 %collective-permute-start.10 = (bf16[32,2,32,128]{3,2,1,0:T(8,128)(2,1)}, bf16[32,2,32,128]{3,2,1,0:T(8,128)(2,1)}, u32[]{:S(2)}, u32[]{:S(2)}) collective-permute-start(bf16[32,2,32,128]{3,2,1,0:T(8,128)(2,1)} %collective-permute-done.8), channel_id=1, source_target_pairs={{0,32},{8,40},{16,48},{24,56},{32,64},{40,72},{48,80},{56,88},{64,... | collective-permute-start | bytes 1572872 | tf_op jit(solution)/shard_map/ppermute | solution.py:284
  69.4 21.8 %collective-permute-start.11 = (bf16[32,2,32,128]{3,2,1,0:T(8,128)(2,1)S(1)}, bf16[32,2,32,128]{3,2,1,0:T(8,128)(2,1)}, u32[]{:S(2)}, u32[]{:S(2)}) collective-permute-start(bf16[32,2,32,128]{3,2,1,0:T(8,128)(2,1)S(1)} %collective-permute-done.9), channel_id=1, source_target_pairs={{0,224},{8,232},{16,240},{24,248},{32,0},{40,8},{48,16},{56,24},{6... | collective-permute-start | bytes 1572872 | tf_op jit(solution)/shard_map/ppermute | solution.py:284
  79.2 45.2 %collective-permute-start.30 = (bf16[2048,128]{1,0:T(8,128)(2,1)}, bf16[2048,128]{1,0:T(8,128)(2,1)}, u32[]{:S(2)}, u32[]{:S(2)}) collective-permute-start(bf16[2048,128]{1,0:T(8,128)(2,1)} %collective-permute-done.29.refs_1_), channel_id=1, source_target_pairs={{0,1},{1,0},{2,3},{3,2},{4,5},{5,4},{6,7},{7,6},{8,9},{9,8},{10,11... | collective-permute-start | bytes 1572872 | tf_op jit(solution)/shard_map/ppermute | solution.py:288
  91.2 28.5 %collective-permute-start.12 = (bf16[32,2,32,128]{3,2,1,0:T(8,128)(2,1)}, bf16[32,2,32,128]{3,2,1,0:T(8,128)(2,1)S(1)}, u32[]{:S(2)}, u32[]{:S(2)}) collective-permute-start(bf16[32,2,32,128]{3,2,1,0:T(8,128)(2,1)} %collective-permute-done.10), channel_id=1, source_target_pairs={{0,32},{8,40},{16,48},{24,56},{32,64},{40,72},{48,80},{56,88},{64,... | collective-permute-start | bytes 1572872 | tf_op jit(solution)/shard_map/ppermute | solution.py:284
  91.2 33.1 %collective-permute-start.13 = (bf16[32,2,32,128]{3,2,1,0:T(8,128)(2,1)}, bf16[32,2,32,128]{3,2,1,0:T(8,128)(2,1)S(1)}, u32[]{:S(2)}, u32[]{:S(2)}) collective-permute-start(bf16[32,2,32,128]{3,2,1,0:T(8,128)(2,1)} %collective-permute-done.11), channel_id=1, source_target_pairs={{0,224},{8,232},{16,240},{24,248},{32,0},{40,8},{48,16},{56,24},{6... | collective-permute-start | bytes 1572872 | tf_op jit(solution)/shard_map/ppermute | solution.py:284
  112.3 22.9 %collective-permute-start.26 = (bf16[32,2,32,128]{3,2,1,0:T(8,128)(2,1)}, bf16[32,2,32,128]{3,2,1,0:T(8,128)(2,1)S(1)}, u32[]{:S(2)}, u32[]{:S(2)}) collective-permute-start(bf16[32,2,32,128]{3,2,1,0:T(8,128)(2,1)} %slice.56), channel_id=1, source_target_pairs={{0,8},{8,16},{16,24},{24,0},{32,40},{40,48},{48,56},{56,32},{64,72... | collective-permute-start | bytes 1572872 | tf_op jit(solution)/shard_map/ppermute | solution.py:284
  114.1 21.0 %collective-permute-start.27 = (bf16[32,2,32,128]{3,2,1,0:T(8,128)(2,1)}, bf16[32,2,32,128]{3,2,1,0:T(8,128)(2,1)S(1)}, u32[]{:S(2)}, u32[]{:S(2)}) collective-permute-start(bf16[32,2,32,128]{3,2,1,0:T(8,128)(2,1)} %slice.57), channel_id=1, source_target_pairs={{0,24},{8,0},{16,8},{24,16},{32,56},{40,32},{48,40},{56,48},{64,88... | collective-permute-start | bytes 1572872 | tf_op jit(solution)/shard_map/ppermute | solution.py:284
  119.7 36.6 %collective-permute-start.3 = (bf16[2048,128]{1,0:T(8,128)(2,1)}, bf16[2048,128]{1,0:T(8,128)(2,1)}, u32[]{:S(2)}, u32[]{:S(2)}) collective-permute-start(bf16[2048,128]{1,0:T(8,128)(2,1)} %q_ref.1), channel_id=1, source_target_pairs={{0,1},{1,0},{2,3},{3,2},{4,5},{5,4},{6,7},{7,6},{8,9},{9,8},{10,11... | collective-permute-start | bytes 1572872 | tf_op jit(solution)/shard_map/ppermute | solution.py:288
  135.1 36.7 %collective-permute-start.37 = (bf16[128,2048]{1,0:T(8,128)(2,1)}, bf16[128,2048]{1,0:T(8,128)(2,1)}, u32[]{:S(2)}, u32[]{:S(2)}) collective-permute-start(bf16[128,2048]{1,0:T(8,128)(2,1)} %refs_0_.1), channel_id=1, source_target_pairs={{0,2},{1,3},{2,0},{3,1},{4,6},{5,7},{6,4},{7,5},{8,10},{9,11},{10,... | collective-permute-start | bytes 1572872 | tf_op jit(solution)/shard_map/ppermute | solution.py:288
  135.1 37.0 %collective-permute-start.39 = (bf16[128,2048]{1,0:T(8,128)(2,1)}, bf16[128,2048]{1,0:T(8,128)(2,1)}, u32[]{:S(2)}, u32[]{:S(2)}) collective-permute-start(bf16[128,2048]{1,0:T(8,128)(2,1)} %refs_0_.1), channel_id=1, source_target_pairs={{0,4},{1,5},{2,6},{3,7},{4,0},{5,1},{6,2},{7,3},{8,12},{9,13},{10,... | collective-permute-start | bytes 1572872 | tf_op jit(solution)/shard_map/ppermute | solution.py:288
  138.6 34.7 %collective-permute-start.41 = (bf16[128,2048]{1,0:T(8,128)(2,1)}, bf16[128,2048]{1,0:T(8,128)(2,1)}, u32[]{:S(2)}, u32[]{:S(2)}) collective-permute-start(bf16[128,2048]{1,0:T(8,128)(2,1)} %refs_0_.1), channel_id=1, source_target_pairs={{0,6},{1,7},{2,4},{3,5},{4,2},{5,3},{6,0},{7,1},{8,14},{9,15},{10,... | collective-permute-start | bytes 1572872 | tf_op jit(solution)/shard_map/ppermute | solution.py:288
  173.3 18.7 %collective-permute-start.35 = (bf16[1,144,512]{2,1,0:T(8,128)(2,1)}, bf16[1,144,512]{2,1,0:T(8,128)(2,1)S(1)}, u32[]{:S(2)}, u32[]{:S(2)}) collective-permute-start(bf16[1,144,512]{2,1,0:T(8,128)(2,1)} %get-tuple-element.29), channel_id=1, source_target_pairs={{0,2},{1,3},{2,0},{3,1},{4,6},{5,7},{6,4},{7,5},{8,10},{9,11},{10,... | collective-permute-start | bytes 442376 | tf_op jit(solution)/shard_map/ppermute | solution.py:288
  173.7 25.9 %collective-permute-start.36 = (bf16[128,2048]{1,0:T(8,128)(2,1)}, bf16[128,2048]{1,0:T(8,128)(2,1)S(1)}, u32[]{:S(2)}, u32[]{:S(2)}) collective-permute-start(bf16[128,2048]{1,0:T(8,128)(2,1)} %refs_0_.1), channel_id=1, source_target_pairs={{0,1},{1,0},{2,3},{3,2},{4,5},{5,4},{6,7},{7,6},{8,9},{9,8},{10,11... | collective-permute-start | bytes 1572872 | tf_op jit(solution)/shard_map/ppermute | solution.py:288
  175.8 23.8 %collective-permute-start.38 = (bf16[128,2048]{1,0:T(8,128)(2,1)}, bf16[128,2048]{1,0:T(8,128)(2,1)S(1)}, u32[]{:S(2)}, u32[]{:S(2)}) collective-permute-start(bf16[128,2048]{1,0:T(8,128)(2,1)} %collective-permute-done.37.refs_2_), channel_id=1, source_target_pairs={{0,1},{1,0},{2,3},{3,2},{4,5},{5,4},{6,7},{7,6},{8,9},{9,8},{10,11... | collective-permute-start | bytes 1572872 | tf_op jit(solution)/shard_map/ppermute | solution.py:288
  179.0 20.6 %collective-permute-start.40 = (bf16[128,2048]{1,0:T(8,128)(2,1)}, bf16[128,2048]{1,0:T(8,128)(2,1)S(1)}, u32[]{:S(2)}, u32[]{:S(2)}) collective-permute-start(bf16[128,2048]{1,0:T(8,128)(2,1)} %collective-permute-done.39.refs_4_), channel_id=1, source_target_pairs={{0,1},{1,0},{2,3},{3,2},{4,5},{5,4},{6,7},{7,6},{8,9},{9,8},{10,11... | collective-permute-start | bytes 1572872 | tf_op jit(solution)/shard_map/ppermute | solution.py:288
  (41 other events, 391.0 us)
Sparse Core Ops, SparseCore 0:
  10.6 133.2 all-gather.1

commit v3 on v2

--- a/solution.py
+++ b/solution.py
@@ -21,8 +21,8 @@
 NEG = -1e30
 F32 = jnp.float32
 BF16 = jnp.bfloat16
-SPLIT = (8, 4, 4)
-VMEM_BYTES = 48 << 20
+SPLIT = (6, 4, 6)
+VMEM_BYTES = 56 << 20
 
 
 def dot_nt(a, b):
@@ -97,58 +97,152 @@
     return ref[i, :HD, :].astype(F32), tail[0:1], tail[1:2] + tail[2:3]
 
 
-def far_kernel(where_ref, *refs, counts):
-    q_refs, refs = refs[:2], refs[2:]
-    sources = []
-    for count in counts:
-        sources.append(refs[:count])
-        refs = refs[count:]
-    out_refs, refs = refs[:2], refs[2:]
-    buffers, sems = refs[:-1], refs[-1]
-    parts = len(counts)
-
-    def fetch(pick, carry):
-        for part in range(parts):
+def fetch(where_ref, sources, targets, picks, sem_of):
+    def one(pick, carry):
+        for part, arrays in enumerate(sources):
             array = where_ref[pick, 2 * part]
             index = where_ref[pick, 2 * part + 1]
-            for number, source in enumerate(sources[part]):
+            for number, source in enumerate(arrays):
 
                 def start(source=source, part=part, index=index):
                     pltpu.make_async_copy(
-                        source.at[index], buffers[part].at[pick], sems.at[pick // SEL, part]
+                        source.at[index], targets[part].at[pick], sem_of(pick, part)
                     ).start()
 
-                if counts[part] == 1:
+                if len(arrays) == 1:
                     start()
                 else:
                     pl.when(array == number)(start)
         return carry
 
-    lax.fori_loop(0, 2 * QB * SEL, fetch, 0)
-
-    def unit(row, q_ref, out_ref, i):
+    lax.fori_loop(0, picks, one, 0)
+
+
+def split_refs(refs, counts):
+    groups = []
+    for count in counts:
+        groups.append(refs[:count])
+        refs = refs[count:]
+    return groups, refs
+
+
+def collect_kernel(where_ref, *refs, counts):
+    sources, refs = split_refs(refs, counts)
+    targets, sem = refs[:-1], refs[-1]
+    picks = GROUP * QB * SEL
+    fetch(where_ref, sources, targets, picks, lambda pick, part: sem.at[part])
+
+    def wait(pick, carry):
+        for part in range(len(counts)):
+
+            def done(part=part):
+                pltpu.make_async_copy(
+                    sources[part][0].at[0], targets[part].at[pick], sem.at[part]
+                ).wait()
+
+            pl.when(where_ref[pick, 2 * part] >= 0)(done)
+        return carry
+
+    lax.fori_loop(0, picks, wait, 0)
+
+
+def collect(where, parts):
+    arrays = [array for part in parts for array in part]
+    hbm = pl.BlockSpec(memory_space=pl.ANY)
+    return pl.pallas_call(
+        functools.partial(collect_kernel, counts=tuple(len(part) for part in parts)),
+        in_specs=[pl.BlockSpec(memory_space=pltpu.SMEM)] + [hbm] * len(arrays),
+        out_specs=[hbm] * len(parts),
+        out_shape=[
+            jax.ShapeDtypeStruct((GROUP * QB * SEL,) + part[0].shape[1:], BF16) for part in parts
+        ],
+        scratch_shapes=[pltpu.SemaphoreType.DMA((len(parts),))],
+        compiler_params=pltpu.CompilerParams(vmem_limit_bytes=VMEM_BYTES),
+        name="collect",
+    )(where, *arrays)
+
+
+def cut_kernel(place_ref, k_ref, v_ref, *refs, spans):
+    out_refs, sem = refs[:-1], refs[-1]
+    row0 = pl.multiple_of(place_ref[0], BLK // GROUP)
+    col0 = pl.multiple_of(place_ref[1], HD)
+    copies = []
+    for out_ref, (block, blocks, first, rows) in zip(out_refs, spans):
+        for which, source in enumerate((k_ref, v_ref)):
+            copy = pltpu.make_async_copy(
+                source.at[pl.ds(block, blocks), pl.ds(row0 + first, rows), pl.ds(col0, HD)],
+                out_ref.at[:, which],
+                sem.at[len(copies)],
+            )
+            copy.start()
+            copies.append(copy)
+    for copy in copies:
+        copy.wait()
+
+
+def cut(place, cache_keys, cache_values, spans):
+    hbm = pl.BlockSpec(memory_space=pl.ANY)
+    view = (BLOCKS, BLK, cache_keys.shape[1])
+    return pl.pallas_call(
+        functools.partial(cut_kernel, spans=spans),
+        in_specs=[pl.BlockSpec(memory_space=pltpu.SMEM)] + [hbm] * 2,
+        out_specs=[hbm] * len(spans),
+        out_shape=[
+            jax.ShapeDtypeStruct((blocks, 2, rows, HD), BF16) for _, blocks, _, rows in spans
+        ],
+        scratch_shapes=[pltpu.SemaphoreType.DMA((2 * len(spans),))],
+        compiler_params=pltpu.CompilerParams(vmem_limit_bytes=VMEM_BYTES),
+        name="cut",
+    )(place, cache_keys.reshape(view), cache_values.reshape(view))
+
+
+def far_kernel(where_ref, *refs, counts):
+    q_refs, refs = refs[:2], refs[2:]
+    sources, refs = split_refs(refs, counts)
+    out_refs, refs = refs[:2], refs[2:]
+    parts = len(counts)
+    buffers, refs = refs[:parts], refs[parts:]
+    score_refs, weight_refs, sems = refs[:2], refs[2:4], refs[4]
+    fetch(where_ref, sources, buffers, 2 * QB * SEL, lambda pick, part: sems.at[pick // SEL, part])
+
+    def joined(row, which):
+        return jnp.concatenate(
+            [buffers[part][row * SEL + j, which] for part in range(parts) for j in range(SEL)],
+            axis=0,
+        )
+
+    def score(row, q_ref, i, score_ref):
         for part in range(parts):
             held = buffers[part].at[pl.ds(row * SEL, SEL)]
             pltpu.make_async_copy(held, held, sems.at[row, part]).wait()
-
-        def joined(which):
-            return jnp.concatenate(
-                [buffers[part][row * SEL + j, which] for part in range(parts) for j in range(SEL)],
-                axis=0,
-            )
-
-        scores = dot_nt(joined(0), q_ref[pl.ds(i * BLK, BLK), :])
-        top = rounded_top(jnp.max(scores, axis=0, keepdims=True))
-        weights = jnp.exp2(scores * SCALE - top)
-        total = jnp.sum(weights, axis=0, keepdims=True)
-        pack_state(out_ref, i, dot_tn(joined(1), weights.astype(BF16)), top, total)
+        score_ref[...] = dot_nt(joined(row, 0), q_ref[pl.ds(i * BLK, BLK), :])
+
+    def soften(score_ref, weight_ref):
+        tops, totals = [], []
+        for lane in range(0, BLK, HD):
+            lanes = slice(lane, lane + HD)
+            top = rounded_top(jnp.max(score_ref[:, lanes], axis=0, keepdims=True))
+            total = jnp.zeros((8, HD), F32)
+            for row in range(0, BLK, 64):
+                weights = jnp.exp2(score_ref[row : row + 64, lanes] * SCALE - top)
+                weight_ref[row : row + 64, lanes] = weights.astype(BF16)
+                total = total + jnp.sum(weights.reshape(8, 8, HD), axis=0)
+            tops.append(top)
+            totals.append(jnp.sum(total, axis=0, keepdims=True))
+        return jnp.concatenate(tops, axis=1), jnp.concatenate(totals, axis=1)
+
+    def finish(row, weight_ref, out_ref, i, top, total):
+        pack_state(out_ref, i, dot_tn(joined(row, 1), weight_ref[...]), top, total)
 
     for half in range(2):
 
         def pair(step, carry, half=half):
-            for k in range(2):
-                i = 2 * step + k
-                unit(half * QB + i, q_refs[half], out_refs[half], i)
+            units = [(half * QB + 2 * step + k, 2 * step + k) for k in range(2)]
+            for k, (row, i) in enumerate(units):
+                score(row, q_refs[half], i, score_refs[k])
+            for k, (row, i) in enumerate(units):
+                top, total = soften(score_refs[k], weight_refs[k])
+                finish(row, weight_refs[k], out_refs[half], i, top, total)
             return carry
 
         lax.fori_loop(0, QB // 2, pair, 0)
@@ -168,6 +262,8 @@
         scratch_shapes=[
             pltpu.VMEM((2 * QB * SEL,) + part[0].shape[1:], BF16) for part in parts
         ]
+        + [pltpu.VMEM((BLK, BLK), F32)] * 2
+        + [pltpu.VMEM((BLK, BLK), BF16)] * 2
         + [pltpu.SemaphoreType.DMA((2 * QB, len(parts)))],
         compiler_params=pltpu.CompilerParams(vmem_limit_bytes=VMEM_BYTES),
         cost_estimate=pl.CostEstimate(
@@ -253,57 +349,44 @@
 def project_kernel(head_ref, a_ref, *refs):
     w_refs, out_ref = refs[:-1], refs[-1]
     rows = jnp.concatenate([a_ref[head_ref[0] ^ i] for i in range(len(w_refs))], axis=1)
-    weight = jnp.concatenate([w_ref[...] for w_ref in w_refs], axis=0)
-    out_ref[...] = jnp.dot(rows, weight, preferred_element_type=F32).astype(BF16)
+    tile = 512
+    for first in range(0, out_ref.shape[1], tile):
+        weight = jnp.concatenate([w_ref[:, first : first + tile] for w_ref in w_refs], axis=0)
+        out_ref[:, first : first + tile] = jnp.dot(
+            rows, weight, preferred_element_type=F32
+        ).astype(BF16)
 
 
 def project(head, parts, weights):
-    heads, rows, _ = parts.shape
-    width = weights[0].shape[1]
-    tile = 512
-    grid_spec = pltpu.PrefetchScalarGridSpec(
-        num_scalar_prefetch=1,
-        grid=(width // tile,),
-        in_specs=[pl.BlockSpec((heads, rows, HD), lambda i, head: (0, 0, 0))]
-        + [pl.BlockSpec((HD, tile), lambda i, head: (0, i))] * heads,
-        out_specs=pl.BlockSpec((rows, tile), lambda i, head: (0, i)),
-    )
+    vmem = pl.BlockSpec(memory_space=pltpu.VMEM)
     return pl.pallas_call(
         project_kernel,
-        grid_spec=grid_spec,
-        out_shape=jax.ShapeDtypeStruct((rows, width), BF16),
+        in_specs=[pl.BlockSpec(memory_space=pltpu.SMEM)] + [vmem] * (1 + len(weights)),
+        out_specs=vmem,
+        out_shape=jax.ShapeDtypeStruct((parts.shape[1], weights[0].shape[1]), BF16),
+        compiler_params=pltpu.CompilerParams(vmem_limit_bytes=24 << 20),
         name="project",
     )(head, parts, *weights)
 
 
-def shift(array, dz, dx):
+def shift(arrays, dz, dx):
     pairs = []
     for z in range(NZ):
         for x in range(NX):
             pairs.append((z * NX + x, (z + dz) % NZ * NX + (x + dx) % NX))
-    return lax.ppermute(array, "ctx", pairs)
+    return [lax.ppermute(array, "ctx", pairs) for array in arrays]
 
 
 def swap(array, bits):
     return lax.ppermute(array, "head", [(h, h ^ bits) for h in range(lax.axis_size("head"))])
 
 
-def ring_four(piece):
-    half = piece.shape[0] // 2
-    below = shift(piece, 0, 1)
-    above = shift(piece, 0, -1)
-    return [piece, below, above, shift(below[:half], 0, 1), shift(above[half:], 0, -1)]
-
-
-def ring_eight(piece):
-    half = piece.shape[0] // 2
-    result = [piece]
-    below = above = piece
-    for _ in range(3):
-        below = shift(below, 1, 0)
-        above = shift(above, -1, 0)
-        result += [below, above]
-    return result + [shift(below[:half], 1, 0), shift(above[half:], -1, 0)]
+def after(value, *earlier):
+    return lax.optimization_barrier((value, earlier))[0]
+
+
+def join(*groups):
+    return jnp.concatenate([array for group in groups for array in group], axis=0)
 
 
 def body(queries, block_picks, span_keys, span_values, cache_keys, cache_values, out_weight):
@@ -314,29 +397,62 @@
     kv = head // GROUP
     share = BLK // GROUP
 
-    def cut(cache, first, rows):
-        view = cache.reshape(BLOCKS, BLK, cache.shape[1])
-        return lax.dynamic_slice(view, (0, part * share + first, kv * HD), (BLOCKS, rows, HD))
-
-    pieces = []
-    first = 0
-    for sixteenths in SPLIT:
-        rows = share * sixteenths // 16
-        pieces.append(
-            jnp.stack([cut(cache_keys, first, rows), cut(cache_values, first, rows)], axis=1)
-        )
-        first += rows
-    gathered = lax.all_gather(pieces[0], "ctx", axis=0, tiled=True)
-    by_x = jnp.concatenate(ring_four(pieces[1]), axis=0)
-    by_z = jnp.concatenate(ring_eight(pieces[2]), axis=0)
-    ring_a = ring_eight(by_x)
-    ring_b = ring_four(by_z)
-    ring_a = [jnp.concatenate(ring_a[:5], axis=0)] + ring_a[5:]
-
-    swapped = swap(queries, 2)
-    group_queries = [queries, swap(queries, 1), swapped, swap(swapped, 1)]
-    group_picks = jnp.stack([block_picks] + [swap(block_picks, r) for r in range(1, GROUP)])
-    picks = group_picks.reshape(GROUP, QB * SEL)
+    rows_s, rows_a, rows_b = [share * sixteenths // 16 for sixteenths in SPLIT]
+    half = BLOCKS // 2
+    spans = [(0, BLOCKS, 0, rows_s)]
+    spans += [(first, half, rows_s + rows_a, rows_b) for first in (0, half)]
+    spans += [(first, half, rows_s, rows_a) for first in (0, half)]
+    place = jnp.stack([part * share, kv * HD]).astype(jnp.int32)
+    piece_s, *rest = cut(place, cache_keys, cache_values, tuple(spans))
+    gathered = lax.all_gather(piece_s, "ctx", axis=0, tiled=True)
+    piece_b, piece_a = rest[:2], rest[2:]
+
+    b1, b2 = shift(piece_b, 1, 0), shift(piece_b, -1, 0)
+    a1, a2 = shift(piece_a, 0, 1), shift(piece_a, 0, -1)
+    a3 = shift(a1[:1], 0, 1) + shift(a2[1:], 0, -1)
+    b3, b4 = shift(b1, 1, 0), shift(b2, -1, 0)
+    wide_a = [join(piece_a, a1), join(a2, a3)]
+    wide_a = after(wide_a, b1, b2)
+    c1, c2 = shift(wide_a, 1, 0), shift(wide_a, -1, 0)
+    b5, b6 = shift(b3, 1, 0), shift(b4, -1, 0)
+    wide_b_low = join(piece_b, b1, b2, b3)
+    d1_low, d2_low = shift([wide_b_low], 0, 1), shift([wide_b_low], 0, -1)
+    b7 = shift(b5[:1], 1, 0) + shift(b6[1:], -1, 0)
+    wide_b_high = join(b4, b5, b6, b7)
+    d1_high, d2_high = shift([wide_b_high], 0, 1), shift([wide_b_high], 0, -1)
+
+    queries_early, picks_early, weight_early = after(
+        (queries, block_picks, out_weight), b3, b4
+    )
+    queries_chip = swap(queries_early, 2)
+    picks_chip = swap(picks_early, 2)
+    weights = [out_weight] + [None] * (heads - 1)
+    for bits in range(2, heads, 2):
+        weights[bits] = swap(weight_early, bits)
+    near_queries = after(queries, b7)
+    near_state = near(near_queries, span_keys, span_values, kv[None])
+
+    c1, c2 = after((c1, c2), wide_b_high, *near_state)
+    c3, c4 = shift(c1, 1, 0), shift(c2, -1, 0)
+    queries_pair, picks_pair, weights_even = after(
+        ([queries, queries_chip], jnp.stack([block_picks, picks_chip]), weights[::2]), c1, c2
+    )
+    picks_pair = [picks_pair, swap(picks_pair, 1)]
+    group_queries = [
+        queries,
+        swap(queries_pair[0], 1),
+        queries_chip,
+        swap(queries_pair[1], 1),
+    ]
+    group_picks = [picks_pair[0][0], picks_pair[1][0], picks_pair[0][1], picks_pair[1][1]]
+    d3 = shift(d1_low, 0, 1)
+    c5, c6 = shift(c3, 1, 0), shift(c4, -1, 0)
+    d3 += shift(d2_high, 0, -1)
+    for i, bits in enumerate(range(0, heads, 2)):
+        weights[bits + 1] = swap(weights_even[i], 1)
+    c7 = shift(c5[:1], 1, 0) + shift(c6[1:], -1, 0)
+
+    picks = jnp.stack(group_picks).reshape(GROUP, QB * SEL)
     owner, local = picks // BLOCKS, picks % BLOCKS
     dz = (owner // NX - ctx // NX) % NZ
     dx = (owner % NX - ctx % NX) % NX
@@ -344,44 +460,51 @@
     order_z = jnp.where(dz == 0, 0, jnp.where(dz > NZ // 2, 2 * (NZ - dz) - 1, 2 * dz))
     order_z = jnp.where(dz == NZ // 2, NZ - 1, order_z)
     place_a = order_x * BLOCKS + local
-    width_a = NX * BLOCKS
-    upper_a = place_a >= width_a // 2
-    array_a = jnp.where(
-        order_z < 5, 0, jnp.where(order_z < 7, order_z - 4, jnp.where(upper_a, 4, 3))
-    )
-    index_a = jnp.where(
-        order_z < 5,
-        order_z * width_a + place_a,
-        jnp.where((order_z == 7) & upper_a, place_a - width_a // 2, place_a),
-    )
+    half_a = NX * BLOCKS // 2
+    upper_a = (place_a >= half_a).astype(jnp.int32)
+    far_a = order_z == NZ - 1
     place_b = order_z * BLOCKS + local
-    width_b = NZ * BLOCKS
-    upper_b = place_b >= width_b // 2
-    array_b = jnp.where(order_x < 3, order_x, jnp.where(upper_b, 4, 3))
-    index_b = jnp.where((order_x == 3) & upper_b, place_b - width_b // 2, place_b)
-    where = jnp.stack(
-        [jnp.zeros_like(picks), picks, array_a, index_a, array_b, index_b], axis=-1
+    half_b = NZ * BLOCKS // 2
+    upper_b = (place_b >= half_b).astype(jnp.int32)
+    far_b = order_x == NX - 1
+    index_a = place_a - half_a * upper_a
+    index_b = place_b - half_b * upper_b
+    early = jnp.stack(
+        [
+            jnp.where(far_a, -1, 2 * order_z + upper_a),
+            index_a,
+            jnp.where(far_b, -1, 2 * order_x + upper_b),
+            index_b,
+        ],
+        axis=-1,
+    ).reshape(GROUP * QB * SEL, 4)
+    order = jnp.arange(GROUP * QB * SEL, dtype=jnp.int32).reshape(GROUP, QB * SEL)
+    late = jnp.stack(
+        [
+            jnp.zeros_like(picks),
+            picks,
+            jnp.where(far_a, 1 + upper_a, 0),
+            jnp.where(far_a, index_a, order),
+            jnp.where(far_b, 1 + upper_b, 0),
+            jnp.where(far_b, index_b, order),
+        ],
+        axis=-1,
     ).astype(jnp.int32)
-
-    weights = [out_weight] + [None] * (heads - 1)
-    for bits in range(2, heads, 2):
-        weights[bits] = swap(out_weight, bits)
-    for bits in range(0, heads, 2):
-        weights[bits + 1] = swap(weights[bits], 1)
-
-    near_state = near(queries, span_keys, span_values, kv[None])
-
-    def far_of(first, second):
+    held_a = [*wide_a, *c1, *c2, *c3, *c4, *c5, *c6]
+    held_b = [wide_b_low, wide_b_high, *d1_low, *d1_high, *d2_low, *d2_high]
+    early_a, early_b = collect(early.astype(jnp.int32), [held_a, held_b])
+
+    def far_of(first, second, where):
         return far(
             jnp.concatenate([where[first], where[second]], axis=0),
             [group_queries[first], group_queries[second]],
-            [[gathered], ring_a, ring_b],
+            [[gathered], [early_a, *c7], [early_b, *d3]],
         )
 
-    far_corner, far_chip = far_of(3, 2)
+    far_corner, far_chip = far_of(3, 2, late)
     for_chip = merge_two(far_chip, swap(far_corner, 1), QB)
     chip_parts = [swap(piece, 2) for piece in for_chip]
-    far_core, far_own = far_of(1, 0)
+    far_core, far_own = far_of(1, 0, after(late, *for_chip))
     here = merge_here(far_own, swap(far_core, 1), near_state)
     attention = merge_last(here, chip_parts)
 

time: 223 us -> 312 us (1.40); the launches traced: 222 us -> 306 us
  Pallas kernels: 36.6 us -> 114 us
  starting transfers between devices: 71.5 us -> 102 us
  local copies, waits for them, and re-layouts: 24.1 us -> 8.56 us
  waiting for transfers between devices: 70.9 us -> 65.6 us
    pallas_call x1 -> x3, Pallas kernels: 5.22 us -> 85.4 us  [the longest x1 64.1 us: collect(): pl.pallas_call(functools.partial(collect_kernel, counts=tuple((len(part)...]
    ppermute x24 -> x40, starting transfers between devices: 37.5 us -> 52 us  [shift(): return [lax.ppermute(array, 'ctx', pairs) for array in arrays]]
    unnamed x57 -> x71, local copies, waits for them, and re-layouts: 16.2 us -> 4.71 us
    ppermute x19 -> x18, starting transfers between devices: 29.7 us -> 39.4 us  [swap(): lax.ppermute(array, 'head', [(h, h ^ bits) for h in range(lax.axis_size('...]
    ppermute x24 -> x40, waiting for transfers between devices: 47.5 us -> 41.2 us  [shift(): return [lax.ppermute(array, 'ctx', pairs) for array in arrays]]
    all_to_all x1, starting transfers between devices: 4.27 us -> 10.3 us  [body(): lax.all_to_all(attention.reshape(heads, share_rows, HD), 'head', split_ax...]
    ppermute x19 -> x18, waiting for transfers between devices: 9.76 us -> 15 us  [swap(): lax.ppermute(array, 'head', [(h, h ^ bits) for h in range(lax.axis_size('...]
    all_gather x1, waiting for transfers between devices: 4.2 us -> 0.02 us  [body(): gathered = lax.all_gather(piece_s, 'ctx', axis=0, tiled=True)]
  transfers between devices with their start and end apart: 45 -> 60, of which waited for: 12 -> 23; matrix products, arithmetic and copies ran while one was open for 9% -> 3% of each run, Pallas kernels for 14% -> 25%
where the time goes in v3:
time: 312 us; the launch traced here: 306 us
  Pallas kernels  114 us (37%)
  starting transfers between devices  102 us (33%)
  waiting for transfers between devices  65.6 us (21%)
  between operations  14.8 us (5%)
  local copies, waits for them, and re-layouts  8.56 us (3%)
    pallas_call x1, Pallas kernels, collect(): pl.pallas_call(functools.partial(collect_kernel, counts=tuple((len(part)...  64.1 us
    ppermute x40, starting transfers between devices, shift(): return [lax.ppermute(array, 'ctx', pairs) for array in arrays]  52 us
    ppermute x40, waiting for transfers between devices, shift(): return [lax.ppermute(array, 'ctx', pairs) for array in arrays]  41.2 us
    ppermute x18, starting transfers between devices, swap(): lax.ppermute(array, 'head', [(h, h ^ bits) for h in range(lax.axis_size('...  39.4 us
    pallas_call x1, Pallas kernels, cut(): pl.pallas_call(functools.partial(cut_kernel, spans=spans), in_specs=[pl.B...  17.7 us
    pallas_call x2, Pallas kernels, far(): pl.pallas_call(functools.partial(far_kernel, counts=tuple((len(part) for...  16.1 us
    ppermute x18, waiting for transfers between devices, swap(): lax.ppermute(array, 'head', [(h, h ^ bits) for h in range(lax.axis_size('...  15 us
    all_to_all x1, starting transfers between devices, body(): lax.all_to_all(attention.reshape(heads, share_rows, HD), 'head', split_ax...  10.3 us
  transfers between devices with their start and end apart: 60, of which 23 were waited for; matrix products, arithmetic and copies ran while one was open for 3% of the time, Pallas kernels for 25%

profile of v3, /device:TPU:1, one launch (start us, length us, event | category | flops | bytes accessed | tf_op | source)
XLA Modules:
  0.0 306.4 jit_solution(16649368363160808598)
XLA Ops:
  7.9 17.7 %cut.1 = (bf16[8,2,48,128]{3,2,1,0:T(8,128)(2,1)}, bf16[4,2,48,128]{3,2,1,0:T(8,128)(2,1)}, bf16[4,2,48,128]{3,2,1,0:T(8,128)(2,1)}, bf16[4,2,32,128]{3,2,1,0:T(8,128)(2,1)}, bf16[4,2,32,128]{3,2,1,0:T(8,128)(2,1)}) custom-call(s32[2]{0:T(128)} %pad_add_fusion.5.place_ref, bf16[8,512,256]{2,1,0:T(8,128)(2,1)} %bitcast.23, bf16[8,512,256]{2,1,0:T(8,128)(2,1)} %bitcast.24), custom_call_target="tpu_custom_call" | custom-call | tf_op jit(solution)/shard_map/cut/pallas_call | solution.py:186
  25.7 6.5 %collective-permute-start.4 = (bf16[4,2,48,128]{3,2,1,0:T(8,128)(2,1)}, bf16[4,2,48,128]{3,2,1,0:T(8,128)(2,1)S(1)}, u32[]{:S(2)}, u32[]{:S(2)}) collective-permute-start(bf16[4,2,48,128]{3,2,1,0:T(8,128)(2,1)} %get-tuple-element.41), channel_id=1, source_target_pairs={{0,224},{8,232},{16,240},{24,248},{32,0},{40,8},{48,16},{56,24},{6... | collective-permute-start | bytes 294920 | tf_op jit(solution)/shard_map/ppermute | solution.py:377
  59.3 11.2 %collective-permute-done.23 = bf16[4,2,48,128]{3,2,1,0:T(8,128)(2,1)S(1)} collective-permute-done((bf16[4,2,48,128]{3,2,1,0:T(8,128)(2,1)S(1)}, bf16[4,2,48,128]{3,2,1,0:T(8,128)(2,1)S(1)}, u32[]{:S(2)}, u32[]{:S(2)}) %collective-permute-start.23) | collective-permute-done | bytes 98336 | tf_op jit(solution)/shard_map/ppermute | solution.py:377
  73.0 2.7 collective-permute-start.28
  78.2 3.2 %collective-permute-start.11 = (bf16[128,2048]{1,0:T(8,128)(2,1)S(1)}, bf16[128,2048]{1,0:T(8,128)(2,1)S(1)}, u32[]{:S(2)}, u32[]{:S(2)}) collective-permute-start(bf16[128,2048]{1,0:T(8,128)(2,1)S(1)} %copy-done), channel_id=1, source_target_pairs={{0,4},{1,5},{2,6},{3,7},{4,0},{5,1},{6,2},{7,3},{8,12},{9,13},{10,... | collective-permute-start | bytes 1572872 | tf_op jit(solution)/shard_map/ppermute | solution.py:381
  82.8 3.6 %collective-permute-start.22 = (bf16[16,2,32,128]{3,2,1,0:T(8,128)(2,1)S(1)}, bf16[16,2,32,128]{3,2,1,0:T(8,128)(2,1)}, u32[]{:S(2)}, u32[]{:S(2)}) collective-permute-start(bf16[16,2,32,128]{3,2,1,0:T(8,128)(2,1)S(1)} %pad_maximum_fusion.1.refs_1_), channel_id=1, source_target_pairs={{0,224},{8,232},{16,240},{24,248},{32,0},{40,8},{48,16},{56,24},{6... | collective-permute-start | bytes 786440 | tf_op jit(solution)/shard_map/ppermute | solution.py:377
  86.5 4.7 %near.1 = (f32[4,128,512]{2,1,0:T(8,128)}, f32[4,1,512]{2,1,0:T(1,128)}, f32[4,1,512]{2,1,0:T(1,128)}) custom-call(s32[1]{0:T(128)} %bitcast.6.kv_ref, bf16[2048,128]{1,0:T(8,128)(2,1)} %refs_1_.1, bf16[2048,256]{1,0:T(8,128)(2,1)} %k_ref.1, bf16[2048,256]{1,0:T(8,128)(2,1)} %v_ref.1), custom_call_target="tpu_custom_call" | custom-call | flops 536870912 | bytes 4194304 | tf_op jit(solution)/shard_map/near/pallas_call | solution.py:75
  93.4 4.4 %collective-permute-done.22.refs_5_ = bf16[16,2,32,128]{3,2,1,0:T(8,128)(2,1)} collective-permute-done((bf16[16,2,32,128]{3,2,1,0:T(8,128)(2,1)S(1)}, bf16[16,2,32,128]{3,2,1,0:T(8,128)(2,1)}, u32[]{:S(2)}, u32[]{:S(2)}) %collective-permute-start.22) | collective-permute-done | bytes 262176 | tf_op jit(solution)/shard_map/ppermute | solution.py:377
  98.2 3.7 %collective-permute-start.33 = (bf16[16,2,32,128]{3,2,1,0:T(8,128)(2,1)}, bf16[16,2,32,128]{3,2,1,0:T(8,128)(2,1)}, u32[]{:S(2)}, u32[]{:S(2)}) collective-permute-start(bf16[16,2,32,128]{3,2,1,0:T(8,128)(2,1)} %collective-permute-done.21.refs_4_), channel_id=1, source_target_pairs={{0,224},{8,232},{16,240},{24,248},{32,0},{40,8},{48,16},{56,24},{6... | collective-permute-start | bytes 786440 | tf_op jit(solution)/shard_map/ppermute | solution.py:377
  101.9 4.5 %collective-permute-done.8.refs_1_ = bf16[2048,128]{1,0:T(8,128)(2,1)} collective-permute-done((bf16[2048,128]{1,0:T(8,128)(2,1)S(1)}, bf16[2048,128]{1,0:T(8,128)(2,1)}, u32[]{:S(2)}, u32[]{:S(2)}) %collective-permute-start.8) | collective-permute-done | bytes 524320 | tf_op jit(solution)/shard_map/ppermute | solution.py:381
  106.4 10.6 %collective-permute-start.29 = (s32[2,4,1,4]{3,1,2,0:T(4,128)S(1)}, s32[2,4,1,4]{3,1,2,0:T(4,128)S(1)}, u32[]{:S(2)}, u32[]{:S(2)}) collective-permute-start(s32[2,4,1,4]{3,1,2,0:T(4,128)S(1)} %pad_add_fusion.1), channel_id=1, source_target_pairs={{0,1},{1,0},{2,3},{3,2},{4,5},{5,4},{6,7},{7,6},{8,9},{9,8},{10,11... | collective-permute-start | bytes 392 | tf_op jit(solution)/shard_map/ppermute | solution.py:381
  119.8 3.0 collective-permute-start.42
  123.3 7.3 %collective-permute-done.34.refs_9_ = bf16[16,2,32,128]{3,2,1,0:T(8,128)(2,1)} collective-permute-done((bf16[16,2,32,128]{3,2,1,0:T(8,128)(2,1)}, bf16[16,2,32,128]{3,2,1,0:T(8,128)(2,1)}, u32[]{:S(2)}, u32[]{:S(2)}) %collective-permute-start.34) | collective-permute-done | bytes 262176 | tf_op jit(solution)/shard_map/ppermute | solution.py:377
  136.4 4.8 %collective-permute-done.37.refs_12_ = bf16[16,2,32,128]{3,2,1,0:T(8,128)(2,1)S(1)} collective-permute-done((bf16[16,2,32,128]{3,2,1,0:T(8,128)(2,1)}, bf16[16,2,32,128]{3,2,1,0:T(8,128)(2,1)S(1)}, u32[]{:S(2)}, u32[]{:S(2)}) %collective-permute-start.37) | collective-permute-done | bytes 262176 | tf_op jit(solution)/shard_map/ppermute | solution.py:377
  148.8 8.9 %collective-permute-start.30 = (bf16[2048,128]{1,0:T(8,128)(2,1)}, bf16[2048,128]{1,0:T(8,128)(2,1)}, u32[]{:S(2)}, u32[]{:S(2)}) collective-permute-start(bf16[2048,128]{1,0:T(8,128)(2,1)} %collective-permute-done.8.refs_1_), channel_id=1, source_target_pairs={{0,1},{1,0},{2,3},{3,2},{4,5},{5,4},{6,7},{7,6},{8,9},{9,8},{10,11... | collective-permute-start | bytes 1572872 | tf_op jit(solution)/shard_map/ppermute | solution.py:381
  157.8 3.6 %collective-permute-start.44 = (bf16[16,2,32,128]{3,2,1,0:T(8,128)(2,1)}, bf16[16,2,32,128]{3,2,1,0:T(8,128)(2,1)S(1)}, u32[]{:S(2)}, u32[]{:S(2)}) collective-permute-start(bf16[16,2,32,128]{3,2,1,0:T(8,128)(2,1)} %collective-permute-done.38.refs_13_), channel_id=1, source_target_pairs={{0,224},{8,232},{16,240},{24,248},{32,0},{40,8},{48,16},{56,24},{6... | collective-permute-start | bytes 786440 | tf_op jit(solution)/shard_map/ppermute | solution.py:377
  162.2 64.1 %collect.1 = (bf16[64,2,32,128]{3,2,1,0:T(8,128)(2,1)}, bf16[64,2,48,128]{3,2,1,0:T(8,128)(2,1)}) custom-call(s32[64,4]{1,0:T(8,128)} %copy.17.where_ref, bf16[16,2,32,128]{3,2,1,0:T(8,128)(2,1)} %copy-done.6, bf16[16,2,32,128]{3,2,1,0:T(8,128)(2,1)} %copy-done.7, bf16[16,2,32,128]{3,2,1,0:T(8,128)(2,1)} %copy-done.12, bf16[16,2,32,128]{3,2,1,0:T(8,128)(2,1)} %copy-done.13, ...), custom_call_target="tpu_custom_call" | custom-call | tf_op jit(solution)/shard_map/collect/pallas_call | solution.py:152
  227.4 8.1 %far.2 = (bf16[4,144,512]{2,1,0:T(8,128)(2,1)}, bf16[4,144,512]{2,1,0:T(8,128)(2,1)}) custom-call(s32[32,6]{1,0:T(8,128)} %copy.18.where_ref, bf16[2048,128]{1,0:T(8,128)(2,1)} %collective-permute-done.30.refs_0_, bf16[2048,128]{1,0:T(8,128)(2,1)} %collective-permute-done.8.refs_1_, bf16[256,2,48,128]{3,2,1,0:T(8,128)(2,1)} %all-gather.2.cloned.1.call-done.refs_2_, ...), custom_call_target="tpu_custom_call" | custom-call | flops 1073741824 | bytes 5242880 | tf_op jit(solution)/shard_map/far/pallas_call | solution.py:255
  235.5 6.6 %collective-permute-start.47 = (bf16[4,144,512]{2,1,0:T(8,128)(2,1)}, bf16[4,144,512]{2,1,0:T(8,128)(2,1)S(1)}, u32[]{:S(2)}, u32[]{:S(2)}) collective-permute-start(bf16[4,144,512]{2,1,0:T(8,128)(2,1)} %get-tuple-element.64), channel_id=1, source_target_pairs={{0,1},{1,0},{2,3},{3,2},{4,5},{5,4},{6,7},{7,6},{8,9},{9,8},{10,11... | collective-permute-start | bytes 1769480 | tf_op jit(solution)/shard_map/ppermute | solution.py:381
  247.7 8.0 %far.3 = (bf16[4,144,512]{2,1,0:T(8,128)(2,1)}, bf16[4,144,512]{2,1,0:T(8,128)(2,1)}) custom-call(s32[32,6]{1,0:T(8,128)} %copy.19.where_ref, bf16[2048,128]{1,0:T(8,128)(2,1)} %collective-permute-done.48.refs_0_, bf16[2048,128]{1,0:T(8,128)(2,1)} %refs_1_.1, bf16[256,2,48,128]{3,2,1,0:T(8,128)(2,1)} %all-gather.2.cloned.1.call-done.refs_2_, ...), custom_call_target="tpu_custom_call" | custom-call | flops 1073741824 | bytes 5242880 | tf_op jit(solution)/shard_map/far/pallas_call | solution.py:255
  270.6 2.9 merge_here.1
  276.0 10.3 %all-to-all-start = ((bf16[8,256,128]{2,1,0:T(8,128)(2,1)}), bf16[8,256,128]{2,1,0:T(8,128)(2,1)S(1)}, u32[]{:S(2)}, u32[]{:S(2)}) async-start(bf16[8,256,128]{2,1,0:T(8,128)(2,1)} %bitcast.25), calls=%async_computation | async-start | bytes 1048576 | tf_op jit(solution)/shard_map/all_to_all | solution.py:512
  286.3 9.5 %all-to-all-done.a_ref = bf16[8,256,128]{2,1,0:T(8,128)(2,1)S(1)} async-done(((bf16[8,256,128]{2,1,0:T(8,128)(2,1)}), bf16[8,256,128]{2,1,0:T(8,128)(2,1)S(1)}, u32[]{:S(2)}, u32[]{:S(2)}) %all-to-all-start) | async-done | bytes 524320 | tf_op jit(solution)/shard_map/all_to_all | solution.py:512
  295.8 3.6 %project.1 = bf16[256,2048]{1,0:T(8,128)(2,1)} custom-call(s32[1]{0:T(128)} %bitcast.7.head_ref, bf16[8,256,128]{2,1,0:T(8,128)(2,1)S(1)} %all-to-all-done.a_ref, bf16[128,2048]{1,0:T(8,128)(2,1)S(1)} %copy-done, bf16[128,2048]{1,0:T(8,128)(2,1)S(1)} %collective-permute-done.54.refs_1_, bf16[128,2048]{1,0:T(8,128)(2,1)S(1)} %collective-permute-done.10.refs_2_, ...), custom_call_target="tpu_custom_call" | custom-call | tf_op jit(solution)/shard_map/project/pallas_call | solution.py:362
  (202 shorter events, 78.1 us)
Async XLA Ops:
  7.2 219.3 %all-gather.2.cloned.1.call-start = ((), (), s32[]{:S(2)}) async-start(), calls=%async_computation.1 | async-start | bytes 6488064 | tf_op jit(solution)/shard_map/all_gather | solution.py:407
  25.7 18.3 %collective-permute-start.4 = (bf16[4,2,48,128]{3,2,1,0:T(8,128)(2,1)}, bf16[4,2,48,128]{3,2,1,0:T(8,128)(2,1)S(1)}, u32[]{:S(2)}, u32[]{:S(2)}) collective-permute-start(bf16[4,2,48,128]{3,2,1,0:T(8,128)(2,1)} %get-tuple-element.41), channel_id=1, source_target_pairs={{0,224},{8,232},{16,240},{24,248},{32,0},{40,8},{48,16},{56,24},{6... | collective-permute-start | bytes 294920 | tf_op jit(solution)/shard_map/ppermute | solution.py:377
  50.1 27.2 %collective-permute-start.19 = (bf16[16,2,32,128]{3,2,1,0:T(8,128)(2,1)S(1)}, bf16[16,2,32,128]{3,2,1,0:T(8,128)(2,1)S(1)}, u32[]{:S(2)}, u32[]{:S(2)}) collective-permute-start(bf16[16,2,32,128]{3,2,1,0:T(8,128)(2,1)S(1)} %pad_maximum_fusion.refs_0_), channel_id=1, source_target_pairs={{0,32},{8,40},{16,48},{24,56},{32,64},{40,72},{48,80},{56,88},{64,... | collective-permute-start | bytes 786440 | tf_op jit(solution)/shard_map/ppermute | solution.py:377
  51.0 27.2 %collective-permute-start.20 = (bf16[16,2,32,128]{3,2,1,0:T(8,128)(2,1)S(1)}, bf16[16,2,32,128]{3,2,1,0:T(8,128)(2,1)S(1)}, u32[]{:S(2)}, u32[]{:S(2)}) collective-permute-start(bf16[16,2,32,128]{3,2,1,0:T(8,128)(2,1)S(1)} %pad_maximum_fusion.1.refs_1_), channel_id=1, source_target_pairs={{0,32},{8,40},{16,48},{24,56},{32,64},{40,72},{48,80},{56,88},{64,... | collective-permute-start | bytes 786440 | tf_op jit(solution)/shard_map/ppermute | solution.py:377
  77.4 20.7 %collective-permute-start.10 = (bf16[128,2048]{1,0:T(8,128)(2,1)S(1)}, bf16[128,2048]{1,0:T(8,128)(2,1)S(1)}, u32[]{:S(2)}, u32[]{:S(2)}) collective-permute-start(bf16[128,2048]{1,0:T(8,128)(2,1)S(1)} %copy-done), channel_id=1, source_target_pairs={{0,2},{1,3},{2,0},{3,1},{4,6},{5,7},{6,4},{7,5},{8,10},{9,11},{10,... | collective-permute-start | bytes 1572872 | tf_op jit(solution)/shard_map/ppermute | solution.py:381
  78.2 19.8 %collective-permute-start.11 = (bf16[128,2048]{1,0:T(8,128)(2,1)S(1)}, bf16[128,2048]{1,0:T(8,128)(2,1)S(1)}, u32[]{:S(2)}, u32[]{:S(2)}) collective-permute-start(bf16[128,2048]{1,0:T(8,128)(2,1)S(1)} %copy-done), channel_id=1, source_target_pairs={{0,4},{1,5},{2,6},{3,7},{4,0},{5,1},{6,2},{7,3},{8,12},{9,13},{10,... | collective-permute-start | bytes 1572872 | tf_op jit(solution)/shard_map/ppermute | solution.py:381
  81.4 16.7 %collective-permute-start.12 = (bf16[128,2048]{1,0:T(8,128)(2,1)S(1)}, bf16[128,2048]{1,0:T(8,128)(2,1)S(1)}, u32[]{:S(2)}, u32[]{:S(2)}) collective-permute-start(bf16[128,2048]{1,0:T(8,128)(2,1)S(1)} %copy-done), channel_id=1, source_target_pairs={{0,6},{1,7},{2,4},{3,5},{4,2},{5,3},{6,0},{7,1},{8,14},{9,15},{10,... | collective-permute-start | bytes 1572872 | tf_op jit(solution)/shard_map/ppermute | solution.py:381
  81.5 25.0 %collective-permute-start.8 = (bf16[2048,128]{1,0:T(8,128)(2,1)S(1)}, bf16[2048,128]{1,0:T(8,128)(2,1)}, u32[]{:S(2)}, u32[]{:S(2)}) collective-permute-start(bf16[2048,128]{1,0:T(8,128)(2,1)S(1)} %copy-done.2), channel_id=1, source_target_pairs={{0,2},{1,3},{2,0},{3,1},{4,6},{5,7},{6,4},{7,5},{8,10},{9,11},{10,... | collective-permute-start | bytes 1572872 | tf_op jit(solution)/shard_map/ppermute | solution.py:381
  97.8 45.3 %collective-permute-start.39 = (bf16[32,2,48,128]{3,2,1,0:T(8,128)(2,1)}, bf16[32,2,48,128]{3,2,1,0:T(8,128)(2,1)}, u32[]{:S(2)}, u32[]{:S(2)}) collective-permute-start(bf16[32,2,48,128]{3,2,1,0:T(8,128)(2,1)} %copy-done.8), channel_id=1, source_target_pairs={{0,8},{8,16},{16,24},{24,0},{32,40},{40,48},{48,56},{56,32},{64,72... | collective-permute-start | bytes 2359304 | tf_op jit(solution)/shard_map/ppermute | solution.py:377
  98.1 21.8 %collective-permute-start.31 = (bf16[16,2,32,128]{3,2,1,0:T(8,128)(2,1)S(1)}, bf16[16,2,32,128]{3,2,1,0:T(8,128)(2,1)S(1)}, u32[]{:S(2)}, u32[]{:S(2)}) collective-permute-start(bf16[16,2,32,128]{3,2,1,0:T(8,128)(2,1)S(1)} %collective-permute-done.19.refs_2_), channel_id=1, source_target_pairs={{0,32},{8,40},{16,48},{24,56},{32,64},{40,72},{48,80},{56,88},{64,... | collective-permute-start | bytes 786440 | tf_op jit(solution)/shard_map/ppermute | solution.py:377
  98.1 24.8 %collective-permute-start.32 = (bf16[16,2,32,128]{3,2,1,0:T(8,128)(2,1)S(1)}, bf16[16,2,32,128]{3,2,1,0:T(8,128)(2,1)}, u32[]{:S(2)}, u32[]{:S(2)}) collective-permute-start(bf16[16,2,32,128]{3,2,1,0:T(8,128)(2,1)S(1)} %collective-permute-done.20.refs_3_), channel_id=1, source_target_pairs={{0,32},{8,40},{16,48},{24,56},{32,64},{40,72},{48,80},{56,88},{64,... | collective-permute-start | bytes 786440 | tf_op jit(solution)/shard_map/ppermute | solution.py:377
  98.2 24.7 %collective-permute-start.33 = (bf16[16,2,32,128]{3,2,1,0:T(8,128)(2,1)}, bf16[16,2,32,128]{3,2,1,0:T(8,128)(2,1)}, u32[]{:S(2)}, u32[]{:S(2)}) collective-permute-start(bf16[16,2,32,128]{3,2,1,0:T(8,128)(2,1)} %collective-permute-done.21.refs_4_), channel_id=1, source_target_pairs={{0,224},{8,232},{16,240},{24,248},{32,0},{40,8},{48,16},{56,24},{6... | collective-permute-start | bytes 786440 | tf_op jit(solution)/shard_map/ppermute | solution.py:377
  119.8 23.6 %collective-permute-start.42 = (bf16[32,2,48,128]{3,2,1,0:T(8,128)(2,1)}, bf16[32,2,48,128]{3,2,1,0:T(8,128)(2,1)}, u32[]{:S(2)}, u32[]{:S(2)}) collective-permute-start(bf16[32,2,48,128]{3,2,1,0:T(8,128)(2,1)} %constant_dynamic-update-slice_fusion.refs_15_), channel_id=1, source_target_pairs={{0,24},{8,0},{16,8},{24,16},{32,56},{40,32},{48,40},{56,48},{64,88... | collective-permute-start | bytes 2359304 | tf_op jit(solution)/shard_map/ppermute | solution.py:377
  130.7 27.0 %collective-permute-start.41 = (bf16[32,2,48,128]{3,2,1,0:T(8,128)(2,1)}, bf16[32,2,48,128]{3,2,1,0:T(8,128)(2,1)}, u32[]{:S(2)}, u32[]{:S(2)}) collective-permute-start(bf16[32,2,48,128]{3,2,1,0:T(8,128)(2,1)} %copy-done.8), channel_id=1, source_target_pairs={{0,24},{8,0},{16,8},{24,16},{32,56},{40,32},{48,40},{56,48},{64,88... | collective-permute-start | bytes 2359304 | tf_op jit(solution)/shard_map/ppermute | solution.py:377
  132.9 24.9 %collective-permute-start.40 = (bf16[32,2,48,128]{3,2,1,0:T(8,128)(2,1)}, bf16[32,2,48,128]{3,2,1,0:T(8,128)(2,1)}, u32[]{:S(2)}, u32[]{:S(2)}) collective-permute-start(bf16[32,2,48,128]{3,2,1,0:T(8,128)(2,1)} %constant_dynamic-update-slice_fusion.refs_15_), channel_id=1, source_target_pairs={{0,8},{8,16},{16,24},{24,0},{32,40},{40,48},{48,56},{56,32},{64,72... | collective-permute-start | bytes 2359304 | tf_op jit(solution)/shard_map/ppermute | solution.py:377
  143.0 83.4 %collective-permute-start.45 = (bf16[32,2,48,128]{3,2,1,0:T(8,128)(2,1)}, bf16[32,2,48,128]{3,2,1,0:T(8,128)(2,1)S(1)}, u32[]{:S(2)}, u32[]{:S(2)}) collective-permute-start(bf16[32,2,48,128]{3,2,1,0:T(8,128)(2,1)} %collective-permute-done.39.refs_16_), channel_id=1, source_target_pairs={{0,8},{8,16},{16,24},{24,0},{32,40},{40,48},{48,56},{56,32},{64,72... | collective-permute-start | bytes 2359304 | tf_op jit(solution)/shard_map/ppermute | solution.py:377
  143.5 82.9 %collective-permute-start.46 = (bf16[32,2,48,128]{3,2,1,0:T(8,128)(2,1)}, bf16[32,2,48,128]{3,2,1,0:T(8,128)(2,1)}, u32[]{:S(2)}, u32[]{:S(2)}) collective-permute-start(bf16[32,2,48,128]{3,2,1,0:T(8,128)(2,1)} %collective-permute-done.42.refs_19_), channel_id=1, source_target_pairs={{0,24},{8,0},{16,8},{24,16},{32,56},{40,32},{48,40},{56,48},{64,88... | collective-permute-start | bytes 2359304 | tf_op jit(solution)/shard_map/ppermute | solution.py:377
  148.8 77.6 %collective-permute-start.30 = (bf16[2048,128]{1,0:T(8,128)(2,1)}, bf16[2048,128]{1,0:T(8,128)(2,1)}, u32[]{:S(2)}, u32[]{:S(2)}) collective-permute-start(bf16[2048,128]{1,0:T(8,128)(2,1)} %collective-permute-done.8.refs_1_), channel_id=1, source_target_pairs={{0,1},{1,0},{2,3},{3,2},{4,5},{5,4},{6,7},{7,6},{8,9},{9,8},{10,11... | collective-permute-start | bytes 1572872 | tf_op jit(solution)/shard_map/ppermute | solution.py:381
  157.7 68.6 %collective-permute-start.43 = (bf16[16,2,32,128]{3,2,1,0:T(8,128)(2,1)}, bf16[16,2,32,128]{3,2,1,0:T(8,128)(2,1)S(1)}, u32[]{:S(2)}, u32[]{:S(2)}) collective-permute-start(bf16[16,2,32,128]{3,2,1,0:T(8,128)(2,1)} %copy-done.15), channel_id=1, source_target_pairs={{0,32},{8,40},{16,48},{24,56},{32,64},{40,72},{48,80},{56,88},{64,... | collective-permute-start | bytes 786440 | tf_op jit(solution)/shard_map/ppermute | solution.py:377
  157.8 68.5 %collective-permute-start.44 = (bf16[16,2,32,128]{3,2,1,0:T(8,128)(2,1)}, bf16[16,2,32,128]{3,2,1,0:T(8,128)(2,1)S(1)}, u32[]{:S(2)}, u32[]{:S(2)}) collective-permute-start(bf16[16,2,32,128]{3,2,1,0:T(8,128)(2,1)} %collective-permute-done.38.refs_13_), channel_id=1, source_target_pairs={{0,224},{8,232},{16,240},{24,248},{32,0},{40,8},{48,16},{56,24},{6... | collective-permute-start | bytes 786440 | tf_op jit(solution)/shard_map/ppermute | solution.py:377
  262.4 23.9 %collective-permute-start.54 = (bf16[128,2048]{1,0:T(8,128)(2,1)S(1)}, bf16[128,2048]{1,0:T(8,128)(2,1)S(1)}, u32[]{:S(2)}, u32[]{:S(2)}) collective-permute-start(bf16[128,2048]{1,0:T(8,128)(2,1)S(1)} %copy-done), channel_id=1, source_target_pairs={{0,1},{1,0},{2,3},{3,2},{4,5},{5,4},{6,7},{7,6},{8,9},{9,8},{10,11... | collective-permute-start | bytes 1572872 | tf_op jit(solution)/shard_map/ppermute | solution.py:381
  265.5 20.8 %collective-permute-start.55 = (bf16[128,2048]{1,0:T(8,128)(2,1)S(1)}, bf16[128,2048]{1,0:T(8,128)(2,1)}, u32[]{:S(2)}, u32[]{:S(2)}) collective-permute-start(bf16[128,2048]{1,0:T(8,128)(2,1)S(1)} %collective-permute-done.10.refs_2_), channel_id=1, source_target_pairs={{0,1},{1,0},{2,3},{3,2},{4,5},{5,4},{6,7},{7,6},{8,9},{9,8},{10,11... | collective-permute-start | bytes 1572872 | tf_op jit(solution)/shard_map/ppermute | solution.py:381
  268.7 17.6 %collective-permute-start.56 = (bf16[128,2048]{1,0:T(8,128)(2,1)S(1)}, bf16[128,2048]{1,0:T(8,128)(2,1)}, u32[]{:S(2)}, u32[]{:S(2)}) collective-permute-start(bf16[128,2048]{1,0:T(8,128)(2,1)S(1)} %collective-permute-done.11.refs_4_), channel_id=1, source_target_pairs={{0,1},{1,0},{2,3},{3,2},{4,5},{5,4},{6,7},{7,6},{8,9},{9,8},{10,11... | collective-permute-start | bytes 1572872 | tf_op jit(solution)/shard_map/ppermute | solution.py:381
  276.0 19.7 %all-to-all-start = ((bf16[8,256,128]{2,1,0:T(8,128)(2,1)}), bf16[8,256,128]{2,1,0:T(8,128)(2,1)S(1)}, u32[]{:S(2)}, u32[]{:S(2)}) async-start(bf16[8,256,128]{2,1,0:T(8,128)(2,1)} %bitcast.25), calls=%async_computation | async-start | bytes 1048576 | tf_op jit(solution)/shard_map/all_to_all | solution.py:512
  (62 other events, 834.8 us)
Sparse Core Ops, SparseCore 0:
  25.8 102.3 all-gather.1

commit v4 on v2

v4 whole, which is shorter than its diff:
```python
import functools
import math

import jax
import jax.numpy as jnp
from jax import lax
from jax.experimental import pallas as pl
from jax.experimental.pallas import tpu as pltpu
from jax.sharding import PartitionSpec as P

HD = 128
GROUP = 4
BLK = 512
SEL = 4
QB = 4
BLOCKS = 8
NX = 4
NZ = 8
TAIL = 16
SCALE = math.log2(math.e) / math.sqrt(HD)
NEG = -1e30
F32 = jnp.float32
BF16 = jnp.bfloat16
SPLIT = (4, 6, 6)
VMEM_BYTES = 56 << 20


def dot_nt(a, b):
    return lax.dot_general(a, b, (((1,), (1,)), ((), ())), preferred_element_type=F32)


def dot_tn(a, b):
    return lax.dot_general(a, b, (((0,), (0,)), ((), ())), preferred_element_type=F32)


def rounded_top(raw):
    return (raw * SCALE).astype(BF16).astype(F32)


def near_kernel(kv_ref, q_ref, k_ref, v_ref, acc_ref, m_ref, l_ref):
    scores = dot_nt(k_ref[...], q_ref[...])
    keys = lax.broadcasted_iota(jnp.int32, (BLK, BLK), 0)
    rows = lax.broadcasted_iota(jnp.int32, (BLK, BLK), 1)
    scores = jnp.where(keys <= rows, scores, NEG)
    top = rounded_top(jnp.max(scores, axis=0, keepdims=True))
    weights = jnp.exp2(scores * SCALE - top)
    m_ref[0] = top
    l_ref[0] = jnp.sum(weights, axis=0, keepdims=True)
    acc_ref[0] = dot_tn(v_ref[...], weights.astype(BF16))


def state_shapes():
    return [
        jax.ShapeDtypeStruct((QB, HD, BLK), F32),
        jax.ShapeDtypeStruct((QB, 1, BLK), F32),
        jax.ShapeDtypeStruct((QB, 1, BLK), F32),
    ]


def near(queries, span_keys, span_values, kv):
    grid_spec = pltpu.PrefetchScalarGridSpec(
        num_scalar_prefetch=1,
        grid=(QB,),
        in_specs=[
            pl.BlockSpec((BLK, HD), lambda i, kv: (i, 0)),
            pl.BlockSpec((BLK, HD), lambda i, kv: (i, kv[0])),
            pl.BlockSpec((BLK, HD), lambda i, kv: (i, kv[0])),
        ],
        out_specs=[
            pl.BlockSpec((1, HD, BLK), lambda i, kv: (i, 0, 0)),
            pl.BlockSpec((1, 1, BLK), lambda i, kv: (i, 0, 0)),
            pl.BlockSpec((1, 1, BLK), lambda i, kv: (i, 0, 0)),
        ],
    )
    return pl.pallas_call(
        near_kernel,
        grid_spec=grid_spec,
        out_shape=state_shapes(),
        cost_estimate=pl.CostEstimate(
            flops=QB * 4 * BLK * BLK * HD, bytes_accessed=4 << 20, transcendentals=QB * BLK * BLK
        ),
        name="near",
    )(kv, queries, span_keys, span_values)


def pack_state(ref, i, out, top, total):
    ref[i, :HD, :] = out.astype(BF16)
    high = total.astype(BF16)
    low = (total - high.astype(F32)).astype(BF16)
    ref[i, HD:, :] = jnp.concatenate(
        [top.astype(BF16), high, low, jnp.zeros((TAIL - 3, out.shape[1]), BF16)], axis=0
    )


def unpack_state(ref, i):
    tail = ref[i, HD:, :].astype(F32)
    return ref[i, :HD, :].astype(F32), tail[0:1], tail[1:2] + tail[2:3]


def far_kernel(where_ref, *refs, arrays):
    q_refs, refs = refs[:2], refs[2:]
    whole_ref, refs = refs[0], refs[1:]
    sources, refs = (refs[:arrays], refs[arrays : 2 * arrays]), refs[2 * arrays :]
    piece_refs, whole_out_ref, refs = refs[:QB], refs[QB], refs[QB + 1 :]
    parts = 1 + len(sources)
    buffers, refs = refs[:parts], refs[parts:]
    score_refs, weight_refs, sems = refs[:2], refs[2:4], refs[4]

    def fetch(pick, carry):
        unit = pick // SEL
        pltpu.make_async_copy(
            whole_ref.at[where_ref[pick, 0]], buffers[0].at[pick], sems.at[unit, 0]
        ).start()
        array, index = where_ref[pick, 1], where_ref[pick, 2]
        for number in range(arrays):

            def start(number=number):
                for part in range(1, parts):
                    pltpu.make_async_copy(
                        sources[part - 1][number].at[index],
                        buffers[part].at[pick],
                        sems.at[unit, part],
                    ).start()

            pl.when(array == number)(start)
        return carry

    lax.fori_loop(0, 2 * QB * SEL, fetch, 0)

    def joined(row, which):
        return jnp.concatenate(
            [buffers[part][row * SEL + j, which] for part in range(parts) for j in range(SEL)],
            axis=0,
        )

    def score(row, q_ref, i, score_ref):
        for part in range(parts):
            held = buffers[part].at[pl.ds(row * SEL, SEL)]
            pltpu.make_async_copy(held, held, sems.at[row, part]).wait()
        score_ref[...] = dot_nt(joined(row, 0), q_ref[pl.ds(i * BLK, BLK), :])

    def soften(score_ref, weight_ref):
        tops, totals = [], []
        for lane in range(0, BLK, HD):
            lanes = slice(lane, lane + HD)
            top = rounded_top(jnp.max(score_ref[:, lanes], axis=0, keepdims=True))
            total = jnp.zeros((8, HD), F32)
            for row in range(0, BLK, 64):
                weights = jnp.exp2(score_ref[row : row + 64, lanes] * SCALE - top)
                weight_ref[row : row + 64, lanes] = weights.astype(BF16)
                total = total + jnp.sum(weights.reshape(8, 8, HD), axis=0)
            tops.append(top)
            totals.append(jnp.sum(total, axis=0, keepdims=True))
        return jnp.concatenate(tops, axis=1), jnp.concatenate(totals, axis=1)

    def finish(row, weight_ref, out_ref, i, top, total):
        pack_state(out_ref, i, dot_tn(joined(row, 1), weight_ref[...]), top, total)

    for first in range(0, 2 * QB, 2):
        units = [first, first + 1]
        for k, row in enumerate(units):
            score(row, q_refs[row // QB], row % QB, score_refs[k])
        for k, row in enumerate(units):
            top, total = soften(score_refs[k], weight_refs[k])
            if row < QB:
                finish(row, weight_refs[k], piece_refs[row], 0, top, total)
            else:
                finish(row, weight_refs[k], whole_out_ref, row % QB, top, total)


def far(where, queries, whole, x_parts):
    pay = HD + TAIL
    vmem = pl.BlockSpec(memory_space=pltpu.VMEM)
    hbm = pl.BlockSpec(memory_space=pl.ANY)
    arrays = [array for part in x_parts for array in part]
    shapes = [whole.shape[1:]] + [part[0].shape[1:] for part in x_parts]
    return pl.pallas_call(
        functools.partial(far_kernel, arrays=len(x_parts[0])),
        in_specs=[pl.BlockSpec(memory_space=pltpu.SMEM)]
        + [vmem] * 2
        + [hbm] * (1 + len(arrays)),
        out_specs=[vmem] * (QB + 1),
        out_shape=[jax.ShapeDtypeStruct((1, pay, BLK), BF16)] * QB
        + [jax.ShapeDtypeStruct((QB, pay, BLK), BF16)],
        scratch_shapes=[pltpu.VMEM((2 * QB * SEL,) + shape, BF16) for shape in shapes]
        + [pltpu.VMEM((BLK, BLK), F32)] * 2
        + [pltpu.VMEM((BLK, BLK), BF16)] * 2
        + [pltpu.SemaphoreType.DMA((2 * QB, len(shapes)))],
        compiler_params=pltpu.CompilerParams(vmem_limit_bytes=VMEM_BYTES),
        cost_estimate=pl.CostEstimate(
            flops=8 * 2 * QB * 4 * BLK * BLK * HD,
            bytes_accessed=5 << 20,
            transcendentals=2 * QB * BLK * BLK,
        ),
        name="far",
    )(where, *queries, whole, *arrays)


def merge_two_kernel(a_ref, *refs):
    b_refs, out_refs = refs[:QB], refs[QB:]
    per = QB // len(out_refs)
    for i in range(QB):
        acc_a, m_a, l_a = unpack_state(a_ref, i)
        acc_b, m_b, l_b = unpack_state(b_refs[i], 0)
        top = jnp.maximum(m_a, m_b)
        f_a = jnp.exp2(m_a - top)
        f_b = jnp.exp2(m_b - top)
        pack_state(
            out_refs[i // per], i % per, f_a * acc_a + f_b * acc_b, top, f_a * l_a + f_b * l_b
        )


def merge_two(mine, others, pieces):
    vmem = pl.BlockSpec(memory_space=pltpu.VMEM)
    shape = (QB // pieces,) + mine.shape[1:]
    return pl.pallas_call(
        merge_two_kernel,
        in_specs=[vmem] * (1 + QB),
        out_specs=[vmem] * pieces,
        out_shape=[jax.ShapeDtypeStruct(shape, BF16)] * pieces,
        name="merge_two",
    )(mine, *others)


def merge_last_kernel(a_ref, *refs):
    core_refs, refs = refs[:QB], refs[QB:]
    (acc_ref, m_ref, l_ref), chip_refs, out_ref = refs[:3], refs[3:-1], refs[-1]
    per = QB // len(chip_refs)
    for i in range(QB):
        states = [unpack_state(a_ref, i), unpack_state(core_refs[i], 0)]
        states.append(unpack_state(chip_refs[i // per], i % per))
        states.append((acc_ref[i], m_ref[i], l_ref[i]))
        top = functools.reduce(jnp.maximum, [m for _, m, _ in states])
        factors = [jnp.exp2(m - top) for _, m, _ in states]
        total = sum(f * l for f, (_, _, l) in zip(factors, states))
        factors = [f / total for f in factors]
        out = sum(f * acc for f, (acc, _, _) in zip(factors, states))
        out_ref[i * BLK : (i + 1) * BLK, :] = out.T.astype(BF16)


def merge_last(mine, core_parts, near_state, chip_parts):
    vmem = pl.BlockSpec(memory_space=pltpu.VMEM)
    arrays = [mine, *core_parts, *near_state, *chip_parts]
    return pl.pallas_call(
        merge_last_kernel,
        in_specs=[vmem] * len(arrays),
        out_specs=vmem,
        out_shape=jax.ShapeDtypeStruct((QB * BLK, HD), BF16),
        name="merge_last",
    )(*arrays)


def project_kernel(head_ref, a_ref, *refs):
    w_refs, out_ref = refs[:-1], refs[-1]
    rows = jnp.concatenate([a_ref[head_ref[0] ^ i] for i in range(len(w_refs))], axis=1)
    tile = 512
    for first in range(0, out_ref.shape[1], tile):
        weight = jnp.concatenate([w_ref[:, first : first + tile] for w_ref in w_refs], axis=0)
        out_ref[:, first : first + tile] = jnp.dot(
            rows, weight, preferred_element_type=F32
        ).astype(BF16)


def project(head, parts, weights):
    vmem = pl.BlockSpec(memory_space=pltpu.VMEM)
    return pl.pallas_call(
        project_kernel,
        in_specs=[pl.BlockSpec(memory_space=pltpu.SMEM)] + [vmem] * (1 + len(weights)),
        out_specs=vmem,
        out_shape=jax.ShapeDtypeStruct((parts.shape[1], weights[0].shape[1]), BF16),
        compiler_params=pltpu.CompilerParams(vmem_limit_bytes=24 << 20),
        name="project",
    )(head, parts, *weights)


def shift(arrays, dz, dx):
    pairs = []
    for z in range(NZ):
        for x in range(NX):
            pairs.append((z * NX + x, (z + dz) % NZ * NX + (x + dx) % NX))
    return [lax.ppermute(array, "ctx", pairs) for array in arrays]


def swap(array, bits):
    return lax.ppermute(array, "head", [(h, h ^ bits) for h in range(lax.axis_size("head"))])


def after(value, *earlier):
    return lax.optimization_barrier((value, earlier))[0]


def spread_x(array):
    half = array.shape[0] // 2
    halves = [array[:half], array[half:]]
    below, above = shift(halves, 0, 1), shift(halves, 0, -1)

    def rest(*earlier):
        low, high = after((below[0], above[1]), *earlier)
        return shift([low], 0, 1) + shift([high], 0, -1)

    return [array, *below, *above], rest


def body(queries, block_picks, span_keys, span_values, cache_keys, cache_values, out_weight):
    heads = lax.axis_size("head")
    head = lax.axis_index("head")
    ctx = lax.axis_index("ctx")
    part = head % GROUP
    kv = head // GROUP
    share = BLK // GROUP
    columns = [[z * NX + x for z in range(NZ)] for x in range(NX)]

    def cut(first, rows):
        pieces = []
        for cache in (cache_keys, cache_values):
            view = cache.reshape(BLOCKS, BLK, cache.shape[1])
            pieces.append(
                lax.dynamic_slice(view, (0, part * share + first, kv * HD), (BLOCKS, rows, HD))
            )
        return jnp.stack(pieces, axis=1)

    rows = [share * sixteenths // 16 for sixteenths in SPLIT]
    columns_0, columns_1 = [
        lax.all_gather(
            cut(first, count), "ctx", axis=0, tiled=True, axis_index_groups=columns
        )
        for first, count in ((0, rows[0]), (rows[0], rows[1]))
    ]
    whole = lax.all_gather(cut(rows[0] + rows[1], rows[2]), "ctx", axis=0, tiled=True)
    x_part_0, rest_0 = spread_x(columns_0)
    x_part_1, rest_1 = spread_x(columns_1)
    x_part_0 = x_part_0 + rest_0()

    queries_chip = swap(queries, 2)
    picks_chip = swap(block_picks, 2)
    weights = [out_weight] + [None] * (heads - 1)
    for bits in range(2, heads, 2):
        weights[bits] = swap(out_weight, bits)
    near_state = near(after(queries, columns_1), span_keys, span_values, kv[None])
    x_part_1 = x_part_1 + rest_1(*near_state)
    queries_pair, picks_pair, weights_even = after(
        ([queries, queries_chip], jnp.stack([block_picks, picks_chip]), weights[::2]), *x_part_0
    )
    group_queries = [queries, swap(queries_pair[0], 1), queries_chip, swap(queries_pair[1], 1)]
    picks_core = swap(picks_pair, 1)
    group_picks = [picks_pair[0], picks_core[0], picks_pair[1], picks_core[1]]
    for i, bits in enumerate(range(0, heads, 2)):
        weights[bits + 1] = swap(weights_even[i], 1)

    picks = jnp.stack(group_picks).reshape(GROUP, QB * SEL)
    owner, local = picks // BLOCKS, picks % BLOCKS
    dx = (owner % NX - ctx % NX) % NX
    place = owner // NX * BLOCKS + local
    half = NZ * BLOCKS // 2
    upper = (place >= half).astype(jnp.int32)
    first_array = jnp.where(dx == 3, 1, jnp.where(dx == 1, 3, 5))
    where = jnp.stack(
        [
            picks,
            jnp.where(dx == 0, 0, first_array + upper),
            jnp.where(dx == 0, place, place - half * upper),
        ],
        axis=-1,
    ).astype(jnp.int32)

    def far_of(first, second, where):
        return far(
            jnp.concatenate([where[first], where[second]], axis=0),
            [group_queries[first], group_queries[second]],
            whole,
            [x_part_0, x_part_1],
        )

    where, group_queries, weights = lax.optimization_barrier((where, group_queries, weights))
    *far_corner, far_chip = far_of(3, 2, where)
    for_chip = merge_two(far_chip, [swap(piece, 1) for piece in far_corner], 2)
    chip_parts = [swap(piece, 2) for piece in for_chip]
    *far_core, far_own = far_of(1, 0, after(where, *for_chip))
    core_parts = [swap(piece, 1) for piece in after(far_core, *chip_parts)]
    attention = merge_last(far_own, core_parts, near_state, chip_parts)

    share_rows = attention.shape[0] // heads
    parts = lax.all_to_all(
        attention.reshape(heads, share_rows, HD), "head", split_axis=0, concat_axis=0, tiled=True
    )
    return attention, project(head[None], parts, weights)


def solution(mesh):
    placed = (
        P("ctx", "head"),
        P("ctx", "head", None),
        P("ctx", None),
        P("ctx", None),
        P("ctx", None),
        P("ctx", None),
        P("head", None),
    )
    return jax.shard_map(
        body,
        mesh=mesh,
        in_specs=placed,
        out_specs=(P("ctx", "head"), P(("ctx", "head"), None)),
        check_vma=False,
    )
```

time: 223 us -> 269 us (1.21)
  waiting for transfers between devices: 70.9 us -> 163 us
  starting transfers between devices: 71.5 us -> 36.2 us
  local copies, waits for them, and re-layouts: 24.1 us -> 9.79 us
  blocking collectives: 0 us -> 13.8 us
  Pallas kernels: 36.6 us -> 29.2 us
    all_gather x1 -> x3, waiting for transfers between devices: 4.2 us -> 69.3 us  [the longest x2 64.2 us: body(): lax.all_gather(cut(first, count), 'ctx', axis=0, tiled=True, axis_index_g...]
    ppermute x24 -> x12, waiting for transfers between devices: 47.5 us -> 83.5 us  [shift(): return [lax.ppermute(array, 'ctx', pairs) for array in arrays]]
    ppermute x24 -> x12, starting transfers between devices: 37.5 us -> 16.6 us  [shift(): return [lax.ppermute(array, 'ctx', pairs) for array in arrays]]
    unnamed x57 -> x20, local copies, waits for them, and re-layouts: 16.2 us -> 1.86 us
    all_to_all x0 -> x1, blocking collectives: none -> 13.8 us  [body(): lax.all_to_all(attention.reshape(heads, share_rows, HD), 'head', split_ax...]
    ppermute x19 -> x22, starting transfers between devices: 29.7 us -> 19.5 us  [swap(): lax.ppermute(array, 'head', [(h, h ^ bits) for h in range(lax.axis_size('...]
    all_to_all x1 -> x0, waiting for transfers between devices: 9.41 us -> none  [body(): lax.all_to_all(attention.reshape(heads, share_rows, HD), 'head', split_ax...]
    pallas_call x6 -> x5, Pallas kernels: 31.9 us -> 24.6 us  [the longest x2 15.8 us: far(): pl.pallas_call(functools.partial(far_kernel, arrays=len(x_parts[0])), in_...]
  transfers between devices with their start and end apart: 45 -> 37, of which waited for: 12 -> 21; matrix products, arithmetic and copies ran while one was open for 9% -> 3% of each run, Pallas kernels for 14% -> 5%
where the time goes in v4:
time: 269 us; the launch traced here: 268 us
  waiting for transfers between devices  163 us (61%)
  starting transfers between devices  36.2 us (13%)
  Pallas kernels  29.2 us (11%)
  between operations  13.9 us (5%)
  blocking collectives  13.8 us (5%)
  local copies, waits for them, and re-layouts  9.79 us (4%)
    ppermute x12, waiting for transfers between devices, shift(): return [lax.ppermute(array, 'ctx', pairs) for array in arrays]  83.5 us
    all_gather x2, waiting for transfers between devices, body(): lax.all_gather(cut(first, count), 'ctx', axis=0, tiled=True, axis_index_g...  64.2 us
    ppermute x22, starting transfers between devices, swap(): lax.ppermute(array, 'head', [(h, h ^ bits) for h in range(lax.axis_size('...  19.5 us
    ppermute x12, starting transfers between devices, shift(): return [lax.ppermute(array, 'ctx', pairs) for array in arrays]  16.6 us
    pallas_call x2, Pallas kernels, far(): pl.pallas_call(functools.partial(far_kernel, arrays=len(x_parts[0])), in_...  15.8 us
    all_to_all x1, blocking collectives, body(): lax.all_to_all(attention.reshape(heads, share_rows, HD), 'head', split_ax...  13.8 us
    ppermute x22, waiting for transfers between devices, swap(): lax.ppermute(array, 'head', [(h, h ^ bits) for h in range(lax.axis_size('...  10.2 us
  transfers between devices with their start and end apart: 37, of which 21 were waited for; matrix products, arithmetic and copies ran while one was open for 3% of the time, Pallas kernels for 5%

profile of v4, /device:TPU:1, one launch (start us, length us, event | category | flops | bytes accessed | tf_op | source)
XLA Modules:
  0.0 268.4 jit_solution(6393263791222531209)
XLA Ops:
  15.7 32.9 %all-gather.4.cloned.1.call-done.refs_3_ = bf16[64,2,32,128]{3,2,1,0:T(8,128)(2,1)} async-done(((bf16[8,2,32,128]{3,2,1,0:T(8,128)(2,1)}), bf16[64,2,32,128]{3,2,1,0:T(8,128)(2,1)}) %all-gather.4.cloned.1.call-update) | async-done | bytes 1048592 | tf_op jit(solution)/shard_map/all_gather | solution.py:324
  50.6 2.4 collective-permute-start.8
  55.5 2.7 collective-permute-start.3
  58.8 31.3 %all-gather.8.cloned.1.call-done.refs_10_ = bf16[64,2,48,128]{3,2,1,0:T(8,128)(2,1)} async-done(((bf16[8,2,48,128]{3,2,1,0:T(8,128)(2,1)}), bf16[64,2,48,128]{3,2,1,0:T(8,128)(2,1)}) %all-gather.8.cloned.1.call-update) | async-done | bytes 1572880 | tf_op jit(solution)/shard_map/all_gather | solution.py:324
  90.1 2.4 fusion.7
  94.4 2.7 collective-permute-start.7
  97.1 2.7 collective-permute-start.10
  99.8 4.7 %near.1 = (f32[4,128,512]{2,1,0:T(8,128)}, f32[4,1,512]{2,1,0:T(1,128)}, f32[4,1,512]{2,1,0:T(1,128)}) custom-call(s32[1]{0:T(128)} %bitcast.10.kv_ref, bf16[2048,128]{1,0:T(8,128)(2,1)} %refs_1_, bf16[2048,256]{1,0:T(8,128)(2,1)} %k_ref.1, bf16[2048,256]{1,0:T(8,128)(2,1)} %v_ref.1), custom_call_target="tpu_custom_call" | custom-call | flops 536870912 | bytes 4194304 | tf_op jit(solution)/shard_map/near/pallas_call | solution.py:75
  104.5 16.6 %collective-permute-done.7.refs_6_ = bf16[32,2,32,128]{3,2,1,0:T(8,128)(2,1)} collective-permute-done((bf16[32,2,32,128]{3,2,1,0:T(8,128)(2,1)S(1)}, bf16[32,2,32,128]{3,2,1,0:T(8,128)(2,1)}, u32[]{:S(2)}, u32[]{:S(2)}) %collective-permute-start.7) | collective-permute-done | bytes 524320 | tf_op jit(solution)/shard_map/ppermute | solution.py:281
  121.1 2.8 %collective-permute-done.9.refs_8_ = bf16[32,2,32,128]{3,2,1,0:T(8,128)(2,1)} collective-permute-done((bf16[32,2,32,128]{3,2,1,0:T(8,128)(2,1)}, bf16[32,2,32,128]{3,2,1,0:T(8,128)(2,1)}, u32[]{:S(2)}, u32[]{:S(2)}) %collective-permute-start.9) | collective-permute-done | bytes 524320 | tf_op jit(solution)/shard_map/ppermute | solution.py:281
  123.9 9.4 %collective-permute-done.10.refs_9_ = bf16[32,2,32,128]{3,2,1,0:T(8,128)(2,1)} collective-permute-done((bf16[32,2,32,128]{3,2,1,0:T(8,128)(2,1)}, bf16[32,2,32,128]{3,2,1,0:T(8,128)(2,1)}, u32[]{:S(2)}, u32[]{:S(2)}) %collective-permute-start.10) | collective-permute-done | bytes 524320 | tf_op jit(solution)/shard_map/ppermute | solution.py:281
  133.3 4.9 %collective-permute-start.11 = (s32[2,4,1,4]{3,1,2,0:T(4,128)S(1)}, s32[2,4,1,4]{3,1,2,0:T(4,128)S(1)}, u32[]{:S(2)}, u32[]{:S(2)}) collective-permute-start(s32[2,4,1,4]{3,1,2,0:T(4,128)S(1)} %pad_add_fusion.2), channel_id=1, source_target_pairs={{0,1},{1,0},{2,3},{3,2},{4,5},{5,4},{6,7},{7,6},{8,9},{9,8},{10,11... | collective-permute-start | bytes 392 | tf_op jit(solution)/shard_map/ppermute | solution.py:285
  141.2 3.2 %collective-permute-start.20 = (bf16[32,2,48,128]{3,2,1,0:T(8,128)(2,1)}, bf16[32,2,48,128]{3,2,1,0:T(8,128)(2,1)}, u32[]{:S(2)}, u32[]{:S(2)}) collective-permute-start(bf16[32,2,48,128]{3,2,1,0:T(8,128)(2,1)} %get-tuple-element.100), channel_id=1, source_target_pairs={{0,24},{8,0},{16,8},{24,16},{32,56},{40,32},{48,40},{56,48},{64,88... | collective-permute-start | bytes 2359304 | tf_op jit(solution)/shard_map/ppermute | solution.py:281
  144.8 2.7 %collective-permute-start.23 = (bf16[32,2,48,128]{3,2,1,0:T(8,128)(2,1)}, bf16[32,2,48,128]{3,2,1,0:T(8,128)(2,1)}, u32[]{:S(2)}, u32[]{:S(2)}) collective-permute-start(bf16[32,2,48,128]{3,2,1,0:T(8,128)(2,1)} %collective-permute-done.21.refs_14_), channel_id=1, source_target_pairs={{0,24},{8,0},{16,8},{24,16},{32,56},{40,32},{48,40},{56,48},{64,88... | collective-permute-start | bytes 2359304 | tf_op jit(solution)/shard_map/ppermute | solution.py:281
  149.1 25.0 %collective-permute-done.19.refs_12_ = bf16[32,2,48,128]{3,2,1,0:T(8,128)(2,1)} collective-permute-done((bf16[32,2,48,128]{3,2,1,0:T(8,128)(2,1)}, bf16[32,2,48,128]{3,2,1,0:T(8,128)(2,1)}, u32[]{:S(2)}, u32[]{:S(2)}) %collective-permute-start.19) | collective-permute-done | bytes 786464 | tf_op jit(solution)/shard_map/ppermute | solution.py:281
  174.2 3.1 %collective-permute-done.20.refs_13_ = bf16[32,2,48,128]{3,2,1,0:T(8,128)(2,1)} collective-permute-done((bf16[32,2,48,128]{3,2,1,0:T(8,128)(2,1)}, bf16[32,2,48,128]{3,2,1,0:T(8,128)(2,1)}, u32[]{:S(2)}, u32[]{:S(2)}) %collective-permute-start.20) | collective-permute-done | bytes 786464 | tf_op jit(solution)/shard_map/ppermute | solution.py:281
  177.3 26.5 %collective-permute-done.22.refs_15_ = bf16[32,2,48,128]{3,2,1,0:T(8,128)(2,1)} collective-permute-done((bf16[32,2,48,128]{3,2,1,0:T(8,128)(2,1)}, bf16[32,2,48,128]{3,2,1,0:T(8,128)(2,1)}, u32[]{:S(2)}, u32[]{:S(2)}) %collective-permute-start.22) | collective-permute-done | bytes 786464 | tf_op jit(solution)/shard_map/ppermute | solution.py:281
  203.8 5.0 %all-gather.6.cloned.1.call-done.refs_2_ = bf16[256,2,48,128]{3,2,1,0:T(8,128)(2,1)} async-done(((bf16[8,2,48,128]{3,2,1,0:T(8,128)(2,1)}), bf16[256,2,48,128]{3,2,1,0:T(8,128)(2,1)}) %all-gather.6.cloned.1.call-update) | async-done | bytes 6291472 | tf_op jit(solution)/shard_map/all_gather | solution.py:329
  208.9 7.9 %far.2 = (bf16[1,144,512]{2,1,0:T(8,128)(2,1)}, bf16[1,144,512]{2,1,0:T(8,128)(2,1)}, bf16[1,144,512]{2,1,0:T(8,128)(2,1)}, bf16[1,144,512]{2,1,0:T(8,128)(2,1)}, bf16[4,144,512]{2,1,0:T(8,128)(2,1)}) custom-call(s32[32,3]{1,0:T(8,128)} %copy.13.where_ref, bf16[2048,128]{1,0:T(8,128)(2,1)} %collective-permute-done.13.refs_0_, ...), custom_call_target="tpu_custom_call" | custom-call | flops 8589934592 | bytes 5242880 | tf_op jit(solution)/shard_map/far/pallas_call | solution.py:177
  224.4 7.9 %far.3 = (bf16[1,144,512]{2,1,0:T(8,128)(2,1)}, bf16[1,144,512]{2,1,0:T(8,128)(2,1)}, bf16[1,144,512]{2,1,0:T(8,128)(2,1)}, bf16[1,144,512]{2,1,0:T(8,128)(2,1)}, bf16[4,144,512]{2,1,0:T(8,128)(2,1)}) custom-call(s32[32,3]{1,0:T(8,128)} %copy.14.where_ref, bf16[2048,128]{1,0:T(8,128)(2,1)} %collective-permute-done.12.refs_0_, bf16[2048,128]{1,0:T(8,128)(2,1)} %refs_1_, ...), custom_call_target="tpu_custom_call" | custom-call | flops 8589934592 | bytes 5242880 | tf_op jit(solution)/shard_map/far/pallas_call | solution.py:177
  232.4 4.8 %collective-permute-done.29.refs_8_ = bf16[2,144,512]{2,1,0:T(8,128)(2,1)} collective-permute-done((bf16[2,144,512]{2,1,0:T(8,128)(2,1)}, bf16[2,144,512]{2,1,0:T(8,128)(2,1)}, u32[]{:S(2)}, u32[]{:S(2)}) %collective-permute-start.29) | collective-permute-done | bytes 294944 | tf_op jit(solution)/shard_map/ppermute | solution.py:285
  240.5 3.2 %merge_last.1 = bf16[2048,128]{1,0:T(8,128)(2,1)} custom-call(bf16[4,144,512]{2,1,0:T(8,128)(2,1)} %get-tuple-element.75.a_ref, bf16[1,144,512]{2,1,0:T(8,128)(2,1)} %collective-permute-done.30.refs_0_, bf16[1,144,512]{2,1,0:T(8,128)(2,1)} %collective-permute-done.31.refs_1_, bf16[1,144,512]{2,1,0:T(8,128)(2,1)} %collective-permute-done.32.refs_2_, ...), custom_call_target="tpu_custom_call" | custom-call | tf_op jit(solution)/shard_map/merge_last/pallas_call | solution.py:244
  243.7 13.8 %all_to_all.5.a_ref = bf16[8,256,128]{2,1,0:T(8,128)(2,1)S(1)} all-to-all(bf16[8,256,128]{2,1,0:T(8,128)(2,1)} %bitcast.33), channel_id=1, replica_groups=mesh['ctx'=32,'head'=8] {'head'}, dimensions={0} | all-to-all | bytes 1048576 | tf_op jit(solution)/shard_map/all_to_all | solution.py:383
  258.6 3.3 %project.1 = bf16[256,2048]{1,0:T(8,128)(2,1)} custom-call(s32[1]{0:T(128)} %bitcast.11.head_ref, bf16[8,256,128]{2,1,0:T(8,128)(2,1)S(1)} %all_to_all.5.a_ref, bf16[128,2048]{1,0:T(8,128)(2,1)S(1)} %copy-done, bf16[128,2048]{1,0:T(8,128)(2,1)S(1)} %collective-permute-done.14.refs_1_, bf16[128,2048]{1,0:T(8,128)(2,1)S(1)} %collective-permute-done.2.refs_2_, ...), custom_call_target="tpu_custom_call" | custom-call | tf_op jit(solution)/shard_map/project/pallas_call | solution.py:266
  (101 shorter events, 32.4 us)
Async XLA Ops:
  7.2 41.4 %all-gather.4.cloned.1.call-start = ((), (), s32[]{:S(2)}) async-start(), calls=%async_computation.1 | async-start | bytes 1179648 | tf_op jit(solution)/shard_map/all_gather | solution.py:324
  8.9 81.2 %all-gather.8.cloned.1.call-start = ((), (), s32[]{:S(2)}) async-start(), calls=%async_computation.3 | async-start | bytes 1769472 | tf_op jit(solution)/shard_map/all_gather | solution.py:324
  10.8 198.1 %all-gather.6.cloned.1.call-start = ((), (), s32[]{:S(2)}) async-start(), calls=%async_computation.2 | async-start | bytes 6488064 | tf_op jit(solution)/shard_map/all_gather | solution.py:329
  11.5 46.6 %collective-permute-start = (bf16[2048,128]{1,0:T(8,128)(2,1)}, bf16[2048,128]{1,0:T(8,128)(2,1)}, u32[]{:S(2)}, u32[]{:S(2)}) collective-permute-start(bf16[2048,128]{1,0:T(8,128)(2,1)} %refs_1_), channel_id=1, source_target_pairs={{0,2},{1,3},{2,0},{3,1},{4,6},{5,7},{6,4},{7,5},{8,10},{9,11},{10,... | collective-permute-start | bytes 1572872 | tf_op jit(solution)/shard_map/ppermute | solution.py:285
  13.8 44.8 %collective-permute-start.4 = (bf16[128,2048]{1,0:T(8,128)(2,1)S(1)}, bf16[128,2048]{1,0:T(8,128)(2,1)S(1)}, u32[]{:S(2)}, u32[]{:S(2)}) collective-permute-start(bf16[128,2048]{1,0:T(8,128)(2,1)S(1)} %copy-done), channel_id=1, source_target_pairs={{0,6},{1,7},{2,4},{3,5},{4,2},{5,3},{6,0},{7,1},{8,14},{9,15},{10,... | collective-permute-start | bytes 1572872 | tf_op jit(solution)/shard_map/ppermute | solution.py:285
  50.6 41.8 %collective-permute-start.8 = (bf16[32,2,32,128]{3,2,1,0:T(8,128)(2,1)}, bf16[32,2,32,128]{3,2,1,0:T(8,128)(2,1)}, u32[]{:S(2)}, u32[]{:S(2)}) collective-permute-start(bf16[32,2,32,128]{3,2,1,0:T(8,128)(2,1)} %get-tuple-element.101), channel_id=1, source_target_pairs={{0,24},{8,0},{16,8},{24,16},{32,56},{40,32},{48,40},{56,48},{64,88... | collective-permute-start | bytes 1572872 | tf_op jit(solution)/shard_map/ppermute | solution.py:281
  53.1 41.4 %collective-permute-start.5 = (bf16[32,2,32,128]{3,2,1,0:T(8,128)(2,1)S(1)}, bf16[32,2,32,128]{3,2,1,0:T(8,128)(2,1)}, u32[]{:S(2)}, u32[]{:S(2)}) collective-permute-start(bf16[32,2,32,128]{3,2,1,0:T(8,128)(2,1)S(1)} %get-tuple-element.102), channel_id=1, source_target_pairs={{0,8},{8,16},{16,24},{24,0},{32,40},{40,48},{48,56},{56,32},{64,72... | collective-permute-start | bytes 1572872 | tf_op jit(solution)/shard_map/ppermute | solution.py:281
  55.5 38.9 %collective-permute-start.3 = (bf16[128,2048]{1,0:T(8,128)(2,1)S(1)}, bf16[128,2048]{1,0:T(8,128)(2,1)S(1)}, u32[]{:S(2)}, u32[]{:S(2)}) collective-permute-start(bf16[128,2048]{1,0:T(8,128)(2,1)S(1)} %copy-done), channel_id=1, source_target_pairs={{0,4},{1,5},{2,6},{3,7},{4,0},{5,1},{6,2},{7,3},{8,12},{9,13},{10,... | collective-permute-start | bytes 1572872 | tf_op jit(solution)/shard_map/ppermute | solution.py:285
  58.2 38.9 %collective-permute-start.2 = (bf16[128,2048]{1,0:T(8,128)(2,1)S(1)}, bf16[128,2048]{1,0:T(8,128)(2,1)S(1)}, u32[]{:S(2)}, u32[]{:S(2)}) collective-permute-start(bf16[128,2048]{1,0:T(8,128)(2,1)S(1)} %copy-done), channel_id=1, source_target_pairs={{0,2},{1,3},{2,0},{3,1},{4,6},{5,7},{6,4},{7,5},{8,10},{9,11},{10,... | collective-permute-start | bytes 1572872 | tf_op jit(solution)/shard_map/ppermute | solution.py:285
  58.5 38.6 %collective-permute-start.6 = (bf16[32,2,32,128]{3,2,1,0:T(8,128)(2,1)}, bf16[32,2,32,128]{3,2,1,0:T(8,128)(2,1)}, u32[]{:S(2)}, u32[]{:S(2)}) collective-permute-start(bf16[32,2,32,128]{3,2,1,0:T(8,128)(2,1)} %get-tuple-element.101), channel_id=1, source_target_pairs={{0,8},{8,16},{16,24},{24,0},{32,40},{40,48},{48,56},{56,32},{64,72... | collective-permute-start | bytes 1572872 | tf_op jit(solution)/shard_map/ppermute | solution.py:281
  92.5 46.9 %collective-permute-start.21 = (bf16[32,2,48,128]{3,2,1,0:T(8,128)(2,1)S(1)}, bf16[32,2,48,128]{3,2,1,0:T(8,128)(2,1)}, u32[]{:S(2)}, u32[]{:S(2)}) collective-permute-start(bf16[32,2,48,128]{3,2,1,0:T(8,128)(2,1)S(1)} %get-tuple-element.99), channel_id=1, source_target_pairs={{0,24},{8,0},{16,8},{24,16},{32,56},{40,32},{48,40},{56,48},{64,88... | collective-permute-start | bytes 2359304 | tf_op jit(solution)/shard_map/ppermute | solution.py:281
  94.4 45.1 %collective-permute-start.18 = (bf16[32,2,48,128]{3,2,1,0:T(8,128)(2,1)}, bf16[32,2,48,128]{3,2,1,0:T(8,128)(2,1)}, u32[]{:S(2)}, u32[]{:S(2)}) collective-permute-start(bf16[32,2,48,128]{3,2,1,0:T(8,128)(2,1)} %get-tuple-element.100), channel_id=1, source_target_pairs={{0,8},{8,16},{16,24},{24,0},{32,40},{40,48},{48,56},{56,32},{64,72... | collective-permute-start | bytes 2359304 | tf_op jit(solution)/shard_map/ppermute | solution.py:281
  94.4 26.7 %collective-permute-start.7 = (bf16[32,2,32,128]{3,2,1,0:T(8,128)(2,1)S(1)}, bf16[32,2,32,128]{3,2,1,0:T(8,128)(2,1)}, u32[]{:S(2)}, u32[]{:S(2)}) collective-permute-start(bf16[32,2,32,128]{3,2,1,0:T(8,128)(2,1)S(1)} %get-tuple-element.102), channel_id=1, source_target_pairs={{0,24},{8,0},{16,8},{24,16},{32,56},{40,32},{48,40},{56,48},{64,88... | collective-permute-start | bytes 1572872 | tf_op jit(solution)/shard_map/ppermute | solution.py:281
  97.1 26.8 %collective-permute-start.9 = (bf16[32,2,32,128]{3,2,1,0:T(8,128)(2,1)}, bf16[32,2,32,128]{3,2,1,0:T(8,128)(2,1)}, u32[]{:S(2)}, u32[]{:S(2)}) collective-permute-start(bf16[32,2,32,128]{3,2,1,0:T(8,128)(2,1)} %collective-permute-done.5.refs_4_), channel_id=1, source_target_pairs={{0,8},{8,16},{16,24},{24,0},{32,40},{40,48},{48,56},{56,32},{64,72... | collective-permute-start | bytes 1572872 | tf_op jit(solution)/shard_map/ppermute | solution.py:281
  97.1 36.2 %collective-permute-start.10 = (bf16[32,2,32,128]{3,2,1,0:T(8,128)(2,1)}, bf16[32,2,32,128]{3,2,1,0:T(8,128)(2,1)}, u32[]{:S(2)}, u32[]{:S(2)}) collective-permute-start(bf16[32,2,32,128]{3,2,1,0:T(8,128)(2,1)} %collective-permute-done.8.refs_7_), channel_id=1, source_target_pairs={{0,24},{8,0},{16,8},{24,16},{32,56},{40,32},{48,40},{56,48},{64,88... | collective-permute-start | bytes 1572872 | tf_op jit(solution)/shard_map/ppermute | solution.py:281
  133.3 5.7 %collective-permute-start.11 = (s32[2,4,1,4]{3,1,2,0:T(4,128)S(1)}, s32[2,4,1,4]{3,1,2,0:T(4,128)S(1)}, u32[]{:S(2)}, u32[]{:S(2)}) collective-permute-start(s32[2,4,1,4]{3,1,2,0:T(4,128)S(1)} %pad_add_fusion.2), channel_id=1, source_target_pairs={{0,1},{1,0},{2,3},{3,2},{4,5},{5,4},{6,7},{7,6},{8,9},{9,8},{10,11... | collective-permute-start | bytes 392 | tf_op jit(solution)/shard_map/ppermute | solution.py:285
  139.0 5.4 %collective-permute-start.14 = (bf16[128,2048]{1,0:T(8,128)(2,1)S(1)}, bf16[128,2048]{1,0:T(8,128)(2,1)S(1)}, u32[]{:S(2)}, u32[]{:S(2)}) collective-permute-start(bf16[128,2048]{1,0:T(8,128)(2,1)S(1)} %copy-done), channel_id=1, source_target_pairs={{0,1},{1,0},{2,3},{3,2},{4,5},{5,4},{6,7},{7,6},{8,9},{9,8},{10,11... | collective-permute-start | bytes 1572872 | tf_op jit(solution)/shard_map/ppermute | solution.py:285
  139.3 5.5 %collective-permute-start.15 = (bf16[128,2048]{1,0:T(8,128)(2,1)S(1)}, bf16[128,2048]{1,0:T(8,128)(2,1)S(1)}, u32[]{:S(2)}, u32[]{:S(2)}) collective-permute-start(bf16[128,2048]{1,0:T(8,128)(2,1)S(1)} %collective-permute-done.2.refs_2_), channel_id=1, source_target_pairs={{0,1},{1,0},{2,3},{3,2},{4,5},{5,4},{6,7},{7,6},{8,9},{9,8},{10,11... | collective-permute-start | bytes 1572872 | tf_op jit(solution)/shard_map/ppermute | solution.py:285
  140.4 33.8 %collective-permute-start.19 = (bf16[32,2,48,128]{3,2,1,0:T(8,128)(2,1)}, bf16[32,2,48,128]{3,2,1,0:T(8,128)(2,1)}, u32[]{:S(2)}, u32[]{:S(2)}) collective-permute-start(bf16[32,2,48,128]{3,2,1,0:T(8,128)(2,1)} %copy-done.3), channel_id=1, source_target_pairs={{0,8},{8,16},{16,24},{24,0},{32,40},{40,48},{48,56},{56,32},{64,72... | collective-permute-start | bytes 2359304 | tf_op jit(solution)/shard_map/ppermute | solution.py:281
  141.2 36.1 %collective-permute-start.20 = (bf16[32,2,48,128]{3,2,1,0:T(8,128)(2,1)}, bf16[32,2,48,128]{3,2,1,0:T(8,128)(2,1)}, u32[]{:S(2)}, u32[]{:S(2)}) collective-permute-start(bf16[32,2,48,128]{3,2,1,0:T(8,128)(2,1)} %get-tuple-element.100), channel_id=1, source_target_pairs={{0,24},{8,0},{16,8},{24,16},{32,56},{40,32},{48,40},{56,48},{64,88... | collective-permute-start | bytes 2359304 | tf_op jit(solution)/shard_map/ppermute | solution.py:281
  144.8 59.0 %collective-permute-start.22 = (bf16[32,2,48,128]{3,2,1,0:T(8,128)(2,1)}, bf16[32,2,48,128]{3,2,1,0:T(8,128)(2,1)}, u32[]{:S(2)}, u32[]{:S(2)}) collective-permute-start(bf16[32,2,48,128]{3,2,1,0:T(8,128)(2,1)} %collective-permute-done.18.refs_11_), channel_id=1, source_target_pairs={{0,8},{8,16},{16,24},{24,0},{32,40},{40,48},{48,56},{56,32},{64,72... | collective-permute-start | bytes 2359304 | tf_op jit(solution)/shard_map/ppermute | solution.py:281
  144.8 59.0 %collective-permute-start.23 = (bf16[32,2,48,128]{3,2,1,0:T(8,128)(2,1)}, bf16[32,2,48,128]{3,2,1,0:T(8,128)(2,1)}, u32[]{:S(2)}, u32[]{:S(2)}) collective-permute-start(bf16[32,2,48,128]{3,2,1,0:T(8,128)(2,1)} %collective-permute-done.21.refs_14_), channel_id=1, source_target_pairs={{0,24},{8,0},{16,8},{24,16},{32,56},{40,32},{48,40},{56,48},{64,88... | collective-permute-start | bytes 2359304 | tf_op jit(solution)/shard_map/ppermute | solution.py:281
  222.2 10.2 %collective-permute-start.28 = (bf16[2,144,512]{2,1,0:T(8,128)(2,1)}, bf16[2,144,512]{2,1,0:T(8,128)(2,1)S(1)}, u32[]{:S(2)}, u32[]{:S(2)}) collective-permute-start(bf16[2,144,512]{2,1,0:T(8,128)(2,1)} %get-tuple-element.70), channel_id=1, source_target_pairs={{0,2},{1,3},{2,0},{3,1},{4,6},{5,7},{6,4},{7,5},{8,10},{9,11},{10,... | collective-permute-start | bytes 884744 | tf_op jit(solution)/shard_map/ppermute | solution.py:285
  223.4 13.8 %collective-permute-start.29 = (bf16[2,144,512]{2,1,0:T(8,128)(2,1)}, bf16[2,144,512]{2,1,0:T(8,128)(2,1)}, u32[]{:S(2)}, u32[]{:S(2)}) collective-permute-start(bf16[2,144,512]{2,1,0:T(8,128)(2,1)} %get-tuple-element.71), channel_id=1, source_target_pairs={{0,2},{1,3},{2,0},{3,1},{4,6},{5,7},{6,4},{7,5},{8,10},{9,11},{10,... | collective-permute-start | bytes 884744 | tf_op jit(solution)/shard_map/ppermute | solution.py:285
  (21 other events, 140.4 us)
Sparse Core Ops, SparseCore 0:
  10.4 38.1 all-gather.3
  50.9 39.0 all-gather.7
  92.7 116.1 all-gather.5

commit v5 on v4

--- a/solution.py
+++ b/solution.py
@@ -14,14 +14,11 @@
 SEL = 4
 QB = 4
 BLOCKS = 8
-NX = 4
-NZ = 8
 TAIL = 16
 SCALE = math.log2(math.e) / math.sqrt(HD)
 NEG = -1e30
 F32 = jnp.float32
 BF16 = jnp.bfloat16
-SPLIT = (4, 6, 6)
 VMEM_BYTES = 56 << 20
 
 
@@ -97,46 +94,23 @@
     return ref[i, :HD, :].astype(F32), tail[0:1], tail[1:2] + tail[2:3]
 
 
-def far_kernel(where_ref, *refs, arrays):
-    q_refs, refs = refs[:2], refs[2:]
-    whole_ref, refs = refs[0], refs[1:]
-    sources, refs = (refs[:arrays], refs[arrays : 2 * arrays]), refs[2 * arrays :]
+def far_kernel(picks_ref, *refs):
+    q_refs, whole_ref, refs = refs[:2], refs[2], refs[3:]
     piece_refs, whole_out_ref, refs = refs[:QB], refs[QB], refs[QB + 1 :]
-    parts = 1 + len(sources)
-    buffers, refs = refs[:parts], refs[parts:]
-    score_refs, weight_refs, sems = refs[:2], refs[2:4], refs[4]
-
-    def fetch(pick, carry):
-        unit = pick // SEL
+    buffer, score_refs, weight_refs, sems = refs[0], refs[1:3], refs[3:5], refs[5]
+    for pick in range(2 * QB * SEL):
         pltpu.make_async_copy(
-            whole_ref.at[where_ref[pick, 0]], buffers[0].at[pick], sems.at[unit, 0]
+            whole_ref.at[picks_ref[pick]], buffer.at[pick], sems.at[pick // SEL]
         ).start()
-        array, index = where_ref[pick, 1], where_ref[pick, 2]
-        for number in range(arrays):
-
-            def start(number=number):
-                for part in range(1, parts):
-                    pltpu.make_async_copy(
-                        sources[part - 1][number].at[index],
-                        buffers[part].at[pick],
-                        sems.at[unit, part],
-                    ).start()
-
-            pl.when(array == number)(start)
-        return carry
-
-    lax.fori_loop(0, 2 * QB * SEL, fetch, 0)
 
     def joined(row, which):
         return jnp.concatenate(
-            [buffers[part][row * SEL + j, which] for part in range(parts) for j in range(SEL)],
-            axis=0,
+            [buffer[row * SEL + j, which] for j in range(SEL)], axis=0
         )
 
     def score(row, q_ref, i, score_ref):
-        for part in range(parts):
-            held = buffers[part].at[pl.ds(row * SEL, SEL)]
-            pltpu.make_async_copy(held, held, sems.at[row, part]).wait()
+        held = buffer.at[pl.ds(row * SEL, SEL)]
+        pltpu.make_async_copy(held, held, sems.at[row]).wait()
         score_ref[...] = dot_nt(joined(row, 0), q_ref[pl.ds(i * BLK, BLK), :])
 
     def soften(score_ref, weight_ref):
@@ -168,24 +142,21 @@
                 finish(row, weight_refs[k], whole_out_ref, row % QB, top, total)
 
 
-def far(where, queries, whole, x_parts):
+def far(picks, queries, whole):
     pay = HD + TAIL
     vmem = pl.BlockSpec(memory_space=pltpu.VMEM)
-    hbm = pl.BlockSpec(memory_space=pl.ANY)
-    arrays = [array for part in x_parts for array in part]
-    shapes = [whole.shape[1:]] + [part[0].shape[1:] for part in x_parts]
-    return pl.pallas_call(
-        functools.partial(far_kernel, arrays=len(x_parts[0])),
+    return pl.pallas_call(
+        far_kernel,
         in_specs=[pl.BlockSpec(memory_space=pltpu.SMEM)]
         + [vmem] * 2
-        + [hbm] * (1 + len(arrays)),
+        + [pl.BlockSpec(memory_space=pl.ANY)],
         out_specs=[vmem] * (QB + 1),
         out_shape=[jax.ShapeDtypeStruct((1, pay, BLK), BF16)] * QB
         + [jax.ShapeDtypeStruct((QB, pay, BLK), BF16)],
-        scratch_shapes=[pltpu.VMEM((2 * QB * SEL,) + shape, BF16) for shape in shapes]
+        scratch_shapes=[pltpu.VMEM((2 * QB * SEL,) + whole.shape[1:], BF16)]
         + [pltpu.VMEM((BLK, BLK), F32)] * 2
         + [pltpu.VMEM((BLK, BLK), BF16)] * 2
-        + [pltpu.SemaphoreType.DMA((2 * QB, len(shapes)))],
+        + [pltpu.SemaphoreType.DMA((2 * QB,))],
         compiler_params=pltpu.CompilerParams(vmem_limit_bytes=VMEM_BYTES),
         cost_estimate=pl.CostEstimate(
             flops=8 * 2 * QB * 4 * BLK * BLK * HD,
@@ -193,7 +164,7 @@
             transcendentals=2 * QB * BLK * BLK,
         ),
         name="far",
-    )(where, *queries, whole, *arrays)
+    )(picks, *queries, whole)
 
 
 def merge_two_kernel(a_ref, *refs):
@@ -273,109 +244,57 @@
     )(head, parts, *weights)
 
 
-def shift(arrays, dz, dx):
-    pairs = []
-    for z in range(NZ):
-        for x in range(NX):
-            pairs.append((z * NX + x, (z + dz) % NZ * NX + (x + dx) % NX))
-    return [lax.ppermute(array, "ctx", pairs) for array in arrays]
-
-
 def swap(array, bits):
     return lax.ppermute(array, "head", [(h, h ^ bits) for h in range(lax.axis_size("head"))])
 
 
 def after(value, *earlier):
     return lax.optimization_barrier((value, earlier))[0]
-
-
-def spread_x(array):
-    half = array.shape[0] // 2
-    halves = [array[:half], array[half:]]
-    below, above = shift(halves, 0, 1), shift(halves, 0, -1)
-
-    def rest(*earlier):
-        low, high = after((below[0], above[1]), *earlier)
-        return shift([low], 0, 1) + shift([high], 0, -1)
-
-    return [array, *below, *above], rest
 
 
 def body(queries, block_picks, span_keys, span_values, cache_keys, cache_values, out_weight):
     heads = lax.axis_size("head")
     head = lax.axis_index("head")
-    ctx = lax.axis_index("ctx")
     part = head % GROUP
     kv = head // GROUP
     share = BLK // GROUP
-    columns = [[z * NX + x for z in range(NZ)] for x in range(NX)]
-
-    def cut(first, rows):
-        pieces = []
-        for cache in (cache_keys, cache_values):
-            view = cache.reshape(BLOCKS, BLK, cache.shape[1])
-            pieces.append(
-                lax.dynamic_slice(view, (0, part * share + first, kv * HD), (BLOCKS, rows, HD))
-            )
-        return jnp.stack(pieces, axis=1)
-
-    rows = [share * sixteenths // 16 for sixteenths in SPLIT]
-    columns_0, columns_1 = [
-        lax.all_gather(
-            cut(first, count), "ctx", axis=0, tiled=True, axis_index_groups=columns
-        )
-        for first, count in ((0, rows[0]), (rows[0], rows[1]))
-    ]
-    whole = lax.all_gather(cut(rows[0] + rows[1], rows[2]), "ctx", axis=0, tiled=True)
-    x_part_0, rest_0 = spread_x(columns_0)
-    x_part_1, rest_1 = spread_x(columns_1)
-    x_part_0 = x_part_0 + rest_0()
+
+    pieces = []
+    for cache in (cache_keys, cache_values):
+        view = cache.reshape(BLOCKS, BLK, cache.shape[1])
+        pieces.append(lax.dynamic_slice(view, (0, part * share, kv * HD), (BLOCKS, share, HD)))
+    whole = lax.all_gather(jnp.stack(pieces, axis=1), "ctx", axis=0, tiled=True)
 
     queries_chip = swap(queries, 2)
     picks_chip = swap(block_picks, 2)
     weights = [out_weight] + [None] * (heads - 1)
     for bits in range(2, heads, 2):
         weights[bits] = swap(out_weight, bits)
-    near_state = near(after(queries, columns_1), span_keys, span_values, kv[None])
-    x_part_1 = x_part_1 + rest_1(*near_state)
-    queries_pair, picks_pair, weights_even = after(
-        ([queries, queries_chip], jnp.stack([block_picks, picks_chip]), weights[::2]), *x_part_0
-    )
+    near_state = near(queries, span_keys, span_values, kv[None])
+    queries_pair = [queries, queries_chip]
+    picks_pair = jnp.stack([block_picks, picks_chip])
     group_queries = [queries, swap(queries_pair[0], 1), queries_chip, swap(queries_pair[1], 1)]
     picks_core = swap(picks_pair, 1)
     group_picks = [picks_pair[0], picks_core[0], picks_pair[1], picks_core[1]]
-    for i, bits in enumerate(range(0, heads, 2)):
-        weights[bits + 1] = swap(weights_even[i], 1)
-
-    picks = jnp.stack(group_picks).reshape(GROUP, QB * SEL)
-    owner, local = picks // BLOCKS, picks % BLOCKS
-    dx = (owner % NX - ctx % NX) % NX
-    place = owner // NX * BLOCKS + local
-    half = NZ * BLOCKS // 2
-    upper = (place >= half).astype(jnp.int32)
-    first_array = jnp.where(dx == 3, 1, jnp.where(dx == 1, 3, 5))
-    where = jnp.stack(
-        [
-            picks,
-            jnp.where(dx == 0, 0, first_array + upper),
-            jnp.where(dx == 0, place, place - half * upper),
-        ],
-        axis=-1,
-    ).astype(jnp.int32)
-
-    def far_of(first, second, where):
+    for bits in range(0, heads, 2):
+        weights[bits + 1] = swap(weights[bits], 1)
+    picks = [group_pick.reshape(QB * SEL) for group_pick in group_picks]
+
+    picks, group_queries, weights, near_state = lax.optimization_barrier(
+        (picks, group_queries, weights, near_state)
+    )
+
+    def far_of(first, second, earlier):
         return far(
-            jnp.concatenate([where[first], where[second]], axis=0),
+            after(jnp.concatenate([picks[first], picks[second]]), *earlier),
             [group_queries[first], group_queries[second]],
             whole,
-            [x_part_0, x_part_1],
         )
 
-    where, group_queries, weights = lax.optimization_barrier((where, group_queries, weights))
-    *far_corner, far_chip = far_of(3, 2, where)
+    *far_corner, far_chip = far_of(3, 2, [])
     for_chip = merge_two(far_chip, [swap(piece, 1) for piece in far_corner], 2)
     chip_parts = [swap(piece, 2) for piece in for_chip]
-    *far_core, far_own = far_of(1, 0, after(where, *for_chip))
+    *far_core, far_own = far_of(1, 0, for_chip)
     core_parts = [swap(piece, 1) for piece in after(far_core, *chip_parts)]
     attention = merge_last(far_own, core_parts, near_state, chip_parts)
 

time: 269 us -> 214 us (0.80)
  waiting for transfers between devices: 163 us -> 127 us
  starting transfers between devices: 36.2 us -> 24 us
  local copies, waits for them, and re-layouts: 9.79 us -> 2.1 us
    ppermute x12 -> x0, waiting for transfers between devices: 83.5 us -> none  [shift(): return [lax.ppermute(array, 'ctx', pairs) for array in arrays]]
    all_gather x3 -> x1, waiting for transfers between devices: 69.3 us -> 97.6 us  [body(): whole = lax.all_gather(jnp.stack(pieces, axis=1), 'ctx', axis=0, tiled=True)]
    ppermute x22, waiting for transfers between devices: 10.2 us -> 29.6 us  [swap(): lax.ppermute(array, 'head', [(h, h ^ bits) for h in range(lax.axis_size('...]
    ppermute x12 -> x0, starting transfers between devices: 16.6 us -> none  [shift(): return [lax.ppermute(array, 'ctx', pairs) for array in arrays]]
    ppermute x22, starting transfers between devices: 19.5 us -> 23.9 us  [swap(): lax.ppermute(array, 'head', [(h, h ^ bits) for h in range(lax.axis_size('...]
    slice x4 -> x0, local copies, waits for them, and re-layouts: 4.44 us -> none  [the longest x2 4.43 us: spread_x(): halves = [array[:half], array[half:]]]
  transfers between devices with their start and end apart: 37 -> 23, of which waited for: 21 -> 14; matrix products, arithmetic and copies ran while one was open for 3% -> 2% of each run, Pallas kernels for 5% -> 6%
where the time goes in v5:
time: 214 us
  waiting for transfers between devices  127 us (59%)
  Pallas kernels  29 us (14%)
  starting transfers between devices  24 us (11%)
  between operations  14.2 us (7%)
  blocking collectives  13.8 us (6%)
  other arithmetic  3.29 us (2%)
    all_gather x1, waiting for transfers between devices, body(): whole = lax.all_gather(jnp.stack(pieces, axis=1), 'ctx', axis=0, tiled=True)  97.6 us
    ppermute x22, waiting for transfers between devices, swap(): lax.ppermute(array, 'head', [(h, h ^ bits) for h in range(lax.axis_size('...  29.6 us
    ppermute x22, starting transfers between devices, swap(): lax.ppermute(array, 'head', [(h, h ^ bits) for h in range(lax.axis_size('...  23.9 us
    pallas_call x2, Pallas kernels, far(): pl.pallas_call(far_kernel, in_specs=[pl.BlockSpec(memory_space=pltpu.SMEM...  15.5 us
    all_to_all x1, blocking collectives, body(): lax.all_to_all(attention.reshape(heads, share_rows, HD), 'head', split_ax...  13.8 us
    pallas_call x1, Pallas kernels, near(): pl.pallas_call(near_kernel, grid_spec=grid_spec, out_shape=state_shapes()...  4.67 us
  transfers between devices with their start and end apart: 23, of which 14 were waited for; matrix products, arithmetic and copies ran while one was open for 2% of the time, Pallas kernels for 6%

profile of v5, /device:TPU:1, one launch (start us, length us, event | category | flops | bytes accessed | tf_op | source)
XLA Modules:
  0.0 213.6 jit_solution(3070446352975225398)
XLA Ops:
  7.3 1.1 dynamic-slice_bitcast_fusion
  9.3 2.2 %collective-permute-start.3 = (bf16[2048,128]{1,0:T(8,128)(2,1)S(1)}, bf16[2048,128]{1,0:T(8,128)(2,1)}, u32[]{:S(2)}, u32[]{:S(2)}) collective-permute-start(bf16[2048,128]{1,0:T(8,128)(2,1)S(1)} %copy-done.1), channel_id=1, source_target_pairs={{0,2},{1,3},{2,0},{3,1},{4,6},{5,7},{6,4},{7,5},{8,10},{9,11},{10,... | collective-permute-start | bytes 1572872 | tf_op jit(solution)/shard_map/ppermute | solution.py:248
  11.5 1.2 collective-permute-start.2
  12.8 1.6 collective-permute-start
  14.4 1.2 collective-permute-start.8
  15.6 6.4 %collective-permute-done = s32[4,1,4]{2,1,0:T(1,128)S(1)} collective-permute-done((s32[4,1,4]{2,1,0:T(1,128)S(1)}, s32[4,1,4]{2,1,0:T(1,128)S(1)}, u32[]{:S(2)}, u32[]{:S(2)}) %collective-permute-start) | collective-permute-done | bytes 96 | tf_op jit(solution)/shard_map/ppermute | solution.py:248
  22.0 5.6 %collective-permute-start.1 = (s32[2,4,1,4]{3,1,2,0:T(4,128)S(1)}, s32[2,4,1,4]{3,1,2,0:T(4,128)S(1)}, u32[]{:S(2)}, u32[]{:S(2)}) collective-permute-start(s32[2,4,1,4]{3,1,2,0:T(4,128)S(1)} %pad_add_fusion), channel_id=1, source_target_pairs={{0,1},{1,0},{2,3},{3,2},{4,5},{5,4},{6,7},{7,6},{8,9},{9,8},{10,11... | collective-permute-start | bytes 392 | tf_op jit(solution)/shard_map/ppermute | solution.py:248
  30.1 6.7 %collective-permute-done.8.refs_4_ = bf16[128,2048]{1,0:T(8,128)(2,1)S(1)} collective-permute-done((bf16[128,2048]{1,0:T(8,128)(2,1)S(1)}, bf16[128,2048]{1,0:T(8,128)(2,1)S(1)}, u32[]{:S(2)}, u32[]{:S(2)}) %collective-permute-start.8) | collective-permute-done | bytes 524320 | tf_op jit(solution)/shard_map/ppermute | solution.py:248
  36.8 2.7 %collective-permute-start.9 = (bf16[128,2048]{1,0:T(8,128)(2,1)S(1)}, bf16[128,2048]{1,0:T(8,128)(2,1)S(1)}, u32[]{:S(2)}, u32[]{:S(2)}) collective-permute-start(bf16[128,2048]{1,0:T(8,128)(2,1)S(1)} %collective-permute-done.8.refs_4_), channel_id=1, source_target_pairs={{0,1},{1,0},{2,3},{3,2},{4,5},{5,4},{6,7},{7,6},{8,9},{9,8},{10,11... | collective-permute-start | bytes 1572872 | tf_op jit(solution)/shard_map/ppermute | solution.py:248
  39.5 5.0 %collective-permute-done.6.refs_2_ = bf16[128,2048]{1,0:T(8,128)(2,1)S(1)} collective-permute-done((bf16[128,2048]{1,0:T(8,128)(2,1)S(1)}, bf16[128,2048]{1,0:T(8,128)(2,1)S(1)}, u32[]{:S(2)}, u32[]{:S(2)}) %collective-permute-start.6) | collective-permute-done | bytes 524320 | tf_op jit(solution)/shard_map/ppermute | solution.py:248
  44.5 2.4 %collective-permute-start.7 = (bf16[128,2048]{1,0:T(8,128)(2,1)S(1)}, bf16[128,2048]{1,0:T(8,128)(2,1)}, u32[]{:S(2)}, u32[]{:S(2)}) collective-permute-start(bf16[128,2048]{1,0:T(8,128)(2,1)S(1)} %collective-permute-done.6.refs_2_), channel_id=1, source_target_pairs={{0,1},{1,0},{2,3},{3,2},{4,5},{5,4},{6,7},{7,6},{8,9},{9,8},{10,11... | collective-permute-start | bytes 1572872 | tf_op jit(solution)/shard_map/ppermute | solution.py:248
  46.9 2.1 %collective-permute-done.10.refs_6_ = bf16[128,2048]{1,0:T(8,128)(2,1)S(1)} collective-permute-done((bf16[128,2048]{1,0:T(8,128)(2,1)S(1)}, bf16[128,2048]{1,0:T(8,128)(2,1)S(1)}, u32[]{:S(2)}, u32[]{:S(2)}) %collective-permute-start.10) | collective-permute-done | bytes 524320 | tf_op jit(solution)/shard_map/ppermute | solution.py:248
  50.8 4.7 %near.1 = (f32[4,128,512]{2,1,0:T(8,128)}, f32[4,1,512]{2,1,0:T(1,128)}, f32[4,1,512]{2,1,0:T(1,128)}) custom-call(s32[1]{0:T(128)} %bitcast.2.kv_ref, bf16[2048,128]{1,0:T(8,128)(2,1)} %refs_1_, bf16[2048,256]{1,0:T(8,128)(2,1)} %k_ref.1, bf16[2048,256]{1,0:T(8,128)(2,1)} %v_ref.1), custom_call_target="tpu_custom_call" | custom-call | flops 536870912 | bytes 4194304 | tf_op jit(solution)/shard_map/near/pallas_call | solution.py:72
  57.0 97.6 %all-gather.2.cloned.1.call-done.refs_2_ = bf16[256,2,128,128]{3,2,1,0:T(8,128)(2,1)} async-done(((bf16[8,2,128,128]{3,2,1,0:T(8,128)(2,1)}), bf16[256,2,128,128]{3,2,1,0:T(8,128)(2,1)}) %all-gather.2.cloned.1.call-update) | async-done | bytes 16777232 | tf_op jit(solution)/shard_map/all_gather | solution.py:266
  154.6 7.7 %far.2 = (bf16[1,144,512]{2,1,0:T(8,128)(2,1)}, bf16[1,144,512]{2,1,0:T(8,128)(2,1)}, bf16[1,144,512]{2,1,0:T(8,128)(2,1)}, bf16[1,144,512]{2,1,0:T(8,128)(2,1)}, bf16[4,144,512]{2,1,0:T(8,128)(2,1)}) custom-call(s32[32]{0:T(128)} %pad_add_fusion.2.picks_ref, bf16[2048,128]{1,0:T(8,128)(2,1)} %collective-permute-done.4.refs_0_, ...), custom_call_target="tpu_custom_call" | custom-call | flops 8589934592 | bytes 5242880 | tf_op jit(solution)/shard_map/far/pallas_call | solution.py:148
  162.4 1.1 collective-permute-start.12
  165.7 2.2 %merge_two.1 = (bf16[2,144,512]{2,1,0:T(8,128)(2,1)}, bf16[2,144,512]{2,1,0:T(8,128)(2,1)}) custom-call(bf16[4,144,512]{2,1,0:T(8,128)(2,1)} %get-tuple-element.50.a_ref, bf16[1,144,512]{2,1,0:T(8,128)(2,1)} %copy-done.3, bf16[1,144,512]{2,1,0:T(8,128)(2,1)} %copy-done.4, bf16[1,144,512]{2,1,0:T(8,128)(2,1)} %collective-permute-done.14.refs_2_, ...), custom_call_target="tpu_custom_call" | custom-call | tf_op jit(solution)/shard_map/merge_two/pallas_call | solution.py:187
  168.0 1.2 collective-permute-start.16
  169.5 7.7 %far.3 = (bf16[1,144,512]{2,1,0:T(8,128)(2,1)}, bf16[1,144,512]{2,1,0:T(8,128)(2,1)}, bf16[1,144,512]{2,1,0:T(8,128)(2,1)}, bf16[1,144,512]{2,1,0:T(8,128)(2,1)}, bf16[4,144,512]{2,1,0:T(8,128)(2,1)}) custom-call(s32[32]{0:T(128)} %pad_add_fusion.1.picks_ref, bf16[2048,128]{1,0:T(8,128)(2,1)} %copy-done.6, bf16[2048,128]{1,0:T(8,128)(2,1)} %refs_1_, ...), custom_call_target="tpu_custom_call" | custom-call | flops 8589934592 | bytes 5242880 | tf_op jit(solution)/shard_map/far/pallas_call | solution.py:148
  177.2 5.8 %collective-permute-done.17.refs_8_ = bf16[2,144,512]{2,1,0:T(8,128)(2,1)} collective-permute-done((bf16[2,144,512]{2,1,0:T(8,128)(2,1)}, bf16[2,144,512]{2,1,0:T(8,128)(2,1)}, u32[]{:S(2)}, u32[]{:S(2)}) %collective-permute-start.17) | collective-permute-done | bytes 294944 | tf_op jit(solution)/shard_map/ppermute | solution.py:248
  183.0 1.0 collective-permute-start.18
  186.3 3.2 %merge_last.1 = bf16[2048,128]{1,0:T(8,128)(2,1)} custom-call(bf16[4,144,512]{2,1,0:T(8,128)(2,1)} %get-tuple-element.60.a_ref, bf16[1,144,512]{2,1,0:T(8,128)(2,1)} %collective-permute-done.18.refs_0_, bf16[1,144,512]{2,1,0:T(8,128)(2,1)} %collective-permute-done.19.refs_1_, bf16[1,144,512]{2,1,0:T(8,128)(2,1)} %collective-permute-done.20.refs_2_, ...), custom_call_target="tpu_custom_call" | custom-call | tf_op jit(solution)/shard_map/merge_last/pallas_call | solution.py:215
  189.5 13.8 %all_to_all.5.a_ref = bf16[8,256,128]{2,1,0:T(8,128)(2,1)S(1)} all-to-all(bf16[8,256,128]{2,1,0:T(8,128)(2,1)} %bitcast.15), channel_id=1, replica_groups=mesh['ctx'=32,'head'=8] {'head'}, dimensions={0} | all-to-all | bytes 1048576 | tf_op jit(solution)/shard_map/all_to_all | solution.py:302
  203.3 3.4 %project.1 = bf16[256,2048]{1,0:T(8,128)(2,1)} custom-call(s32[1]{0:T(128)} %bitcast.7.head_ref, bf16[8,256,128]{2,1,0:T(8,128)(2,1)S(1)} %all_to_all.5.a_ref, bf16[128,2048]{1,0:T(8,128)(2,1)S(1)} %copy-done, bf16[128,2048]{1,0:T(8,128)(2,1)S(1)} %collective-permute-done.5.refs_1_, bf16[128,2048]{1,0:T(8,128)(2,1)S(1)} %collective-permute-done.6.refs_2_, ...), custom_call_target="tpu_custom_call" | custom-call | tf_op jit(solution)/shard_map/project/pallas_call | solution.py:237
  (57 shorter events, 11.4 us)
Async XLA Ops:
  7.2 147.4 %all-gather.2.cloned.1.call-start = ((), (), s32[]{:S(2)}) async-start(), calls=%async_computation.1 | async-start | bytes 17301504 | tf_op jit(solution)/shard_map/all_gather | solution.py:266
  9.3 20.1 %collective-permute-start.3 = (bf16[2048,128]{1,0:T(8,128)(2,1)S(1)}, bf16[2048,128]{1,0:T(8,128)(2,1)}, u32[]{:S(2)}, u32[]{:S(2)}) collective-permute-start(bf16[2048,128]{1,0:T(8,128)(2,1)S(1)} %copy-done.1), channel_id=1, source_target_pairs={{0,2},{1,3},{2,0},{3,1},{4,6},{5,7},{6,4},{7,5},{8,10},{9,11},{10,... | collective-permute-start | bytes 1572872 | tf_op jit(solution)/shard_map/ppermute | solution.py:248
  11.5 18.5 %collective-permute-start.2 = (bf16[2048,128]{1,0:T(8,128)(2,1)S(1)}, bf16[2048,128]{1,0:T(8,128)(2,1)S(1)}, u32[]{:S(2)}, u32[]{:S(2)}) collective-permute-start(bf16[2048,128]{1,0:T(8,128)(2,1)S(1)} %copy-done.1), channel_id=1, source_target_pairs={{0,1},{1,0},{2,3},{3,2},{4,5},{5,4},{6,7},{7,6},{8,9},{9,8},{10,11... | collective-permute-start | bytes 1572872 | tf_op jit(solution)/shard_map/ppermute | solution.py:248
  12.8 9.2 %collective-permute-start = (s32[4,1,4]{2,1,0:T(1,128)S(1)}, s32[4,1,4]{2,1,0:T(1,128)S(1)}, u32[]{:S(2)}, u32[]{:S(2)}) collective-permute-start(s32[4,1,4]{2,1,0:T(1,128)S(1)} %copy-done.5), channel_id=1, source_target_pairs={{0,2},{1,3},{2,0},{3,1},{4,6},{5,7},{6,4},{7,5},{8,10},{9,11},{10,... | collective-permute-start | bytes 200 | tf_op jit(solution)/shard_map/ppermute | solution.py:248
  14.4 22.4 %collective-permute-start.8 = (bf16[128,2048]{1,0:T(8,128)(2,1)S(1)}, bf16[128,2048]{1,0:T(8,128)(2,1)S(1)}, u32[]{:S(2)}, u32[]{:S(2)}) collective-permute-start(bf16[128,2048]{1,0:T(8,128)(2,1)S(1)} %copy-done), channel_id=1, source_target_pairs={{0,4},{1,5},{2,6},{3,7},{4,0},{5,1},{6,2},{7,3},{8,12},{9,13},{10,... | collective-permute-start | bytes 1572872 | tf_op jit(solution)/shard_map/ppermute | solution.py:248
  22.0 6.5 %collective-permute-start.1 = (s32[2,4,1,4]{3,1,2,0:T(4,128)S(1)}, s32[2,4,1,4]{3,1,2,0:T(4,128)S(1)}, u32[]{:S(2)}, u32[]{:S(2)}) collective-permute-start(s32[2,4,1,4]{3,1,2,0:T(4,128)S(1)} %pad_add_fusion), channel_id=1, source_target_pairs={{0,1},{1,0},{2,3},{3,2},{4,5},{5,4},{6,7},{7,6},{8,9},{9,8},{10,11... | collective-permute-start | bytes 392 | tf_op jit(solution)/shard_map/ppermute | solution.py:248
  27.6 16.9 %collective-permute-start.6 = (bf16[128,2048]{1,0:T(8,128)(2,1)S(1)}, bf16[128,2048]{1,0:T(8,128)(2,1)S(1)}, u32[]{:S(2)}, u32[]{:S(2)}) collective-permute-start(bf16[128,2048]{1,0:T(8,128)(2,1)S(1)} %copy-done), channel_id=1, source_target_pairs={{0,2},{1,3},{2,0},{3,1},{4,6},{5,7},{6,4},{7,5},{8,10},{9,11},{10,... | collective-permute-start | bytes 1572872 | tf_op jit(solution)/shard_map/ppermute | solution.py:248
  28.4 20.6 %collective-permute-start.10 = (bf16[128,2048]{1,0:T(8,128)(2,1)S(1)}, bf16[128,2048]{1,0:T(8,128)(2,1)S(1)}, u32[]{:S(2)}, u32[]{:S(2)}) collective-permute-start(bf16[128,2048]{1,0:T(8,128)(2,1)S(1)} %copy-done), channel_id=1, source_target_pairs={{0,6},{1,7},{2,4},{3,5},{4,2},{5,3},{6,0},{7,1},{8,14},{9,15},{10,... | collective-permute-start | bytes 1572872 | tf_op jit(solution)/shard_map/ppermute | solution.py:248
  29.4 27.0 %collective-permute-start.5 = (bf16[128,2048]{1,0:T(8,128)(2,1)S(1)}, bf16[128,2048]{1,0:T(8,128)(2,1)S(1)}, u32[]{:S(2)}, u32[]{:S(2)}) collective-permute-start(bf16[128,2048]{1,0:T(8,128)(2,1)S(1)} %copy-done), channel_id=1, source_target_pairs={{0,1},{1,0},{2,3},{3,2},{4,5},{5,4},{6,7},{7,6},{8,9},{9,8},{10,11... | collective-permute-start | bytes 1572872 | tf_op jit(solution)/shard_map/ppermute | solution.py:248
  30.0 19.1 %copy-start.6 = (bf16[2048,128]{1,0:T(8,128)(2,1)}, bf16[2048,128]{1,0:T(8,128)(2,1)S(1)}, u32[]{:S(2)}) copy-start(bf16[2048,128]{1,0:T(8,128)(2,1)S(1)} %collective-permute-done.2.refs_0_) | copy-start | bytes 1572868
  30.0 26.4 %collective-permute-start.4 = (bf16[2048,128]{1,0:T(8,128)(2,1)}, bf16[2048,128]{1,0:T(8,128)(2,1)}, u32[]{:S(2)}, u32[]{:S(2)}) collective-permute-start(bf16[2048,128]{1,0:T(8,128)(2,1)} %collective-permute-done.3.refs_1_), channel_id=1, source_target_pairs={{0,1},{1,0},{2,3},{3,2},{4,5},{5,4},{6,7},{7,6},{8,9},{9,8},{10,11... | collective-permute-start | bytes 1572872 | tf_op jit(solution)/shard_map/ppermute | solution.py:248
  36.8 19.6 %collective-permute-start.9 = (bf16[128,2048]{1,0:T(8,128)(2,1)S(1)}, bf16[128,2048]{1,0:T(8,128)(2,1)S(1)}, u32[]{:S(2)}, u32[]{:S(2)}) collective-permute-start(bf16[128,2048]{1,0:T(8,128)(2,1)S(1)} %collective-permute-done.8.refs_4_), channel_id=1, source_target_pairs={{0,1},{1,0},{2,3},{3,2},{4,5},{5,4},{6,7},{7,6},{8,9},{9,8},{10,11... | collective-permute-start | bytes 1572872 | tf_op jit(solution)/shard_map/ppermute | solution.py:248
  44.5 11.9 %collective-permute-start.7 = (bf16[128,2048]{1,0:T(8,128)(2,1)S(1)}, bf16[128,2048]{1,0:T(8,128)(2,1)}, u32[]{:S(2)}, u32[]{:S(2)}) collective-permute-start(bf16[128,2048]{1,0:T(8,128)(2,1)S(1)} %collective-permute-done.6.refs_2_), channel_id=1, source_target_pairs={{0,1},{1,0},{2,3},{3,2},{4,5},{5,4},{6,7},{7,6},{8,9},{9,8},{10,11... | collective-permute-start | bytes 1572872 | tf_op jit(solution)/shard_map/ppermute | solution.py:248
  49.1 7.4 %collective-permute-start.11 = (bf16[128,2048]{1,0:T(8,128)(2,1)S(1)}, bf16[128,2048]{1,0:T(8,128)(2,1)}, u32[]{:S(2)}, u32[]{:S(2)}) collective-permute-start(bf16[128,2048]{1,0:T(8,128)(2,1)S(1)} %collective-permute-done.10.refs_6_), channel_id=1, source_target_pairs={{0,1},{1,0},{2,3},{3,2},{4,5},{5,4},{6,7},{7,6},{8,9},{9,8},{10,11... | collective-permute-start | bytes 1572872 | tf_op jit(solution)/shard_map/ppermute | solution.py:248
  162.4 2.3 %collective-permute-start.12 = (bf16[1,144,512]{2,1,0:T(8,128)(2,1)}, bf16[1,144,512]{2,1,0:T(8,128)(2,1)S(1)}, u32[]{:S(2)}, u32[]{:S(2)}) collective-permute-start(bf16[1,144,512]{2,1,0:T(8,128)(2,1)} %get-tuple-element.51), channel_id=1, source_target_pairs={{0,1},{1,0},{2,3},{3,2},{4,5},{5,4},{6,7},{7,6},{8,9},{9,8},{10,11... | collective-permute-start | bytes 442376 | tf_op jit(solution)/shard_map/ppermute | solution.py:248
  163.5 1.6 collective-permute-start.13
  163.6 1.8 collective-permute-start.14
  164.0 1.7 collective-permute-start.15
  168.0 9.2 %collective-permute-start.16 = (bf16[2,144,512]{2,1,0:T(8,128)(2,1)}, bf16[2,144,512]{2,1,0:T(8,128)(2,1)S(1)}, u32[]{:S(2)}, u32[]{:S(2)}) collective-permute-start(bf16[2,144,512]{2,1,0:T(8,128)(2,1)} %get-tuple-element.55), channel_id=1, source_target_pairs={{0,2},{1,3},{2,0},{3,1},{4,6},{5,7},{6,4},{7,5},{8,10},{9,11},{10,... | collective-permute-start | bytes 884744 | tf_op jit(solution)/shard_map/ppermute | solution.py:248
  169.2 13.8 %collective-permute-start.17 = (bf16[2,144,512]{2,1,0:T(8,128)(2,1)}, bf16[2,144,512]{2,1,0:T(8,128)(2,1)}, u32[]{:S(2)}, u32[]{:S(2)}) collective-permute-start(bf16[2,144,512]{2,1,0:T(8,128)(2,1)} %get-tuple-element.56), channel_id=1, source_target_pairs={{0,2},{1,3},{2,0},{3,1},{4,6},{5,7},{6,4},{7,5},{8,10},{9,11},{10,... | collective-permute-start | bytes 884744 | tf_op jit(solution)/shard_map/ppermute | solution.py:248
  183.0 2.4 %collective-permute-start.18 = (bf16[1,144,512]{2,1,0:T(8,128)(2,1)}, bf16[1,144,512]{2,1,0:T(8,128)(2,1)}, u32[]{:S(2)}, u32[]{:S(2)}) collective-permute-start(bf16[1,144,512]{2,1,0:T(8,128)(2,1)} %get-tuple-element.65), channel_id=1, source_target_pairs={{0,1},{1,0},{2,3},{3,2},{4,5},{5,4},{6,7},{7,6},{8,9},{9,8},{10,11... | collective-permute-start | bytes 442376 | tf_op jit(solution)/shard_map/ppermute | solution.py:248
  184.1 1.7 collective-permute-start.19
  184.1 1.9 collective-permute-start.20
  184.6 1.7 collective-permute-start.21
  (6 other events, 25.7 us)
Sparse Core Ops, SparseCore 0:
  10.6 143.9 all-gather.1

commit v6 on v5

--- a/solution.py
+++ b/solution.py
@@ -80,11 +80,11 @@
     )(kv, queries, span_keys, span_values)
 
 
-def pack_state(ref, i, out, top, total):
-    ref[i, :HD, :] = out.astype(BF16)
+def pack_state(ref, i, out, top, total, columns=slice(None)):
+    ref[i, :HD, columns] = out.astype(BF16)
     high = total.astype(BF16)
     low = (total - high.astype(F32)).astype(BF16)
-    ref[i, HD:, :] = jnp.concatenate(
+    ref[i, HD:, columns] = jnp.concatenate(
         [top.astype(BF16), high, low, jnp.zeros((TAIL - 3, out.shape[1]), BF16)], axis=0
     )
 
@@ -95,27 +95,27 @@
 
 
 def far_kernel(picks_ref, *refs):
-    q_refs, whole_ref, refs = refs[:2], refs[2], refs[3:]
-    piece_refs, whole_out_ref, refs = refs[:QB], refs[QB], refs[QB + 1 :]
-    buffer, score_refs, weight_refs, sems = refs[0], refs[1:3], refs[3:5], refs[5]
+    q_refs, whole_ref, out_refs, refs = refs[:2], refs[2], refs[3:5], refs[5:]
+    buffer, score_refs, weight_refs, sem = refs[0], refs[1:3], refs[3:5], refs[5]
     for pick in range(2 * QB * SEL):
-        pltpu.make_async_copy(
-            whole_ref.at[picks_ref[pick]], buffer.at[pick], sems.at[pick // SEL]
-        ).start()
+        pltpu.make_async_copy(whole_ref.at[picks_ref[pick]], buffer.at[pick], sem).start()
+    pltpu.make_async_copy(buffer, buffer, sem).wait()
+    step_columns = BLK // 2
+    steps = [(row, first) for row in range(2 * QB) for first in range(0, BLK, step_columns)]
+    sums = {}
 
     def joined(row, which):
-        return jnp.concatenate(
-            [buffer[row * SEL + j, which] for j in range(SEL)], axis=0
-        )
-
-    def score(row, q_ref, i, score_ref):
-        held = buffer.at[pl.ds(row * SEL, SEL)]
-        pltpu.make_async_copy(held, held, sems.at[row]).wait()
-        score_ref[...] = dot_nt(joined(row, 0), q_ref[pl.ds(i * BLK, BLK), :])
-
-    def soften(score_ref, weight_ref):
+        return jnp.concatenate([buffer[row * SEL + j, which] for j in range(SEL)], axis=0)
+
+    def score(number):
+        row, first = steps[number]
+        tokens = pl.ds(row % QB * BLK + first, step_columns)
+        score_refs[number % 2][...] = dot_nt(joined(row, 0), q_refs[row // QB][tokens, :])
+
+    def soften(number):
+        score_ref, weight_ref = score_refs[number % 2], weight_refs[number % 2]
         tops, totals = [], []
-        for lane in range(0, BLK, HD):
+        for lane in range(0, step_columns, HD):
             lanes = slice(lane, lane + HD)
             top = rounded_top(jnp.max(score_ref[:, lanes], axis=0, keepdims=True))
             total = jnp.zeros((8, HD), F32)
@@ -125,21 +125,22 @@
                 total = total + jnp.sum(weights.reshape(8, 8, HD), axis=0)
             tops.append(top)
             totals.append(jnp.sum(total, axis=0, keepdims=True))
-        return jnp.concatenate(tops, axis=1), jnp.concatenate(totals, axis=1)
-
-    def finish(row, weight_ref, out_ref, i, top, total):
-        pack_state(out_ref, i, dot_tn(joined(row, 1), weight_ref[...]), top, total)
-
-    for first in range(0, 2 * QB, 2):
-        units = [first, first + 1]
-        for k, row in enumerate(units):
-            score(row, q_refs[row // QB], row % QB, score_refs[k])
-        for k, row in enumerate(units):
-            top, total = soften(score_refs[k], weight_refs[k])
-            if row < QB:
-                finish(row, weight_refs[k], piece_refs[row], 0, top, total)
-            else:
-                finish(row, weight_refs[k], whole_out_ref, row % QB, top, total)
+        sums[number] = jnp.concatenate(tops, axis=1), jnp.concatenate(totals, axis=1)
+
+    def finish(number):
+        row, first = steps[number]
+        top, total = sums.pop(number)
+        out = dot_tn(joined(row, 1), weight_refs[number % 2][...])
+        columns = slice(first, first + step_columns)
+        pack_state(out_refs[row // QB], row % QB, out, top, total, columns)
+
+    for number in range(len(steps) + 2):
+        if number < len(steps):
+            score(number)
+        if number >= 2:
+            finish(number - 2)
+        if 1 <= number <= len(steps):
+            soften(number - 1)
 
 
 def far(picks, queries, whole):
@@ -150,13 +151,12 @@
         in_specs=[pl.BlockSpec(memory_space=pltpu.SMEM)]
         + [vmem] * 2
         + [pl.BlockSpec(memory_space=pl.ANY)],
-        out_specs=[vmem] * (QB + 1),
-        out_shape=[jax.ShapeDtypeStruct((1, pay, BLK), BF16)] * QB
-        + [jax.ShapeDtypeStruct((QB, pay, BLK), BF16)],
+        out_specs=[vmem] * 2,
+        out_shape=[jax.ShapeDtypeStruct((QB, pay, BLK), BF16)] * 2,
         scratch_shapes=[pltpu.VMEM((2 * QB * SEL,) + whole.shape[1:], BF16)]
-        + [pltpu.VMEM((BLK, BLK), F32)] * 2
-        + [pltpu.VMEM((BLK, BLK), BF16)] * 2
-        + [pltpu.SemaphoreType.DMA((2 * QB,))],
+        + [pltpu.VMEM((BLK, BLK // 2), F32)] * 2
+        + [pltpu.VMEM((BLK, BLK // 2), BF16)] * 2
+        + [pltpu.SemaphoreType.DMA],
         compiler_params=pltpu.CompilerParams(vmem_limit_bytes=VMEM_BYTES),
         cost_estimate=pl.CostEstimate(
             flops=8 * 2 * QB * 4 * BLK * BLK * HD,
@@ -167,12 +167,11 @@
     )(picks, *queries, whole)
 
 
-def merge_two_kernel(a_ref, *refs):
-    b_refs, out_refs = refs[:QB], refs[QB:]
+def merge_two_kernel(a_ref, b_ref, *out_refs):
     per = QB // len(out_refs)
     for i in range(QB):
         acc_a, m_a, l_a = unpack_state(a_ref, i)
-        acc_b, m_b, l_b = unpack_state(b_refs[i], 0)
+        acc_b, m_b, l_b = unpack_state(b_ref, i)
         top = jnp.maximum(m_a, m_b)
         f_a = jnp.exp2(m_a - top)
         f_b = jnp.exp2(m_b - top)
@@ -181,49 +180,61 @@
         )
 
 
-def merge_two(mine, others, pieces):
+def merge_two(mine, other, pieces):
     vmem = pl.BlockSpec(memory_space=pltpu.VMEM)
     shape = (QB // pieces,) + mine.shape[1:]
     return pl.pallas_call(
         merge_two_kernel,
-        in_specs=[vmem] * (1 + QB),
+        in_specs=[vmem] * 2,
         out_specs=[vmem] * pieces,
         out_shape=[jax.ShapeDtypeStruct(shape, BF16)] * pieces,
         name="merge_two",
-    )(mine, *others)
-
-
-def merge_last_kernel(a_ref, *refs):
-    core_refs, refs = refs[:QB], refs[QB:]
-    (acc_ref, m_ref, l_ref), chip_refs, out_ref = refs[:3], refs[3:-1], refs[-1]
-    per = QB // len(chip_refs)
+    )(mine, other)
+
+
+def merge_last_kernel(head_ref, a_ref, b_ref, acc_ref, m_ref, l_ref, *refs, pieces):
+    chip_refs, out_ref, share_refs = refs[:pieces], refs[pieces], refs[pieces + 1 :]
+    per = QB // pieces
+    rows = QB * BLK // len(share_refs)
     for i in range(QB):
-        states = [unpack_state(a_ref, i), unpack_state(core_refs[i], 0)]
+        states = [unpack_state(a_ref, i), unpack_state(b_ref, i)]
         states.append(unpack_state(chip_refs[i // per], i % per))
         states.append((acc_ref[i], m_ref[i], l_ref[i]))
         top = functools.reduce(jnp.maximum, [m for _, m, _ in states])
         factors = [jnp.exp2(m - top) for _, m, _ in states]
         total = sum(f * l for f, (_, _, l) in zip(factors, states))
         factors = [f / total for f in factors]
-        out = sum(f * acc for f, (acc, _, _) in zip(factors, states))
-        out_ref[i * BLK : (i + 1) * BLK, :] = out.T.astype(BF16)
-
-
-def merge_last(mine, core_parts, near_state, chip_parts):
+        out = sum(f * acc for f, (acc, _, _) in zip(factors, states)).T.astype(BF16)
+        out_ref[i * BLK : (i + 1) * BLK, :] = out
+        for first in range(0, BLK, rows):
+            owner = (i * BLK + first) // rows
+            for r, share_ref in enumerate(share_refs):
+
+                def keep(share_ref=share_ref, first=first, out=out):
+                    share_ref[...] = out[first : first + rows, :]
+
+                pl.when(head_ref[0] ^ r == owner)(keep)
+
+
+def merge_last(head, heads, mine, core_part, near_state, chip_parts):
     vmem = pl.BlockSpec(memory_space=pltpu.VMEM)
-    arrays = [mine, *core_parts, *near_state, *chip_parts]
-    return pl.pallas_call(
-        merge_last_kernel,
-        in_specs=[vmem] * len(arrays),
-        out_specs=vmem,
-        out_shape=jax.ShapeDtypeStruct((QB * BLK, HD), BF16),
+    arrays = [mine, core_part, *near_state, *chip_parts]
+    rows = QB * BLK
+    attention, *shares = pl.pallas_call(
+        functools.partial(merge_last_kernel, pieces=len(chip_parts)),
+        in_specs=[pl.BlockSpec(memory_space=pltpu.SMEM)] + [vmem] * len(arrays),
+        out_specs=[vmem] * (1 + heads),
+        out_shape=[jax.ShapeDtypeStruct((rows, HD), BF16)]
+        + [jax.ShapeDtypeStruct((rows // heads, HD), BF16)] * heads,
         name="merge_last",
-    )(*arrays)
-
-
-def project_kernel(head_ref, a_ref, *refs):
-    w_refs, out_ref = refs[:-1], refs[-1]
-    rows = jnp.concatenate([a_ref[head_ref[0] ^ i] for i in range(len(w_refs))], axis=1)
+    )(head, *arrays)
+    return attention, shares
+
+
+def project_kernel(*refs):
+    heads = len(refs) // 2
+    a_refs, w_refs, out_ref = refs[:heads], refs[heads:-1], refs[-1]
+    rows = jnp.concatenate([a_ref[...] for a_ref in a_refs], axis=1)
     tile = 512
     for first in range(0, out_ref.shape[1], tile):
         weight = jnp.concatenate([w_ref[:, first : first + tile] for w_ref in w_refs], axis=0)
@@ -232,16 +243,16 @@
         ).astype(BF16)
 
 
-def project(head, parts, weights):
+def project(parts, weights):
     vmem = pl.BlockSpec(memory_space=pltpu.VMEM)
     return pl.pallas_call(
         project_kernel,
-        in_specs=[pl.BlockSpec(memory_space=pltpu.SMEM)] + [vmem] * (1 + len(weights)),
+        in_specs=[vmem] * (len(parts) + len(weights)),
         out_specs=vmem,
-        out_shape=jax.ShapeDtypeStruct((parts.shape[1], weights[0].shape[1]), BF16),
+        out_shape=jax.ShapeDtypeStruct((parts[0].shape[0], weights[0].shape[1]), BF16),
         compiler_params=pltpu.CompilerParams(vmem_limit_bytes=24 << 20),
         name="project",
-    )(head, parts, *weights)
+    )(*parts, *weights)
 
 
 def swap(array, bits):
@@ -291,18 +302,16 @@
             whole,
         )
 
-    *far_corner, far_chip = far_of(3, 2, [])
-    for_chip = merge_two(far_chip, [swap(piece, 1) for piece in far_corner], 2)
+    far_corner, far_chip = far_of(3, 2, [])
+    for_chip = merge_two(far_chip, swap(far_corner, 1), 2)
     chip_parts = [swap(piece, 2) for piece in for_chip]
-    *far_core, far_own = far_of(1, 0, for_chip)
-    core_parts = [swap(piece, 1) for piece in after(far_core, *chip_parts)]
-    attention = merge_last(far_own, core_parts, near_state, chip_parts)
-
-    share_rows = attention.shape[0] // heads
-    parts = lax.all_to_all(
-        attention.reshape(heads, share_rows, HD), "head", split_axis=0, concat_axis=0, tiled=True
-    )
-    return attention, project(head[None], parts, weights)
+    far_core, far_own = far_of(1, 0, for_chip)
+    core_part = swap(after(far_core, *chip_parts), 1)
+    attention, shares = merge_last(
+        head[None], heads, far_own, core_part, near_state, chip_parts
+    )
+    parts = [shares[0]] + [swap(shares[r], r) for r in range(1, heads)]
+    return attention, project(parts, weights)
 
 
 def solution(mesh):

time: 214 us -> 214 us (level)
  blocking collectives: 13.8 us -> 0 us
  starting transfers between devices: 24 us -> 31.5 us
  waiting for transfers between devices: 127 us -> 134 us
    all_to_all x1 -> x0, blocking collectives: 13.8 us -> none  [body(): lax.all_to_all(attention.reshape(heads, share_rows, HD), 'head', split_ax...]
    ppermute x22 -> x23, starting transfers between devices: 23.9 us -> 31.4 us  [swap(): lax.ppermute(array, 'head', [(h, h ^ bits) for h in range(lax.axis_size('...]
    ppermute x22 -> x23, waiting for transfers between devices: 29.6 us -> 36.5 us  [swap(): lax.ppermute(array, 'head', [(h, h ^ bits) for h in range(lax.axis_size('...]
  transfers between devices with their start and end apart: 23 -> 24, of which waited for: 14 -> 14; matrix products, arithmetic and copies ran while one was open for 2% -> 2% of each run, Pallas kernels for 6% -> 5%
where the time goes in v6:
time: 214 us
  waiting for transfers between devices  134 us (63%)
  starting transfers between devices  31.5 us (15%)
  Pallas kernels  27.7 us (13%)
  between operations  14.2 us (7%)
  other arithmetic  3.37 us (2%)
  local copies, waits for them, and re-layouts  2.9 us (1%)
    all_gather x1, waiting for transfers between devices, body(): whole = lax.all_gather(jnp.stack(pieces, axis=1), 'ctx', axis=0, tiled=True)  97.5 us
    ppermute x23, waiting for transfers between devices, swap(): lax.ppermute(array, 'head', [(h, h ^ bits) for h in range(lax.axis_size('...  36.5 us
    ppermute x23, starting transfers between devices, swap(): lax.ppermute(array, 'head', [(h, h ^ bits) for h in range(lax.axis_size('...  31.4 us
    pallas_call x2, Pallas kernels, far(): pl.pallas_call(far_kernel, in_specs=[pl.BlockSpec(memory_space=pltpu.SMEM...  13.4 us
    pallas_call x1, Pallas kernels, near(): pl.pallas_call(near_kernel, grid_spec=grid_spec, out_shape=state_shapes()...  4.67 us
  transfers between devices with their start and end apart: 24, of which 14 were waited for; matrix products, arithmetic and copies ran while one was open for 2% of the time, Pallas kernels for 5%

profile of v6, /device:TPU:1, one launch (start us, length us, event | category | flops | bytes accessed | tf_op | source)
XLA Modules:
  0.0 213.6 jit_solution(9134678009438806685)
XLA Ops:
  9.3 2.2 %collective-permute-start.3 = (bf16[2048,128]{1,0:T(8,128)(2,1)S(1)}, bf16[2048,128]{1,0:T(8,128)(2,1)}, u32[]{:S(2)}, u32[]{:S(2)}) collective-permute-start(bf16[2048,128]{1,0:T(8,128)(2,1)S(1)} %copy-done.2), channel_id=1, source_target_pairs={{0,2},{1,3},{2,0},{3,1},{4,6},{5,7},{6,4},{7,5},{8,10},{9,11},{10,... | collective-permute-start | bytes 1572872 | tf_op jit(solution)/shard_map/ppermute | solution.py:259
  12.7 1.6 collective-permute-start
  15.6 6.4 %collective-permute-done = s32[4,1,4]{2,1,0:T(1,128)S(1)} collective-permute-done((s32[4,1,4]{2,1,0:T(1,128)S(1)}, s32[4,1,4]{2,1,0:T(1,128)S(1)}, u32[]{:S(2)}, u32[]{:S(2)}) %collective-permute-start) | collective-permute-done | bytes 96 | tf_op jit(solution)/shard_map/ppermute | solution.py:259
  22.0 5.6 %collective-permute-start.1 = (s32[2,4,1,4]{3,1,2,0:T(4,128)S(1)}, s32[2,4,1,4]{3,1,2,0:T(4,128)S(1)}, u32[]{:S(2)}, u32[]{:S(2)}) collective-permute-start(s32[2,4,1,4]{3,1,2,0:T(4,128)S(1)} %pad_add_fusion), channel_id=1, source_target_pairs={{0,1},{1,0},{2,3},{3,2},{4,5},{5,4},{6,7},{7,6},{8,9},{9,8},{10,11... | collective-permute-start | bytes 392 | tf_op jit(solution)/shard_map/ppermute | solution.py:259
  30.1 6.7 %collective-permute-done.8.refs_12_ = bf16[128,2048]{1,0:T(8,128)(2,1)S(1)} collective-permute-done((bf16[128,2048]{1,0:T(8,128)(2,1)S(1)}, bf16[128,2048]{1,0:T(8,128)(2,1)S(1)}, u32[]{:S(2)}, u32[]{:S(2)}) %collective-permute-start.8) | collective-permute-done | bytes 524320 | tf_op jit(solution)/shard_map/ppermute | solution.py:259
  36.8 2.7 %collective-permute-start.9 = (bf16[128,2048]{1,0:T(8,128)(2,1)S(1)}, bf16[128,2048]{1,0:T(8,128)(2,1)S(1)}, u32[]{:S(2)}, u32[]{:S(2)}) collective-permute-start(bf16[128,2048]{1,0:T(8,128)(2,1)S(1)} %collective-permute-done.8.refs_12_), channel_id=1, source_target_pairs={{0,1},{1,0},{2,3},{3,2},{4,5},{5,4},{6,7},{7,6},{8,9},{9,8},{10,11... | collective-permute-start | bytes 1572872 | tf_op jit(solution)/shard_map/ppermute | solution.py:259
  39.5 5.0 %collective-permute-done.6.refs_10_ = bf16[128,2048]{1,0:T(8,128)(2,1)S(1)} collective-permute-done((bf16[128,2048]{1,0:T(8,128)(2,1)S(1)}, bf16[128,2048]{1,0:T(8,128)(2,1)S(1)}, u32[]{:S(2)}, u32[]{:S(2)}) %collective-permute-start.6) | collective-permute-done | bytes 524320 | tf_op jit(solution)/shard_map/ppermute | solution.py:259
  44.5 2.4 %collective-permute-start.7 = (bf16[128,2048]{1,0:T(8,128)(2,1)S(1)}, bf16[128,2048]{1,0:T(8,128)(2,1)}, u32[]{:S(2)}, u32[]{:S(2)}) collective-permute-start(bf16[128,2048]{1,0:T(8,128)(2,1)S(1)} %collective-permute-done.6.refs_10_), channel_id=1, source_target_pairs={{0,1},{1,0},{2,3},{3,2},{4,5},{5,4},{6,7},{7,6},{8,9},{9,8},{10,11... | collective-permute-start | bytes 1572872 | tf_op jit(solution)/shard_map/ppermute | solution.py:259
  46.9 2.1 %collective-permute-done.10.refs_14_ = bf16[128,2048]{1,0:T(8,128)(2,1)S(1)} collective-permute-done((bf16[128,2048]{1,0:T(8,128)(2,1)S(1)}, bf16[128,2048]{1,0:T(8,128)(2,1)S(1)}, u32[]{:S(2)}, u32[]{:S(2)}) %collective-permute-start.10) | collective-permute-done | bytes 524320 | tf_op jit(solution)/shard_map/ppermute | solution.py:259
  50.8 4.7 %near.1 = (f32[4,128,512]{2,1,0:T(8,128)}, f32[4,1,512]{2,1,0:T(1,128)}, f32[4,1,512]{2,1,0:T(1,128)}) custom-call(s32[1]{0:T(128)} %bitcast.3.kv_ref, bf16[2048,128]{1,0:T(8,128)(2,1)} %refs_1_, bf16[2048,256]{1,0:T(8,128)(2,1)} %k_ref.1, bf16[2048,256]{1,0:T(8,128)(2,1)} %v_ref.1), custom_call_target="tpu_custom_call" | custom-call | flops 536870912 | bytes 4194304 | tf_op jit(solution)/shard_map/near/pallas_call | solution.py:72
  57.1 97.5 %all-gather.2.cloned.1.call-done.refs_2_ = bf16[256,2,128,128]{3,2,1,0:T(8,128)(2,1)} async-done(((bf16[8,2,128,128]{3,2,1,0:T(8,128)(2,1)}), bf16[256,2,128,128]{3,2,1,0:T(8,128)(2,1)}) %all-gather.2.cloned.1.call-update) | async-done | bytes 16777232 | tf_op jit(solution)/shard_map/all_gather | solution.py:277
  154.6 6.7 %far.2 = (bf16[4,144,512]{2,1,0:T(8,128)(2,1)}, bf16[4,144,512]{2,1,0:T(8,128)(2,1)}) custom-call(s32[32]{0:T(128)} %pad_add_fusion.2.picks_ref, bf16[2048,128]{1,0:T(8,128)(2,1)} %collective-permute-done.4.refs_0_, bf16[2048,128]{1,0:T(8,128)(2,1)} %collective-permute-done.3.refs_1_, bf16[256,2,128,128]{3,2,1,0:T(8,128)(2,1)} %all-gather.2.cloned.1.call-done.refs_2_), custom_call_target="tpu_custom_call" | custom-call | flops 8589934592 | bytes 5242880 | tf_op jit(solution)/shard_map/far/pallas_call | solution.py:149
  163.1 1.4 collective-permute-done.12.b_ref
  164.4 2.2 %merge_two.1 = (bf16[2,144,512]{2,1,0:T(8,128)(2,1)}, bf16[2,144,512]{2,1,0:T(8,128)(2,1)}) custom-call(bf16[4,144,512]{2,1,0:T(8,128)(2,1)} %get-tuple-element.50.a_ref, bf16[4,144,512]{2,1,0:T(8,128)(2,1)} %collective-permute-done.12.b_ref), custom_call_target="tpu_custom_call" | custom-call | tf_op jit(solution)/shard_map/merge_two/pallas_call | solution.py:186
  168.1 6.7 %far.3 = (bf16[4,144,512]{2,1,0:T(8,128)(2,1)}, bf16[4,144,512]{2,1,0:T(8,128)(2,1)}) custom-call(s32[32]{0:T(128)} %pad_add_fusion.1.picks_ref, bf16[2048,128]{1,0:T(8,128)(2,1)} %copy-done.5, bf16[2048,128]{1,0:T(8,128)(2,1)} %refs_1_, bf16[256,2,128,128]{3,2,1,0:T(8,128)(2,1)} %all-gather.2.cloned.1.call-done.refs_2_), custom_call_target="tpu_custom_call" | custom-call | flops 8589934592 | bytes 5242880 | tf_op jit(solution)/shard_map/far/pallas_call | solution.py:149
  175.1 6.4 %collective-permute-done.14.refs_1_ = bf16[2,144,512]{2,1,0:T(8,128)(2,1)} collective-permute-done((bf16[2,144,512]{2,1,0:T(8,128)(2,1)}, bf16[2,144,512]{2,1,0:T(8,128)(2,1)}, u32[]{:S(2)}, u32[]{:S(2)}) %collective-permute-start.14) | collective-permute-done | bytes 294944 | tf_op jit(solution)/shard_map/ppermute | solution.py:259
  182.7 2.0 collective-permute-done.15.b_ref
  184.7 4.0 %merge_last.1 = (bf16[2048,128]{1,0:T(8,128)(2,1)}, bf16[256,128]{1,0:T(8,128)(2,1)}, bf16[256,128]{1,0:T(8,128)(2,1)}, bf16[256,128]{1,0:T(8,128)(2,1)}, bf16[2...) custom-call(s32[1]{0:T(128)} %bitcast.head_ref, ...), custom_call_target="tpu_custom_call" | custom-call | tf_op jit(solution)/shard_map/merge_last/pallas_call | solution.py:223
  190.8 2.7 %collective-permute-start.19 = (bf16[256,128]{1,0:T(8,128)(2,1)}, bf16[256,128]{1,0:T(8,128)(2,1)S(1)}, u32[]{:S(2)}, u32[]{:S(2)}) collective-permute-start(bf16[256,128]{1,0:T(8,128)(2,1)} %get-tuple-element.68), channel_id=1, source_target_pairs={{0,4},{1,5},{2,6},{3,7},{4,0},{5,1},{6,2},{7,3},{8,12},{9,13},{10,... | collective-permute-start | bytes 196616 | tf_op jit(solution)/shard_map/ppermute | solution.py:259
  194.1 2.5 %collective-permute-start.21 = (bf16[256,128]{1,0:T(8,128)(2,1)}, bf16[256,128]{1,0:T(8,128)(2,1)S(1)}, u32[]{:S(2)}, u32[]{:S(2)}) collective-permute-start(bf16[256,128]{1,0:T(8,128)(2,1)} %get-tuple-element.70), channel_id=1, source_target_pairs={{0,6},{1,7},{2,4},{3,5},{4,2},{5,3},{6,0},{7,1},{8,14},{9,15},{10,... | collective-permute-start | bytes 196616 | tf_op jit(solution)/shard_map/ppermute | solution.py:259
  197.8 1.8 collective-permute-done.20.refs_5_
  199.6 1.5 collective-permute-done.21.refs_6_
  201.1 1.4 collective-permute-done.22.refs_7_
  203.4 3.4 %project.1 = bf16[256,2048]{1,0:T(8,128)(2,1)} custom-call(bf16[256,128]{1,0:T(8,128)(2,1)S(1)} %copy-done.1, bf16[256,128]{1,0:T(8,128)(2,1)S(1)} %collective-permute-done.16.refs_1_, bf16[256,128]{1,0:T(8,128)(2,1)S(1)} %collective-permute-done.17.refs_2_, bf16[256,128]{1,0:T(8,128)(2,1)S(1)} %collective-permute-done.18.refs_3_, ...), custom_call_target="tpu_custom_call" | custom-call | tf_op jit(solution)/shard_map/project/pallas_call | solution.py:248
  (56 shorter events, 19.8 us)
Async XLA Ops:
  7.2 147.4 %all-gather.2.cloned.1.call-start = ((), (), s32[]{:S(2)}) async-start(), calls=%async_computation | async-start | bytes 17301504 | tf_op jit(solution)/shard_map/all_gather | solution.py:277
  9.3 20.1 %collective-permute-start.3 = (bf16[2048,128]{1,0:T(8,128)(2,1)S(1)}, bf16[2048,128]{1,0:T(8,128)(2,1)}, u32[]{:S(2)}, u32[]{:S(2)}) collective-permute-start(bf16[2048,128]{1,0:T(8,128)(2,1)S(1)} %copy-done.2), channel_id=1, source_target_pairs={{0,2},{1,3},{2,0},{3,1},{4,6},{5,7},{6,4},{7,5},{8,10},{9,11},{10,... | collective-permute-start | bytes 1572872 | tf_op jit(solution)/shard_map/ppermute | solution.py:259
  11.5 18.5 %collective-permute-start.2 = (bf16[2048,128]{1,0:T(8,128)(2,1)S(1)}, bf16[2048,128]{1,0:T(8,128)(2,1)S(1)}, u32[]{:S(2)}, u32[]{:S(2)}) collective-permute-start(bf16[2048,128]{1,0:T(8,128)(2,1)S(1)} %copy-done.2), channel_id=1, source_target_pairs={{0,1},{1,0},{2,3},{3,2},{4,5},{5,4},{6,7},{7,6},{8,9},{9,8},{10,11... | collective-permute-start | bytes 1572872 | tf_op jit(solution)/shard_map/ppermute | solution.py:259
  12.7 9.2 %collective-permute-start = (s32[4,1,4]{2,1,0:T(1,128)S(1)}, s32[4,1,4]{2,1,0:T(1,128)S(1)}, u32[]{:S(2)}, u32[]{:S(2)}) collective-permute-start(s32[4,1,4]{2,1,0:T(1,128)S(1)} %copy-done.4), channel_id=1, source_target_pairs={{0,2},{1,3},{2,0},{3,1},{4,6},{5,7},{6,4},{7,5},{8,10},{9,11},{10,... | collective-permute-start | bytes 200 | tf_op jit(solution)/shard_map/ppermute | solution.py:259
  14.4 22.4 %collective-permute-start.8 = (bf16[128,2048]{1,0:T(8,128)(2,1)S(1)}, bf16[128,2048]{1,0:T(8,128)(2,1)S(1)}, u32[]{:S(2)}, u32[]{:S(2)}) collective-permute-start(bf16[128,2048]{1,0:T(8,128)(2,1)S(1)} %copy-done), channel_id=1, source_target_pairs={{0,4},{1,5},{2,6},{3,7},{4,0},{5,1},{6,2},{7,3},{8,12},{9,13},{10,... | collective-permute-start | bytes 1572872 | tf_op jit(solution)/shard_map/ppermute | solution.py:259
  22.0 6.5 %collective-permute-start.1 = (s32[2,4,1,4]{3,1,2,0:T(4,128)S(1)}, s32[2,4,1,4]{3,1,2,0:T(4,128)S(1)}, u32[]{:S(2)}, u32[]{:S(2)}) collective-permute-start(s32[2,4,1,4]{3,1,2,0:T(4,128)S(1)} %pad_add_fusion), channel_id=1, source_target_pairs={{0,1},{1,0},{2,3},{3,2},{4,5},{5,4},{6,7},{7,6},{8,9},{9,8},{10,11... | collective-permute-start | bytes 392 | tf_op jit(solution)/shard_map/ppermute | solution.py:259
  27.6 16.9 %collective-permute-start.6 = (bf16[128,2048]{1,0:T(8,128)(2,1)S(1)}, bf16[128,2048]{1,0:T(8,128)(2,1)S(1)}, u32[]{:S(2)}, u32[]{:S(2)}) collective-permute-start(bf16[128,2048]{1,0:T(8,128)(2,1)S(1)} %copy-done), channel_id=1, source_target_pairs={{0,2},{1,3},{2,0},{3,1},{4,6},{5,7},{6,4},{7,5},{8,10},{9,11},{10,... | collective-permute-start | bytes 1572872 | tf_op jit(solution)/shard_map/ppermute | solution.py:259
  28.4 20.6 %collective-permute-start.10 = (bf16[128,2048]{1,0:T(8,128)(2,1)S(1)}, bf16[128,2048]{1,0:T(8,128)(2,1)S(1)}, u32[]{:S(2)}, u32[]{:S(2)}) collective-permute-start(bf16[128,2048]{1,0:T(8,128)(2,1)S(1)} %copy-done), channel_id=1, source_target_pairs={{0,6},{1,7},{2,4},{3,5},{4,2},{5,3},{6,0},{7,1},{8,14},{9,15},{10,... | collective-permute-start | bytes 1572872 | tf_op jit(solution)/shard_map/ppermute | solution.py:259
  29.4 27.0 %collective-permute-start.5 = (bf16[128,2048]{1,0:T(8,128)(2,1)S(1)}, bf16[128,2048]{1,0:T(8,128)(2,1)S(1)}, u32[]{:S(2)}, u32[]{:S(2)}) collective-permute-start(bf16[128,2048]{1,0:T(8,128)(2,1)S(1)} %copy-done), channel_id=1, source_target_pairs={{0,1},{1,0},{2,3},{3,2},{4,5},{5,4},{6,7},{7,6},{8,9},{9,8},{10,11... | collective-permute-start | bytes 1572872 | tf_op jit(solution)/shard_map/ppermute | solution.py:259
  30.0 26.4 %collective-permute-start.4 = (bf16[2048,128]{1,0:T(8,128)(2,1)}, bf16[2048,128]{1,0:T(8,128)(2,1)}, u32[]{:S(2)}, u32[]{:S(2)}) collective-permute-start(bf16[2048,128]{1,0:T(8,128)(2,1)} %collective-permute-done.3.refs_1_), channel_id=1, source_target_pairs={{0,1},{1,0},{2,3},{3,2},{4,5},{5,4},{6,7},{7,6},{8,9},{9,8},{10,11... | collective-permute-start | bytes 1572872 | tf_op jit(solution)/shard_map/ppermute | solution.py:259
  36.8 19.6 %collective-permute-start.9 = (bf16[128,2048]{1,0:T(8,128)(2,1)S(1)}, bf16[128,2048]{1,0:T(8,128)(2,1)S(1)}, u32[]{:S(2)}, u32[]{:S(2)}) collective-permute-start(bf16[128,2048]{1,0:T(8,128)(2,1)S(1)} %collective-permute-done.8.refs_12_), channel_id=1, source_target_pairs={{0,1},{1,0},{2,3},{3,2},{4,5},{5,4},{6,7},{7,6},{8,9},{9,8},{10,11... | collective-permute-start | bytes 1572872 | tf_op jit(solution)/shard_map/ppermute | solution.py:259
  44.5 11.9 %collective-permute-start.7 = (bf16[128,2048]{1,0:T(8,128)(2,1)S(1)}, bf16[128,2048]{1,0:T(8,128)(2,1)}, u32[]{:S(2)}, u32[]{:S(2)}) collective-permute-start(bf16[128,2048]{1,0:T(8,128)(2,1)S(1)} %collective-permute-done.6.refs_10_), channel_id=1, source_target_pairs={{0,1},{1,0},{2,3},{3,2},{4,5},{5,4},{6,7},{7,6},{8,9},{9,8},{10,11... | collective-permute-start | bytes 1572872 | tf_op jit(solution)/shard_map/ppermute | solution.py:259
  49.1 7.4 %collective-permute-start.11 = (bf16[128,2048]{1,0:T(8,128)(2,1)S(1)}, bf16[128,2048]{1,0:T(8,128)(2,1)}, u32[]{:S(2)}, u32[]{:S(2)}) collective-permute-start(bf16[128,2048]{1,0:T(8,128)(2,1)S(1)} %collective-permute-done.10.refs_14_), channel_id=1, source_target_pairs={{0,1},{1,0},{2,3},{3,2},{4,5},{5,4},{6,7},{7,6},{8,9},{9,8},{10,11... | collective-permute-start | bytes 1572872 | tf_op jit(solution)/shard_map/ppermute | solution.py:259
  161.3 3.1 %collective-permute-start.12 = (bf16[4,144,512]{2,1,0:T(8,128)(2,1)}, bf16[4,144,512]{2,1,0:T(8,128)(2,1)}, u32[]{:S(2)}, u32[]{:S(2)}) collective-permute-start(bf16[4,144,512]{2,1,0:T(8,128)(2,1)} %get-tuple-element.51), channel_id=1, source_target_pairs={{0,1},{1,0},{2,3},{3,2},{4,5},{5,4},{6,7},{7,6},{8,9},{9,8},{10,11... | collective-permute-start | bytes 1769480 | tf_op jit(solution)/shard_map/ppermute | solution.py:259
  166.7 8.4 %collective-permute-start.13 = (bf16[2,144,512]{2,1,0:T(8,128)(2,1)}, bf16[2,144,512]{2,1,0:T(8,128)(2,1)S(1)}, u32[]{:S(2)}, u32[]{:S(2)}) collective-permute-start(bf16[2,144,512]{2,1,0:T(8,128)(2,1)} %get-tuple-element.52), channel_id=1, source_target_pairs={{0,2},{1,3},{2,0},{3,1},{4,6},{5,7},{6,4},{7,5},{8,10},{9,11},{10,... | collective-permute-start | bytes 884744 | tf_op jit(solution)/shard_map/ppermute | solution.py:259
  167.9 13.7 %collective-permute-start.14 = (bf16[2,144,512]{2,1,0:T(8,128)(2,1)}, bf16[2,144,512]{2,1,0:T(8,128)(2,1)}, u32[]{:S(2)}, u32[]{:S(2)}) collective-permute-start(bf16[2,144,512]{2,1,0:T(8,128)(2,1)} %get-tuple-element.53), channel_id=1, source_target_pairs={{0,2},{1,3},{2,0},{3,1},{4,6},{5,7},{6,4},{7,5},{8,10},{9,11},{10,... | collective-permute-start | bytes 884744 | tf_op jit(solution)/shard_map/ppermute | solution.py:259
  181.5 3.2 %collective-permute-start.15 = (bf16[4,144,512]{2,1,0:T(8,128)(2,1)}, bf16[4,144,512]{2,1,0:T(8,128)(2,1)}, u32[]{:S(2)}, u32[]{:S(2)}) collective-permute-start(bf16[4,144,512]{2,1,0:T(8,128)(2,1)} %get-tuple-element.59), channel_id=1, source_target_pairs={{0,1},{1,0},{2,3},{3,2},{4,5},{5,4},{6,7},{7,6},{8,9},{9,8},{10,11... | collective-permute-start | bytes 1769480 | tf_op jit(solution)/shard_map/ppermute | solution.py:259
  188.6 5.4 %collective-permute-start.16 = (bf16[256,128]{1,0:T(8,128)(2,1)}, bf16[256,128]{1,0:T(8,128)(2,1)S(1)}, u32[]{:S(2)}, u32[]{:S(2)}) collective-permute-start(bf16[256,128]{1,0:T(8,128)(2,1)} %get-tuple-element.65), channel_id=1, source_target_pairs={{0,1},{1,0},{2,3},{3,2},{4,5},{5,4},{6,7},{7,6},{8,9},{9,8},{10,11... | collective-permute-start | bytes 196616 | tf_op jit(solution)/shard_map/ppermute | solution.py:259
  189.1 7.5 %collective-permute-start.17 = (bf16[256,128]{1,0:T(8,128)(2,1)}, bf16[256,128]{1,0:T(8,128)(2,1)S(1)}, u32[]{:S(2)}, u32[]{:S(2)}) collective-permute-start(bf16[256,128]{1,0:T(8,128)(2,1)} %get-tuple-element.66), channel_id=1, source_target_pairs={{0,2},{1,3},{2,0},{3,1},{4,6},{5,7},{6,4},{7,5},{8,10},{9,11},{10,... | collective-permute-start | bytes 196616 | tf_op jit(solution)/shard_map/ppermute | solution.py:259
  190.3 6.8 %collective-permute-start.18 = (bf16[256,128]{1,0:T(8,128)(2,1)}, bf16[256,128]{1,0:T(8,128)(2,1)S(1)}, u32[]{:S(2)}, u32[]{:S(2)}) collective-permute-start(bf16[256,128]{1,0:T(8,128)(2,1)} %get-tuple-element.67), channel_id=1, source_target_pairs={{0,3},{1,2},{2,1},{3,0},{4,7},{5,6},{6,5},{7,4},{8,11},{9,10},{10,... | collective-permute-start | bytes 196616 | tf_op jit(solution)/shard_map/ppermute | solution.py:259
  190.8 7.0 %collective-permute-start.19 = (bf16[256,128]{1,0:T(8,128)(2,1)}, bf16[256,128]{1,0:T(8,128)(2,1)S(1)}, u32[]{:S(2)}, u32[]{:S(2)}) collective-permute-start(bf16[256,128]{1,0:T(8,128)(2,1)} %get-tuple-element.68), channel_id=1, source_target_pairs={{0,4},{1,5},{2,6},{3,7},{4,0},{5,1},{6,2},{7,3},{8,12},{9,13},{10,... | collective-permute-start | bytes 196616 | tf_op jit(solution)/shard_map/ppermute | solution.py:259
  193.6 6.0 %collective-permute-start.20 = (bf16[256,128]{1,0:T(8,128)(2,1)}, bf16[256,128]{1,0:T(8,128)(2,1)S(1)}, u32[]{:S(2)}, u32[]{:S(2)}) collective-permute-start(bf16[256,128]{1,0:T(8,128)(2,1)} %get-tuple-element.69), channel_id=1, source_target_pairs={{0,5},{1,4},{2,7},{3,6},{4,1},{5,0},{6,3},{7,2},{8,13},{9,12},{10,... | collective-permute-start | bytes 196616 | tf_op jit(solution)/shard_map/ppermute | solution.py:259
  194.1 7.1 %collective-permute-start.21 = (bf16[256,128]{1,0:T(8,128)(2,1)}, bf16[256,128]{1,0:T(8,128)(2,1)S(1)}, u32[]{:S(2)}, u32[]{:S(2)}) collective-permute-start(bf16[256,128]{1,0:T(8,128)(2,1)} %get-tuple-element.70), channel_id=1, source_target_pairs={{0,6},{1,7},{2,4},{3,5},{4,2},{5,3},{6,0},{7,1},{8,14},{9,15},{10,... | collective-permute-start | bytes 196616 | tf_op jit(solution)/shard_map/ppermute | solution.py:259
  196.5 6.0 %collective-permute-start.22 = (bf16[256,128]{1,0:T(8,128)(2,1)}, bf16[256,128]{1,0:T(8,128)(2,1)S(1)}, u32[]{:S(2)}, u32[]{:S(2)}) collective-permute-start(bf16[256,128]{1,0:T(8,128)(2,1)} %get-tuple-element.71), channel_id=1, source_target_pairs={{0,7},{1,6},{2,5},{3,4},{4,3},{5,2},{6,1},{7,0},{8,15},{9,14},{10,... | collective-permute-start | bytes 196616 | tf_op jit(solution)/shard_map/ppermute | solution.py:259
  (6 other events, 44.4 us)
Sparse Core Ops, SparseCore 0:
  10.6 143.9 all-gather.1

commit v7 on v6

--- a/solution.py
+++ b/solution.py
@@ -19,6 +19,9 @@
 NEG = -1e30
 F32 = jnp.float32
 BF16 = jnp.bfloat16
+NX = 4
+NZ = 8
+RING_ROWS = 32
 VMEM_BYTES = 56 << 20
 
 
@@ -94,18 +97,27 @@
     return ref[i, :HD, :].astype(F32), tail[0:1], tail[1:2] + tail[2:3]
 
 
-def far_kernel(picks_ref, *refs):
-    q_refs, whole_ref, out_refs, refs = refs[:2], refs[2], refs[3:5], refs[5:]
-    buffer, score_refs, weight_refs, sem = refs[0], refs[1:3], refs[3:5], refs[5]
-    for pick in range(2 * QB * SEL):
-        pltpu.make_async_copy(whole_ref.at[picks_ref[pick]], buffer.at[pick], sem).start()
-    pltpu.make_async_copy(buffer, buffer, sem).wait()
+def far_kernel(picks_ref, *refs, half):
+    q_refs, whole_ref, early_ref, refs = refs[:2], refs[2], refs[3], refs[4:]
+    out_refs, (buffer, early), refs = refs[:2], refs[2:4], refs[4:]
+    score_refs, weight_refs, sems = refs[:2], refs[2:4], refs[4]
+    picks = 2 * QB * SEL
+    early_copy = pltpu.make_async_copy(
+        early_ref.at[pl.ds(half * picks, picks)], early, sems.at[0]
+    )
+    early_copy.start()
+    for pick in range(picks):
+        pltpu.make_async_copy(whole_ref.at[picks_ref[pick]], buffer.at[pick], sems.at[1]).start()
+    early_copy.wait()
+    pltpu.make_async_copy(buffer, buffer, sems.at[1]).wait()
     step_columns = BLK // 2
     steps = [(row, first) for row in range(2 * QB) for first in range(0, BLK, step_columns)]
     sums = {}
 
     def joined(row, which):
-        return jnp.concatenate([buffer[row * SEL + j, which] for j in range(SEL)], axis=0)
+        return jnp.concatenate(
+            [held[row * SEL + j, which] for held in (buffer, early) for j in range(SEL)], axis=0
+        )
 
     def score(number):
         row, first = steps[number]
@@ -143,20 +155,22 @@
             soften(number - 1)
 
 
-def far(picks, queries, whole):
+def far(picks, queries, whole, early, half):
     pay = HD + TAIL
     vmem = pl.BlockSpec(memory_space=pltpu.VMEM)
     return pl.pallas_call(
-        far_kernel,
+        functools.partial(far_kernel, half=half),
         in_specs=[pl.BlockSpec(memory_space=pltpu.SMEM)]
         + [vmem] * 2
-        + [pl.BlockSpec(memory_space=pl.ANY)],
+        + [pl.BlockSpec(memory_space=pl.ANY)] * 2,
         out_specs=[vmem] * 2,
         out_shape=[jax.ShapeDtypeStruct((QB, pay, BLK), BF16)] * 2,
-        scratch_shapes=[pltpu.VMEM((2 * QB * SEL,) + whole.shape[1:], BF16)]
+        scratch_shapes=[
+            pltpu.VMEM((2 * QB * SEL,) + array.shape[1:], BF16) for array in (whole, early)
+        ]
         + [pltpu.VMEM((BLK, BLK // 2), F32)] * 2
         + [pltpu.VMEM((BLK, BLK // 2), BF16)] * 2
-        + [pltpu.SemaphoreType.DMA],
+        + [pltpu.SemaphoreType.DMA((2,))],
         compiler_params=pltpu.CompilerParams(vmem_limit_bytes=VMEM_BYTES),
         cost_estimate=pl.CostEstimate(
             flops=8 * 2 * QB * 4 * BLK * BLK * HD,
@@ -164,7 +178,37 @@
             transcendentals=2 * QB * BLK * BLK,
         ),
         name="far",
-    )(picks, *queries, whole)
+    )(picks, *queries, whole, early)
+
+
+def collect_kernel(where_ref, *refs):
+    sources, out_ref, sem = refs[:-2], refs[-2], refs[-1]
+
+    def fetch(pick, carry):
+        array, index = where_ref[pick, 0], where_ref[pick, 1]
+        for number, source in enumerate(sources):
+
+            def start(source=source):
+                pltpu.make_async_copy(source.at[index], out_ref.at[pick], sem).start()
+
+            pl.when(array == number)(start)
+        return carry
+
+    lax.fori_loop(0, out_ref.shape[0], fetch, 0)
+    pltpu.make_async_copy(out_ref, out_ref, sem).wait()
+
+
+def collect(where, arrays):
+    return pl.pallas_call(
+        collect_kernel,
+        in_specs=[pl.BlockSpec(memory_space=pltpu.SMEM)]
+        + [pl.BlockSpec(memory_space=pl.ANY)] * len(arrays),
+        out_specs=pl.BlockSpec(memory_space=pltpu.VMEM),
+        out_shape=jax.ShapeDtypeStruct((where.shape[0],) + arrays[0].shape[1:], BF16),
+        scratch_shapes=[pltpu.SemaphoreType.DMA],
+        compiler_params=pltpu.CompilerParams(vmem_limit_bytes=VMEM_BYTES),
+        name="collect",
+    )(where, *arrays)
 
 
 def merge_two_kernel(a_ref, b_ref, *out_refs):
@@ -255,6 +299,14 @@
     )(*parts, *weights)
 
 
+def shift(array, dz, dx):
+    pairs = []
+    for z in range(NZ):
+        for x in range(NX):
+            pairs.append((z * NX + x, (z + dz) % NZ * NX + (x + dx) % NX))
+    return lax.ppermute(array, "ctx", pairs)
+
+
 def swap(array, bits):
     return lax.ppermute(array, "head", [(h, h ^ bits) for h in range(lax.axis_size("head"))])
 
@@ -270,42 +322,78 @@
     kv = head // GROUP
     share = BLK // GROUP
 
-    pieces = []
-    for cache in (cache_keys, cache_values):
-        view = cache.reshape(BLOCKS, BLK, cache.shape[1])
-        pieces.append(lax.dynamic_slice(view, (0, part * share, kv * HD), (BLOCKS, share, HD)))
-    whole = lax.all_gather(jnp.stack(pieces, axis=1), "ctx", axis=0, tiled=True)
-
-    queries_chip = swap(queries, 2)
-    picks_chip = swap(block_picks, 2)
+    def cut(first, rows):
+        pieces = []
+        for cache in (cache_keys, cache_values):
+            view = cache.reshape(BLOCKS, BLK, cache.shape[1])
+            pieces.append(
+                lax.dynamic_slice(view, (0, part * share + first, kv * HD), (BLOCKS, rows, HD))
+            )
+        return jnp.stack(pieces, axis=1)
+
+    whole = lax.all_gather(cut(0, share - RING_ROWS), "ctx", axis=0, tiled=True)
+
+    ring = cut(share - RING_ROWS, RING_ROWS)
+    z1, z2 = shift(ring, 1, 0), shift(ring, -1, 0)
+    z3, z4 = shift(z1, 1, 0), shift(z2, -1, 0)
+    low = jnp.concatenate([ring, z1, z2, z3], axis=0)
+    x1_low, x2_low = shift(low, 0, 1), shift(low, 0, -1)
+    z5, z6 = shift(z3, 1, 0), shift(z4, -1, 0)
+    half = BLOCKS // 2
+    z7, z8 = shift(z5[:half], 1, 0), shift(z6[half:], -1, 0)
+    high = jnp.concatenate([z4, z5, z6, z7, z8], axis=0)
+    x1_high, x2_high = shift(high, 0, 1), shift(high, 0, -1)
+    x3_low, x3_high = shift(x1_low, 0, 1), shift(x2_high, 0, -1)
+    ring_arrays = [low, high, x1_low, x1_high, x2_low, x2_high, x3_low, x3_high]
+
+    queries_early, picks_early, weight_early = after(
+        (queries, block_picks, out_weight), *ring_arrays[:6]
+    )
+    queries_pair = [queries, swap(queries_early, 2)]
+    picks_pair = jnp.stack([block_picks, swap(picks_early, 2)])
     weights = [out_weight] + [None] * (heads - 1)
     for bits in range(2, heads, 2):
-        weights[bits] = swap(out_weight, bits)
-    near_state = near(queries, span_keys, span_values, kv[None])
-    queries_pair = [queries, queries_chip]
-    picks_pair = jnp.stack([block_picks, picks_chip])
-    group_queries = [queries, swap(queries_pair[0], 1), queries_chip, swap(queries_pair[1], 1)]
+        weights[bits] = swap(weight_early, bits)
+    near_state = near(queries_early, span_keys, span_values, kv[None])
+    queries_pair, picks_pair, weights[::2] = after(
+        (queries_pair, picks_pair, weights[::2]), *ring_arrays
+    )
+    group_queries = [queries, swap(queries_pair[0], 1), queries_pair[1], swap(queries_pair[1], 1)]
     picks_core = swap(picks_pair, 1)
     group_picks = [picks_pair[0], picks_core[0], picks_pair[1], picks_core[1]]
     for bits in range(0, heads, 2):
         weights[bits + 1] = swap(weights[bits], 1)
     picks = [group_pick.reshape(QB * SEL) for group_pick in group_picks]
 
-    picks, group_queries, weights, near_state = lax.optimization_barrier(
-        (picks, group_queries, weights, near_state)
-    )
-
-    def far_of(first, second, earlier):
+    every_pick = jnp.concatenate(picks[::-1])
+    owner, local = every_pick // BLOCKS, every_pick % BLOCKS
+    ctx = lax.axis_index("ctx")
+    dz = (owner // NX - ctx // NX) % NZ
+    dx = (owner % NX - ctx % NX) % NX
+    order_x = jnp.where(dx == 0, 0, jnp.where(dx == 3, 1, jnp.where(dx == 1, 2, 3)))
+    order_z = jnp.where(dz == 0, 0, jnp.where(dz > NZ // 2, 2 * (NZ - dz) - 1, 2 * dz))
+    place = jnp.where(dz == NZ // 2, NZ - 1, order_z) * BLOCKS + local
+    upper = (place >= low.shape[0]).astype(jnp.int32)
+    where = jnp.stack([2 * order_x + upper, place - low.shape[0] * upper], axis=-1)
+    early = collect(where.astype(jnp.int32), ring_arrays)
+
+    picks, group_queries, weights, near_state, early = lax.optimization_barrier(
+        (picks, group_queries, weights, near_state, early)
+    )
+
+    def far_of(first, second, earlier, half):
         return far(
             after(jnp.concatenate([picks[first], picks[second]]), *earlier),
             [group_queries[first], group_queries[second]],
             whole,
+            early,
+            half,
         )
 
-    far_corner, far_chip = far_of(3, 2, [])
+    far_corner, far_chip = far_of(3, 2, [], 0)
     for_chip = merge_two(far_chip, swap(far_corner, 1), 2)
     chip_parts = [swap(piece, 2) for piece in for_chip]
-    far_core, far_own = far_of(1, 0, for_chip)
+    far_core, far_own = far_of(1, 0, for_chip, 1)
     core_part = swap(after(far_core, *chip_parts), 1)
     attention, shares = merge_last(
         head[None], heads, far_own, core_part, near_state, chip_parts

time: 214 us -> 198 us (0.925)
  waiting for transfers between devices: 134 us -> 96.3 us
  starting transfers between devices: 31.5 us -> 48.6 us
  Pallas kernels: 27.7 us -> 31.5 us
    all_gather x1, waiting for transfers between devices: 97.5 us -> 36.4 us  [body(): whole = lax.all_gather(cut(0, share - RING_ROWS), 'ctx', axis=0, tiled=True)]
    ppermute x0 -> x14, waiting for transfers between devices: none -> 31.6 us  [shift(): return lax.ppermute(array, 'ctx', pairs)]
    ppermute x0 -> x14, starting transfers between devices: none -> 21.9 us  [shift(): return lax.ppermute(array, 'ctx', pairs)]
    ppermute x23, waiting for transfers between devices: 36.5 us -> 28.3 us  [swap(): lax.ppermute(array, 'head', [(h, h ^ bits) for h in range(lax.axis_size('...]
    ppermute x23, starting transfers between devices: 31.4 us -> 26.6 us  [swap(): lax.ppermute(array, 'head', [(h, h ^ bits) for h in range(lax.axis_size('...]
    pallas_call x2 -> x3, Pallas kernels: 13.4 us -> 17.2 us  [the longest x2 13.2 us: far(): pl.pallas_call(functools.partial(far_kernel, half=half), in_specs=[pl.Blo...]
  transfers between devices with their start and end apart: 24 -> 38, of which waited for: 14 -> 20; matrix products, arithmetic and copies ran while one was open for 2% -> 2% of each run, Pallas kernels for 5% -> 8%
where the time goes in v7:
time: 198 us; the launch traced here: 197 us
  waiting for transfers between devices  96.3 us (49%)
  starting transfers between devices  48.6 us (25%)
  Pallas kernels  31.5 us (16%)
  between operations  14.4 us (7%)
  local copies, waits for them, and re-layouts  4.31 us (2%)
  other arithmetic  2.17 us (1%)
    all_gather x1, waiting for transfers between devices, body(): whole = lax.all_gather(cut(0, share - RING_ROWS), 'ctx', axis=0, tiled=True)  36.4 us
    ppermute x14, waiting for transfers between devices, shift(): return lax.ppermute(array, 'ctx', pairs)  31.6 us
    ppermute x23, waiting for transfers between devices, swap(): lax.ppermute(array, 'head', [(h, h ^ bits) for h in range(lax.axis_size('...  28.3 us
    ppermute x23, starting transfers between devices, swap(): lax.ppermute(array, 'head', [(h, h ^ bits) for h in range(lax.axis_size('...  26.6 us
    ppermute x14, starting transfers between devices, shift(): return lax.ppermute(array, 'ctx', pairs)  21.9 us
    pallas_call x2, Pallas kernels, far(): pl.pallas_call(functools.partial(far_kernel, half=half), in_specs=[pl.Blo...  13.2 us
    pallas_call x1, Pallas kernels, near(): pl.pallas_call(near_kernel, grid_spec=grid_spec, out_shape=state_shapes()...  4.67 us
    pallas_call x1, Pallas kernels, merge_last(): pl.pallas_call(functools.partial(merge_last_kernel, pieces=len(chip_parts...  3.98 us
  transfers between devices with their start and end apart: 38, of which 20 were waited for; matrix products, arithmetic and copies ran while one was open for 2% of the time, Pallas kernels for 8%

profile of v7, /device:TPU:1, one launch (start us, length us, event | category | flops | bytes accessed | tf_op | source)
XLA Modules:
  0.0 197.2 jit_solution(4620988282636539911)
XLA Ops:
  10.1 6.5 %collective-permute-start.1 = (bf16[8,2,32,128]{3,2,1,0:T(8,128)(2,1)S(1)}, bf16[8,2,32,128]{3,2,1,0:T(8,128)(2,1)S(1)}, u32[]{:S(2)}, u32[]{:S(2)}) collective-permute-start(bf16[8,2,32,128]{3,2,1,0:T(8,128)(2,1)S(1)} %pad_maximum_fusion.2), channel_id=1, source_target_pairs={{0,224},{8,232},{16,240},{24,248},{32,0},{40,8},{48,16},{56,24},{6... | collective-permute-start | bytes 393224 | tf_op jit(solution)/shard_map/ppermute | solution.py:307
  18.7 3.4 %collective-permute-start.3 = (bf16[8,2,32,128]{3,2,1,0:T(8,128)(2,1)S(1)}, bf16[8,2,32,128]{3,2,1,0:T(8,128)(2,1)S(1)}, u32[]{:S(2)}, u32[]{:S(2)}) collective-permute-start(bf16[8,2,32,128]{3,2,1,0:T(8,128)(2,1)S(1)} %collective-permute-done.1), channel_id=1, source_target_pairs={{0,224},{8,232},{16,240},{24,248},{32,0},{40,8},{48,16},{56,24},{6... | collective-permute-start | bytes 393224 | tf_op jit(solution)/shard_map/ppermute | solution.py:307
  24.1 3.1 %collective-permute-start.5 = (bf16[8,2,32,128]{3,2,1,0:T(8,128)(2,1)S(1)}, bf16[8,2,32,128]{3,2,1,0:T(8,128)(2,1)S(1)}, u32[]{:S(2)}, u32[]{:S(2)}) collective-permute-start(bf16[8,2,32,128]{3,2,1,0:T(8,128)(2,1)S(1)} %collective-permute-done.3), channel_id=1, source_target_pairs={{0,224},{8,232},{16,240},{24,248},{32,0},{40,8},{48,16},{56,24},{6... | collective-permute-start | bytes 393224 | tf_op jit(solution)/shard_map/ppermute | solution.py:307
  27.2 2.6 %collective-permute-start.10 = (bf16[32,2,32,128]{3,2,1,0:T(8,128)(2,1)S(1)}, bf16[32,2,32,128]{3,2,1,0:T(8,128)(2,1)S(1)}, u32[]{:S(2)}, u32[]{:S(2)}) collective-permute-start(bf16[32,2,32,128]{3,2,1,0:T(8,128)(2,1)S(1)} %pad_maximum_fusion.refs_0_), channel_id=1, source_target_pairs={{0,24},{8,0},{16,8},{24,16},{32,56},{40,32},{48,40},{56,48},{64,88... | collective-permute-start | bytes 1572872 | tf_op jit(solution)/shard_map/ppermute | solution.py:307
  30.8 3.5 %collective-permute-start.7 = (bf16[4,2,32,128]{3,2,1,0:T(8,128)(2,1)S(1)}, bf16[4,2,32,128]{3,2,1,0:T(8,128)(2,1)S(1)}, u32[]{:S(2)}, u32[]{:S(2)}) collective-permute-start(bf16[4,2,32,128]{3,2,1,0:T(8,128)(2,1)S(1)} %slice.25), channel_id=1, source_target_pairs={{0,224},{8,232},{16,240},{24,248},{32,0},{40,8},{48,16},{56,24},{6... | collective-permute-start | bytes 196616 | tf_op jit(solution)/shard_map/ppermute | solution.py:307
  34.5 5.1 %collective-permute-done.6 = bf16[4,2,32,128]{3,2,1,0:T(8,128)(2,1)S(1)} collective-permute-done((bf16[4,2,32,128]{3,2,1,0:T(8,128)(2,1)S(1)}, bf16[4,2,32,128]{3,2,1,0:T(8,128)(2,1)S(1)}, u32[]{:S(2)}, u32[]{:S(2)}) %collective-permute-start.6) | collective-permute-done | bytes 65568 | tf_op jit(solution)/shard_map/ppermute | solution.py:307
  39.7 2.3 %collective-permute-start.11 = (bf16[32,2,32,128]{3,2,1,0:T(8,128)(2,1)S(1)}, bf16[32,2,32,128]{3,2,1,0:T(8,128)(2,1)S(1)}, u32[]{:S(2)}, u32[]{:S(2)}) collective-permute-start(bf16[32,2,32,128]{3,2,1,0:T(8,128)(2,1)S(1)} %constant_dynamic-update-slice_fusion.refs_1_), channel_id=1, source_target_pairs={{0,24},{8,0},{16,8},{24,16},{32,56},{40,32},{48,40},{56,48},{64,88... | collective-permute-start | bytes 1572872 | tf_op jit(solution)/shard_map/ppermute | solution.py:307
  42.0 2.5 %collective-permute-done.8.refs_2_ = bf16[32,2,32,128]{3,2,1,0:T(8,128)(2,1)S(1)} collective-permute-done((bf16[32,2,32,128]{3,2,1,0:T(8,128)(2,1)S(1)}, bf16[32,2,32,128]{3,2,1,0:T(8,128)(2,1)S(1)}, u32[]{:S(2)}, u32[]{:S(2)}) %collective-permute-start.8) | collective-permute-done | bytes 524320 | tf_op jit(solution)/shard_map/ppermute | solution.py:307
  46.0 11.5 %collective-permute-done.11.refs_5_ = bf16[32,2,32,128]{3,2,1,0:T(8,128)(2,1)S(1)} collective-permute-done((bf16[32,2,32,128]{3,2,1,0:T(8,128)(2,1)S(1)}, bf16[32,2,32,128]{3,2,1,0:T(8,128)(2,1)S(1)}, u32[]{:S(2)}, u32[]{:S(2)}) %collective-permute-start.11) | collective-permute-done | bytes 524320 | tf_op jit(solution)/shard_map/ppermute | solution.py:307
  59.7 2.6 %collective-permute-start.16 = (bf16[128,2048]{1,0:T(8,128)(2,1)S(1)}, bf16[128,2048]{1,0:T(8,128)(2,1)S(1)}, u32[]{:S(2)}, u32[]{:S(2)}) collective-permute-start(bf16[128,2048]{1,0:T(8,128)(2,1)S(1)} %copy-done), channel_id=1, source_target_pairs={{0,6},{1,7},{2,4},{3,5},{4,2},{5,3},{6,0},{7,1},{8,14},{9,15},{10,... | collective-permute-start | bytes 1572872 | tf_op jit(solution)/shard_map/ppermute | solution.py:311
  63.4 5.6 %collective-permute-done.17.refs_6_ = bf16[32,2,32,128]{3,2,1,0:T(8,128)(2,1)} collective-permute-done((bf16[32,2,32,128]{3,2,1,0:T(8,128)(2,1)S(1)}, bf16[32,2,32,128]{3,2,1,0:T(8,128)(2,1)}, u32[]{:S(2)}, u32[]{:S(2)}) %collective-permute-start.17) | collective-permute-done | bytes 524320 | tf_op jit(solution)/shard_map/ppermute | solution.py:307
  70.3 4.7 %near.1 = (f32[4,128,512]{2,1,0:T(8,128)}, f32[4,1,512]{2,1,0:T(1,128)}, f32[4,1,512]{2,1,0:T(1,128)}) custom-call(s32[1]{0:T(128)} %bitcast.7.kv_ref, bf16[2048,128]{1,0:T(8,128)(2,1)} %refs_1_, bf16[2048,256]{1,0:T(8,128)(2,1)} %k_ref.1, bf16[2048,256]{1,0:T(8,128)(2,1)} %v_ref.1), custom_call_target="tpu_custom_call" | custom-call | flops 536870912 | bytes 4194304 | tf_op jit(solution)/shard_map/near/pallas_call | solution.py:75
  75.0 6.5 %collective-permute-done.15.refs_12_ = bf16[128,2048]{1,0:T(8,128)(2,1)S(1)} collective-permute-done((bf16[128,2048]{1,0:T(8,128)(2,1)S(1)}, bf16[128,2048]{1,0:T(8,128)(2,1)S(1)}, u32[]{:S(2)}, u32[]{:S(2)}) %collective-permute-start.15) | collective-permute-done | bytes 524320 | tf_op jit(solution)/shard_map/ppermute | solution.py:311
  81.5 7.9 %collective-permute-done.14.refs_10_ = bf16[128,2048]{1,0:T(8,128)(2,1)S(1)} collective-permute-done((bf16[128,2048]{1,0:T(8,128)(2,1)S(1)}, bf16[128,2048]{1,0:T(8,128)(2,1)S(1)}, u32[]{:S(2)}, u32[]{:S(2)}) %collective-permute-start.14) | collective-permute-done | bytes 524320 | tf_op jit(solution)/shard_map/ppermute | solution.py:311
  89.4 6.6 %collective-permute-start.20 = (bf16[2048,128]{1,0:T(8,128)(2,1)}, bf16[2048,128]{1,0:T(8,128)(2,1)}, u32[]{:S(2)}, u32[]{:S(2)}) collective-permute-start(bf16[2048,128]{1,0:T(8,128)(2,1)} %refs_1_), channel_id=1, source_target_pairs={{0,1},{1,0},{2,3},{3,2},{4,5},{5,4},{6,7},{7,6},{8,9},{9,8},{10,11... | collective-permute-start | bytes 1572872 | tf_op jit(solution)/shard_map/ppermute | solution.py:311
  99.3 4.0 %collect.1.refs_3_ = bf16[64,2,32,128]{3,2,1,0:T(8,128)(2,1)} custom-call(s32[64,2]{1,0:T(8,128)} %copy.13.where_ref, bf16[32,2,32,128]{3,2,1,0:T(8,128)(2,1)} %copy-done.2, bf16[32,2,32,128]{3,2,1,0:T(8,128)(2,1)} %copy-done.3, bf16[32,2,32,128]{3,2,1,0:T(8,128)(2,1)} %copy-done.5, bf16[32,2,32,128]{3,2,1,0:T(8,128)(2,1)} %copy-done.7, ...), custom_call_target="tpu_custom_call" | custom-call | tf_op jit(solution)/shard_map/collect/pallas_call | solution.py:202
  103.9 36.4 %all-gather.2.cloned.1.call-done.refs_2_ = bf16[256,2,96,128]{3,2,1,0:T(8,128)(2,1)} async-done(((bf16[8,2,96,128]{3,2,1,0:T(8,128)(2,1)}), bf16[256,2,96,128]{3,2,1,0:T(8,128)(2,1)}) %all-gather.2.cloned.1.call-update) | async-done | bytes 12582928 | tf_op jit(solution)/shard_map/all_gather | solution.py:334
  140.3 6.6 %far.2 = (bf16[4,144,512]{2,1,0:T(8,128)(2,1)}, bf16[4,144,512]{2,1,0:T(8,128)(2,1)}) custom-call(s32[32]{0:T(128)} %pad_add_fusion.4.picks_ref, bf16[2048,128]{1,0:T(8,128)(2,1)} %collective-permute-done.21.refs_0_, bf16[2048,128]{1,0:T(8,128)(2,1)} %collective-permute-done.12.refs_1_, bf16[256,2,96,128]{3,2,1,0:T(8,128)(2,1)} %all-gather.2.cloned.1.call-done.refs_2_, ...), custom_call_target="tpu_custom_call" | custom-call | flops 8589934592 | bytes 5242880 | tf_op jit(solution)/shard_map/far/pallas_call | solution.py:161
  153.5 6.6 %far.3 = (bf16[4,144,512]{2,1,0:T(8,128)(2,1)}, bf16[4,144,512]{2,1,0:T(8,128)(2,1)}) custom-call(s32[32]{0:T(128)} %pad_add_fusion.3.picks_ref, bf16[2048,128]{1,0:T(8,128)(2,1)} %collective-permute-done.20.refs_0_, bf16[2048,128]{1,0:T(8,128)(2,1)} %refs_1_, bf16[256,2,96,128]{3,2,1,0:T(8,128)(2,1)} %all-gather.2.cloned.1.call-done.refs_2_, ...), custom_call_target="tpu_custom_call" | custom-call | flops 8589934592 | bytes 5242880 | tf_op jit(solution)/shard_map/far/pallas_call | solution.py:161
  160.4 6.4 %collective-permute-done.28.refs_1_ = bf16[2,144,512]{2,1,0:T(8,128)(2,1)} collective-permute-done((bf16[2,144,512]{2,1,0:T(8,128)(2,1)}, bf16[2,144,512]{2,1,0:T(8,128)(2,1)}, u32[]{:S(2)}, u32[]{:S(2)}) %collective-permute-start.28) | collective-permute-done | bytes 294944 | tf_op jit(solution)/shard_map/ppermute | solution.py:311
  170.0 4.0 %merge_last.1 = (bf16[2048,128]{1,0:T(8,128)(2,1)}, bf16[256,128]{1,0:T(8,128)(2,1)}, bf16[256,128]{1,0:T(8,128)(2,1)}, bf16[256,128]{1,0:T(8,128)(2,1)}, bf16[2...) custom-call(s32[1]{0:T(128)} %bitcast.head_ref, ...), custom_call_target="tpu_custom_call" | custom-call | tf_op jit(solution)/shard_map/merge_last/pallas_call | solution.py:267
  176.7 2.7 %collective-permute-start.34 = (bf16[256,128]{1,0:T(8,128)(2,1)}, bf16[256,128]{1,0:T(8,128)(2,1)S(1)}, u32[]{:S(2)}, u32[]{:S(2)}) collective-permute-start(bf16[256,128]{1,0:T(8,128)(2,1)} %get-tuple-element.91), channel_id=1, source_target_pairs={{0,5},{1,4},{2,7},{3,6},{4,1},{5,0},{6,3},{7,2},{8,13},{9,12},{10,... | collective-permute-start | bytes 196616 | tf_op jit(solution)/shard_map/ppermute | solution.py:311
  179.8 2.6 %collective-permute-start.36 = (bf16[256,128]{1,0:T(8,128)(2,1)}, bf16[256,128]{1,0:T(8,128)(2,1)S(1)}, u32[]{:S(2)}, u32[]{:S(2)}) collective-permute-start(bf16[256,128]{1,0:T(8,128)(2,1)} %get-tuple-element.93), channel_id=1, source_target_pairs={{0,7},{1,6},{2,5},{3,4},{4,3},{5,2},{6,1},{7,0},{8,15},{9,14},{10,... | collective-permute-start | bytes 196616 | tf_op jit(solution)/shard_map/ppermute | solution.py:311
  186.9 3.4 %project.1 = bf16[256,2048]{1,0:T(8,128)(2,1)} custom-call(bf16[256,128]{1,0:T(8,128)(2,1)S(1)} %copy-done.1, bf16[256,128]{1,0:T(8,128)(2,1)S(1)} %collective-permute-done.30.refs_1_, bf16[256,128]{1,0:T(8,128)(2,1)S(1)} %collective-permute-done.31.refs_2_, bf16[256,128]{1,0:T(8,128)(2,1)S(1)} %collective-permute-done.32.refs_3_, ...), custom_call_target="tpu_custom_call" | custom-call | tf_op jit(solution)/shard_map/project/pallas_call | solution.py:292
  (112 shorter events, 35.8 us)
Async XLA Ops:
  7.2 133.1 %all-gather.2.cloned.1.call-start = ((), (), s32[]{:S(2)}) async-start(), calls=%async_computation | async-start | bytes 12976128 | tf_op jit(solution)/shard_map/all_gather | solution.py:334
  10.1 8.6 %collective-permute-start.1 = (bf16[8,2,32,128]{3,2,1,0:T(8,128)(2,1)S(1)}, bf16[8,2,32,128]{3,2,1,0:T(8,128)(2,1)S(1)}, u32[]{:S(2)}, u32[]{:S(2)}) collective-permute-start(bf16[8,2,32,128]{3,2,1,0:T(8,128)(2,1)S(1)} %pad_maximum_fusion.2), channel_id=1, source_target_pairs={{0,224},{8,232},{16,240},{24,248},{32,0},{40,8},{48,16},{56,24},{6... | collective-permute-start | bytes 393224 | tf_op jit(solution)/shard_map/ppermute | solution.py:307
  24.1 6.8 %collective-permute-start.5 = (bf16[8,2,32,128]{3,2,1,0:T(8,128)(2,1)S(1)}, bf16[8,2,32,128]{3,2,1,0:T(8,128)(2,1)S(1)}, u32[]{:S(2)}, u32[]{:S(2)}) collective-permute-start(bf16[8,2,32,128]{3,2,1,0:T(8,128)(2,1)S(1)} %collective-permute-done.3), channel_id=1, source_target_pairs={{0,224},{8,232},{16,240},{24,248},{32,0},{40,8},{48,16},{56,24},{6... | collective-permute-start | bytes 393224 | tf_op jit(solution)/shard_map/ppermute | solution.py:307
  27.2 7.2 %collective-permute-start.4 = (bf16[8,2,32,128]{3,2,1,0:T(8,128)(2,1)S(1)}, bf16[8,2,32,128]{3,2,1,0:T(8,128)(2,1)S(1)}, u32[]{:S(2)}, u32[]{:S(2)}) collective-permute-start(bf16[8,2,32,128]{3,2,1,0:T(8,128)(2,1)S(1)} %collective-permute-done.2), channel_id=1, source_target_pairs={{0,32},{8,40},{16,48},{24,56},{32,64},{40,72},{48,80},{56,88},{64,... | collective-permute-start | bytes 393224 | tf_op jit(solution)/shard_map/ppermute | solution.py:307
  27.2 18.8 %collective-permute-start.10 = (bf16[32,2,32,128]{3,2,1,0:T(8,128)(2,1)S(1)}, bf16[32,2,32,128]{3,2,1,0:T(8,128)(2,1)S(1)}, u32[]{:S(2)}, u32[]{:S(2)}) collective-permute-start(bf16[32,2,32,128]{3,2,1,0:T(8,128)(2,1)S(1)} %pad_maximum_fusion.refs_0_), channel_id=1, source_target_pairs={{0,24},{8,0},{16,8},{24,16},{32,56},{40,32},{48,40},{56,48},{64,88... | collective-permute-start | bytes 1572872 | tf_op jit(solution)/shard_map/ppermute | solution.py:307
  29.8 14.7 %collective-permute-start.8 = (bf16[32,2,32,128]{3,2,1,0:T(8,128)(2,1)S(1)}, bf16[32,2,32,128]{3,2,1,0:T(8,128)(2,1)S(1)}, u32[]{:S(2)}, u32[]{:S(2)}) collective-permute-start(bf16[32,2,32,128]{3,2,1,0:T(8,128)(2,1)S(1)} %pad_maximum_fusion.refs_0_), channel_id=1, source_target_pairs={{0,8},{8,16},{16,24},{24,0},{32,40},{40,48},{48,56},{56,32},{64,72... | collective-permute-start | bytes 1572872 | tf_op jit(solution)/shard_map/ppermute | solution.py:307
  30.8 8.8 %collective-permute-start.7 = (bf16[4,2,32,128]{3,2,1,0:T(8,128)(2,1)S(1)}, bf16[4,2,32,128]{3,2,1,0:T(8,128)(2,1)S(1)}, u32[]{:S(2)}, u32[]{:S(2)}) collective-permute-start(bf16[4,2,32,128]{3,2,1,0:T(8,128)(2,1)S(1)} %slice.25), channel_id=1, source_target_pairs={{0,224},{8,232},{16,240},{24,248},{32,0},{40,8},{48,16},{56,24},{6... | collective-permute-start | bytes 196616 | tf_op jit(solution)/shard_map/ppermute | solution.py:307
  39.7 17.8 %collective-permute-start.11 = (bf16[32,2,32,128]{3,2,1,0:T(8,128)(2,1)S(1)}, bf16[32,2,32,128]{3,2,1,0:T(8,128)(2,1)S(1)}, u32[]{:S(2)}, u32[]{:S(2)}) collective-permute-start(bf16[32,2,32,128]{3,2,1,0:T(8,128)(2,1)S(1)} %constant_dynamic-update-slice_fusion.refs_1_), channel_id=1, source_target_pairs={{0,24},{8,0},{16,8},{24,16},{32,56},{40,32},{48,40},{56,48},{64,88... | collective-permute-start | bytes 1572872 | tf_op jit(solution)/shard_map/ppermute | solution.py:307
  42.0 15.7 %collective-permute-start.9 = (bf16[32,2,32,128]{3,2,1,0:T(8,128)(2,1)S(1)}, bf16[32,2,32,128]{3,2,1,0:T(8,128)(2,1)S(1)}, u32[]{:S(2)}, u32[]{:S(2)}) collective-permute-start(bf16[32,2,32,128]{3,2,1,0:T(8,128)(2,1)S(1)} %constant_dynamic-update-slice_fusion.refs_1_), channel_id=1, source_target_pairs={{0,8},{8,16},{16,24},{24,0},{32,40},{40,48},{48,56},{56,32},{64,72... | collective-permute-start | bytes 1572872 | tf_op jit(solution)/shard_map/ppermute | solution.py:307
  44.5 24.5 %collective-permute-start.17 = (bf16[32,2,32,128]{3,2,1,0:T(8,128)(2,1)S(1)}, bf16[32,2,32,128]{3,2,1,0:T(8,128)(2,1)}, u32[]{:S(2)}, u32[]{:S(2)}) collective-permute-start(bf16[32,2,32,128]{3,2,1,0:T(8,128)(2,1)S(1)} %collective-permute-done.8.refs_2_), channel_id=1, source_target_pairs={{0,8},{8,16},{16,24},{24,0},{32,40},{40,48},{48,56},{56,32},{64,72... | collective-permute-start | bytes 1572872 | tf_op jit(solution)/shard_map/ppermute | solution.py:307
  58.9 16.0 %collective-permute-start.12 = (bf16[2048,128]{1,0:T(8,128)(2,1)}, bf16[2048,128]{1,0:T(8,128)(2,1)}, u32[]{:S(2)}, u32[]{:S(2)}) collective-permute-start(bf16[2048,128]{1,0:T(8,128)(2,1)} %refs_1_), channel_id=1, source_target_pairs={{0,2},{1,3},{2,0},{3,1},{4,6},{5,7},{6,4},{7,5},{8,10},{9,11},{10,... | collective-permute-start | bytes 1572872 | tf_op jit(solution)/shard_map/ppermute | solution.py:311
  59.7 15.3 %collective-permute-start.16 = (bf16[128,2048]{1,0:T(8,128)(2,1)S(1)}, bf16[128,2048]{1,0:T(8,128)(2,1)S(1)}, u32[]{:S(2)}, u32[]{:S(2)}) collective-permute-start(bf16[128,2048]{1,0:T(8,128)(2,1)S(1)} %copy-done), channel_id=1, source_target_pairs={{0,6},{1,7},{2,4},{3,5},{4,2},{5,3},{6,0},{7,1},{8,14},{9,15},{10,... | collective-permute-start | bytes 1572872 | tf_op jit(solution)/shard_map/ppermute | solution.py:311
  62.3 12.7 %collective-permute-start.18 = (bf16[32,2,32,128]{3,2,1,0:T(8,128)(2,1)S(1)}, bf16[32,2,32,128]{3,2,1,0:T(8,128)(2,1)S(1)}, u32[]{:S(2)}, u32[]{:S(2)}) collective-permute-start(bf16[32,2,32,128]{3,2,1,0:T(8,128)(2,1)S(1)} %collective-permute-done.11.refs_5_), channel_id=1, source_target_pairs={{0,24},{8,0},{16,8},{24,16},{32,56},{40,32},{48,40},{56,48},{64,88... | collective-permute-start | bytes 1572872 | tf_op jit(solution)/shard_map/ppermute | solution.py:307
  62.8 18.7 %collective-permute-start.15 = (bf16[128,2048]{1,0:T(8,128)(2,1)S(1)}, bf16[128,2048]{1,0:T(8,128)(2,1)S(1)}, u32[]{:S(2)}, u32[]{:S(2)}) collective-permute-start(bf16[128,2048]{1,0:T(8,128)(2,1)S(1)} %copy-done), channel_id=1, source_target_pairs={{0,4},{1,5},{2,6},{3,7},{4,0},{5,1},{6,2},{7,3},{8,12},{9,13},{10,... | collective-permute-start | bytes 1572872 | tf_op jit(solution)/shard_map/ppermute | solution.py:311
  69.1 20.3 %collective-permute-start.14 = (bf16[128,2048]{1,0:T(8,128)(2,1)S(1)}, bf16[128,2048]{1,0:T(8,128)(2,1)S(1)}, u32[]{:S(2)}, u32[]{:S(2)}) collective-permute-start(bf16[128,2048]{1,0:T(8,128)(2,1)S(1)} %copy-done), channel_id=1, source_target_pairs={{0,2},{1,3},{2,0},{3,1},{4,6},{5,7},{6,4},{7,5},{8,10},{9,11},{10,... | collective-permute-start | bytes 1572872 | tf_op jit(solution)/shard_map/ppermute | solution.py:311
  89.4 8.9 %collective-permute-start.20 = (bf16[2048,128]{1,0:T(8,128)(2,1)}, bf16[2048,128]{1,0:T(8,128)(2,1)}, u32[]{:S(2)}, u32[]{:S(2)}) collective-permute-start(bf16[2048,128]{1,0:T(8,128)(2,1)} %refs_1_), channel_id=1, source_target_pairs={{0,1},{1,0},{2,3},{3,2},{4,5},{5,4},{6,7},{7,6},{8,9},{9,8},{10,11... | collective-permute-start | bytes 1572872 | tf_op jit(solution)/shard_map/ppermute | solution.py:311
  96.4 6.9 %collective-permute-start.21 = (bf16[2048,128]{1,0:T(8,128)(2,1)}, bf16[2048,128]{1,0:T(8,128)(2,1)}, u32[]{:S(2)}, u32[]{:S(2)}) collective-permute-start(bf16[2048,128]{1,0:T(8,128)(2,1)} %collective-permute-done.12.refs_1_), channel_id=1, source_target_pairs={{0,1},{1,0},{2,3},{3,2},{4,5},{5,4},{6,7},{7,6},{8,9},{9,8},{10,11... | collective-permute-start | bytes 1572872 | tf_op jit(solution)/shard_map/ppermute | solution.py:311
  96.8 6.4 %collective-permute-start.22 = (bf16[128,2048]{1,0:T(8,128)(2,1)S(1)}, bf16[128,2048]{1,0:T(8,128)(2,1)S(1)}, u32[]{:S(2)}, u32[]{:S(2)}) collective-permute-start(bf16[128,2048]{1,0:T(8,128)(2,1)S(1)} %copy-done), channel_id=1, source_target_pairs={{0,1},{1,0},{2,3},{3,2},{4,5},{5,4},{6,7},{7,6},{8,9},{9,8},{10,11... | collective-permute-start | bytes 1572872 | tf_op jit(solution)/shard_map/ppermute | solution.py:311
  97.0 6.3 %collective-permute-start.23 = (bf16[128,2048]{1,0:T(8,128)(2,1)S(1)}, bf16[128,2048]{1,0:T(8,128)(2,1)S(1)}, u32[]{:S(2)}, u32[]{:S(2)}) collective-permute-start(bf16[128,2048]{1,0:T(8,128)(2,1)S(1)} %collective-permute-done.14.refs_10_), channel_id=1, source_target_pairs={{0,1},{1,0},{2,3},{3,2},{4,5},{5,4},{6,7},{7,6},{8,9},{9,8},{10,11... | collective-permute-start | bytes 1572872 | tf_op jit(solution)/shard_map/ppermute | solution.py:311
  152.0 8.4 %collective-permute-start.27 = (bf16[2,144,512]{2,1,0:T(8,128)(2,1)}, bf16[2,144,512]{2,1,0:T(8,128)(2,1)S(1)}, u32[]{:S(2)}, u32[]{:S(2)}) collective-permute-start(bf16[2,144,512]{2,1,0:T(8,128)(2,1)} %get-tuple-element.74), channel_id=1, source_target_pairs={{0,2},{1,3},{2,0},{3,1},{4,6},{5,7},{6,4},{7,5},{8,10},{9,11},{10,... | collective-permute-start | bytes 884744 | tf_op jit(solution)/shard_map/ppermute | solution.py:311
  152.3 14.5 %collective-permute-start.28 = (bf16[2,144,512]{2,1,0:T(8,128)(2,1)}, bf16[2,144,512]{2,1,0:T(8,128)(2,1)}, u32[]{:S(2)}, u32[]{:S(2)}) collective-permute-start(bf16[2,144,512]{2,1,0:T(8,128)(2,1)} %get-tuple-element.75), channel_id=1, source_target_pairs={{0,2},{1,3},{2,0},{3,1},{4,6},{5,7},{6,4},{7,5},{8,10},{9,11},{10,... | collective-permute-start | bytes 884744 | tf_op jit(solution)/shard_map/ppermute | solution.py:311
  174.8 7.7 %collective-permute-start.32 = (bf16[256,128]{1,0:T(8,128)(2,1)}, bf16[256,128]{1,0:T(8,128)(2,1)S(1)}, u32[]{:S(2)}, u32[]{:S(2)}) collective-permute-start(bf16[256,128]{1,0:T(8,128)(2,1)} %get-tuple-element.89), channel_id=1, source_target_pairs={{0,3},{1,2},{2,1},{3,0},{4,7},{5,6},{6,5},{7,4},{8,11},{9,10},{10,... | collective-permute-start | bytes 196616 | tf_op jit(solution)/shard_map/ppermute | solution.py:311
  176.2 6.2 %collective-permute-start.33 = (bf16[256,128]{1,0:T(8,128)(2,1)}, bf16[256,128]{1,0:T(8,128)(2,1)S(1)}, u32[]{:S(2)}, u32[]{:S(2)}) collective-permute-start(bf16[256,128]{1,0:T(8,128)(2,1)} %get-tuple-element.90), channel_id=1, source_target_pairs={{0,4},{1,5},{2,6},{3,7},{4,0},{5,1},{6,2},{7,3},{8,12},{9,13},{10,... | collective-permute-start | bytes 196616 | tf_op jit(solution)/shard_map/ppermute | solution.py:311
  176.7 6.5 %collective-permute-start.34 = (bf16[256,128]{1,0:T(8,128)(2,1)}, bf16[256,128]{1,0:T(8,128)(2,1)S(1)}, u32[]{:S(2)}, u32[]{:S(2)}) collective-permute-start(bf16[256,128]{1,0:T(8,128)(2,1)} %get-tuple-element.91), channel_id=1, source_target_pairs={{0,5},{1,4},{2,7},{3,6},{4,1},{5,0},{6,3},{7,2},{8,13},{9,12},{10,... | collective-permute-start | bytes 196616 | tf_op jit(solution)/shard_map/ppermute | solution.py:311
  (25 other events, 352.7 us)
Sparse Core Ops, SparseCore 0:
  10.6 129.6 all-gather.1

commit v8 on v7

--- a/solution.py
+++ b/solution.py
@@ -11,6 +11,7 @@
 HD = 128
 GROUP = 4
 BLK = 512
+HALF = BLK // 2
 SEL = 4
 QB = 4
 BLOCKS = 8
@@ -21,7 +22,7 @@
 BF16 = jnp.bfloat16
 NX = 4
 NZ = 8
-RING_ROWS = 32
+RING_ROWS = 48
 VMEM_BYTES = 56 << 20
 
 
@@ -37,57 +38,51 @@
     return (raw * SCALE).astype(BF16).astype(F32)
 
 
-def near_kernel(kv_ref, q_ref, k_ref, v_ref, acc_ref, m_ref, l_ref):
-    scores = dot_nt(k_ref[...], q_ref[...])
-    keys = lax.broadcasted_iota(jnp.int32, (BLK, BLK), 0)
-    rows = lax.broadcasted_iota(jnp.int32, (BLK, BLK), 1)
-    scores = jnp.where(keys <= rows, scores, NEG)
-    top = rounded_top(jnp.max(scores, axis=0, keepdims=True))
-    weights = jnp.exp2(scores * SCALE - top)
-    m_ref[0] = top
-    l_ref[0] = jnp.sum(weights, axis=0, keepdims=True)
-    acc_ref[0] = dot_tn(v_ref[...], weights.astype(BF16))
-
-
-def state_shapes():
-    return [
-        jax.ShapeDtypeStruct((QB, HD, BLK), F32),
-        jax.ShapeDtypeStruct((QB, 1, BLK), F32),
-        jax.ShapeDtypeStruct((QB, 1, BLK), F32),
-    ]
-
-
-def near(queries, span_keys, span_values, kv):
+def near_kernel(place_ref, *refs):
+    q_refs, (k_ref, v_ref, acc_ref, m_ref, l_ref) = refs[:2], refs[2:]
+    keys = lax.broadcasted_iota(jnp.int32, (BLK, HALF), 0)
+    rows = lax.broadcasted_iota(jnp.int32, (BLK, HALF), 1) + place_ref[1] * HALF
+    for r, q_ref in enumerate(q_refs):
+        scores = jnp.where(keys <= rows, dot_nt(k_ref[...], q_ref[...]), NEG)
+        top = rounded_top(jnp.max(scores, axis=0, keepdims=True))
+        weights = jnp.exp2(scores * SCALE - top)
+        m_ref[0, r] = top
+        l_ref[0, r] = jnp.sum(weights, axis=0, keepdims=True)
+        acc_ref[0, r] = dot_tn(v_ref[...], weights.astype(BF16))
+
+
+def near(place, queries, span_keys, span_values):
     grid_spec = pltpu.PrefetchScalarGridSpec(
         num_scalar_prefetch=1,
         grid=(QB,),
-        in_specs=[
-            pl.BlockSpec((BLK, HD), lambda i, kv: (i, 0)),
-            pl.BlockSpec((BLK, HD), lambda i, kv: (i, kv[0])),
-            pl.BlockSpec((BLK, HD), lambda i, kv: (i, kv[0])),
-        ],
+        in_specs=[pl.BlockSpec((HALF, HD), lambda i, place: (2 * i + place[1], 0))] * 2
+        + [pl.BlockSpec((BLK, HD), lambda i, place: (i, place[0]))] * 2,
         out_specs=[
-            pl.BlockSpec((1, HD, BLK), lambda i, kv: (i, 0, 0)),
-            pl.BlockSpec((1, 1, BLK), lambda i, kv: (i, 0, 0)),
-            pl.BlockSpec((1, 1, BLK), lambda i, kv: (i, 0, 0)),
+            pl.BlockSpec((1, 2, HD, HALF), lambda i, place: (i, 0, 0, 0)),
+            pl.BlockSpec((1, 2, 1, HALF), lambda i, place: (i, 0, 0, 0)),
+            pl.BlockSpec((1, 2, 1, HALF), lambda i, place: (i, 0, 0, 0)),
         ],
     )
     return pl.pallas_call(
         near_kernel,
         grid_spec=grid_spec,
-        out_shape=state_shapes(),
+        out_shape=[
+            jax.ShapeDtypeStruct((QB, 2, HD, HALF), F32),
+            jax.ShapeDtypeStruct((QB, 2, 1, HALF), F32),
+            jax.ShapeDtypeStruct((QB, 2, 1, HALF), F32),
+        ],
         cost_estimate=pl.CostEstimate(
             flops=QB * 4 * BLK * BLK * HD, bytes_accessed=4 << 20, transcendentals=QB * BLK * BLK
         ),
         name="near",
-    )(kv, queries, span_keys, span_values)
-
-
-def pack_state(ref, i, out, top, total, columns=slice(None)):
-    ref[i, :HD, columns] = out.astype(BF16)
+    )(place, *queries, span_keys, span_values)
+
+
+def pack_state(ref, i, out, top, total):
+    ref[i, :HD, :] = out.astype(BF16)
     high = total.astype(BF16)
     low = (total - high.astype(F32)).astype(BF16)
-    ref[i, HD:, columns] = jnp.concatenate(
+    ref[i, HD:, :] = jnp.concatenate(
         [top.astype(BF16), high, low, jnp.zeros((TAIL - 3, out.shape[1]), BF16)], axis=0
     )
 
@@ -107,12 +102,15 @@
     )
     early_copy.start()
     for pick in range(picks):
-        pltpu.make_async_copy(whole_ref.at[picks_ref[pick]], buffer.at[pick], sems.at[1]).start()
+        sem = sems.at[1 if pick < SEL else 2]
+        pltpu.make_async_copy(whole_ref.at[picks_ref[pick]], buffer.at[pick], sem).start()
     early_copy.wait()
-    pltpu.make_async_copy(buffer, buffer, sems.at[1]).wait()
-    step_columns = BLK // 2
-    steps = [(row, first) for row in range(2 * QB) for first in range(0, BLK, step_columns)]
+    steps = [(row, k) for row in range(2 * QB) for k in range(2)]
     sums = {}
+
+    def fetched(first, count, sem):
+        held = buffer.at[pl.ds(first, count)]
+        pltpu.make_async_copy(held, held, sem).wait()
 
     def joined(row, which):
         return jnp.concatenate(
@@ -120,14 +118,19 @@
         )
 
     def score(number):
-        row, first = steps[number]
-        tokens = pl.ds(row % QB * BLK + first, step_columns)
+        row, k = steps[number]
+        if number == 0:
+            fetched(0, SEL, sems.at[1])
+        if number == 2:
+            fetched(SEL, picks - SEL, sems.at[2])
+        first = row % QB * BLK + (picks_ref[picks] ^ k) * HALF
+        tokens = pl.ds(pl.multiple_of(first, HALF), HALF)
         score_refs[number % 2][...] = dot_nt(joined(row, 0), q_refs[row // QB][tokens, :])
 
     def soften(number):
         score_ref, weight_ref = score_refs[number % 2], weight_refs[number % 2]
         tops, totals = [], []
-        for lane in range(0, step_columns, HD):
+        for lane in range(0, HALF, HD):
             lanes = slice(lane, lane + HD)
             top = rounded_top(jnp.max(score_ref[:, lanes], axis=0, keepdims=True))
             total = jnp.zeros((8, HD), F32)
@@ -140,11 +143,10 @@
         sums[number] = jnp.concatenate(tops, axis=1), jnp.concatenate(totals, axis=1)
 
     def finish(number):
-        row, first = steps[number]
+        row, k = steps[number]
         top, total = sums.pop(number)
         out = dot_tn(joined(row, 1), weight_refs[number % 2][...])
-        columns = slice(first, first + step_columns)
-        pack_state(out_refs[row // QB], row % QB, out, top, total, columns)
+        pack_state(out_refs[k], row, out, top, total)
 
     for number in range(len(steps) + 2):
         if number < len(steps):
@@ -164,13 +166,13 @@
         + [vmem] * 2
         + [pl.BlockSpec(memory_space=pl.ANY)] * 2,
         out_specs=[vmem] * 2,
-        out_shape=[jax.ShapeDtypeStruct((QB, pay, BLK), BF16)] * 2,
+        out_shape=[jax.ShapeDtypeStruct((2 * QB, pay, HALF), BF16)] * 2,
         scratch_shapes=[
             pltpu.VMEM((2 * QB * SEL,) + array.shape[1:], BF16) for array in (whole, early)
         ]
-        + [pltpu.VMEM((BLK, BLK // 2), F32)] * 2
-        + [pltpu.VMEM((BLK, BLK // 2), BF16)] * 2
-        + [pltpu.SemaphoreType.DMA((2,))],
+        + [pltpu.VMEM((BLK, HALF), F32)] * 2
+        + [pltpu.VMEM((BLK, HALF), BF16)] * 2
+        + [pltpu.SemaphoreType.DMA((3,))],
         compiler_params=pltpu.CompilerParams(vmem_limit_bytes=VMEM_BYTES),
         cost_estimate=pl.CostEstimate(
             flops=8 * 2 * QB * 4 * BLK * BLK * HD,
@@ -211,74 +213,88 @@
     )(where, *arrays)
 
 
+def crossed(row):
+    return (row + QB) % (2 * QB)
+
+
 def merge_two_kernel(a_ref, b_ref, *out_refs):
-    per = QB // len(out_refs)
-    for i in range(QB):
-        acc_a, m_a, l_a = unpack_state(a_ref, i)
-        acc_b, m_b, l_b = unpack_state(b_ref, i)
+    for row in range(2 * QB):
+        acc_a, m_a, l_a = unpack_state(a_ref, row)
+        acc_b, m_b, l_b = unpack_state(b_ref, crossed(row))
         top = jnp.maximum(m_a, m_b)
         f_a = jnp.exp2(m_a - top)
         f_b = jnp.exp2(m_b - top)
-        pack_state(
-            out_refs[i // per], i % per, f_a * acc_a + f_b * acc_b, top, f_a * l_a + f_b * l_b
-        )
-
-
-def merge_two(mine, other, pieces):
+        out = f_a * acc_a + f_b * acc_b
+        pack_state(out_refs[row // QB], row % QB, out, top, f_a * l_a + f_b * l_b)
+
+
+def merge_two(mine, other):
     vmem = pl.BlockSpec(memory_space=pltpu.VMEM)
-    shape = (QB // pieces,) + mine.shape[1:]
     return pl.pallas_call(
         merge_two_kernel,
         in_specs=[vmem] * 2,
-        out_specs=[vmem] * pieces,
-        out_shape=[jax.ShapeDtypeStruct(shape, BF16)] * pieces,
+        out_specs=[vmem] * 2,
+        out_shape=[jax.ShapeDtypeStruct((QB,) + mine.shape[1:], BF16)] * 2,
         name="merge_two",
     )(mine, other)
 
 
-def merge_last_kernel(head_ref, a_ref, b_ref, acc_ref, m_ref, l_ref, *refs, pieces):
-    chip_refs, out_ref, share_refs = refs[:pieces], refs[pieces], refs[pieces + 1 :]
-    per = QB // pieces
-    rows = QB * BLK // len(share_refs)
-    for i in range(QB):
-        states = [unpack_state(a_ref, i), unpack_state(b_ref, i)]
-        states.append(unpack_state(chip_refs[i // per], i % per))
-        states.append((acc_ref[i], m_ref[i], l_ref[i]))
+def merge_last_kernel(chip_ref, a_ref, b_ref, acc_ref, m_ref, l_ref, *refs):
+    chip_refs, half_refs, share_refs = refs[:2], refs[2:4], refs[4:]
+    for row in range(2 * QB):
+        r, i = row // QB, row % QB
+        states = [unpack_state(a_ref, row), unpack_state(b_ref, crossed(row))]
+        states.append(unpack_state(chip_refs[r], i))
+        states.append((acc_ref[i, r], m_ref[i, r], l_ref[i, r]))
         top = functools.reduce(jnp.maximum, [m for _, m, _ in states])
         factors = [jnp.exp2(m - top) for _, m, _ in states]
         total = sum(f * l for f, (_, _, l) in zip(factors, states))
         factors = [f / total for f in factors]
         out = sum(f * acc for f, (acc, _, _) in zip(factors, states)).T.astype(BF16)
-        out_ref[i * BLK : (i + 1) * BLK, :] = out
-        for first in range(0, BLK, rows):
-            owner = (i * BLK + first) // rows
-            for r, share_ref in enumerate(share_refs):
-
-                def keep(share_ref=share_ref, first=first, out=out):
-                    share_ref[...] = out[first : first + rows, :]
-
-                pl.when(head_ref[0] ^ r == owner)(keep)
-
-
-def merge_last(head, heads, mine, core_part, near_state, chip_parts):
+        half_refs[r][i] = out
+        for n, share_ref in enumerate(share_refs):
+
+            def keep(share_ref=share_ref, r=r, out=out):
+                share_ref[r] = out
+
+            pl.when(chip_ref[0] ^ n == i)(keep)
+
+
+def merge_last(chip, mine, core_part, near_state, chip_parts):
     vmem = pl.BlockSpec(memory_space=pltpu.VMEM)
     arrays = [mine, core_part, *near_state, *chip_parts]
-    rows = QB * BLK
-    attention, *shares = pl.pallas_call(
-        functools.partial(merge_last_kernel, pieces=len(chip_parts)),
+    own, other, *shares = pl.pallas_call(
+        merge_last_kernel,
         in_specs=[pl.BlockSpec(memory_space=pltpu.SMEM)] + [vmem] * len(arrays),
-        out_specs=[vmem] * (1 + heads),
-        out_shape=[jax.ShapeDtypeStruct((rows, HD), BF16)]
-        + [jax.ShapeDtypeStruct((rows // heads, HD), BF16)] * heads,
+        out_specs=[vmem] * (2 + QB),
+        out_shape=[jax.ShapeDtypeStruct((QB, HALF, HD), BF16)] * 2
+        + [jax.ShapeDtypeStruct((2, HALF, HD), BF16)] * QB,
         name="merge_last",
-    )(head, *arrays)
-    return attention, shares
+    )(chip, *arrays)
+    return own, other, shares
+
+
+def assemble_kernel(core_ref, own_ref, other_ref, out_ref):
+    for i in range(QB):
+        for k, ref in enumerate((own_ref, other_ref)):
+            first = pl.multiple_of(i * BLK + (core_ref[0] ^ k) * HALF, HALF)
+            out_ref[pl.ds(first, HALF), :] = ref[i]
+
+
+def assemble(core, own, other):
+    vmem = pl.BlockSpec(memory_space=pltpu.VMEM)
+    return pl.pallas_call(
+        assemble_kernel,
+        in_specs=[pl.BlockSpec(memory_space=pltpu.SMEM)] + [vmem] * 2,
+        out_specs=vmem,
+        out_shape=jax.ShapeDtypeStruct((QB * BLK, HD), BF16),
+        name="assemble",
+    )(core, own, other)
 
 
 def project_kernel(*refs):
-    heads = len(refs) // 2
-    a_refs, w_refs, out_ref = refs[:heads], refs[heads:-1], refs[-1]
-    rows = jnp.concatenate([a_ref[...] for a_ref in a_refs], axis=1)
+    a_refs, w_refs, out_ref = refs[:QB], refs[QB:-1], refs[-1]
+    rows = jnp.concatenate([a_ref[r] for a_ref in a_refs for r in range(2)], axis=1)
     tile = 512
     for first in range(0, out_ref.shape[1], tile):
         weight = jnp.concatenate([w_ref[:, first : first + tile] for w_ref in w_refs], axis=0)
@@ -293,7 +309,7 @@
         project_kernel,
         in_specs=[vmem] * (len(parts) + len(weights)),
         out_specs=vmem,
-        out_shape=jax.ShapeDtypeStruct((parts[0].shape[0], weights[0].shape[1]), BF16),
+        out_shape=jax.ShapeDtypeStruct((parts[0].shape[1], weights[0].shape[1]), BF16),
         compiler_params=pltpu.CompilerParams(vmem_limit_bytes=24 << 20),
         name="project",
     )(*parts, *weights)
@@ -347,25 +363,28 @@
     ring_arrays = [low, high, x1_low, x1_high, x2_low, x2_high, x3_low, x3_high]
 
     queries_early, picks_early, weight_early = after(
-        (queries, block_picks, out_weight), *ring_arrays[:6]
+        (queries, block_picks, out_weight), x1_low, x2_low
     )
     queries_pair = [queries, swap(queries_early, 2)]
     picks_pair = jnp.stack([block_picks, swap(picks_early, 2)])
     weights = [out_weight] + [None] * (heads - 1)
     for bits in range(2, heads, 2):
         weights[bits] = swap(weight_early, bits)
-    near_state = near(queries_early, span_keys, span_values, kv[None])
     queries_pair, picks_pair, weights[::2] = after(
         (queries_pair, picks_pair, weights[::2]), *ring_arrays
     )
     group_queries = [queries, swap(queries_pair[0], 1), queries_pair[1], swap(queries_pair[1], 1)]
+    core, chip = head % 2, head // 2
+    near_state = near(
+        jnp.stack([kv, core]).astype(jnp.int32), group_queries[:2], span_keys, span_values
+    )
     picks_core = swap(picks_pair, 1)
     group_picks = [picks_pair[0], picks_core[0], picks_pair[1], picks_core[1]]
     for bits in range(0, heads, 2):
         weights[bits + 1] = swap(weights[bits], 1)
     picks = [group_pick.reshape(QB * SEL) for group_pick in group_picks]
 
-    every_pick = jnp.concatenate(picks[::-1])
+    every_pick = jnp.concatenate([picks[r] for r in (2, 3, 0, 1)])
     owner, local = every_pick // BLOCKS, every_pick % BLOCKS
     ctx = lax.axis_index("ctx")
     dz = (owner // NX - ctx // NX) % NZ
@@ -383,23 +402,22 @@
 
     def far_of(first, second, earlier, half):
         return far(
-            after(jnp.concatenate([picks[first], picks[second]]), *earlier),
+            after(jnp.concatenate([picks[first], picks[second], core[None]]), *earlier),
             [group_queries[first], group_queries[second]],
             whole,
             early,
             half,
         )
 
-    far_corner, far_chip = far_of(3, 2, [], 0)
-    for_chip = merge_two(far_chip, swap(far_corner, 1), 2)
+    chip_here, chip_there = far_of(2, 3, [], 0)
+    for_chip = merge_two(chip_here, swap(chip_there, 1))
     chip_parts = [swap(piece, 2) for piece in for_chip]
-    far_core, far_own = far_of(1, 0, for_chip, 1)
-    core_part = swap(after(far_core, *chip_parts), 1)
-    attention, shares = merge_last(
-        head[None], heads, far_own, core_part, near_state, chip_parts
-    )
-    parts = [shares[0]] + [swap(shares[r], r) for r in range(1, heads)]
-    return attention, project(parts, weights)
+    own_here, own_there = far_of(0, 1, for_chip, 1)
+    core_part = swap(after(own_there, *chip_parts), 1)
+    own, other, shares = merge_last(chip[None], own_here, core_part, near_state, chip_parts)
+    parts = [shares[0]] + [swap(shares[n], 2 * n) for n in range(1, QB)]
+    attention = assemble(core[None], own, swap(other, 1))
+    return attention, project(after(parts, attention), weights)
 
 
 def solution(mesh):

time: 198 us -> 200 us (1.010)
  Pallas kernels: 31.5 us -> 35.5 us
    all_gather x1, waiting for transfers between devices: 36.4 us -> 12.6 us  [body(): whole = lax.all_gather(cut(0, share - RING_ROWS), 'ctx', axis=0, tiled=True)]
    ppermute x14, waiting for transfers between devices: 31.6 us -> 47.5 us  [shift(): return lax.ppermute(array, 'ctx', pairs)]
    ppermute x23 -> x20, waiting for transfers between devices: 28.3 us -> 34.6 us  [swap(): lax.ppermute(array, 'head', [(h, h ^ bits) for h in range(lax.axis_size('...]
    pallas_call x2 -> x3, Pallas kernels: 8.65 us -> 12.6 us  [the longest x1 6.68 us: near(): pl.pallas_call(near_kernel, grid_spec=grid_spec, out_shape=[jax.ShapeDtyp...]
    ppermute x23 -> x20, starting transfers between devices: 26.6 us -> 22.8 us  [swap(): lax.ppermute(array, 'head', [(h, h ^ bits) for h in range(lax.axis_size('...]
    ppermute x14, starting transfers between devices: 21.9 us -> 25.1 us  [shift(): return lax.ppermute(array, 'ctx', pairs)]
  transfers between devices with their start and end apart: 38 -> 35, of which waited for: 20 -> 22; matrix products, arithmetic and copies ran while one was open for 2% -> 2% of each run, Pallas kernels for 8% -> 10%
where the time goes in v8:
time: 200 us
  waiting for transfers between devices  94.7 us (47%)
  starting transfers between devices  47.9 us (24%)
  Pallas kernels  35.5 us (18%)
  between operations  14.3 us (7%)
  local copies, waits for them, and re-layouts  4.46 us (2%)
  other arithmetic  2.77 us (1%)
    ppermute x14, waiting for transfers between devices, shift(): return lax.ppermute(array, 'ctx', pairs)  47.5 us
    ppermute x20, waiting for transfers between devices, swap(): lax.ppermute(array, 'head', [(h, h ^ bits) for h in range(lax.axis_size('...  34.6 us
    ppermute x14, starting transfers between devices, shift(): return lax.ppermute(array, 'ctx', pairs)  25.1 us
    ppermute x20, starting transfers between devices, swap(): lax.ppermute(array, 'head', [(h, h ^ bits) for h in range(lax.axis_size('...  22.8 us
    pallas_call x2, Pallas kernels, far(): pl.pallas_call(functools.partial(far_kernel, half=half), in_specs=[pl.Blo...  13 us
    all_gather x1, waiting for transfers between devices, body(): whole = lax.all_gather(cut(0, share - RING_ROWS), 'ctx', axis=0, tiled=True)  12.6 us
    pallas_call x1, Pallas kernels, near(): pl.pallas_call(near_kernel, grid_spec=grid_spec, out_shape=[jax.ShapeDtyp...  6.68 us
    pallas_call x1, Pallas kernels, collect(): pl.pallas_call(collect_kernel, in_specs=[pl.BlockSpec(memory_space=pltpu....  4.24 us
  transfers between devices with their start and end apart: 35, of which 22 were waited for; matrix products, arithmetic and copies ran while one was open for 2% of the time, Pallas kernels for 10%

profile of v8, /device:TPU:1, one launch (start us, length us, event | category | flops | bytes accessed | tf_op | source)
XLA Modules:
  0.0 199.6 jit_solution(13590600846064877909)
XLA Ops:
  12.7 4.0 %collective-permute-start.1 = (bf16[8,2,48,128]{3,2,1,0:T(8,128)(2,1)S(1)}, bf16[8,2,48,128]{3,2,1,0:T(8,128)(2,1)S(1)}, u32[]{:S(2)}, u32[]{:S(2)}) collective-permute-start(bf16[8,2,48,128]{3,2,1,0:T(8,128)(2,1)S(1)} %pad_maximum_fusion.2), channel_id=1, source_target_pairs={{0,224},{8,232},{16,240},{24,248},{32,0},{40,8},{48,16},{56,24},{6... | collective-permute-start | bytes 589832 | tf_op jit(solution)/shard_map/ppermute | solution.py:323
  16.7 4.5 %collective-permute-done = bf16[8,2,48,128]{3,2,1,0:T(8,128)(2,1)S(1)} collective-permute-done((bf16[8,2,48,128]{3,2,1,0:T(8,128)(2,1)S(1)}, bf16[8,2,48,128]{3,2,1,0:T(8,128)(2,1)S(1)}, u32[]{:S(2)}, u32[]{:S(2)}) %collective-permute-start) | collective-permute-done | bytes 196640 | tf_op jit(solution)/shard_map/ppermute | solution.py:323
  23.9 3.7 %collective-permute-done.2 = bf16[8,2,48,128]{3,2,1,0:T(8,128)(2,1)S(1)} collective-permute-done((bf16[8,2,48,128]{3,2,1,0:T(8,128)(2,1)S(1)}, bf16[8,2,48,128]{3,2,1,0:T(8,128)(2,1)S(1)}, u32[]{:S(2)}, u32[]{:S(2)}) %collective-permute-start.2) | collective-permute-done | bytes 196640 | tf_op jit(solution)/shard_map/ppermute | solution.py:323
  33.2 2.9 %collective-permute-done.11 = bf16[8,2,48,128]{3,2,1,0:T(8,128)(2,1)S(1)} collective-permute-done((bf16[8,2,48,128]{3,2,1,0:T(8,128)(2,1)S(1)}, bf16[8,2,48,128]{3,2,1,0:T(8,128)(2,1)S(1)}, u32[]{:S(2)}, u32[]{:S(2)}) %collective-permute-start.11) | collective-permute-done | bytes 196640 | tf_op jit(solution)/shard_map/ppermute | solution.py:323
  36.2 2.7 %collective-permute-start.14 = (bf16[4,2,48,128]{3,2,1,0:T(8,128)(2,1)S(1)}, bf16[4,2,48,128]{3,2,1,0:T(8,128)(2,1)S(1)}, u32[]{:S(2)}, u32[]{:S(2)}) collective-permute-start(bf16[4,2,48,128]{3,2,1,0:T(8,128)(2,1)S(1)} %slice.25), channel_id=1, source_target_pairs={{0,224},{8,232},{16,240},{24,248},{32,0},{40,8},{48,16},{56,24},{6... | collective-permute-start | bytes 294920 | tf_op jit(solution)/shard_map/ppermute | solution.py:323
  39.0 2.8 %collective-permute-done.13 = bf16[4,2,48,128]{3,2,1,0:T(8,128)(2,1)S(1)} collective-permute-done((bf16[4,2,48,128]{3,2,1,0:T(8,128)(2,1)S(1)}, bf16[4,2,48,128]{3,2,1,0:T(8,128)(2,1)S(1)}, u32[]{:S(2)}, u32[]{:S(2)}) %collective-permute-start.13) | collective-permute-done | bytes 98336 | tf_op jit(solution)/shard_map/ppermute | solution.py:323
  42.1 3.2 %collective-permute-start.16 = (bf16[32,2,48,128]{3,2,1,0:T(8,128)(2,1)S(1)}, bf16[32,2,48,128]{3,2,1,0:T(8,128)(2,1)}, u32[]{:S(2)}, u32[]{:S(2)}) collective-permute-start(bf16[32,2,48,128]{3,2,1,0:T(8,128)(2,1)S(1)} %constant_dynamic-update-slice_fusion.refs_1_), channel_id=1, source_target_pairs={{0,24},{8,0},{16,8},{24,16},{32,56},{40,32},{48,40},{56,48},{64,88... | collective-permute-start | bytes 2359304 | tf_op jit(solution)/shard_map/ppermute | solution.py:323
  45.2 6.8 %collective-permute-done.3.refs_2_ = bf16[32,2,48,128]{3,2,1,0:T(8,128)(2,1)S(1)} collective-permute-done((bf16[32,2,48,128]{3,2,1,0:T(8,128)(2,1)S(1)}, bf16[32,2,48,128]{3,2,1,0:T(8,128)(2,1)S(1)}, u32[]{:S(2)}, u32[]{:S(2)}) %collective-permute-start.3) | collective-permute-done | bytes 786464 | tf_op jit(solution)/shard_map/ppermute | solution.py:323
  54.5 16.0 %collective-permute-done.16.refs_5_ = bf16[32,2,48,128]{3,2,1,0:T(8,128)(2,1)} collective-permute-done((bf16[32,2,48,128]{3,2,1,0:T(8,128)(2,1)S(1)}, bf16[32,2,48,128]{3,2,1,0:T(8,128)(2,1)}, u32[]{:S(2)}, u32[]{:S(2)}) %collective-permute-start.16) | collective-permute-done | bytes 786464 | tf_op jit(solution)/shard_map/ppermute | solution.py:323
  70.5 3.5 %collective-permute-start.18 = (bf16[32,2,48,128]{3,2,1,0:T(8,128)(2,1)}, bf16[32,2,48,128]{3,2,1,0:T(8,128)(2,1)}, u32[]{:S(2)}, u32[]{:S(2)}) collective-permute-start(bf16[32,2,48,128]{3,2,1,0:T(8,128)(2,1)} %collective-permute-done.16.refs_5_), channel_id=1, source_target_pairs={{0,24},{8,0},{16,8},{24,16},{32,56},{40,32},{48,40},{56,48},{64,88... | collective-permute-start | bytes 2359304 | tf_op jit(solution)/shard_map/ppermute | solution.py:323
  81.4 3.9 %collective-permute-done.7.refs_6_ = bf16[128,2048]{1,0:T(8,128)(2,1)S(1)} collective-permute-done((bf16[128,2048]{1,0:T(8,128)(2,1)S(1)}, bf16[128,2048]{1,0:T(8,128)(2,1)S(1)}, u32[]{:S(2)}, u32[]{:S(2)}) %collective-permute-start.7) | collective-permute-done | bytes 524320 | tf_op jit(solution)/shard_map/ppermute | solution.py:327
  85.4 9.4 %collective-permute-done.8.refs_8_ = bf16[128,2048]{1,0:T(8,128)(2,1)S(1)} collective-permute-done((bf16[128,2048]{1,0:T(8,128)(2,1)S(1)}, bf16[128,2048]{1,0:T(8,128)(2,1)S(1)}, u32[]{:S(2)}, u32[]{:S(2)}) %collective-permute-start.8) | collective-permute-done | bytes 524320 | tf_op jit(solution)/shard_map/ppermute | solution.py:327
  96.7 5.2 %collective-permute-done.17.refs_6_ = bf16[32,2,48,128]{3,2,1,0:T(8,128)(2,1)} collective-permute-done((bf16[32,2,48,128]{3,2,1,0:T(8,128)(2,1)S(1)}, bf16[32,2,48,128]{3,2,1,0:T(8,128)(2,1)}, u32[]{:S(2)}, u32[]{:S(2)}) %collective-permute-start.17) | collective-permute-done | bytes 786464 | tf_op jit(solution)/shard_map/ppermute | solution.py:323
  101.9 5.0 %collective-permute-done.18.refs_7_ = bf16[32,2,48,128]{3,2,1,0:T(8,128)(2,1)} collective-permute-done((bf16[32,2,48,128]{3,2,1,0:T(8,128)(2,1)}, bf16[32,2,48,128]{3,2,1,0:T(8,128)(2,1)}, u32[]{:S(2)}, u32[]{:S(2)}) %collective-permute-start.18) | collective-permute-done | bytes 786464 | tf_op jit(solution)/shard_map/ppermute | solution.py:323
  106.9 7.2 %collective-permute-start.19 = (s32[2,4,1,4]{3,1,2,0:T(4,128)S(1)}, s32[2,4,1,4]{3,1,2,0:T(4,128)S(1)}, u32[]{:S(2)}, u32[]{:S(2)}) collective-permute-start(s32[2,4,1,4]{3,1,2,0:T(4,128)S(1)} %pad_add_fusion), channel_id=1, source_target_pairs={{0,1},{1,0},{2,3},{3,2},{4,5},{5,4},{6,7},{7,6},{8,9},{9,8},{10,11... | collective-permute-start | bytes 392 | tf_op jit(solution)/shard_map/ppermute | solution.py:327
  117.2 4.2 %collect.1.refs_3_ = bf16[64,2,48,128]{3,2,1,0:T(8,128)(2,1)} custom-call(s32[64,2]{1,0:T(8,128)} %copy.13.where_ref, bf16[32,2,48,128]{3,2,1,0:T(8,128)(2,1)} %copy-done.2, bf16[32,2,48,128]{3,2,1,0:T(8,128)(2,1)} %copy-done.3, bf16[32,2,48,128]{3,2,1,0:T(8,128)(2,1)} %copy-done.4, bf16[32,2,48,128]{3,2,1,0:T(8,128)(2,1)} %collective-permute-done.15.refs_3_, ...), custom_call_target="tpu_custom_call" | custom-call | tf_op jit(solution)/shard_map/collect/pallas_call | solution.py:204
  121.5 6.7 %near.1 = (f32[4,2,128,256]{3,2,1,0:T(8,128)}, f32[4,2,1,256]{3,2,1,0:T(1,128)}, f32[4,2,1,256]{3,2,1,0:T(1,128)}) custom-call(s32[2]{0:T(128)} %pad_add_fusion.2.place_ref, bf16[2048,128]{1,0:T(8,128)(2,1)} %refs_0_.2, bf16[2048,128]{1,0:T(8,128)(2,1)} %collective-permute-done.20.refs_1_, bf16[2048,256]{1,0:T(8,128)(2,1)} %refs_2_.1, bf16[2048,256]{1,0:T(8,128)(2,1)} %refs_3_.1), custom_call_target="tpu_custom_call" | custom-call | flops 536870912 | bytes 4194304 | tf_op jit(solution)/shard_map/near/pallas_call | solution.py:66
  128.8 12.6 %all-gather.2.cloned.1.call-done.refs_2_ = bf16[256,2,80,128]{3,2,1,0:T(8,128)(2,1)} async-done(((bf16[8,2,80,128]{3,2,1,0:T(8,128)(2,1)}), bf16[256,2,80,128]{3,2,1,0:T(8,128)(2,1)}) %all-gather.2.cloned.1.call-update) | async-done | bytes 10485776 | tf_op jit(solution)/shard_map/all_gather | solution.py:350
  141.4 6.5 %far.2 = (bf16[8,144,256]{2,1,0:T(8,128)(2,1)}, bf16[8,144,256]{2,1,0:T(8,128)(2,1)}) custom-call(s32[33]{0:T(128)} %add_add_fusion.1.picks_ref, bf16[2048,128]{1,0:T(8,128)(2,1)} %collective-permute-done.5.refs_0_, bf16[2048,128]{1,0:T(8,128)(2,1)} %collective-permute-done.21.refs_1_, bf16[256,2,80,128]{3,2,1,0:T(8,128)(2,1)} %all-gather.2.cloned.1.call-done.refs_2_, ...), custom_call_target="tpu_custom_call" | custom-call | flops 8589934592 | bytes 5242880 | tf_op jit(solution)/shard_map/far/pallas_call | solution.py:163
  154.5 6.5 %far.3 = (bf16[8,144,256]{2,1,0:T(8,128)(2,1)}, bf16[8,144,256]{2,1,0:T(8,128)(2,1)}) custom-call(s32[33]{0:T(128)} %add_add_fusion.picks_ref, bf16[2048,128]{1,0:T(8,128)(2,1)} %refs_0_.2, bf16[2048,128]{1,0:T(8,128)(2,1)} %collective-permute-done.20.refs_1_, bf16[256,2,80,128]{3,2,1,0:T(8,128)(2,1)} %all-gather.2.cloned.1.call-done.refs_2_, ...), custom_call_target="tpu_custom_call" | custom-call | flops 8589934592 | bytes 5242880 | tf_op jit(solution)/shard_map/far/pallas_call | solution.py:163
  161.5 6.4 %collective-permute-done.28.refs_1_ = bf16[4,144,256]{2,1,0:T(8,128)(2,1)} collective-permute-done((bf16[4,144,256]{2,1,0:T(8,128)(2,1)}, bf16[4,144,256]{2,1,0:T(8,128)(2,1)}, u32[]{:S(2)}, u32[]{:S(2)}) %collective-permute-start.28) | collective-permute-done | bytes 294944 | tf_op jit(solution)/shard_map/ppermute | solution.py:327
  171.1 4.0 %merge_last.1 = (bf16[4,256,128]{2,1,0:T(8,128)(2,1)}, bf16[4,256,128]{2,1,0:T(8,128)(2,1)}, bf16[2,256,128]{2,1,0:T(8,128)(2,1)}, bf16[2,256,128]{2,1,0:T(8,128...) custom-call(s32[1]{0:T(128)} %bitcast.1.chip_ref, bf16[8,144,256]{2,1,0:T(8,128)(2,1)} %get-tuple-element.80.a_ref, ...), custom_call_target="tpu_custom_call" | custom-call | tf_op jit(solution)/shard_map/merge_last/pallas_call | solution.py:266
  181.3 4.7 %collective-permute-done.32.refs_2_ = bf16[2,256,128]{2,1,0:T(8,128)(2,1)S(1)} collective-permute-done((bf16[2,256,128]{2,1,0:T(8,128)(2,1)}, bf16[2,256,128]{2,1,0:T(8,128)(2,1)S(1)}, u32[]{:S(2)}, u32[]{:S(2)}) %collective-permute-start.32) | collective-permute-done | bytes 131104 | tf_op jit(solution)/shard_map/ppermute | solution.py:327
  189.4 3.4 %project.1 = bf16[256,2048]{1,0:T(8,128)(2,1)} custom-call(bf16[2,256,128]{2,1,0:T(8,128)(2,1)S(1)} %copy-done.1, bf16[2,256,128]{2,1,0:T(8,128)(2,1)S(1)} %collective-permute-done.31.refs_1_, bf16[2,256,128]{2,1,0:T(8,128)(2,1)S(1)} %collective-permute-done.32.refs_2_, bf16[2,256,128]{2,1,0:T(8,128)(2,1)S(1)} %collective-permute-done.33.refs_3_, ...), custom_call_target="tpu_custom_call" | custom-call | tf_op jit(solution)/shard_map/project/pallas_call | solution.py:308
  (102 shorter events, 49.4 us)
Async XLA Ops:
  7.2 134.2 %all-gather.2.cloned.1.call-start = ((), (), s32[]{:S(2)}) async-start(), calls=%async_computation | async-start | bytes 10813440 | tf_op jit(solution)/shard_map/all_gather | solution.py:350
  10.1 11.1 %collective-permute-start = (bf16[8,2,48,128]{3,2,1,0:T(8,128)(2,1)S(1)}, bf16[8,2,48,128]{3,2,1,0:T(8,128)(2,1)S(1)}, u32[]{:S(2)}, u32[]{:S(2)}) collective-permute-start(bf16[8,2,48,128]{3,2,1,0:T(8,128)(2,1)S(1)} %pad_maximum_fusion.2), channel_id=1, source_target_pairs={{0,32},{8,40},{16,48},{24,56},{32,64},{40,72},{48,80},{56,88},{64,... | collective-permute-start | bytes 589832 | tf_op jit(solution)/shard_map/ppermute | solution.py:323
  12.7 8.6 %collective-permute-start.1 = (bf16[8,2,48,128]{3,2,1,0:T(8,128)(2,1)S(1)}, bf16[8,2,48,128]{3,2,1,0:T(8,128)(2,1)S(1)}, u32[]{:S(2)}, u32[]{:S(2)}) collective-permute-start(bf16[8,2,48,128]{3,2,1,0:T(8,128)(2,1)S(1)} %pad_maximum_fusion.2), channel_id=1, source_target_pairs={{0,224},{8,232},{16,240},{24,248},{32,0},{40,8},{48,16},{56,24},{6... | collective-permute-start | bytes 589832 | tf_op jit(solution)/shard_map/ppermute | solution.py:323
  27.6 8.5 %collective-permute-start.11 = (bf16[8,2,48,128]{3,2,1,0:T(8,128)(2,1)S(1)}, bf16[8,2,48,128]{3,2,1,0:T(8,128)(2,1)S(1)}, u32[]{:S(2)}, u32[]{:S(2)}) collective-permute-start(bf16[8,2,48,128]{3,2,1,0:T(8,128)(2,1)S(1)} %collective-permute-done.2), channel_id=1, source_target_pairs={{0,32},{8,40},{16,48},{24,56},{32,64},{40,72},{48,80},{56,88},{64,... | collective-permute-start | bytes 589832 | tf_op jit(solution)/shard_map/ppermute | solution.py:323
  27.6 8.5 %collective-permute-start.12 = (bf16[8,2,48,128]{3,2,1,0:T(8,128)(2,1)S(1)}, bf16[8,2,48,128]{3,2,1,0:T(8,128)(2,1)S(1)}, u32[]{:S(2)}, u32[]{:S(2)}) collective-permute-start(bf16[8,2,48,128]{3,2,1,0:T(8,128)(2,1)S(1)} %collective-permute-done.10), channel_id=1, source_target_pairs={{0,224},{8,232},{16,240},{24,248},{32,0},{40,8},{48,16},{56,24},{6... | collective-permute-start | bytes 589832 | tf_op jit(solution)/shard_map/ppermute | solution.py:323
  30.4 21.7 %collective-permute-start.3 = (bf16[32,2,48,128]{3,2,1,0:T(8,128)(2,1)S(1)}, bf16[32,2,48,128]{3,2,1,0:T(8,128)(2,1)S(1)}, u32[]{:S(2)}, u32[]{:S(2)}) collective-permute-start(bf16[32,2,48,128]{3,2,1,0:T(8,128)(2,1)S(1)} %pad_maximum_fusion.refs_0_), channel_id=1, source_target_pairs={{0,8},{8,16},{16,24},{24,0},{32,40},{40,48},{48,56},{56,32},{64,72... | collective-permute-start | bytes 2359304 | tf_op jit(solution)/shard_map/ppermute | solution.py:323
  31.7 20.7 %collective-permute-start.4 = (bf16[32,2,48,128]{3,2,1,0:T(8,128)(2,1)S(1)}, bf16[32,2,48,128]{3,2,1,0:T(8,128)(2,1)S(1)}, u32[]{:S(2)}, u32[]{:S(2)}) collective-permute-start(bf16[32,2,48,128]{3,2,1,0:T(8,128)(2,1)S(1)} %pad_maximum_fusion.refs_0_), channel_id=1, source_target_pairs={{0,24},{8,0},{16,8},{24,16},{32,56},{40,32},{48,40},{56,48},{64,88... | collective-permute-start | bytes 2359304 | tf_op jit(solution)/shard_map/ppermute | solution.py:323
  42.1 28.5 %collective-permute-start.16 = (bf16[32,2,48,128]{3,2,1,0:T(8,128)(2,1)S(1)}, bf16[32,2,48,128]{3,2,1,0:T(8,128)(2,1)}, u32[]{:S(2)}, u32[]{:S(2)}) collective-permute-start(bf16[32,2,48,128]{3,2,1,0:T(8,128)(2,1)S(1)} %constant_dynamic-update-slice_fusion.refs_1_), channel_id=1, source_target_pairs={{0,24},{8,0},{16,8},{24,16},{32,56},{40,32},{48,40},{56,48},{64,88... | collective-permute-start | bytes 2359304 | tf_op jit(solution)/shard_map/ppermute | solution.py:323
  45.2 33.0 %collective-permute-start.15 = (bf16[32,2,48,128]{3,2,1,0:T(8,128)(2,1)S(1)}, bf16[32,2,48,128]{3,2,1,0:T(8,128)(2,1)}, u32[]{:S(2)}, u32[]{:S(2)}) collective-permute-start(bf16[32,2,48,128]{3,2,1,0:T(8,128)(2,1)S(1)} %constant_dynamic-update-slice_fusion.refs_1_), channel_id=1, source_target_pairs={{0,8},{8,16},{16,24},{24,0},{32,40},{40,48},{48,56},{56,32},{64,72... | collective-permute-start | bytes 2359304 | tf_op jit(solution)/shard_map/ppermute | solution.py:323
  52.5 27.9 %collective-permute-start.5 = (bf16[2048,128]{1,0:T(8,128)(2,1)}, bf16[2048,128]{1,0:T(8,128)(2,1)}, u32[]{:S(2)}, u32[]{:S(2)}) collective-permute-start(bf16[2048,128]{1,0:T(8,128)(2,1)} %refs_0_.2), channel_id=1, source_target_pairs={{0,2},{1,3},{2,0},{3,1},{4,6},{5,7},{6,4},{7,5},{8,10},{9,11},{10,... | collective-permute-start | bytes 1572872 | tf_op jit(solution)/shard_map/ppermute | solution.py:327
  53.7 48.2 %collective-permute-start.17 = (bf16[32,2,48,128]{3,2,1,0:T(8,128)(2,1)S(1)}, bf16[32,2,48,128]{3,2,1,0:T(8,128)(2,1)}, u32[]{:S(2)}, u32[]{:S(2)}) collective-permute-start(bf16[32,2,48,128]{3,2,1,0:T(8,128)(2,1)S(1)} %collective-permute-done.3.refs_2_), channel_id=1, source_target_pairs={{0,8},{8,16},{16,24},{24,0},{32,40},{40,48},{48,56},{56,32},{64,72... | collective-permute-start | bytes 2359304 | tf_op jit(solution)/shard_map/ppermute | solution.py:323
  70.5 36.3 %collective-permute-start.18 = (bf16[32,2,48,128]{3,2,1,0:T(8,128)(2,1)}, bf16[32,2,48,128]{3,2,1,0:T(8,128)(2,1)}, u32[]{:S(2)}, u32[]{:S(2)}) collective-permute-start(bf16[32,2,48,128]{3,2,1,0:T(8,128)(2,1)} %collective-permute-done.16.refs_5_), channel_id=1, source_target_pairs={{0,24},{8,0},{16,8},{24,16},{32,56},{40,32},{48,40},{56,48},{64,88... | collective-permute-start | bytes 2359304 | tf_op jit(solution)/shard_map/ppermute | solution.py:323
  76.9 8.5 %collective-permute-start.7 = (bf16[128,2048]{1,0:T(8,128)(2,1)S(1)}, bf16[128,2048]{1,0:T(8,128)(2,1)S(1)}, u32[]{:S(2)}, u32[]{:S(2)}) collective-permute-start(bf16[128,2048]{1,0:T(8,128)(2,1)S(1)} %copy-done), channel_id=1, source_target_pairs={{0,2},{1,3},{2,0},{3,1},{4,6},{5,7},{6,4},{7,5},{8,10},{9,11},{10,... | collective-permute-start | bytes 1572872 | tf_op jit(solution)/shard_map/ppermute | solution.py:327
  78.2 16.6 %collective-permute-start.8 = (bf16[128,2048]{1,0:T(8,128)(2,1)S(1)}, bf16[128,2048]{1,0:T(8,128)(2,1)S(1)}, u32[]{:S(2)}, u32[]{:S(2)}) collective-permute-start(bf16[128,2048]{1,0:T(8,128)(2,1)S(1)} %copy-done), channel_id=1, source_target_pairs={{0,4},{1,5},{2,6},{3,7},{4,0},{5,1},{6,2},{7,3},{8,12},{9,13},{10,... | collective-permute-start | bytes 1572872 | tf_op jit(solution)/shard_map/ppermute | solution.py:327
  80.4 16.4 %collective-permute-start.9 = (bf16[128,2048]{1,0:T(8,128)(2,1)S(1)}, bf16[128,2048]{1,0:T(8,128)(2,1)S(1)}, u32[]{:S(2)}, u32[]{:S(2)}) collective-permute-start(bf16[128,2048]{1,0:T(8,128)(2,1)S(1)} %copy-done), channel_id=1, source_target_pairs={{0,6},{1,7},{2,4},{3,5},{4,2},{5,3},{6,0},{7,1},{8,14},{9,15},{10,... | collective-permute-start | bytes 1572872 | tf_op jit(solution)/shard_map/ppermute | solution.py:327
  106.9 8.6 %collective-permute-start.19 = (s32[2,4,1,4]{3,1,2,0:T(4,128)S(1)}, s32[2,4,1,4]{3,1,2,0:T(4,128)S(1)}, u32[]{:S(2)}, u32[]{:S(2)}) collective-permute-start(s32[2,4,1,4]{3,1,2,0:T(4,128)S(1)} %pad_add_fusion), channel_id=1, source_target_pairs={{0,1},{1,0},{2,3},{3,2},{4,5},{5,4},{6,7},{7,6},{8,9},{9,8},{10,11... | collective-permute-start | bytes 392 | tf_op jit(solution)/shard_map/ppermute | solution.py:327
  114.4 13.8 %collective-permute-start.21 = (bf16[2048,128]{1,0:T(8,128)(2,1)}, bf16[2048,128]{1,0:T(8,128)(2,1)}, u32[]{:S(2)}, u32[]{:S(2)}) collective-permute-start(bf16[2048,128]{1,0:T(8,128)(2,1)} %collective-permute-done.5.refs_0_), channel_id=1, source_target_pairs={{0,1},{1,0},{2,3},{3,2},{4,5},{5,4},{6,7},{7,6},{8,9},{9,8},{10,11... | collective-permute-start | bytes 1572872 | tf_op jit(solution)/shard_map/ppermute | solution.py:327
  114.9 13.2 %collective-permute-start.22 = (bf16[128,2048]{1,0:T(8,128)(2,1)S(1)}, bf16[128,2048]{1,0:T(8,128)(2,1)S(1)}, u32[]{:S(2)}, u32[]{:S(2)}) collective-permute-start(bf16[128,2048]{1,0:T(8,128)(2,1)S(1)} %copy-done), channel_id=1, source_target_pairs={{0,1},{1,0},{2,3},{3,2},{4,5},{5,4},{6,7},{7,6},{8,9},{9,8},{10,11... | collective-permute-start | bytes 1572872 | tf_op jit(solution)/shard_map/ppermute | solution.py:327
  115.0 13.1 %collective-permute-start.23 = (bf16[128,2048]{1,0:T(8,128)(2,1)S(1)}, bf16[128,2048]{1,0:T(8,128)(2,1)S(1)}, u32[]{:S(2)}, u32[]{:S(2)}) collective-permute-start(bf16[128,2048]{1,0:T(8,128)(2,1)S(1)} %collective-permute-done.7.refs_6_), channel_id=1, source_target_pairs={{0,1},{1,0},{2,3},{3,2},{4,5},{5,4},{6,7},{7,6},{8,9},{9,8},{10,11... | collective-permute-start | bytes 1572872 | tf_op jit(solution)/shard_map/ppermute | solution.py:327
  115.4 12.7 %collective-permute-start.24 = (bf16[128,2048]{1,0:T(8,128)(2,1)S(1)}, bf16[128,2048]{1,0:T(8,128)(2,1)}, u32[]{:S(2)}, u32[]{:S(2)}) collective-permute-start(bf16[128,2048]{1,0:T(8,128)(2,1)S(1)} %collective-permute-done.8.refs_8_), channel_id=1, source_target_pairs={{0,1},{1,0},{2,3},{3,2},{4,5},{5,4},{6,7},{7,6},{8,9},{9,8},{10,11... | collective-permute-start | bytes 1572872 | tf_op jit(solution)/shard_map/ppermute | solution.py:327
  116.3 11.9 %collective-permute-start.25 = (bf16[128,2048]{1,0:T(8,128)(2,1)S(1)}, bf16[128,2048]{1,0:T(8,128)(2,1)}, u32[]{:S(2)}, u32[]{:S(2)}) collective-permute-start(bf16[128,2048]{1,0:T(8,128)(2,1)S(1)} %collective-permute-done.9.refs_10_), channel_id=1, source_target_pairs={{0,1},{1,0},{2,3},{3,2},{4,5},{5,4},{6,7},{7,6},{8,9},{9,8},{10,11... | collective-permute-start | bytes 1572872 | tf_op jit(solution)/shard_map/ppermute | solution.py:327
  154.3 13.6 %collective-permute-start.28 = (bf16[4,144,256]{2,1,0:T(8,128)(2,1)}, bf16[4,144,256]{2,1,0:T(8,128)(2,1)}, u32[]{:S(2)}, u32[]{:S(2)}) collective-permute-start(bf16[4,144,256]{2,1,0:T(8,128)(2,1)} %get-tuple-element.76), channel_id=1, source_target_pairs={{0,2},{1,3},{2,0},{3,1},{4,6},{5,7},{6,4},{7,5},{8,10},{9,11},{10,... | collective-permute-start | bytes 884744 | tf_op jit(solution)/shard_map/ppermute | solution.py:327
  176.8 9.2 %collective-permute-start.32 = (bf16[2,256,128]{2,1,0:T(8,128)(2,1)}, bf16[2,256,128]{2,1,0:T(8,128)(2,1)S(1)}, u32[]{:S(2)}, u32[]{:S(2)}) collective-permute-start(bf16[2,256,128]{2,1,0:T(8,128)(2,1)} %get-tuple-element.90), channel_id=1, source_target_pairs={{0,4},{1,5},{2,6},{3,7},{4,0},{5,1},{6,2},{7,3},{8,12},{9,13},{10,... | collective-permute-start | bytes 393224 | tf_op jit(solution)/shard_map/ppermute | solution.py:327
  179.4 9.1 %collective-permute-start.33 = (bf16[2,256,128]{2,1,0:T(8,128)(2,1)}, bf16[2,256,128]{2,1,0:T(8,128)(2,1)S(1)}, u32[]{:S(2)}, u32[]{:S(2)}) collective-permute-start(bf16[2,256,128]{2,1,0:T(8,128)(2,1)} %get-tuple-element.91), channel_id=1, source_target_pairs={{0,6},{1,7},{2,4},{3,5},{4,2},{5,3},{6,0},{7,1},{8,14},{9,15},{10,... | collective-permute-start | bytes 393224 | tf_op jit(solution)/shard_map/ppermute | solution.py:327
  (19 other events, 370.8 us)
Sparse Core Ops, SparseCore 0:
  11.1 130.2 all-gather.1

commit v9 on v8

--- a/solution.py
+++ b/solution.py
@@ -22,7 +22,7 @@
 BF16 = jnp.bfloat16
 NX = 4
 NZ = 8
-RING_ROWS = 48
+RING_ROWS = 32
 VMEM_BYTES = 56 << 20
 
 
@@ -135,9 +135,9 @@
             top = rounded_top(jnp.max(score_ref[:, lanes], axis=0, keepdims=True))
             total = jnp.zeros((8, HD), F32)
             for row in range(0, BLK, 64):
-                weights = jnp.exp2(score_ref[row : row + 64, lanes] * SCALE - top)
-                weight_ref[row : row + 64, lanes] = weights.astype(BF16)
-                total = total + jnp.sum(weights.reshape(8, 8, HD), axis=0)
+                weights = jnp.exp2((score_ref[row : row + 64, lanes] * SCALE - top).astype(BF16))
+                weight_ref[row : row + 64, lanes] = weights
+                total = total + jnp.sum(weights.astype(F32).reshape(8, 8, HD), axis=0)
             tops.append(top)
             totals.append(jnp.sum(total, axis=0, keepdims=True))
         sums[number] = jnp.concatenate(tops, axis=1), jnp.concatenate(totals, axis=1)
@@ -310,7 +310,7 @@
         in_specs=[vmem] * (len(parts) + len(weights)),
         out_specs=vmem,
         out_shape=jax.ShapeDtypeStruct((parts[0].shape[1], weights[0].shape[1]), BF16),
-        compiler_params=pltpu.CompilerParams(vmem_limit_bytes=24 << 20),
+        compiler_params=pltpu.CompilerParams(vmem_limit_bytes=VMEM_BYTES),
         name="project",
     )(*parts, *weights)
 
@@ -362,22 +362,24 @@
     x3_low, x3_high = shift(x1_low, 0, 1), shift(x2_high, 0, -1)
     ring_arrays = [low, high, x1_low, x1_high, x2_low, x2_high, x3_low, x3_high]
 
+    core, chip = head % 2, head // 2
+    queries_core = swap(after(queries, low), 1)
+    near_queries = after([queries, queries_core], *ring_arrays[2:6])
+    near_state = near(
+        jnp.stack([kv, core]).astype(jnp.int32), near_queries, span_keys, span_values
+    )
     queries_early, picks_early, weight_early = after(
-        (queries, block_picks, out_weight), x1_low, x2_low
-    )
-    queries_pair = [queries, swap(queries_early, 2)]
+        (queries, block_picks, out_weight), *ring_arrays[2:6]
+    )
+    queries_chip = swap(queries_early, 2)
     picks_pair = jnp.stack([block_picks, swap(picks_early, 2)])
     weights = [out_weight] + [None] * (heads - 1)
     for bits in range(2, heads, 2):
         weights[bits] = swap(weight_early, bits)
-    queries_pair, picks_pair, weights[::2] = after(
-        (queries_pair, picks_pair, weights[::2]), *ring_arrays
-    )
-    group_queries = [queries, swap(queries_pair[0], 1), queries_pair[1], swap(queries_pair[1], 1)]
-    core, chip = head % 2, head // 2
-    near_state = near(
-        jnp.stack([kv, core]).astype(jnp.int32), group_queries[:2], span_keys, span_values
-    )
+    queries_chip, picks_pair, weights[::2] = after(
+        (queries_chip, picks_pair, weights[::2]), *ring_arrays
+    )
+    group_queries = [queries, queries_core, queries_chip, swap(queries_chip, 1)]
     picks_core = swap(picks_pair, 1)
     group_picks = [picks_pair[0], picks_core[0], picks_pair[1], picks_core[1]]
     for bits in range(0, heads, 2):

time: 200 us -> 199 us (level)
  waiting for transfers between devices: 94.7 us -> 88.8 us
  local copies, waits for them, and re-layouts: 4.46 us -> 7.25 us
    all_gather x1, waiting for transfers between devices: 12.6 us -> 36.7 us  [body(): whole = lax.all_gather(cut(0, share - RING_ROWS), 'ctx', axis=0, tiled=True)]
    ppermute x14, waiting for transfers between devices: 47.5 us -> 27.2 us  [shift(): return lax.ppermute(array, 'ctx', pairs)]
    ppermute x20, waiting for transfers between devices: 34.6 us -> 24.8 us  [swap(): lax.ppermute(array, 'head', [(h, h ^ bits) for h in range(lax.axis_size('...]
    ppermute x20, starting transfers between devices: 22.8 us -> 26.2 us  [swap(): lax.ppermute(array, 'head', [(h, h ^ bits) for h in range(lax.axis_size('...]
    ppermute x14, starting transfers between devices: 25.1 us -> 21.9 us  [shift(): return lax.ppermute(array, 'ctx', pairs)]
    unnamed x20 -> x40, local copies, waits for them, and re-layouts: 1.02 us -> 3.89 us
  transfers between devices with their start and end apart: 35 -> 35, of which waited for: 22 -> 16; matrix products, arithmetic and copies ran while one was open for 2% -> 2% of each run, Pallas kernels for 10% -> 10%
where the time goes in v9:
time: 199 us; the launch traced here: 198 us
  waiting for transfers between devices  88.8 us (45%)
  starting transfers between devices  48.2 us (24%)
  Pallas kernels  36.9 us (19%)
  between operations  14.4 us (7%)
  local copies, waits for them, and re-layouts  7.25 us (4%)
  other arithmetic  2.91 us (1%)
    all_gather x1, waiting for transfers between devices, body(): whole = lax.all_gather(cut(0, share - RING_ROWS), 'ctx', axis=0, tiled=True)  36.7 us
    ppermute x14, waiting for transfers between devices, shift(): return lax.ppermute(array, 'ctx', pairs)  27.2 us
    ppermute x20, starting transfers between devices, swap(): lax.ppermute(array, 'head', [(h, h ^ bits) for h in range(lax.axis_size('...  26.2 us
    ppermute x20, waiting for transfers between devices, swap(): lax.ppermute(array, 'head', [(h, h ^ bits) for h in range(lax.axis_size('...  24.8 us
    ppermute x14, starting transfers between devices, shift(): return lax.ppermute(array, 'ctx', pairs)  21.9 us
    pallas_call x2, Pallas kernels, far(): pl.pallas_call(functools.partial(far_kernel, half=half), in_specs=[pl.Blo...  13.5 us
    pallas_call x1, Pallas kernels, near(): pl.pallas_call(near_kernel, grid_spec=grid_spec, out_shape=[jax.ShapeDtyp...  6.65 us
    pallas_call x1, Pallas kernels, project(): pl.pallas_call(project_kernel, in_specs=[vmem] * (len(parts) + len(weight...  4.59 us
  transfers between devices with their start and end apart: 35, of which 16 were waited for; matrix products, arithmetic and copies ran while one was open for 2% of the time, Pallas kernels for 10%

profile of v9, /device:TPU:1, one launch (start us, length us, event | category | flops | bytes accessed | tf_op | source)
XLA Modules:
  0.0 198.4 jit_solution(13272447873286071796)
XLA Ops:
  10.1 6.5 %collective-permute-start.1 = (bf16[8,2,32,128]{3,2,1,0:T(8,128)(2,1)S(1)}, bf16[8,2,32,128]{3,2,1,0:T(8,128)(2,1)S(1)}, u32[]{:S(2)}, u32[]{:S(2)}) collective-permute-start(bf16[8,2,32,128]{3,2,1,0:T(8,128)(2,1)S(1)} %pad_maximum_fusion.2), channel_id=1, source_target_pairs={{0,224},{8,232},{16,240},{24,248},{32,0},{40,8},{48,16},{56,24},{6... | collective-permute-start | bytes 393224 | tf_op jit(solution)/shard_map/ppermute | solution.py:323
  18.7 3.4 %collective-permute-start.4 = (bf16[8,2,32,128]{3,2,1,0:T(8,128)(2,1)S(1)}, bf16[8,2,32,128]{3,2,1,0:T(8,128)(2,1)S(1)}, u32[]{:S(2)}, u32[]{:S(2)}) collective-permute-start(bf16[8,2,32,128]{3,2,1,0:T(8,128)(2,1)S(1)} %collective-permute-done.1), channel_id=1, source_target_pairs={{0,224},{8,232},{16,240},{24,248},{32,0},{40,8},{48,16},{56,24},{6... | collective-permute-start | bytes 393224 | tf_op jit(solution)/shard_map/ppermute | solution.py:323
  24.1 3.1 %collective-permute-start.6 = (bf16[8,2,32,128]{3,2,1,0:T(8,128)(2,1)S(1)}, bf16[8,2,32,128]{3,2,1,0:T(8,128)(2,1)S(1)}, u32[]{:S(2)}, u32[]{:S(2)}) collective-permute-start(bf16[8,2,32,128]{3,2,1,0:T(8,128)(2,1)S(1)} %collective-permute-done.4), channel_id=1, source_target_pairs={{0,224},{8,232},{16,240},{24,248},{32,0},{40,8},{48,16},{56,24},{6... | collective-permute-start | bytes 393224 | tf_op jit(solution)/shard_map/ppermute | solution.py:323
  27.2 2.6 %collective-permute-start.10 = (bf16[32,2,32,128]{3,2,1,0:T(8,128)(2,1)S(1)}, bf16[32,2,32,128]{3,2,1,0:T(8,128)(2,1)S(1)}, u32[]{:S(2)}, u32[]{:S(2)}) collective-permute-start(bf16[32,2,32,128]{3,2,1,0:T(8,128)(2,1)S(1)} %pad_maximum_fusion.refs_0_), channel_id=1, source_target_pairs={{0,24},{8,0},{16,8},{24,16},{32,56},{40,32},{48,40},{56,48},{64,88... | collective-permute-start | bytes 1572872 | tf_op jit(solution)/shard_map/ppermute | solution.py:323
  30.8 3.5 %collective-permute-start.8 = (bf16[4,2,32,128]{3,2,1,0:T(8,128)(2,1)S(1)}, bf16[4,2,32,128]{3,2,1,0:T(8,128)(2,1)S(1)}, u32[]{:S(2)}, u32[]{:S(2)}) collective-permute-start(bf16[4,2,32,128]{3,2,1,0:T(8,128)(2,1)S(1)} %slice.25), channel_id=1, source_target_pairs={{0,224},{8,232},{16,240},{24,248},{32,0},{40,8},{48,16},{56,24},{6... | collective-permute-start | bytes 196616 | tf_op jit(solution)/shard_map/ppermute | solution.py:323
  34.5 5.1 %collective-permute-done.7 = bf16[4,2,32,128]{3,2,1,0:T(8,128)(2,1)S(1)} collective-permute-done((bf16[4,2,32,128]{3,2,1,0:T(8,128)(2,1)S(1)}, bf16[4,2,32,128]{3,2,1,0:T(8,128)(2,1)S(1)}, u32[]{:S(2)}, u32[]{:S(2)}) %collective-permute-start.7) | collective-permute-done | bytes 65568 | tf_op jit(solution)/shard_map/ppermute | solution.py:323
  39.7 2.3 %collective-permute-start.11 = (bf16[32,2,32,128]{3,2,1,0:T(8,128)(2,1)S(1)}, bf16[32,2,32,128]{3,2,1,0:T(8,128)(2,1)S(1)}, u32[]{:S(2)}, u32[]{:S(2)}) collective-permute-start(bf16[32,2,32,128]{3,2,1,0:T(8,128)(2,1)S(1)} %constant_dynamic-update-slice_fusion.refs_1_), channel_id=1, source_target_pairs={{0,24},{8,0},{16,8},{24,16},{32,56},{40,32},{48,40},{56,48},{64,88... | collective-permute-start | bytes 1572872 | tf_op jit(solution)/shard_map/ppermute | solution.py:323
  42.0 4.4 %collective-permute-start.20 = (bf16[2048,128]{1,0:T(8,128)(2,1)}, bf16[2048,128]{1,0:T(8,128)(2,1)S(1)}, u32[]{:S(2)}, u32[]{:S(2)}) collective-permute-start(bf16[2048,128]{1,0:T(8,128)(2,1)} %refs_0_.1), channel_id=1, source_target_pairs={{0,1},{1,0},{2,3},{3,2},{4,5},{5,4},{6,7},{7,6},{8,9},{9,8},{10,11... | collective-permute-start | bytes 1572872 | tf_op jit(solution)/shard_map/ppermute | solution.py:327
  46.5 11.1 %collective-permute-done.11.refs_5_ = bf16[32,2,32,128]{3,2,1,0:T(8,128)(2,1)S(1)} collective-permute-done((bf16[32,2,32,128]{3,2,1,0:T(8,128)(2,1)S(1)}, bf16[32,2,32,128]{3,2,1,0:T(8,128)(2,1)S(1)}, u32[]{:S(2)}, u32[]{:S(2)}) %collective-permute-start.11) | collective-permute-done | bytes 524320 | tf_op jit(solution)/shard_map/ppermute | solution.py:323
  59.3 3.0 %collective-permute-start.16 = (bf16[128,2048]{1,0:T(8,128)(2,1)}, bf16[128,2048]{1,0:T(8,128)(2,1)}, u32[]{:S(2)}, u32[]{:S(2)}) collective-permute-start(bf16[128,2048]{1,0:T(8,128)(2,1)} %refs_4_), channel_id=1, source_target_pairs={{0,6},{1,7},{2,4},{3,5},{4,2},{5,3},{6,0},{7,1},{8,14},{9,15},{10,... | collective-permute-start | bytes 1572872 | tf_op jit(solution)/shard_map/ppermute | solution.py:327
  63.3 5.6 %collective-permute-done.17.refs_6_ = bf16[32,2,32,128]{3,2,1,0:T(8,128)(2,1)S(1)} collective-permute-done((bf16[32,2,32,128]{3,2,1,0:T(8,128)(2,1)S(1)}, bf16[32,2,32,128]{3,2,1,0:T(8,128)(2,1)S(1)}, u32[]{:S(2)}, u32[]{:S(2)}) %collective-permute-start.17) | collective-permute-done | bytes 524320 | tf_op jit(solution)/shard_map/ppermute | solution.py:323
  71.6 6.7 %near.1 = (f32[4,2,128,256]{3,2,1,0:T(8,128)}, f32[4,2,1,256]{3,2,1,0:T(1,128)}, f32[4,2,1,256]{3,2,1,0:T(1,128)}) custom-call(s32[2]{0:T(128)} %pad_add_fusion.2.place_ref, bf16[2048,128]{1,0:T(8,128)(2,1)} %refs_0_.1, bf16[2048,128]{1,0:T(8,128)(2,1)} %copy-done.9, bf16[2048,256]{1,0:T(8,128)(2,1)} %refs_2_.1, bf16[2048,256]{1,0:T(8,128)(2,1)} %refs_3_.1), custom_call_target="tpu_custom_call" | custom-call | flops 536870912 | bytes 4194304 | tf_op jit(solution)/shard_map/near/pallas_call | solution.py:66
  79.7 9.9 %collective-permute-done.14.refs_6_ = bf16[128,2048]{1,0:T(8,128)(2,1)} collective-permute-done((bf16[128,2048]{1,0:T(8,128)(2,1)}, bf16[128,2048]{1,0:T(8,128)(2,1)}, u32[]{:S(2)}, u32[]{:S(2)}) %collective-permute-start.14) | collective-permute-done | bytes 524320 | tf_op jit(solution)/shard_map/ppermute | solution.py:327
  89.9 6.6 %collective-permute-start.19 = (s32[2,4,1,4]{3,1,2,0:T(4,128)S(1)}, s32[2,4,1,4]{3,1,2,0:T(4,128)S(1)}, u32[]{:S(2)}, u32[]{:S(2)}) collective-permute-start(s32[2,4,1,4]{3,1,2,0:T(4,128)S(1)} %pad_add_fusion), channel_id=1, source_target_pairs={{0,1},{1,0},{2,3},{3,2},{4,5},{5,4},{6,7},{7,6},{8,9},{9,8},{10,11... | collective-permute-start | bytes 392 | tf_op jit(solution)/shard_map/ppermute | solution.py:327
  98.9 4.0 %collect.1.refs_3_ = bf16[64,2,32,128]{3,2,1,0:T(8,128)(2,1)} custom-call(s32[64,2]{1,0:T(8,128)} %copy.13.where_ref, bf16[32,2,32,128]{3,2,1,0:T(8,128)(2,1)} %copy-done, bf16[32,2,32,128]{3,2,1,0:T(8,128)(2,1)} %copy-done.1, bf16[32,2,32,128]{3,2,1,0:T(8,128)(2,1)} %copy-done.5, bf16[32,2,32,128]{3,2,1,0:T(8,128)(2,1)} %copy-done.7, ...), custom_call_target="tpu_custom_call" | custom-call | tf_op jit(solution)/shard_map/collect/pallas_call | solution.py:204
  103.6 36.7 %all-gather.2.cloned.1.call-done.refs_2_ = bf16[256,2,96,128]{3,2,1,0:T(8,128)(2,1)} async-done(((bf16[8,2,96,128]{3,2,1,0:T(8,128)(2,1)}), bf16[256,2,96,128]{3,2,1,0:T(8,128)(2,1)}) %all-gather.2.cloned.1.call-update) | async-done | bytes 12582928 | tf_op jit(solution)/shard_map/all_gather | solution.py:350
  140.3 6.8 %far.2 = (bf16[8,144,256]{2,1,0:T(8,128)(2,1)}, bf16[8,144,256]{2,1,0:T(8,128)(2,1)}) custom-call(s32[33]{0:T(128)} %add_add_fusion.1.picks_ref, bf16[2048,128]{1,0:T(8,128)(2,1)} %collective-permute-done.12.refs_0_, bf16[2048,128]{1,0:T(8,128)(2,1)} %collective-permute-done.21.refs_1_, bf16[256,2,96,128]{3,2,1,0:T(8,128)(2,1)} %all-gather.2.cloned.1.call-done.refs_2_, ...), custom_call_target="tpu_custom_call" | custom-call | flops 8589934592 | bytes 5242880 | tf_op jit(solution)/shard_map/far/pallas_call | solution.py:163
  150.7 2.2 %merge_two.1 = (bf16[4,144,256]{2,1,0:T(8,128)(2,1)}, bf16[4,144,256]{2,1,0:T(8,128)(2,1)}) custom-call(bf16[8,144,256]{2,1,0:T(8,128)(2,1)} %get-tuple-element.77.a_ref, bf16[8,144,256]{2,1,0:T(8,128)(2,1)} %copy-done.2), custom_call_target="tpu_custom_call" | custom-call | tf_op jit(solution)/shard_map/merge_two/pallas_call | solution.py:233
  154.4 6.8 %far.3 = (bf16[8,144,256]{2,1,0:T(8,128)(2,1)}, bf16[8,144,256]{2,1,0:T(8,128)(2,1)}) custom-call(s32[33]{0:T(128)} %add_add_fusion.picks_ref, bf16[2048,128]{1,0:T(8,128)(2,1)} %refs_0_.1, bf16[2048,128]{1,0:T(8,128)(2,1)} %copy-done.9, bf16[256,2,96,128]{3,2,1,0:T(8,128)(2,1)} %all-gather.2.cloned.1.call-done.refs_2_, bf16[64,2,32,128]{3,2,1,0:T(8,128)(2,1)} %collect.1.refs_3_), custom_call_target="tpu_custom_call" | custom-call | flops 8589934592 | bytes 5242880 | tf_op jit(solution)/shard_map/far/pallas_call | solution.py:163
  161.3 6.3 %collective-permute-done.28.refs_1_ = bf16[4,144,256]{2,1,0:T(8,128)(2,1)S(1)} collective-permute-done((bf16[4,144,256]{2,1,0:T(8,128)(2,1)}, bf16[4,144,256]{2,1,0:T(8,128)(2,1)S(1)}, u32[]{:S(2)}, u32[]{:S(2)}) %collective-permute-start.28) | collective-permute-done | bytes 294944 | tf_op jit(solution)/shard_map/ppermute | solution.py:327
  171.5 4.1 %merge_last.1 = (bf16[4,256,128]{2,1,0:T(8,128)(2,1)}, bf16[4,256,128]{2,1,0:T(8,128)(2,1)}, bf16[2,256,128]{2,1,0:T(8,128)(2,1)}, bf16[2,256,128]{2,1,0:T(8,128...) custom-call(s32[1]{0:T(128)} %bitcast.1.chip_ref, bf16[8,144,256]{2,1,0:T(8,128)(2,1)} %get-tuple-element.84.a_ref, ...), custom_call_target="tpu_custom_call" | custom-call | tf_op jit(solution)/shard_map/merge_last/pallas_call | solution.py:266
  177.2 2.6 %collective-permute-start.33 = (bf16[2,256,128]{2,1,0:T(8,128)(2,1)}, bf16[2,256,128]{2,1,0:T(8,128)(2,1)S(1)}, u32[]{:S(2)}, u32[]{:S(2)}) collective-permute-start(bf16[2,256,128]{2,1,0:T(8,128)(2,1)} %get-tuple-element.95), channel_id=1, source_target_pairs={{0,6},{1,7},{2,4},{3,5},{4,2},{5,3},{6,0},{7,1},{8,14},{9,15},{10,... | collective-permute-start | bytes 393224 | tf_op jit(solution)/shard_map/ppermute | solution.py:327
  183.8 2.5 %collective-permute-done.33.refs_3_ = bf16[2,256,128]{2,1,0:T(8,128)(2,1)S(1)} collective-permute-done((bf16[2,256,128]{2,1,0:T(8,128)(2,1)}, bf16[2,256,128]{2,1,0:T(8,128)(2,1)S(1)}, u32[]{:S(2)}, u32[]{:S(2)}) %collective-permute-start.33) | collective-permute-done | bytes 131104 | tf_op jit(solution)/shard_map/ppermute | solution.py:327
  186.9 4.6 %project.1 = bf16[256,2048]{1,0:T(8,128)(2,1)} custom-call(bf16[2,256,128]{2,1,0:T(8,128)(2,1)} %get-tuple-element.96.refs_0_, bf16[2,256,128]{2,1,0:T(8,128)(2,1)} %copy-done.14, bf16[2,256,128]{2,1,0:T(8,128)(2,1)} %copy-done.15, bf16[2,256,128]{2,1,0:T(8,128)(2,1)} %copy-done.16, bf16[128,2048]{1,0:T(8,128)(2,1)} %refs_4_, bf16[128,2048]{1,0:T(8,128)(2,1)} %copy-done.10, ...), custom_call_target="tpu_custom_call" | custom-call | tf_op jit(solution)/shard_map/project/pallas_call | solution.py:308
  (122 shorter events, 33.9 us)
Async XLA Ops:
  7.2 133.1 %all-gather.2.cloned.1.call-start = ((), (), s32[]{:S(2)}) async-start(), calls=%async_computation | async-start | bytes 12976128 | tf_op jit(solution)/shard_map/all_gather | solution.py:350
  10.1 8.6 %collective-permute-start.1 = (bf16[8,2,32,128]{3,2,1,0:T(8,128)(2,1)S(1)}, bf16[8,2,32,128]{3,2,1,0:T(8,128)(2,1)S(1)}, u32[]{:S(2)}, u32[]{:S(2)}) collective-permute-start(bf16[8,2,32,128]{3,2,1,0:T(8,128)(2,1)S(1)} %pad_maximum_fusion.2), channel_id=1, source_target_pairs={{0,224},{8,232},{16,240},{24,248},{32,0},{40,8},{48,16},{56,24},{6... | collective-permute-start | bytes 393224 | tf_op jit(solution)/shard_map/ppermute | solution.py:323
  24.1 6.8 %collective-permute-start.6 = (bf16[8,2,32,128]{3,2,1,0:T(8,128)(2,1)S(1)}, bf16[8,2,32,128]{3,2,1,0:T(8,128)(2,1)S(1)}, u32[]{:S(2)}, u32[]{:S(2)}) collective-permute-start(bf16[8,2,32,128]{3,2,1,0:T(8,128)(2,1)S(1)} %collective-permute-done.4), channel_id=1, source_target_pairs={{0,224},{8,232},{16,240},{24,248},{32,0},{40,8},{48,16},{56,24},{6... | collective-permute-start | bytes 393224 | tf_op jit(solution)/shard_map/ppermute | solution.py:323
  27.2 7.2 %collective-permute-start.5 = (bf16[8,2,32,128]{3,2,1,0:T(8,128)(2,1)S(1)}, bf16[8,2,32,128]{3,2,1,0:T(8,128)(2,1)S(1)}, u32[]{:S(2)}, u32[]{:S(2)}) collective-permute-start(bf16[8,2,32,128]{3,2,1,0:T(8,128)(2,1)S(1)} %collective-permute-done.2), channel_id=1, source_target_pairs={{0,32},{8,40},{16,48},{24,56},{32,64},{40,72},{48,80},{56,88},{64,... | collective-permute-start | bytes 393224 | tf_op jit(solution)/shard_map/ppermute | solution.py:323
  27.2 19.2 %collective-permute-start.10 = (bf16[32,2,32,128]{3,2,1,0:T(8,128)(2,1)S(1)}, bf16[32,2,32,128]{3,2,1,0:T(8,128)(2,1)S(1)}, u32[]{:S(2)}, u32[]{:S(2)}) collective-permute-start(bf16[32,2,32,128]{3,2,1,0:T(8,128)(2,1)S(1)} %pad_maximum_fusion.refs_0_), channel_id=1, source_target_pairs={{0,24},{8,0},{16,8},{24,16},{32,56},{40,32},{48,40},{56,48},{64,88... | collective-permute-start | bytes 1572872 | tf_op jit(solution)/shard_map/ppermute | solution.py:323
  29.8 16.6 %collective-permute-start.3 = (bf16[32,2,32,128]{3,2,1,0:T(8,128)(2,1)S(1)}, bf16[32,2,32,128]{3,2,1,0:T(8,128)(2,1)S(1)}, u32[]{:S(2)}, u32[]{:S(2)}) collective-permute-start(bf16[32,2,32,128]{3,2,1,0:T(8,128)(2,1)S(1)} %pad_maximum_fusion.refs_0_), channel_id=1, source_target_pairs={{0,8},{8,16},{16,24},{24,0},{32,40},{40,48},{48,56},{56,32},{64,72... | collective-permute-start | bytes 1572872 | tf_op jit(solution)/shard_map/ppermute | solution.py:323
  30.8 8.8 %collective-permute-start.8 = (bf16[4,2,32,128]{3,2,1,0:T(8,128)(2,1)S(1)}, bf16[4,2,32,128]{3,2,1,0:T(8,128)(2,1)S(1)}, u32[]{:S(2)}, u32[]{:S(2)}) collective-permute-start(bf16[4,2,32,128]{3,2,1,0:T(8,128)(2,1)S(1)} %slice.25), channel_id=1, source_target_pairs={{0,224},{8,232},{16,240},{24,248},{32,0},{40,8},{48,16},{56,24},{6... | collective-permute-start | bytes 196616 | tf_op jit(solution)/shard_map/ppermute | solution.py:323
  39.7 17.8 %collective-permute-start.11 = (bf16[32,2,32,128]{3,2,1,0:T(8,128)(2,1)S(1)}, bf16[32,2,32,128]{3,2,1,0:T(8,128)(2,1)S(1)}, u32[]{:S(2)}, u32[]{:S(2)}) collective-permute-start(bf16[32,2,32,128]{3,2,1,0:T(8,128)(2,1)S(1)} %constant_dynamic-update-slice_fusion.refs_1_), channel_id=1, source_target_pairs={{0,24},{8,0},{16,8},{24,16},{32,56},{40,32},{48,40},{56,48},{64,88... | collective-permute-start | bytes 1572872 | tf_op jit(solution)/shard_map/ppermute | solution.py:323
  42.0 15.8 %collective-permute-start.9 = (bf16[32,2,32,128]{3,2,1,0:T(8,128)(2,1)S(1)}, bf16[32,2,32,128]{3,2,1,0:T(8,128)(2,1)S(1)}, u32[]{:S(2)}, u32[]{:S(2)}) collective-permute-start(bf16[32,2,32,128]{3,2,1,0:T(8,128)(2,1)S(1)} %constant_dynamic-update-slice_fusion.refs_1_), channel_id=1, source_target_pairs={{0,8},{8,16},{16,24},{24,0},{32,40},{40,48},{48,56},{56,32},{64,72... | collective-permute-start | bytes 1572872 | tf_op jit(solution)/shard_map/ppermute | solution.py:323
  42.0 20.3 %collective-permute-start.20 = (bf16[2048,128]{1,0:T(8,128)(2,1)}, bf16[2048,128]{1,0:T(8,128)(2,1)S(1)}, u32[]{:S(2)}, u32[]{:S(2)}) collective-permute-start(bf16[2048,128]{1,0:T(8,128)(2,1)} %refs_0_.1), channel_id=1, source_target_pairs={{0,1},{1,0},{2,3},{3,2},{4,5},{5,4},{6,7},{7,6},{8,9},{9,8},{10,11... | collective-permute-start | bytes 1572872 | tf_op jit(solution)/shard_map/ppermute | solution.py:327
  46.4 22.5 %collective-permute-start.17 = (bf16[32,2,32,128]{3,2,1,0:T(8,128)(2,1)S(1)}, bf16[32,2,32,128]{3,2,1,0:T(8,128)(2,1)S(1)}, u32[]{:S(2)}, u32[]{:S(2)}) collective-permute-start(bf16[32,2,32,128]{3,2,1,0:T(8,128)(2,1)S(1)} %collective-permute-done.3.refs_2_), channel_id=1, source_target_pairs={{0,8},{8,16},{16,24},{24,0},{32,40},{40,48},{48,56},{56,32},{64,72... | collective-permute-start | bytes 1572872 | tf_op jit(solution)/shard_map/ppermute | solution.py:323
  59.0 19.3 %collective-permute-start.12 = (bf16[2048,128]{1,0:T(8,128)(2,1)}, bf16[2048,128]{1,0:T(8,128)(2,1)}, u32[]{:S(2)}, u32[]{:S(2)}) collective-permute-start(bf16[2048,128]{1,0:T(8,128)(2,1)} %refs_0_.1), channel_id=1, source_target_pairs={{0,2},{1,3},{2,0},{3,1},{4,6},{5,7},{6,4},{7,5},{8,10},{9,11},{10,... | collective-permute-start | bytes 1572872 | tf_op jit(solution)/shard_map/ppermute | solution.py:327
  59.3 19.0 %collective-permute-start.16 = (bf16[128,2048]{1,0:T(8,128)(2,1)}, bf16[128,2048]{1,0:T(8,128)(2,1)}, u32[]{:S(2)}, u32[]{:S(2)}) collective-permute-start(bf16[128,2048]{1,0:T(8,128)(2,1)} %refs_4_), channel_id=1, source_target_pairs={{0,6},{1,7},{2,4},{3,5},{4,2},{5,3},{6,0},{7,1},{8,14},{9,15},{10,... | collective-permute-start | bytes 1572872 | tf_op jit(solution)/shard_map/ppermute | solution.py:327
  62.3 16.0 %collective-permute-start.18 = (bf16[32,2,32,128]{3,2,1,0:T(8,128)(2,1)S(1)}, bf16[32,2,32,128]{3,2,1,0:T(8,128)(2,1)}, u32[]{:S(2)}, u32[]{:S(2)}) collective-permute-start(bf16[32,2,32,128]{3,2,1,0:T(8,128)(2,1)S(1)} %collective-permute-done.11.refs_5_), channel_id=1, source_target_pairs={{0,24},{8,0},{16,8},{24,16},{32,56},{40,32},{48,40},{56,48},{64,88... | collective-permute-start | bytes 1572872 | tf_op jit(solution)/shard_map/ppermute | solution.py:323
  62.8 16.9 %collective-permute-start.15 = (bf16[128,2048]{1,0:T(8,128)(2,1)}, bf16[128,2048]{1,0:T(8,128)(2,1)}, u32[]{:S(2)}, u32[]{:S(2)}) collective-permute-start(bf16[128,2048]{1,0:T(8,128)(2,1)} %refs_4_), channel_id=1, source_target_pairs={{0,4},{1,5},{2,6},{3,7},{4,0},{5,1},{6,2},{7,3},{8,12},{9,13},{10,... | collective-permute-start | bytes 1572872 | tf_op jit(solution)/shard_map/ppermute | solution.py:327
  69.8 19.8 %collective-permute-start.14 = (bf16[128,2048]{1,0:T(8,128)(2,1)}, bf16[128,2048]{1,0:T(8,128)(2,1)}, u32[]{:S(2)}, u32[]{:S(2)}) collective-permute-start(bf16[128,2048]{1,0:T(8,128)(2,1)} %refs_4_), channel_id=1, source_target_pairs={{0,2},{1,3},{2,0},{3,1},{4,6},{5,7},{6,4},{7,5},{8,10},{9,11},{10,... | collective-permute-start | bytes 1572872 | tf_op jit(solution)/shard_map/ppermute | solution.py:327
  89.9 7.6 %collective-permute-start.19 = (s32[2,4,1,4]{3,1,2,0:T(4,128)S(1)}, s32[2,4,1,4]{3,1,2,0:T(4,128)S(1)}, u32[]{:S(2)}, u32[]{:S(2)}) collective-permute-start(s32[2,4,1,4]{3,1,2,0:T(4,128)S(1)} %pad_add_fusion), channel_id=1, source_target_pairs={{0,1},{1,0},{2,3},{3,2},{4,5},{5,4},{6,7},{7,6},{8,9},{9,8},{10,11... | collective-permute-start | bytes 392 | tf_op jit(solution)/shard_map/ppermute | solution.py:327
  96.5 6.4 %collective-permute-start.21 = (bf16[2048,128]{1,0:T(8,128)(2,1)}, bf16[2048,128]{1,0:T(8,128)(2,1)}, u32[]{:S(2)}, u32[]{:S(2)}) collective-permute-start(bf16[2048,128]{1,0:T(8,128)(2,1)} %collective-permute-done.12.refs_0_), channel_id=1, source_target_pairs={{0,1},{1,0},{2,3},{3,2},{4,5},{5,4},{6,7},{7,6},{8,9},{9,8},{10,11... | collective-permute-start | bytes 1572872 | tf_op jit(solution)/shard_map/ppermute | solution.py:327
  96.6 6.3 %collective-permute-start.22 = (bf16[128,2048]{1,0:T(8,128)(2,1)}, bf16[128,2048]{1,0:T(8,128)(2,1)S(1)}, u32[]{:S(2)}, u32[]{:S(2)}) collective-permute-start(bf16[128,2048]{1,0:T(8,128)(2,1)} %refs_4_), channel_id=1, source_target_pairs={{0,1},{1,0},{2,3},{3,2},{4,5},{5,4},{6,7},{7,6},{8,9},{9,8},{10,11... | collective-permute-start | bytes 1572872 | tf_op jit(solution)/shard_map/ppermute | solution.py:327
  152.9 8.4 %collective-permute-start.27 = (bf16[4,144,256]{2,1,0:T(8,128)(2,1)}, bf16[4,144,256]{2,1,0:T(8,128)(2,1)S(1)}, u32[]{:S(2)}, u32[]{:S(2)}) collective-permute-start(bf16[4,144,256]{2,1,0:T(8,128)(2,1)} %get-tuple-element.79), channel_id=1, source_target_pairs={{0,2},{1,3},{2,0},{3,1},{4,6},{5,7},{6,4},{7,5},{8,10},{9,11},{10,... | collective-permute-start | bytes 884744 | tf_op jit(solution)/shard_map/ppermute | solution.py:327
  152.9 14.7 %collective-permute-start.28 = (bf16[4,144,256]{2,1,0:T(8,128)(2,1)}, bf16[4,144,256]{2,1,0:T(8,128)(2,1)S(1)}, u32[]{:S(2)}, u32[]{:S(2)}) collective-permute-start(bf16[4,144,256]{2,1,0:T(8,128)(2,1)} %get-tuple-element.80), channel_id=1, source_target_pairs={{0,2},{1,3},{2,0},{3,1},{4,6},{5,7},{6,4},{7,5},{8,10},{9,11},{10,... | collective-permute-start | bytes 884744 | tf_op jit(solution)/shard_map/ppermute | solution.py:327
  176.0 6.4 %collective-permute-start.31 = (bf16[2,256,128]{2,1,0:T(8,128)(2,1)}, bf16[2,256,128]{2,1,0:T(8,128)(2,1)S(1)}, u32[]{:S(2)}, u32[]{:S(2)}) collective-permute-start(bf16[2,256,128]{2,1,0:T(8,128)(2,1)} %get-tuple-element.93), channel_id=1, source_target_pairs={{0,2},{1,3},{2,0},{3,1},{4,6},{5,7},{6,4},{7,5},{8,10},{9,11},{10,... | collective-permute-start | bytes 393224 | tf_op jit(solution)/shard_map/ppermute | solution.py:327
  176.0 7.8 %collective-permute-start.32 = (bf16[2,256,128]{2,1,0:T(8,128)(2,1)}, bf16[2,256,128]{2,1,0:T(8,128)(2,1)S(1)}, u32[]{:S(2)}, u32[]{:S(2)}) collective-permute-start(bf16[2,256,128]{2,1,0:T(8,128)(2,1)} %get-tuple-element.94), channel_id=1, source_target_pairs={{0,4},{1,5},{2,6},{3,7},{4,0},{5,1},{6,2},{7,3},{8,12},{9,13},{10,... | collective-permute-start | bytes 393224 | tf_op jit(solution)/shard_map/ppermute | solution.py:327
  177.2 9.1 %collective-permute-start.33 = (bf16[2,256,128]{2,1,0:T(8,128)(2,1)}, bf16[2,256,128]{2,1,0:T(8,128)(2,1)S(1)}, u32[]{:S(2)}, u32[]{:S(2)}) collective-permute-start(bf16[2,256,128]{2,1,0:T(8,128)(2,1)} %get-tuple-element.95), channel_id=1, source_target_pairs={{0,6},{1,7},{2,4},{3,5},{4,2},{5,3},{6,0},{7,1},{8,14},{9,15},{10,... | collective-permute-start | bytes 393224 | tf_op jit(solution)/shard_map/ppermute | solution.py:327
  (29 other events, 473.7 us)
Sparse Core Ops, SparseCore 0:
  10.6 129.6 all-gather.1

commit v10 on v9

--- a/solution.py
+++ b/solution.py
@@ -92,6 +92,27 @@
     return ref[i, :HD, :].astype(F32), tail[0:1], tail[1:2] + tail[2:3]
 
 
+def scale_kernel(*refs):
+    count = len(refs) // 2
+    for q_ref, out_ref in zip(refs[:count], refs[count:]):
+        scaled = q_ref[...].astype(F32) * SCALE
+        high = scaled.astype(BF16)
+        out_ref[:, :HD] = high
+        out_ref[:, HD:] = (scaled - high.astype(F32)).astype(BF16)
+
+
+def scale(queries):
+    count = len(queries)
+    return pl.pallas_call(
+        scale_kernel,
+        grid=(QB,),
+        in_specs=[pl.BlockSpec((BLK, HD), lambda i: (i, 0))] * count,
+        out_specs=[pl.BlockSpec((BLK, 2 * HD), lambda i: (i, 0))] * count,
+        out_shape=[jax.ShapeDtypeStruct((QB * BLK, 2 * HD), BF16)] * count,
+        name="scale",
+    )(*queries)
+
+
 def far_kernel(picks_ref, *refs, half):
     q_refs, whole_ref, early_ref, refs = refs[:2], refs[2], refs[3], refs[4:]
     out_refs, (buffer, early), refs = refs[:2], refs[2:4], refs[4:]
@@ -125,19 +146,21 @@
             fetched(SEL, picks - SEL, sems.at[2])
         first = row % QB * BLK + (picks_ref[picks] ^ k) * HALF
         tokens = pl.ds(pl.multiple_of(first, HALF), HALF)
-        score_refs[number % 2][...] = dot_nt(joined(row, 0), q_refs[row // QB][tokens, :])
+        keys = joined(row, 0)
+        twice = jnp.concatenate([keys, keys], axis=1)
+        score_refs[number % 2][...] = dot_nt(twice, q_refs[row // QB][tokens, :])
 
     def soften(number):
         score_ref, weight_ref = score_refs[number % 2], weight_refs[number % 2]
         tops, totals = [], []
         for lane in range(0, HALF, HD):
             lanes = slice(lane, lane + HD)
-            top = rounded_top(jnp.max(score_ref[:, lanes], axis=0, keepdims=True))
+            top = jnp.max(score_ref[:, lanes], axis=0, keepdims=True).astype(BF16).astype(F32)
             total = jnp.zeros((8, HD), F32)
             for row in range(0, BLK, 64):
-                weights = jnp.exp2((score_ref[row : row + 64, lanes] * SCALE - top).astype(BF16))
-                weight_ref[row : row + 64, lanes] = weights
-                total = total + jnp.sum(weights.astype(F32).reshape(8, 8, HD), axis=0)
+                weights = jnp.exp2(score_ref[row : row + 64, lanes] - top)
+                weight_ref[row : row + 64, lanes] = weights.astype(BF16)
+                total = total + jnp.sum(weights.reshape(8, 8, HD), axis=0)
             tops.append(top)
             totals.append(jnp.sum(total, axis=0, keepdims=True))
         sums[number] = jnp.concatenate(tops, axis=1), jnp.concatenate(totals, axis=1)
@@ -239,12 +262,38 @@
     )(mine, other)
 
 
+def merge_chip_kernel(acc_ref, m_ref, l_ref, *refs):
+    chip_refs, (acc_out, m_out, l_out) = refs[:2], refs[2:]
+    for row in range(2 * QB):
+        r, i = row // QB, row % QB
+        acc, m, l = unpack_state(chip_refs[r], i)
+        top = jnp.maximum(m, m_ref[i, r])
+        f_chip = jnp.exp2(m - top)
+        f_near = jnp.exp2(m_ref[i, r] - top)
+        m_out[i, r] = top
+        l_out[i, r] = f_chip * l + f_near * l_ref[i, r]
+        acc_out[i, r] = f_chip * acc + f_near * acc_ref[i, r]
+
+
+def merge_chip(near_state, chip_parts):
+    vmem = pl.BlockSpec(memory_space=pltpu.VMEM)
+    return pl.pallas_call(
+        merge_chip_kernel,
+        in_specs=[vmem] * 5,
+        out_specs=[vmem] * 3,
+        out_shape=[jax.ShapeDtypeStruct(array.shape, F32) for array in near_state],
+        cost_estimate=pl.CostEstimate(
+            flops=8 * QB * 4 * BLK * BLK * HD, bytes_accessed=4 << 20, transcendentals=8 * BLK
+        ),
+        name="merge_chip",
+    )(*near_state, *chip_parts)
+
+
 def merge_last_kernel(chip_ref, a_ref, b_ref, acc_ref, m_ref, l_ref, *refs):
-    chip_refs, half_refs, share_refs = refs[:2], refs[2:4], refs[4:]
+    half_refs, share_refs = refs[:2], refs[2:]
     for row in range(2 * QB):
         r, i = row // QB, row % QB
         states = [unpack_state(a_ref, row), unpack_state(b_ref, crossed(row))]
-        states.append(unpack_state(chip_refs[r], i))
         states.append((acc_ref[i, r], m_ref[i, r], l_ref[i, r]))
         top = functools.reduce(jnp.maximum, [m for _, m, _ in states])
         factors = [jnp.exp2(m - top) for _, m, _ in states]
@@ -260,9 +309,9 @@
             pl.when(chip_ref[0] ^ n == i)(keep)
 
 
-def merge_last(chip, mine, core_part, near_state, chip_parts):
-    vmem = pl.BlockSpec(memory_space=pltpu.VMEM)
-    arrays = [mine, core_part, *near_state, *chip_parts]
+def merge_last(chip, mine, core_part, other_state):
+    vmem = pl.BlockSpec(memory_space=pltpu.VMEM)
+    arrays = [mine, core_part, *other_state]
     own, other, *shares = pl.pallas_call(
         merge_last_kernel,
         in_specs=[pl.BlockSpec(memory_space=pltpu.SMEM)] + [vmem] * len(arrays),
@@ -310,7 +359,7 @@
         in_specs=[vmem] * (len(parts) + len(weights)),
         out_specs=vmem,
         out_shape=jax.ShapeDtypeStruct((parts[0].shape[1], weights[0].shape[1]), BF16),
-        compiler_params=pltpu.CompilerParams(vmem_limit_bytes=VMEM_BYTES),
+        compiler_params=pltpu.CompilerParams(vmem_limit_bytes=24 << 20),
         name="project",
     )(*parts, *weights)
 
@@ -399,7 +448,7 @@
     early = collect(where.astype(jnp.int32), ring_arrays)
 
     picks, group_queries, weights, near_state, early = lax.optimization_barrier(
-        (picks, group_queries, weights, near_state, early)
+        (picks, scale(group_queries), weights, near_state, early)
     )
 
     def far_of(first, second, earlier, half):
@@ -415,8 +464,9 @@
     for_chip = merge_two(chip_here, swap(chip_there, 1))
     chip_parts = [swap(piece, 2) for piece in for_chip]
     own_here, own_there = far_of(0, 1, for_chip, 1)
-    core_part = swap(after(own_there, *chip_parts), 1)
-    own, other, shares = merge_last(chip[None], own_here, core_part, near_state, chip_parts)
+    core_part = swap(own_there, 1)
+    other_state = merge_chip(near_state, chip_parts)
+    own, other, shares = merge_last(chip[None], own_here, core_part, other_state)
     parts = [shares[0]] + [swap(shares[n], 2 * n) for n in range(1, QB)]
     attention = assemble(core[None], own, swap(other, 1))
     return attention, project(after(parts, attention), weights)

time: 199 us -> 203 us (1.020)
  Pallas kernels: 36.9 us -> 42.5 us
  starting transfers between devices: 48.2 us -> 52.6 us
  waiting for transfers between devices: 88.8 us -> 84.8 us
  local copies, waits for them, and re-layouts: 7.25 us -> 5.16 us
    all_gather x1, waiting for transfers between devices: 36.7 us -> 17.1 us  [body(): whole = lax.all_gather(cut(0, share - RING_ROWS), 'ctx', axis=0, tiled=True)]
    ppermute x20, waiting for transfers between devices: 24.8 us -> 34.5 us  [swap(): lax.ppermute(array, 'head', [(h, h ^ bits) for h in range(lax.axis_size('...]
    pallas_call x0 -> x2, Pallas kernels: none -> 7.02 us  [the longest x1 4.47 us: scale(): pl.pallas_call(scale_kernel, grid=(QB,), in_specs=[pl.BlockSpec((BLK, HD)...]
    ppermute x14, waiting for transfers between devices: 27.2 us -> 33.2 us  [shift(): return lax.ppermute(array, 'ctx', pairs)]
    ppermute x20, starting transfers between devices: 26.2 us -> 31.5 us  [swap(): lax.ppermute(array, 'head', [(h, h ^ bits) for h in range(lax.axis_size('...]
    unnamed x40 -> x28, local copies, waits for them, and re-layouts: 3.89 us -> 1.81 us
  transfers between devices with their start and end apart: 35 -> 35, of which waited for: 16 -> 16; matrix products, arithmetic and copies ran while one was open for 2% -> 2% of each run, Pallas kernels for 10% -> 13%
where the time goes in v10:
time: 203 us; the launch traced here: 202 us
  waiting for transfers between devices  84.8 us (42%)
  starting transfers between devices  52.6 us (26%)
  Pallas kernels  42.5 us (21%)
  between operations  14.3 us (7%)
  local copies, waits for them, and re-layouts  5.16 us (3%)
  other arithmetic  2.94 us (1%)
    ppermute x20, waiting for transfers between devices, swap(): lax.ppermute(array, 'head', [(h, h ^ bits) for h in range(lax.axis_size('...  34.5 us
    ppermute x14, waiting for transfers between devices, shift(): return lax.ppermute(array, 'ctx', pairs)  33.2 us
    ppermute x20, starting transfers between devices, swap(): lax.ppermute(array, 'head', [(h, h ^ bits) for h in range(lax.axis_size('...  31.5 us
    ppermute x14, starting transfers between devices, shift(): return lax.ppermute(array, 'ctx', pairs)  21 us
    all_gather x1, waiting for transfers between devices, body(): whole = lax.all_gather(cut(0, share - RING_ROWS), 'ctx', axis=0, tiled=True)  17.1 us
    pallas_call x2, Pallas kernels, far(): pl.pallas_call(functools.partial(far_kernel, half=half), in_specs=[pl.Blo...  13.5 us
    pallas_call x1, Pallas kernels, near(): pl.pallas_call(near_kernel, grid_spec=grid_spec, out_shape=[jax.ShapeDtyp...  6.69 us
    pallas_call x1, Pallas kernels, scale(): pl.pallas_call(scale_kernel, grid=(QB,), in_specs=[pl.BlockSpec((BLK, HD)...  4.47 us
  transfers between devices with their start and end apart: 35, of which 16 were waited for; matrix products, arithmetic and copies ran while one was open for 2% of the time, Pallas kernels for 13%

profile of v10, /device:TPU:1, one launch (start us, length us, event | category | flops | bytes accessed | tf_op | source)
XLA Modules:
  0.0 202.3 jit_solution(8388461536000531404)
XLA Ops:
  10.1 2.5 %collective-permute-start = (bf16[8,2,32,128]{3,2,1,0:T(8,128)(2,1)S(1)}, bf16[8,2,32,128]{3,2,1,0:T(8,128)(2,1)S(1)}, u32[]{:S(2)}, u32[]{:S(2)}) collective-permute-start(bf16[8,2,32,128]{3,2,1,0:T(8,128)(2,1)S(1)} %pad_maximum_fusion.2), channel_id=1, source_target_pairs={{0,32},{8,40},{16,48},{24,56},{32,64},{40,72},{48,80},{56,88},{64,... | collective-permute-start | bytes 393224 | tf_op jit(solution)/shard_map/ppermute | solution.py:372
  12.7 4.0 %collective-permute-start.1 = (bf16[8,2,32,128]{3,2,1,0:T(8,128)(2,1)S(1)}, bf16[8,2,32,128]{3,2,1,0:T(8,128)(2,1)S(1)}, u32[]{:S(2)}, u32[]{:S(2)}) collective-permute-start(bf16[8,2,32,128]{3,2,1,0:T(8,128)(2,1)S(1)} %pad_maximum_fusion.2), channel_id=1, source_target_pairs={{0,224},{8,232},{16,240},{24,248},{32,0},{40,8},{48,16},{56,24},{6... | collective-permute-start | bytes 393224 | tf_op jit(solution)/shard_map/ppermute | solution.py:372
  16.7 3.1 %collective-permute-done = bf16[8,2,32,128]{3,2,1,0:T(8,128)(2,1)S(1)} collective-permute-done((bf16[8,2,32,128]{3,2,1,0:T(8,128)(2,1)S(1)}, bf16[8,2,32,128]{3,2,1,0:T(8,128)(2,1)S(1)}, u32[]{:S(2)}, u32[]{:S(2)}) %collective-permute-start) | collective-permute-done | bytes 131104 | tf_op jit(solution)/shard_map/ppermute | solution.py:372
  19.8 2.7 %collective-permute-start.4 = (bf16[8,2,32,128]{3,2,1,0:T(8,128)(2,1)S(1)}, bf16[8,2,32,128]{3,2,1,0:T(8,128)(2,1)S(1)}, u32[]{:S(2)}, u32[]{:S(2)}) collective-permute-start(bf16[8,2,32,128]{3,2,1,0:T(8,128)(2,1)S(1)} %collective-permute-done.1), channel_id=1, source_target_pairs={{0,224},{8,232},{16,240},{24,248},{32,0},{40,8},{48,16},{56,24},{6... | collective-permute-start | bytes 393224 | tf_op jit(solution)/shard_map/ppermute | solution.py:372
  24.9 2.7 %collective-permute-start.6 = (bf16[8,2,32,128]{3,2,1,0:T(8,128)(2,1)S(1)}, bf16[8,2,32,128]{3,2,1,0:T(8,128)(2,1)S(1)}, u32[]{:S(2)}, u32[]{:S(2)}) collective-permute-start(bf16[8,2,32,128]{3,2,1,0:T(8,128)(2,1)S(1)} %collective-permute-done.4), channel_id=1, source_target_pairs={{0,224},{8,232},{16,240},{24,248},{32,0},{40,8},{48,16},{56,24},{6... | collective-permute-start | bytes 393224 | tf_op jit(solution)/shard_map/ppermute | solution.py:372
  31.7 3.5 %collective-permute-start.8 = (bf16[4,2,32,128]{3,2,1,0:T(8,128)(2,1)S(1)}, bf16[4,2,32,128]{3,2,1,0:T(8,128)(2,1)S(1)}, u32[]{:S(2)}, u32[]{:S(2)}) collective-permute-start(bf16[4,2,32,128]{3,2,1,0:T(8,128)(2,1)S(1)} %slice.25), channel_id=1, source_target_pairs={{0,224},{8,232},{16,240},{24,248},{32,0},{40,8},{48,16},{56,24},{6... | collective-permute-start | bytes 196616 | tf_op jit(solution)/shard_map/ppermute | solution.py:372
  39.7 6.1 %collective-permute-start.20 = (bf16[2048,128]{1,0:T(8,128)(2,1)S(1)}, bf16[2048,128]{1,0:T(8,128)(2,1)S(1)}, u32[]{:S(2)}, u32[]{:S(2)}) collective-permute-start(bf16[2048,128]{1,0:T(8,128)(2,1)S(1)} %copy-done.3), channel_id=1, source_target_pairs={{0,1},{1,0},{2,3},{3,2},{4,5},{5,4},{6,7},{7,6},{8,9},{9,8},{10,11... | collective-permute-start | bytes 1572872 | tf_op jit(solution)/shard_map/ppermute | solution.py:376
  47.7 11.1 %collective-permute-done.9.refs_3_ = bf16[32,2,32,128]{3,2,1,0:T(8,128)(2,1)S(1)} collective-permute-done((bf16[32,2,32,128]{3,2,1,0:T(8,128)(2,1)S(1)}, bf16[32,2,32,128]{3,2,1,0:T(8,128)(2,1)S(1)}, u32[]{:S(2)}, u32[]{:S(2)}) %collective-permute-start.9) | collective-permute-done | bytes 524320 | tf_op jit(solution)/shard_map/ppermute | solution.py:372
  63.7 17.3 %collective-permute-done.13 = s32[4,1,4]{2,1,0:T(1,128)S(1)} collective-permute-done((s32[4,1,4]{2,1,0:T(1,128)S(1)}, s32[4,1,4]{2,1,0:T(1,128)S(1)}, u32[]{:S(2)}, u32[]{:S(2)}) %collective-permute-start.13) | collective-permute-done | bytes 96 | tf_op jit(solution)/shard_map/ppermute | solution.py:376
  84.0 6.7 %near.1 = (f32[4,2,128,256]{3,2,1,0:T(8,128)}, f32[4,2,1,256]{3,2,1,0:T(1,128)}, f32[4,2,1,256]{3,2,1,0:T(1,128)}) custom-call(s32[2]{0:T(128)} %pad_add_fusion.2.place_ref, bf16[2048,128]{1,0:T(8,128)(2,1)} %refs_0_.2, bf16[2048,128]{1,0:T(8,128)(2,1)} %copy-done.4, bf16[2048,256]{1,0:T(8,128)(2,1)} %refs_2_.1, bf16[2048,256]{1,0:T(8,128)(2,1)} %refs_3_.1), custom_call_target="tpu_custom_call" | custom-call | flops 536870912 | bytes 4194304 | tf_op jit(solution)/shard_map/near/pallas_call | solution.py:66
  93.9 11.9 %collective-permute-done.18.refs_7_ = bf16[32,2,32,128]{3,2,1,0:T(8,128)(2,1)} collective-permute-done((bf16[32,2,32,128]{3,2,1,0:T(8,128)(2,1)}, bf16[32,2,32,128]{3,2,1,0:T(8,128)(2,1)}, u32[]{:S(2)}, u32[]{:S(2)}) %collective-permute-start.18) | collective-permute-done | bytes 524320 | tf_op jit(solution)/shard_map/ppermute | solution.py:372
  105.8 9.3 %collective-permute-start.19 = (s32[2,4,1,4]{3,1,2,0:T(4,128)S(1)}, s32[2,4,1,4]{3,1,2,0:T(4,128)S(1)}, u32[]{:S(2)}, u32[]{:S(2)}) collective-permute-start(s32[2,4,1,4]{3,1,2,0:T(4,128)S(1)} %pad_add_fusion), channel_id=1, source_target_pairs={{0,1},{1,0},{2,3},{3,2},{4,5},{5,4},{6,7},{7,6},{8,9},{9,8},{10,11... | collective-permute-start | bytes 392 | tf_op jit(solution)/shard_map/ppermute | solution.py:376
  117.7 3.9 %collect.1.refs_3_ = bf16[64,2,32,128]{3,2,1,0:T(8,128)(2,1)} custom-call(s32[64,2]{1,0:T(8,128)} %copy.13.where_ref, bf16[32,2,32,128]{3,2,1,0:T(8,128)(2,1)} %copy-done.2, bf16[32,2,32,128]{3,2,1,0:T(8,128)(2,1)} %copy-done.5, bf16[32,2,32,128]{3,2,1,0:T(8,128)(2,1)} %copy-done.6, bf16[32,2,32,128]{3,2,1,0:T(8,128)(2,1)} %copy-done.8, ...), custom_call_target="tpu_custom_call" | custom-call | tf_op jit(solution)/shard_map/collect/pallas_call | solution.py:227
  121.7 4.5 %scale.1 = (bf16[2048,256]{1,0:T(8,128)(2,1)}, bf16[2048,256]{1,0:T(8,128)(2,1)}, bf16[2048,256]{1,0:T(8,128)(2,1)}, bf16[2048,256]{1,0:T(8,128)(2,1)}) custom-call(bf16[2048,128]{1,0:T(8,128)(2,1)} %refs_0_.2, bf16[2048,128]{1,0:T(8,128)(2,1)} %copy-done.4, bf16[2048,128]{1,0:T(8,128)(2,1)} %collective-permute-done.12.refs_2_, ...), custom_call_target="tpu_custom_call" | custom-call | tf_op jit(solution)/shard_map/scale/pallas_call | solution.py:106
  126.8 17.1 %all-gather.2.cloned.1.call-done.refs_2_ = bf16[256,2,96,128]{3,2,1,0:T(8,128)(2,1)} async-done(((bf16[8,2,96,128]{3,2,1,0:T(8,128)(2,1)}), bf16[256,2,96,128]{3,2,1,0:T(8,128)(2,1)}) %all-gather.2.cloned.1.call-update) | async-done | bytes 12582928 | tf_op jit(solution)/shard_map/all_gather | solution.py:399
  143.9 6.8 %far.2 = (bf16[8,144,256]{2,1,0:T(8,128)(2,1)}, bf16[8,144,256]{2,1,0:T(8,128)(2,1)}) custom-call(s32[33]{0:T(128)} %add_add_fusion.1.picks_ref, bf16[2048,256]{1,0:T(8,128)(2,1)} %get-tuple-element.84.refs_0_, bf16[2048,256]{1,0:T(8,128)(2,1)} %get-tuple-element.85.refs_1_, bf16[256,2,96,128]{3,2,1,0:T(8,128)(2,1)} %all-gather.2.cloned.1.call-done.refs_2_, ...), custom_call_target="tpu_custom_call" | custom-call | flops 8589934592 | bytes 5242880 | tf_op jit(solution)/shard_map/far/pallas_call | solution.py:186
  157.5 6.8 %far.3 = (bf16[8,144,256]{2,1,0:T(8,128)(2,1)}, bf16[8,144,256]{2,1,0:T(8,128)(2,1)}) custom-call(s32[33]{0:T(128)} %add_add_fusion.picks_ref, bf16[2048,256]{1,0:T(8,128)(2,1)} %get-tuple-element.92.refs_0_, bf16[2048,256]{1,0:T(8,128)(2,1)} %get-tuple-element.93.refs_1_, bf16[256,2,96,128]{3,2,1,0:T(8,128)(2,1)} %all-gather.2.cloned.1.call-done.refs_2_, ...), custom_call_target="tpu_custom_call" | custom-call | flops 8589934592 | bytes 5242880 | tf_op jit(solution)/shard_map/far/pallas_call | solution.py:186
  165.4 5.5 %collective-permute-done.29.refs_1_ = bf16[4,144,256]{2,1,0:T(8,128)(2,1)} collective-permute-done((bf16[4,144,256]{2,1,0:T(8,128)(2,1)}, bf16[4,144,256]{2,1,0:T(8,128)(2,1)}, u32[]{:S(2)}, u32[]{:S(2)}) %collective-permute-start.29) | collective-permute-done | bytes 294944 | tf_op jit(solution)/shard_map/ppermute | solution.py:376
  170.9 2.5 %merge_chip.1 = (f32[4,2,128,256]{3,2,1,0:T(8,128)}, f32[4,2,1,256]{3,2,1,0:T(1,128)}, f32[4,2,1,256]{3,2,1,0:T(1,128)}) custom-call(f32[4,2,128,256]{3,2,1,0:T(8,128)} %get-tuple-element.96.acc_ref, f32[4,2,1,256]{3,2,1,0:T(1,128)} %get-tuple-element.97.m_ref, f32[4,2,1,256]{3,2,1,0:T(1,128)} %get-tuple-element.98.l_ref, bf16[4,144,256]{2,1,0:T(8,128)(2,1)} %copy-done.11, ...), custom_call_target="tpu_custom_call" | custom-call | flops 4294967296 | bytes 4194304 | tf_op jit(solution)/shard_map/merge_chip/pallas_call | solution.py:280
  173.4 3.8 %merge_last.1 = (bf16[4,256,128]{2,1,0:T(8,128)(2,1)}, bf16[4,256,128]{2,1,0:T(8,128)(2,1)}, bf16[2,256,128]{2,1,0:T(8,128)(2,1)}, bf16[2,256,128]{2,1,0:T(8,128...) custom-call(s32[1]{0:T(128)} %bitcast.1.chip_ref, bf16[8,144,256]{2,1,0:T(8,128)(2,1)} %get-tuple-element.94.a_ref, ...), custom_call_target="tpu_custom_call" | custom-call | tf_op jit(solution)/shard_map/merge_last/pallas_call | solution.py:315
  179.6 2.4 %collective-permute-start.32 = (bf16[2,256,128]{2,1,0:T(8,128)(2,1)}, bf16[2,256,128]{2,1,0:T(8,128)(2,1)S(1)}, u32[]{:S(2)}, u32[]{:S(2)}) collective-permute-start(bf16[2,256,128]{2,1,0:T(8,128)(2,1)} %get-tuple-element.106), channel_id=1, source_target_pairs={{0,4},{1,5},{2,6},{3,7},{4,0},{5,1},{6,2},{7,3},{8,12},{9,13},{10,... | collective-permute-start | bytes 393224 | tf_op jit(solution)/shard_map/ppermute | solution.py:376
  184.1 4.5 %collective-permute-done.32.refs_2_ = bf16[2,256,128]{2,1,0:T(8,128)(2,1)S(1)} collective-permute-done((bf16[2,256,128]{2,1,0:T(8,128)(2,1)}, bf16[2,256,128]{2,1,0:T(8,128)(2,1)S(1)}, u32[]{:S(2)}, u32[]{:S(2)}) %collective-permute-start.32) | collective-permute-done | bytes 131104 | tf_op jit(solution)/shard_map/ppermute | solution.py:376
  188.6 2.5 %collective-permute-done.33.refs_3_ = bf16[2,256,128]{2,1,0:T(8,128)(2,1)S(1)} collective-permute-done((bf16[2,256,128]{2,1,0:T(8,128)(2,1)}, bf16[2,256,128]{2,1,0:T(8,128)(2,1)S(1)}, u32[]{:S(2)}, u32[]{:S(2)}) %collective-permute-start.33) | collective-permute-done | bytes 131104 | tf_op jit(solution)/shard_map/ppermute | solution.py:376
  192.1 3.4 %project.1 = bf16[256,2048]{1,0:T(8,128)(2,1)} custom-call(bf16[2,256,128]{2,1,0:T(8,128)(2,1)S(1)} %copy-done.1, bf16[2,256,128]{2,1,0:T(8,128)(2,1)S(1)} %collective-permute-done.31.refs_1_, bf16[2,256,128]{2,1,0:T(8,128)(2,1)S(1)} %collective-permute-done.32.refs_2_, bf16[2,256,128]{2,1,0:T(8,128)(2,1)S(1)} %collective-permute-done.33.refs_3_, ...), custom_call_target="tpu_custom_call" | custom-call | tf_op jit(solution)/shard_map/project/pallas_call | solution.py:357
  (112 shorter events, 43.3 us)
Async XLA Ops:
  7.2 136.7 %all-gather.2.cloned.1.call-start = ((), (), s32[]{:S(2)}) async-start(), calls=%async_computation | async-start | bytes 12976128 | tf_op jit(solution)/shard_map/all_gather | solution.py:399
  10.1 9.7 %collective-permute-start = (bf16[8,2,32,128]{3,2,1,0:T(8,128)(2,1)S(1)}, bf16[8,2,32,128]{3,2,1,0:T(8,128)(2,1)S(1)}, u32[]{:S(2)}, u32[]{:S(2)}) collective-permute-start(bf16[8,2,32,128]{3,2,1,0:T(8,128)(2,1)S(1)} %pad_maximum_fusion.2), channel_id=1, source_target_pairs={{0,32},{8,40},{16,48},{24,56},{32,64},{40,72},{48,80},{56,88},{64,... | collective-permute-start | bytes 393224 | tf_op jit(solution)/shard_map/ppermute | solution.py:372
  27.6 20.1 %collective-permute-start.3 = (bf16[32,2,32,128]{3,2,1,0:T(8,128)(2,1)S(1)}, bf16[32,2,32,128]{3,2,1,0:T(8,128)(2,1)S(1)}, u32[]{:S(2)}, u32[]{:S(2)}) collective-permute-start(bf16[32,2,32,128]{3,2,1,0:T(8,128)(2,1)S(1)} %pad_maximum_fusion.refs_0_), channel_id=1, source_target_pairs={{0,8},{8,16},{16,24},{24,0},{32,40},{40,48},{48,56},{56,32},{64,72... | collective-permute-start | bytes 1572872 | tf_op jit(solution)/shard_map/ppermute | solution.py:372
  28.9 18.8 %collective-permute-start.10 = (bf16[32,2,32,128]{3,2,1,0:T(8,128)(2,1)S(1)}, bf16[32,2,32,128]{3,2,1,0:T(8,128)(2,1)S(1)}, u32[]{:S(2)}, u32[]{:S(2)}) collective-permute-start(bf16[32,2,32,128]{3,2,1,0:T(8,128)(2,1)S(1)} %pad_maximum_fusion.refs_0_), channel_id=1, source_target_pairs={{0,24},{8,0},{16,8},{24,16},{32,56},{40,32},{48,40},{56,48},{64,88... | collective-permute-start | bytes 1572872 | tf_op jit(solution)/shard_map/ppermute | solution.py:372
  37.0 21.8 %collective-permute-start.9 = (bf16[32,2,32,128]{3,2,1,0:T(8,128)(2,1)S(1)}, bf16[32,2,32,128]{3,2,1,0:T(8,128)(2,1)S(1)}, u32[]{:S(2)}, u32[]{:S(2)}) collective-permute-start(bf16[32,2,32,128]{3,2,1,0:T(8,128)(2,1)S(1)} %constant_dynamic-update-slice_fusion.refs_1_), channel_id=1, source_target_pairs={{0,8},{8,16},{16,24},{24,0},{32,40},{40,48},{48,56},{56,32},{64,72... | collective-permute-start | bytes 1572872 | tf_op jit(solution)/shard_map/ppermute | solution.py:372
  38.3 20.5 %collective-permute-start.11 = (bf16[32,2,32,128]{3,2,1,0:T(8,128)(2,1)S(1)}, bf16[32,2,32,128]{3,2,1,0:T(8,128)(2,1)}, u32[]{:S(2)}, u32[]{:S(2)}) collective-permute-start(bf16[32,2,32,128]{3,2,1,0:T(8,128)(2,1)S(1)} %constant_dynamic-update-slice_fusion.refs_1_), channel_id=1, source_target_pairs={{0,24},{8,0},{16,8},{24,16},{32,56},{40,32},{48,40},{56,48},{64,88... | collective-permute-start | bytes 1572872 | tf_op jit(solution)/shard_map/ppermute | solution.py:372
  39.7 22.8 %collective-permute-start.20 = (bf16[2048,128]{1,0:T(8,128)(2,1)S(1)}, bf16[2048,128]{1,0:T(8,128)(2,1)S(1)}, u32[]{:S(2)}, u32[]{:S(2)}) collective-permute-start(bf16[2048,128]{1,0:T(8,128)(2,1)S(1)} %copy-done.3), channel_id=1, source_target_pairs={{0,1},{1,0},{2,3},{3,2},{4,5},{5,4},{6,7},{7,6},{8,9},{9,8},{10,11... | collective-permute-start | bytes 1572872 | tf_op jit(solution)/shard_map/ppermute | solution.py:376
  47.7 34.8 %collective-permute-start.17 = (bf16[32,2,32,128]{3,2,1,0:T(8,128)(2,1)S(1)}, bf16[32,2,32,128]{3,2,1,0:T(8,128)(2,1)S(1)}, u32[]{:S(2)}, u32[]{:S(2)}) collective-permute-start(bf16[32,2,32,128]{3,2,1,0:T(8,128)(2,1)S(1)} %collective-permute-done.3.refs_2_), channel_id=1, source_target_pairs={{0,8},{8,16},{16,24},{24,0},{32,40},{40,48},{48,56},{56,32},{64,72... | collective-permute-start | bytes 1572872 | tf_op jit(solution)/shard_map/ppermute | solution.py:372
  58.9 33.4 %collective-permute-start.14 = (bf16[128,2048]{1,0:T(8,128)(2,1)S(1)}, bf16[128,2048]{1,0:T(8,128)(2,1)S(1)}, u32[]{:S(2)}, u32[]{:S(2)}) collective-permute-start(bf16[128,2048]{1,0:T(8,128)(2,1)S(1)} %copy-done), channel_id=1, source_target_pairs={{0,2},{1,3},{2,0},{3,1},{4,6},{5,7},{6,4},{7,5},{8,10},{9,11},{10,... | collective-permute-start | bytes 1572872 | tf_op jit(solution)/shard_map/ppermute | solution.py:376
  60.2 32.1 %collective-permute-start.15 = (bf16[128,2048]{1,0:T(8,128)(2,1)S(1)}, bf16[128,2048]{1,0:T(8,128)(2,1)S(1)}, u32[]{:S(2)}, u32[]{:S(2)}) collective-permute-start(bf16[128,2048]{1,0:T(8,128)(2,1)S(1)} %copy-done), channel_id=1, source_target_pairs={{0,4},{1,5},{2,6},{3,7},{4,0},{5,1},{6,2},{7,3},{8,12},{9,13},{10,... | collective-permute-start | bytes 1572872 | tf_op jit(solution)/shard_map/ppermute | solution.py:376
  62.3 18.8 %collective-permute-start.13 = (s32[4,1,4]{2,1,0:T(1,128)S(1)}, s32[4,1,4]{2,1,0:T(1,128)S(1)}, u32[]{:S(2)}, u32[]{:S(2)}) collective-permute-start(s32[4,1,4]{2,1,0:T(1,128)S(1)} %copy-done.10), channel_id=1, source_target_pairs={{0,2},{1,3},{2,0},{3,1},{4,6},{5,7},{6,4},{7,5},{8,10},{9,11},{10,... | collective-permute-start | bytes 200 | tf_op jit(solution)/shard_map/ppermute | solution.py:376
  62.5 29.8 %collective-permute-start.12 = (bf16[2048,128]{1,0:T(8,128)(2,1)S(1)}, bf16[2048,128]{1,0:T(8,128)(2,1)}, u32[]{:S(2)}, u32[]{:S(2)}) collective-permute-start(bf16[2048,128]{1,0:T(8,128)(2,1)S(1)} %copy-done.3), channel_id=1, source_target_pairs={{0,2},{1,3},{2,0},{3,1},{4,6},{5,7},{6,4},{7,5},{8,10},{9,11},{10,... | collective-permute-start | bytes 1572872 | tf_op jit(solution)/shard_map/ppermute | solution.py:376
  81.0 12.9 %collective-permute-start.16 = (bf16[128,2048]{1,0:T(8,128)(2,1)S(1)}, bf16[128,2048]{1,0:T(8,128)(2,1)S(1)}, u32[]{:S(2)}, u32[]{:S(2)}) collective-permute-start(bf16[128,2048]{1,0:T(8,128)(2,1)S(1)} %copy-done), channel_id=1, source_target_pairs={{0,6},{1,7},{2,4},{3,5},{4,2},{5,3},{6,0},{7,1},{8,14},{9,15},{10,... | collective-permute-start | bytes 1572872 | tf_op jit(solution)/shard_map/ppermute | solution.py:376
  83.3 22.5 %collective-permute-start.18 = (bf16[32,2,32,128]{3,2,1,0:T(8,128)(2,1)}, bf16[32,2,32,128]{3,2,1,0:T(8,128)(2,1)}, u32[]{:S(2)}, u32[]{:S(2)}) collective-permute-start(bf16[32,2,32,128]{3,2,1,0:T(8,128)(2,1)} %collective-permute-done.11.refs_5_), channel_id=1, source_target_pairs={{0,24},{8,0},{16,8},{24,16},{32,56},{40,32},{48,40},{56,48},{64,88... | collective-permute-start | bytes 1572872 | tf_op jit(solution)/shard_map/ppermute | solution.py:372
  105.8 10.6 %collective-permute-start.19 = (s32[2,4,1,4]{3,1,2,0:T(4,128)S(1)}, s32[2,4,1,4]{3,1,2,0:T(4,128)S(1)}, u32[]{:S(2)}, u32[]{:S(2)}) collective-permute-start(s32[2,4,1,4]{3,1,2,0:T(4,128)S(1)} %pad_add_fusion), channel_id=1, source_target_pairs={{0,1},{1,0},{2,3},{3,2},{4,5},{5,4},{6,7},{7,6},{8,9},{9,8},{10,11... | collective-permute-start | bytes 392 | tf_op jit(solution)/shard_map/ppermute | solution.py:376
  115.4 10.8 %collective-permute-start.22 = (bf16[128,2048]{1,0:T(8,128)(2,1)S(1)}, bf16[128,2048]{1,0:T(8,128)(2,1)S(1)}, u32[]{:S(2)}, u32[]{:S(2)}) collective-permute-start(bf16[128,2048]{1,0:T(8,128)(2,1)S(1)} %copy-done), channel_id=1, source_target_pairs={{0,1},{1,0},{2,3},{3,2},{4,5},{5,4},{6,7},{7,6},{8,9},{9,8},{10,11... | collective-permute-start | bytes 1572872 | tf_op jit(solution)/shard_map/ppermute | solution.py:376
  115.9 10.3 %collective-permute-start.23 = (bf16[128,2048]{1,0:T(8,128)(2,1)S(1)}, bf16[128,2048]{1,0:T(8,128)(2,1)S(1)}, u32[]{:S(2)}, u32[]{:S(2)}) collective-permute-start(bf16[128,2048]{1,0:T(8,128)(2,1)S(1)} %collective-permute-done.14.refs_6_), channel_id=1, source_target_pairs={{0,1},{1,0},{2,3},{3,2},{4,5},{5,4},{6,7},{7,6},{8,9},{9,8},{10,11... | collective-permute-start | bytes 1572872 | tf_op jit(solution)/shard_map/ppermute | solution.py:376
  116.0 10.2 %collective-permute-start.24 = (bf16[128,2048]{1,0:T(8,128)(2,1)S(1)}, bf16[128,2048]{1,0:T(8,128)(2,1)}, u32[]{:S(2)}, u32[]{:S(2)}) collective-permute-start(bf16[128,2048]{1,0:T(8,128)(2,1)S(1)} %collective-permute-done.15.refs_8_), channel_id=1, source_target_pairs={{0,1},{1,0},{2,3},{3,2},{4,5},{5,4},{6,7},{7,6},{8,9},{9,8},{10,11... | collective-permute-start | bytes 1572872 | tf_op jit(solution)/shard_map/ppermute | solution.py:376
  116.4 9.8 %collective-permute-start.25 = (bf16[128,2048]{1,0:T(8,128)(2,1)S(1)}, bf16[128,2048]{1,0:T(8,128)(2,1)}, u32[]{:S(2)}, u32[]{:S(2)}) collective-permute-start(bf16[128,2048]{1,0:T(8,128)(2,1)S(1)} %collective-permute-done.16.refs_10_), channel_id=1, source_target_pairs={{0,1},{1,0},{2,3},{3,2},{4,5},{5,4},{6,7},{7,6},{8,9},{9,8},{10,11... | collective-permute-start | bytes 1572872 | tf_op jit(solution)/shard_map/ppermute | solution.py:376
  156.0 9.3 %collective-permute-start.28 = (bf16[4,144,256]{2,1,0:T(8,128)(2,1)}, bf16[4,144,256]{2,1,0:T(8,128)(2,1)S(1)}, u32[]{:S(2)}, u32[]{:S(2)}) collective-permute-start(bf16[4,144,256]{2,1,0:T(8,128)(2,1)} %get-tuple-element.89), channel_id=1, source_target_pairs={{0,2},{1,3},{2,0},{3,1},{4,6},{5,7},{6,4},{7,5},{8,10},{9,11},{10,... | collective-permute-start | bytes 884744 | tf_op jit(solution)/shard_map/ppermute | solution.py:376
  157.2 13.7 %collective-permute-start.29 = (bf16[4,144,256]{2,1,0:T(8,128)(2,1)}, bf16[4,144,256]{2,1,0:T(8,128)(2,1)}, u32[]{:S(2)}, u32[]{:S(2)}) collective-permute-start(bf16[4,144,256]{2,1,0:T(8,128)(2,1)} %get-tuple-element.90), channel_id=1, source_target_pairs={{0,2},{1,3},{2,0},{3,1},{4,6},{5,7},{6,4},{7,5},{8,10},{9,11},{10,... | collective-permute-start | bytes 884744 | tf_op jit(solution)/shard_map/ppermute | solution.py:376
  164.3 9.1 %collective-permute-start.27 = (bf16[8,144,256]{2,1,0:T(8,128)(2,1)}, bf16[8,144,256]{2,1,0:T(8,128)(2,1)}, u32[]{:S(2)}, u32[]{:S(2)}) collective-permute-start(bf16[8,144,256]{2,1,0:T(8,128)(2,1)} %get-tuple-element.95), channel_id=1, source_target_pairs={{0,1},{1,0},{2,3},{3,2},{4,5},{5,4},{6,7},{7,6},{8,9},{9,8},{10,11... | collective-permute-start | bytes 1769480 | tf_op jit(solution)/shard_map/ppermute | solution.py:376
  179.6 9.1 %collective-permute-start.32 = (bf16[2,256,128]{2,1,0:T(8,128)(2,1)}, bf16[2,256,128]{2,1,0:T(8,128)(2,1)S(1)}, u32[]{:S(2)}, u32[]{:S(2)}) collective-permute-start(bf16[2,256,128]{2,1,0:T(8,128)(2,1)} %get-tuple-element.106), channel_id=1, source_target_pairs={{0,4},{1,5},{2,6},{3,7},{4,0},{5,1},{6,2},{7,3},{8,12},{9,13},{10,... | collective-permute-start | bytes 393224 | tf_op jit(solution)/shard_map/ppermute | solution.py:376
  182.0 9.2 %collective-permute-start.33 = (bf16[2,256,128]{2,1,0:T(8,128)(2,1)}, bf16[2,256,128]{2,1,0:T(8,128)(2,1)S(1)}, u32[]{:S(2)}, u32[]{:S(2)}) collective-permute-start(bf16[2,256,128]{2,1,0:T(8,128)(2,1)} %get-tuple-element.107), channel_id=1, source_target_pairs={{0,6},{1,7},{2,4},{3,5},{4,2},{5,3},{6,0},{7,1},{8,14},{9,15},{10,... | collective-permute-start | bytes 393224 | tf_op jit(solution)/shard_map/ppermute | solution.py:376
  (23 other events, 332.5 us)
Sparse Core Ops, SparseCore 0:
  10.6 133.2 all-gather.1

commit v11 on v9

--- a/solution.py
+++ b/solution.py
@@ -135,9 +135,9 @@
             top = rounded_top(jnp.max(score_ref[:, lanes], axis=0, keepdims=True))
             total = jnp.zeros((8, HD), F32)
             for row in range(0, BLK, 64):
-                weights = jnp.exp2((score_ref[row : row + 64, lanes] * SCALE - top).astype(BF16))
-                weight_ref[row : row + 64, lanes] = weights
-                total = total + jnp.sum(weights.astype(F32).reshape(8, 8, HD), axis=0)
+                weights = jnp.exp2(score_ref[row : row + 64, lanes] * SCALE - top)
+                weight_ref[row : row + 64, lanes] = weights.astype(BF16)
+                total = total + jnp.sum(weights.reshape(8, 8, HD), axis=0)
             tops.append(top)
             totals.append(jnp.sum(total, axis=0, keepdims=True))
         sums[number] = jnp.concatenate(tops, axis=1), jnp.concatenate(totals, axis=1)
@@ -239,6 +239,21 @@
     )(mine, other)
 
 
+def hold(arrays):
+    hbm = pl.BlockSpec(memory_space=pl.ANY)
+    return pl.pallas_call(
+        lambda *refs: None,
+        in_specs=[hbm] * len(arrays),
+        out_specs=[hbm] * len(arrays),
+        out_shape=[jax.ShapeDtypeStruct(array.shape, array.dtype) for array in arrays],
+        input_output_aliases={n: n for n in range(len(arrays))},
+        cost_estimate=pl.CostEstimate(
+            flops=8 * QB * 4 * BLK * BLK * HD, bytes_accessed=4 << 20, transcendentals=8 * BLK
+        ),
+        name="hold",
+    )(*arrays)
+
+
 def merge_last_kernel(chip_ref, a_ref, b_ref, acc_ref, m_ref, l_ref, *refs):
     chip_refs, half_refs, share_refs = refs[:2], refs[2:4], refs[4:]
     for row in range(2 * QB):
@@ -310,7 +325,7 @@
         in_specs=[vmem] * (len(parts) + len(weights)),
         out_specs=vmem,
         out_shape=jax.ShapeDtypeStruct((parts[0].shape[1], weights[0].shape[1]), BF16),
-        compiler_params=pltpu.CompilerParams(vmem_limit_bytes=VMEM_BYTES),
+        compiler_params=pltpu.CompilerParams(vmem_limit_bytes=24 << 20),
         name="project",
     )(*parts, *weights)
 
@@ -368,11 +383,10 @@
     near_state = near(
         jnp.stack([kv, core]).astype(jnp.int32), near_queries, span_keys, span_values
     )
-    queries_early, picks_early, weight_early = after(
-        (queries, block_picks, out_weight), *ring_arrays[2:6]
-    )
+    picks_chip = swap(after(block_picks, x1_low, x2_low), 2)
+    queries_early, weight_early = after((queries, out_weight), x3_low, picks_chip)
     queries_chip = swap(queries_early, 2)
-    picks_pair = jnp.stack([block_picks, swap(picks_early, 2)])
+    picks_pair = jnp.stack([block_picks, picks_chip])
     weights = [out_weight] + [None] * (heads - 1)
     for bits in range(2, heads, 2):
         weights[bits] = swap(weight_early, bits)
@@ -415,7 +429,8 @@
     for_chip = merge_two(chip_here, swap(chip_there, 1))
     chip_parts = [swap(piece, 2) for piece in for_chip]
     own_here, own_there = far_of(0, 1, for_chip, 1)
-    core_part = swap(after(own_there, *chip_parts), 1)
+    core_part = swap(own_there, 1)
+    chip_parts = hold(chip_parts)
     own, other, shares = merge_last(chip[None], own_here, core_part, near_state, chip_parts)
     parts = [shares[0]] + [swap(shares[n], 2 * n) for n in range(1, QB)]
     attention = assemble(core[None], own, swap(other, 1))

time: 199 us -> 194 us (0.975)
  waiting for transfers between devices: 88.8 us -> 82.9 us
  starting transfers between devices: 48.2 us -> 53.2 us
  local copies, waits for them, and re-layouts: 7.25 us -> 5.16 us
  Pallas kernels: 36.9 us -> 34.9 us
    ppermute x14, waiting for transfers between devices: 27.2 us -> 21.7 us  [shift(): return lax.ppermute(array, 'ctx', pairs)]
    ppermute x20, starting transfers between devices: 26.2 us -> 30.7 us  [swap(): lax.ppermute(array, 'head', [(h, h ^ bits) for h in range(lax.axis_size('...]
    all_gather x1, waiting for transfers between devices: 36.7 us -> 33.6 us  [body(): whole = lax.all_gather(cut(0, share - RING_ROWS), 'ctx', axis=0, tiled=True)]
    ppermute x20, waiting for transfers between devices: 24.8 us -> 27.5 us  [swap(): lax.ppermute(array, 'head', [(h, h ^ bits) for h in range(lax.axis_size('...]
    unnamed x40 -> x26, local copies, waits for them, and re-layouts: 3.89 us -> 1.8 us
  transfers between devices with their start and end apart: 35 -> 35, of which waited for: 16 -> 14; matrix products, arithmetic and copies ran while one was open for 2% -> 2% of each run, Pallas kernels for 10% -> 10%
where the time goes in v11:
time: 194 us; the launch traced here: 193 us
  waiting for transfers between devices  82.9 us (43%)
  starting transfers between devices  53.2 us (27%)
  Pallas kernels  34.9 us (18%)
  between operations  14.3 us (7%)
  local copies, waits for them, and re-layouts  5.16 us (3%)
  other arithmetic  2.78 us (1%)
    all_gather x1, waiting for transfers between devices, body(): whole = lax.all_gather(cut(0, share - RING_ROWS), 'ctx', axis=0, tiled=True)  33.6 us
    ppermute x20, starting transfers between devices, swap(): lax.ppermute(array, 'head', [(h, h ^ bits) for h in range(lax.axis_size('...  30.7 us
    ppermute x20, waiting for transfers between devices, swap(): lax.ppermute(array, 'head', [(h, h ^ bits) for h in range(lax.axis_size('...  27.5 us
    ppermute x14, starting transfers between devices, shift(): return lax.ppermute(array, 'ctx', pairs)  22.5 us
    ppermute x14, waiting for transfers between devices, shift(): return lax.ppermute(array, 'ctx', pairs)  21.7 us
    pallas_call x2, Pallas kernels, far(): pl.pallas_call(functools.partial(far_kernel, half=half), in_specs=[pl.Blo...  12.7 us
    pallas_call x1, Pallas kernels, near(): pl.pallas_call(near_kernel, grid_spec=grid_spec, out_shape=[jax.ShapeDtyp...  6.66 us
    pallas_call x1, Pallas kernels, collect(): pl.pallas_call(collect_kernel, in_specs=[pl.BlockSpec(memory_space=pltpu....  4.01 us
  transfers between devices with their start and end apart: 35, of which 14 were waited for; matrix products, arithmetic and copies ran while one was open for 2% of the time, Pallas kernels for 10%

profile of v11, /device:TPU:1, one launch (start us, length us, event | category | flops | bytes accessed | tf_op | source)
XLA Modules:
  0.0 193.2 jit_solution(11947251067540447377)
XLA Ops:
  10.1 6.5 %collective-permute-start.1 = (bf16[8,2,32,128]{3,2,1,0:T(8,128)(2,1)S(1)}, bf16[8,2,32,128]{3,2,1,0:T(8,128)(2,1)S(1)}, u32[]{:S(2)}, u32[]{:S(2)}) collective-permute-start(bf16[8,2,32,128]{3,2,1,0:T(8,128)(2,1)S(1)} %pad_maximum_fusion.2), channel_id=1, source_target_pairs={{0,224},{8,232},{16,240},{24,248},{32,0},{40,8},{48,16},{56,24},{6... | collective-permute-start | bytes 393224 | tf_op jit(solution)/shard_map/ppermute | solution.py:338
  18.7 3.4 %collective-permute-start.11 = (bf16[8,2,32,128]{3,2,1,0:T(8,128)(2,1)S(1)}, bf16[8,2,32,128]{3,2,1,0:T(8,128)(2,1)S(1)}, u32[]{:S(2)}, u32[]{:S(2)}) collective-permute-start(bf16[8,2,32,128]{3,2,1,0:T(8,128)(2,1)S(1)} %collective-permute-done.1), channel_id=1, source_target_pairs={{0,224},{8,232},{16,240},{24,248},{32,0},{40,8},{48,16},{56,24},{6... | collective-permute-start | bytes 393224 | tf_op jit(solution)/shard_map/ppermute | solution.py:338
  24.1 3.1 %collective-permute-start.13 = (bf16[8,2,32,128]{3,2,1,0:T(8,128)(2,1)S(1)}, bf16[8,2,32,128]{3,2,1,0:T(8,128)(2,1)S(1)}, u32[]{:S(2)}, u32[]{:S(2)}) collective-permute-start(bf16[8,2,32,128]{3,2,1,0:T(8,128)(2,1)S(1)} %collective-permute-done.11), channel_id=1, source_target_pairs={{0,224},{8,232},{16,240},{24,248},{32,0},{40,8},{48,16},{56,24},{6... | collective-permute-start | bytes 393224 | tf_op jit(solution)/shard_map/ppermute | solution.py:338
  27.2 2.6 %collective-permute-start.5 = (bf16[32,2,32,128]{3,2,1,0:T(8,128)(2,1)S(1)}, bf16[32,2,32,128]{3,2,1,0:T(8,128)(2,1)S(1)}, u32[]{:S(2)}, u32[]{:S(2)}) collective-permute-start(bf16[32,2,32,128]{3,2,1,0:T(8,128)(2,1)S(1)} %pad_maximum_fusion.refs_0_), channel_id=1, source_target_pairs={{0,24},{8,0},{16,8},{24,16},{32,56},{40,32},{48,40},{56,48},{64,88... | collective-permute-start | bytes 1572872 | tf_op jit(solution)/shard_map/ppermute | solution.py:338
  30.8 3.5 %collective-permute-start.15 = (bf16[4,2,32,128]{3,2,1,0:T(8,128)(2,1)S(1)}, bf16[4,2,32,128]{3,2,1,0:T(8,128)(2,1)S(1)}, u32[]{:S(2)}, u32[]{:S(2)}) collective-permute-start(bf16[4,2,32,128]{3,2,1,0:T(8,128)(2,1)S(1)} %slice.25), channel_id=1, source_target_pairs={{0,224},{8,232},{16,240},{24,248},{32,0},{40,8},{48,16},{56,24},{6... | collective-permute-start | bytes 196616 | tf_op jit(solution)/shard_map/ppermute | solution.py:338
  34.5 5.1 %collective-permute-done.14 = bf16[4,2,32,128]{3,2,1,0:T(8,128)(2,1)S(1)} collective-permute-done((bf16[4,2,32,128]{3,2,1,0:T(8,128)(2,1)S(1)}, bf16[4,2,32,128]{3,2,1,0:T(8,128)(2,1)S(1)}, u32[]{:S(2)}, u32[]{:S(2)}) %collective-permute-start.14) | collective-permute-done | bytes 65568 | tf_op jit(solution)/shard_map/ppermute | solution.py:338
  42.0 2.5 %collective-permute-done.3.refs_2_ = bf16[32,2,32,128]{3,2,1,0:T(8,128)(2,1)S(1)} collective-permute-done((bf16[32,2,32,128]{3,2,1,0:T(8,128)(2,1)S(1)}, bf16[32,2,32,128]{3,2,1,0:T(8,128)(2,1)S(1)}, u32[]{:S(2)}, u32[]{:S(2)}) %collective-permute-start.3) | collective-permute-done | bytes 524320 | tf_op jit(solution)/shard_map/ppermute | solution.py:338
  44.5 5.2 %collective-permute-start.20 = (bf16[2048,128]{1,0:T(8,128)(2,1)}, bf16[2048,128]{1,0:T(8,128)(2,1)}, u32[]{:S(2)}, u32[]{:S(2)}) collective-permute-start(bf16[2048,128]{1,0:T(8,128)(2,1)} %refs_0_.1), channel_id=1, source_target_pairs={{0,1},{1,0},{2,3},{3,2},{4,5},{5,4},{6,7},{7,6},{8,9},{9,8},{10,11... | collective-permute-start | bytes 1572872 | tf_op jit(solution)/shard_map/ppermute | solution.py:342
  51.5 6.0 %collective-permute-done.17.refs_5_ = bf16[32,2,32,128]{3,2,1,0:T(8,128)(2,1)S(1)} collective-permute-done((bf16[32,2,32,128]{3,2,1,0:T(8,128)(2,1)S(1)}, bf16[32,2,32,128]{3,2,1,0:T(8,128)(2,1)S(1)}, u32[]{:S(2)}, u32[]{:S(2)}) %collective-permute-start.17) | collective-permute-done | bytes 524320 | tf_op jit(solution)/shard_map/ppermute | solution.py:338
  63.3 2.9 %collective-permute-done.16.refs_3_ = bf16[32,2,32,128]{3,2,1,0:T(8,128)(2,1)} collective-permute-done((bf16[32,2,32,128]{3,2,1,0:T(8,128)(2,1)S(1)}, bf16[32,2,32,128]{3,2,1,0:T(8,128)(2,1)}, u32[]{:S(2)}, u32[]{:S(2)}) %collective-permute-start.16) | collective-permute-done | bytes 524320 | tf_op jit(solution)/shard_map/ppermute | solution.py:338
  68.3 6.7 %near.1 = (f32[4,2,128,256]{3,2,1,0:T(8,128)}, f32[4,2,1,256]{3,2,1,0:T(1,128)}, f32[4,2,1,256]{3,2,1,0:T(1,128)}) custom-call(s32[2]{0:T(128)} %pad_add_fusion.2.place_ref, bf16[2048,128]{1,0:T(8,128)(2,1)} %refs_0_.1, bf16[2048,128]{1,0:T(8,128)(2,1)} %collective-permute-done.20.refs_1_, bf16[2048,256]{1,0:T(8,128)(2,1)} %refs_2_.1, bf16[2048,256]{1,0:T(8,128)(2,1)} %refs_3_.1), custom_call_target="tpu_custom_call" | custom-call | flops 536870912 | bytes 4194304 | tf_op jit(solution)/shard_map/near/pallas_call | solution.py:66
  75.0 4.4 %collective-permute-done.9.refs_8_ = bf16[128,2048]{1,0:T(8,128)(2,1)S(1)} collective-permute-done((bf16[128,2048]{1,0:T(8,128)(2,1)S(1)}, bf16[128,2048]{1,0:T(8,128)(2,1)S(1)}, u32[]{:S(2)}, u32[]{:S(2)}) %collective-permute-start.9) | collective-permute-done | bytes 524320 | tf_op jit(solution)/shard_map/ppermute | solution.py:342
  79.4 8.4 %collective-permute-done.8.refs_6_ = bf16[128,2048]{1,0:T(8,128)(2,1)S(1)} collective-permute-done((bf16[128,2048]{1,0:T(8,128)(2,1)S(1)}, bf16[128,2048]{1,0:T(8,128)(2,1)S(1)}, u32[]{:S(2)}, u32[]{:S(2)}) %collective-permute-start.8) | collective-permute-done | bytes 524320 | tf_op jit(solution)/shard_map/ppermute | solution.py:342
  88.2 8.3 %collective-permute-start.19 = (s32[2,4,1,4]{3,1,2,0:T(4,128)S(1)}, s32[2,4,1,4]{3,1,2,0:T(4,128)S(1)}, u32[]{:S(2)}, u32[]{:S(2)}) collective-permute-start(s32[2,4,1,4]{3,1,2,0:T(4,128)S(1)} %pad_add_fusion), channel_id=1, source_target_pairs={{0,1},{1,0},{2,3},{3,2},{4,5},{5,4},{6,7},{7,6},{8,9},{9,8},{10,11... | collective-permute-start | bytes 392 | tf_op jit(solution)/shard_map/ppermute | solution.py:342
  98.8 4.0 %collect.1.refs_3_ = bf16[64,2,32,128]{3,2,1,0:T(8,128)(2,1)} custom-call(s32[64,2]{1,0:T(8,128)} %copy.15.where_ref, bf16[32,2,32,128]{3,2,1,0:T(8,128)(2,1)} %copy-done.2, bf16[32,2,32,128]{3,2,1,0:T(8,128)(2,1)} %copy-done.3, bf16[32,2,32,128]{3,2,1,0:T(8,128)(2,1)} %copy-done.5, bf16[32,2,32,128]{3,2,1,0:T(8,128)(2,1)} %collective-permute-done.16.refs_3_, ...), custom_call_target="tpu_custom_call" | custom-call | tf_op jit(solution)/shard_map/collect/pallas_call | solution.py:204
  103.5 33.6 %all-gather.2.cloned.1.call-done.refs_2_ = bf16[256,2,96,128]{3,2,1,0:T(8,128)(2,1)} async-done(((bf16[8,2,96,128]{3,2,1,0:T(8,128)(2,1)}), bf16[256,2,96,128]{3,2,1,0:T(8,128)(2,1)}) %all-gather.2.cloned.1.call-update) | async-done | bytes 12582928 | tf_op jit(solution)/shard_map/all_gather | solution.py:365
  137.1 6.4 %far.2 = (bf16[8,144,256]{2,1,0:T(8,128)(2,1)}, bf16[8,144,256]{2,1,0:T(8,128)(2,1)}) custom-call(s32[33]{0:T(128)} %add_add_fusion.1.picks_ref, bf16[2048,128]{1,0:T(8,128)(2,1)} %collective-permute-done.7.refs_0_, bf16[2048,128]{1,0:T(8,128)(2,1)} %collective-permute-done.21.refs_1_, bf16[256,2,96,128]{3,2,1,0:T(8,128)(2,1)} %all-gather.2.cloned.1.call-done.refs_2_, ...), custom_call_target="tpu_custom_call" | custom-call | flops 8589934592 | bytes 5242880 | tf_op jit(solution)/shard_map/far/pallas_call | solution.py:163
  150.1 6.4 %far.3 = (bf16[8,144,256]{2,1,0:T(8,128)(2,1)}, bf16[8,144,256]{2,1,0:T(8,128)(2,1)}) custom-call(s32[33]{0:T(128)} %add_add_fusion.picks_ref, bf16[2048,128]{1,0:T(8,128)(2,1)} %refs_0_.1, bf16[2048,128]{1,0:T(8,128)(2,1)} %collective-permute-done.20.refs_1_, bf16[256,2,96,128]{3,2,1,0:T(8,128)(2,1)} %all-gather.2.cloned.1.call-done.refs_2_, ...), custom_call_target="tpu_custom_call" | custom-call | flops 8589934592 | bytes 5242880 | tf_op jit(solution)/shard_map/far/pallas_call | solution.py:163
  157.5 6.0 %collective-permute-done.29.refs_1_ = bf16[4,144,256]{2,1,0:T(8,128)(2,1)} collective-permute-done((bf16[4,144,256]{2,1,0:T(8,128)(2,1)}, bf16[4,144,256]{2,1,0:T(8,128)(2,1)}, u32[]{:S(2)}, u32[]{:S(2)}) %collective-permute-start.29) | collective-permute-done | bytes 294944 | tf_op jit(solution)/shard_map/ppermute | solution.py:342
  163.5 4.0 %merge_last.1 = (bf16[4,256,128]{2,1,0:T(8,128)(2,1)}, bf16[4,256,128]{2,1,0:T(8,128)(2,1)}, bf16[2,256,128]{2,1,0:T(8,128)(2,1)}, bf16[2,256,128]{2,1,0:T(8,128...) custom-call(s32[1]{0:T(128)} %bitcast.1.chip_ref, bf16[8,144,256]{2,1,0:T(8,128)(2,1)} %get-tuple-element.85.a_ref, ...), custom_call_target="tpu_custom_call" | custom-call | tf_op jit(solution)/shard_map/merge_last/pallas_call | solution.py:281
  170.1 2.8 %collective-permute-start.32 = (bf16[2,256,128]{2,1,0:T(8,128)(2,1)}, bf16[2,256,128]{2,1,0:T(8,128)(2,1)S(1)}, u32[]{:S(2)}, u32[]{:S(2)}) collective-permute-start(bf16[2,256,128]{2,1,0:T(8,128)(2,1)} %get-tuple-element.96), channel_id=1, source_target_pairs={{0,4},{1,5},{2,6},{3,7},{4,0},{5,1},{6,2},{7,3},{8,12},{9,13},{10,... | collective-permute-start | bytes 393224 | tf_op jit(solution)/shard_map/ppermute | solution.py:342
  174.7 4.8 %collective-permute-done.32.refs_2_ = bf16[2,256,128]{2,1,0:T(8,128)(2,1)S(1)} collective-permute-done((bf16[2,256,128]{2,1,0:T(8,128)(2,1)}, bf16[2,256,128]{2,1,0:T(8,128)(2,1)S(1)}, u32[]{:S(2)}, u32[]{:S(2)}) %collective-permute-start.32) | collective-permute-done | bytes 131104 | tf_op jit(solution)/shard_map/ppermute | solution.py:342
  179.5 2.5 %collective-permute-done.33.refs_3_ = bf16[2,256,128]{2,1,0:T(8,128)(2,1)S(1)} collective-permute-done((bf16[2,256,128]{2,1,0:T(8,128)(2,1)}, bf16[2,256,128]{2,1,0:T(8,128)(2,1)S(1)}, u32[]{:S(2)}, u32[]{:S(2)}) %collective-permute-start.33) | collective-permute-done | bytes 131104 | tf_op jit(solution)/shard_map/ppermute | solution.py:342
  183.0 3.4 %project.1 = bf16[256,2048]{1,0:T(8,128)(2,1)} custom-call(bf16[2,256,128]{2,1,0:T(8,128)(2,1)S(1)} %copy-done.1, bf16[2,256,128]{2,1,0:T(8,128)(2,1)S(1)} %collective-permute-done.31.refs_1_, bf16[2,256,128]{2,1,0:T(8,128)(2,1)S(1)} %collective-permute-done.32.refs_2_, bf16[2,256,128]{2,1,0:T(8,128)(2,1)S(1)} %collective-permute-done.33.refs_3_, ...), custom_call_target="tpu_custom_call" | custom-call | tf_op jit(solution)/shard_map/project/pallas_call | solution.py:323
  (109 shorter events, 36.4 us)
Async XLA Ops:
  7.2 130.0 %all-gather.2.cloned.1.call-start = ((), (), s32[]{:S(2)}) async-start(), calls=%async_computation | async-start | bytes 12976128 | tf_op jit(solution)/shard_map/all_gather | solution.py:365
  10.1 8.6 %collective-permute-start.1 = (bf16[8,2,32,128]{3,2,1,0:T(8,128)(2,1)S(1)}, bf16[8,2,32,128]{3,2,1,0:T(8,128)(2,1)S(1)}, u32[]{:S(2)}, u32[]{:S(2)}) collective-permute-start(bf16[8,2,32,128]{3,2,1,0:T(8,128)(2,1)S(1)} %pad_maximum_fusion.2), channel_id=1, source_target_pairs={{0,224},{8,232},{16,240},{24,248},{32,0},{40,8},{48,16},{56,24},{6... | collective-permute-start | bytes 393224 | tf_op jit(solution)/shard_map/ppermute | solution.py:338
  24.1 6.7 %collective-permute-start.13 = (bf16[8,2,32,128]{3,2,1,0:T(8,128)(2,1)S(1)}, bf16[8,2,32,128]{3,2,1,0:T(8,128)(2,1)S(1)}, u32[]{:S(2)}, u32[]{:S(2)}) collective-permute-start(bf16[8,2,32,128]{3,2,1,0:T(8,128)(2,1)S(1)} %collective-permute-done.11), channel_id=1, source_target_pairs={{0,224},{8,232},{16,240},{24,248},{32,0},{40,8},{48,16},{56,24},{6... | collective-permute-start | bytes 393224 | tf_op jit(solution)/shard_map/ppermute | solution.py:338
  27.2 7.2 %collective-permute-start.12 = (bf16[8,2,32,128]{3,2,1,0:T(8,128)(2,1)S(1)}, bf16[8,2,32,128]{3,2,1,0:T(8,128)(2,1)S(1)}, u32[]{:S(2)}, u32[]{:S(2)}) collective-permute-start(bf16[8,2,32,128]{3,2,1,0:T(8,128)(2,1)S(1)} %collective-permute-done.2), channel_id=1, source_target_pairs={{0,32},{8,40},{16,48},{24,56},{32,64},{40,72},{48,80},{56,88},{64,... | collective-permute-start | bytes 393224 | tf_op jit(solution)/shard_map/ppermute | solution.py:338
  27.2 22.8 %collective-permute-start.5 = (bf16[32,2,32,128]{3,2,1,0:T(8,128)(2,1)S(1)}, bf16[32,2,32,128]{3,2,1,0:T(8,128)(2,1)S(1)}, u32[]{:S(2)}, u32[]{:S(2)}) collective-permute-start(bf16[32,2,32,128]{3,2,1,0:T(8,128)(2,1)S(1)} %pad_maximum_fusion.refs_0_), channel_id=1, source_target_pairs={{0,24},{8,0},{16,8},{24,16},{32,56},{40,32},{48,40},{56,48},{64,88... | collective-permute-start | bytes 1572872 | tf_op jit(solution)/shard_map/ppermute | solution.py:338
  29.8 14.7 %collective-permute-start.3 = (bf16[32,2,32,128]{3,2,1,0:T(8,128)(2,1)S(1)}, bf16[32,2,32,128]{3,2,1,0:T(8,128)(2,1)S(1)}, u32[]{:S(2)}, u32[]{:S(2)}) collective-permute-start(bf16[32,2,32,128]{3,2,1,0:T(8,128)(2,1)S(1)} %pad_maximum_fusion.refs_0_), channel_id=1, source_target_pairs={{0,8},{8,16},{16,24},{24,0},{32,40},{40,48},{48,56},{56,32},{64,72... | collective-permute-start | bytes 1572872 | tf_op jit(solution)/shard_map/ppermute | solution.py:338
  30.8 8.8 %collective-permute-start.15 = (bf16[4,2,32,128]{3,2,1,0:T(8,128)(2,1)S(1)}, bf16[4,2,32,128]{3,2,1,0:T(8,128)(2,1)S(1)}, u32[]{:S(2)}, u32[]{:S(2)}) collective-permute-start(bf16[4,2,32,128]{3,2,1,0:T(8,128)(2,1)S(1)} %slice.25), channel_id=1, source_target_pairs={{0,224},{8,232},{16,240},{24,248},{32,0},{40,8},{48,16},{56,24},{6... | collective-permute-start | bytes 196616 | tf_op jit(solution)/shard_map/ppermute | solution.py:338
  39.7 17.8 %collective-permute-start.17 = (bf16[32,2,32,128]{3,2,1,0:T(8,128)(2,1)S(1)}, bf16[32,2,32,128]{3,2,1,0:T(8,128)(2,1)S(1)}, u32[]{:S(2)}, u32[]{:S(2)}) collective-permute-start(bf16[32,2,32,128]{3,2,1,0:T(8,128)(2,1)S(1)} %constant_dynamic-update-slice_fusion.refs_1_), channel_id=1, source_target_pairs={{0,24},{8,0},{16,8},{24,16},{32,56},{40,32},{48,40},{56,48},{64,88... | collective-permute-start | bytes 1572872 | tf_op jit(solution)/shard_map/ppermute | solution.py:338
  44.5 13.8 %collective-permute-start.4 = (bf16[32,2,32,128]{3,2,1,0:T(8,128)(2,1)S(1)}, bf16[32,2,32,128]{3,2,1,0:T(8,128)(2,1)S(1)}, u32[]{:S(2)}, u32[]{:S(2)}) collective-permute-start(bf16[32,2,32,128]{3,2,1,0:T(8,128)(2,1)S(1)} %collective-permute-done.3.refs_2_), channel_id=1, source_target_pairs={{0,8},{8,16},{16,24},{24,0},{32,40},{40,48},{48,56},{56,32},{64,72... | collective-permute-start | bytes 1572872 | tf_op jit(solution)/shard_map/ppermute | solution.py:338
  44.5 18.0 %collective-permute-start.20 = (bf16[2048,128]{1,0:T(8,128)(2,1)}, bf16[2048,128]{1,0:T(8,128)(2,1)}, u32[]{:S(2)}, u32[]{:S(2)}) collective-permute-start(bf16[2048,128]{1,0:T(8,128)(2,1)} %refs_0_.1), channel_id=1, source_target_pairs={{0,1},{1,0},{2,3},{3,2},{4,5},{5,4},{6,7},{7,6},{8,9},{9,8},{10,11... | collective-permute-start | bytes 1572872 | tf_op jit(solution)/shard_map/ppermute | solution.py:342
  49.7 16.5 %collective-permute-start.16 = (bf16[32,2,32,128]{3,2,1,0:T(8,128)(2,1)S(1)}, bf16[32,2,32,128]{3,2,1,0:T(8,128)(2,1)}, u32[]{:S(2)}, u32[]{:S(2)}) collective-permute-start(bf16[32,2,32,128]{3,2,1,0:T(8,128)(2,1)S(1)} %constant_dynamic-update-slice_fusion.refs_1_), channel_id=1, source_target_pairs={{0,8},{8,16},{16,24},{24,0},{32,40},{40,48},{48,56},{56,32},{64,72... | collective-permute-start | bytes 1572872 | tf_op jit(solution)/shard_map/ppermute | solution.py:338
  50.0 8.2 %collective-permute-start.6 = (s32[4,1,4]{2,1,0:T(1,128)S(1)}, s32[4,1,4]{2,1,0:T(1,128)S(1)}, u32[]{:S(2)}, u32[]{:S(2)}) collective-permute-start(s32[4,1,4]{2,1,0:T(1,128)S(1)} %copy-done.10), channel_id=1, source_target_pairs={{0,2},{1,3},{2,0},{3,1},{4,6},{5,7},{6,4},{7,5},{8,10},{9,11},{10,... | collective-permute-start | bytes 200 | tf_op jit(solution)/shard_map/ppermute | solution.py:342
  57.5 17.5 %collective-permute-start.18 = (bf16[32,2,32,128]{3,2,1,0:T(8,128)(2,1)S(1)}, bf16[32,2,32,128]{3,2,1,0:T(8,128)(2,1)S(1)}, u32[]{:S(2)}, u32[]{:S(2)}) collective-permute-start(bf16[32,2,32,128]{3,2,1,0:T(8,128)(2,1)S(1)} %collective-permute-done.17.refs_5_), channel_id=1, source_target_pairs={{0,24},{8,0},{16,8},{24,16},{32,56},{40,32},{48,40},{56,48},{64,88... | collective-permute-start | bytes 1572872 | tf_op jit(solution)/shard_map/ppermute | solution.py:338
  59.1 15.9 %collective-permute-start.7 = (bf16[2048,128]{1,0:T(8,128)(2,1)}, bf16[2048,128]{1,0:T(8,128)(2,1)}, u32[]{:S(2)}, u32[]{:S(2)}) collective-permute-start(bf16[2048,128]{1,0:T(8,128)(2,1)} %refs_0_.1), channel_id=1, source_target_pairs={{0,2},{1,3},{2,0},{3,1},{4,6},{5,7},{6,4},{7,5},{8,10},{9,11},{10,... | collective-permute-start | bytes 1572872 | tf_op jit(solution)/shard_map/ppermute | solution.py:342
  60.3 14.7 %collective-permute-start.10 = (bf16[128,2048]{1,0:T(8,128)(2,1)S(1)}, bf16[128,2048]{1,0:T(8,128)(2,1)S(1)}, u32[]{:S(2)}, u32[]{:S(2)}) collective-permute-start(bf16[128,2048]{1,0:T(8,128)(2,1)S(1)} %copy-done), channel_id=1, source_target_pairs={{0,6},{1,7},{2,4},{3,5},{4,2},{5,3},{6,0},{7,1},{8,14},{9,15},{10,... | collective-permute-start | bytes 1572872 | tf_op jit(solution)/shard_map/ppermute | solution.py:342
  62.5 16.9 %collective-permute-start.9 = (bf16[128,2048]{1,0:T(8,128)(2,1)S(1)}, bf16[128,2048]{1,0:T(8,128)(2,1)S(1)}, u32[]{:S(2)}, u32[]{:S(2)}) collective-permute-start(bf16[128,2048]{1,0:T(8,128)(2,1)S(1)} %copy-done), channel_id=1, source_target_pairs={{0,4},{1,5},{2,6},{3,7},{4,0},{5,1},{6,2},{7,3},{8,12},{9,13},{10,... | collective-permute-start | bytes 1572872 | tf_op jit(solution)/shard_map/ppermute | solution.py:342
  66.2 21.6 %collective-permute-start.8 = (bf16[128,2048]{1,0:T(8,128)(2,1)S(1)}, bf16[128,2048]{1,0:T(8,128)(2,1)S(1)}, u32[]{:S(2)}, u32[]{:S(2)}) collective-permute-start(bf16[128,2048]{1,0:T(8,128)(2,1)S(1)} %copy-done), channel_id=1, source_target_pairs={{0,2},{1,3},{2,0},{3,1},{4,6},{5,7},{6,4},{7,5},{8,10},{9,11},{10,... | collective-permute-start | bytes 1572872 | tf_op jit(solution)/shard_map/ppermute | solution.py:342
  88.2 9.3 %collective-permute-start.19 = (s32[2,4,1,4]{3,1,2,0:T(4,128)S(1)}, s32[2,4,1,4]{3,1,2,0:T(4,128)S(1)}, u32[]{:S(2)}, u32[]{:S(2)}) collective-permute-start(s32[2,4,1,4]{3,1,2,0:T(4,128)S(1)} %pad_add_fusion), channel_id=1, source_target_pairs={{0,1},{1,0},{2,3},{3,2},{4,5},{5,4},{6,7},{7,6},{8,9},{9,8},{10,11... | collective-permute-start | bytes 392 | tf_op jit(solution)/shard_map/ppermute | solution.py:342
  96.5 6.4 %collective-permute-start.21 = (bf16[2048,128]{1,0:T(8,128)(2,1)}, bf16[2048,128]{1,0:T(8,128)(2,1)}, u32[]{:S(2)}, u32[]{:S(2)}) collective-permute-start(bf16[2048,128]{1,0:T(8,128)(2,1)} %collective-permute-done.7.refs_0_), channel_id=1, source_target_pairs={{0,1},{1,0},{2,3},{3,2},{4,5},{5,4},{6,7},{7,6},{8,9},{9,8},{10,11... | collective-permute-start | bytes 1572872 | tf_op jit(solution)/shard_map/ppermute | solution.py:342
  148.6 8.9 %collective-permute-start.28 = (bf16[4,144,256]{2,1,0:T(8,128)(2,1)}, bf16[4,144,256]{2,1,0:T(8,128)(2,1)S(1)}, u32[]{:S(2)}, u32[]{:S(2)}) collective-permute-start(bf16[4,144,256]{2,1,0:T(8,128)(2,1)} %get-tuple-element.80), channel_id=1, source_target_pairs={{0,2},{1,3},{2,0},{3,1},{4,6},{5,7},{6,4},{7,5},{8,10},{9,11},{10,... | collective-permute-start | bytes 884744 | tf_op jit(solution)/shard_map/ppermute | solution.py:342
  150.0 13.5 %collective-permute-start.29 = (bf16[4,144,256]{2,1,0:T(8,128)(2,1)}, bf16[4,144,256]{2,1,0:T(8,128)(2,1)}, u32[]{:S(2)}, u32[]{:S(2)}) collective-permute-start(bf16[4,144,256]{2,1,0:T(8,128)(2,1)} %get-tuple-element.81), channel_id=1, source_target_pairs={{0,2},{1,3},{2,0},{3,1},{4,6},{5,7},{6,4},{7,5},{8,10},{9,11},{10,... | collective-permute-start | bytes 884744 | tf_op jit(solution)/shard_map/ppermute | solution.py:342
  156.5 7.0 %collective-permute-start.27 = (bf16[8,144,256]{2,1,0:T(8,128)(2,1)}, bf16[8,144,256]{2,1,0:T(8,128)(2,1)}, u32[]{:S(2)}, u32[]{:S(2)}) collective-permute-start(bf16[8,144,256]{2,1,0:T(8,128)(2,1)} %get-tuple-element.86), channel_id=1, source_target_pairs={{0,1},{1,0},{2,3},{3,2},{4,5},{5,4},{6,7},{7,6},{8,9},{9,8},{10,11... | collective-permute-start | bytes 1769480 | tf_op jit(solution)/shard_map/ppermute | solution.py:342
  170.1 9.5 %collective-permute-start.32 = (bf16[2,256,128]{2,1,0:T(8,128)(2,1)}, bf16[2,256,128]{2,1,0:T(8,128)(2,1)S(1)}, u32[]{:S(2)}, u32[]{:S(2)}) collective-permute-start(bf16[2,256,128]{2,1,0:T(8,128)(2,1)} %get-tuple-element.96), channel_id=1, source_target_pairs={{0,4},{1,5},{2,6},{3,7},{4,0},{5,1},{6,2},{7,3},{8,12},{9,13},{10,... | collective-permute-start | bytes 393224 | tf_op jit(solution)/shard_map/ppermute | solution.py:342
  172.9 9.2 %collective-permute-start.33 = (bf16[2,256,128]{2,1,0:T(8,128)(2,1)}, bf16[2,256,128]{2,1,0:T(8,128)(2,1)S(1)}, u32[]{:S(2)}, u32[]{:S(2)}) collective-permute-start(bf16[2,256,128]{2,1,0:T(8,128)(2,1)} %get-tuple-element.97), channel_id=1, source_target_pairs={{0,6},{1,7},{2,4},{3,5},{4,2},{5,3},{6,0},{7,1},{8,14},{9,15},{10,... | collective-permute-start | bytes 393224 | tf_op jit(solution)/shard_map/ppermute | solution.py:342
  (22 other events, 321.4 us)
Sparse Core Ops, SparseCore 0:
  10.6 126.5 all-gather.1

commit v12 on v11

--- a/solution.py
+++ b/solution.py
@@ -22,7 +22,7 @@
 BF16 = jnp.bfloat16
 NX = 4
 NZ = 8
-RING_ROWS = 32
+RING_ROWS = 48
 VMEM_BYTES = 56 << 20
 
 
@@ -367,24 +367,27 @@
     ring = cut(share - RING_ROWS, RING_ROWS)
     z1, z2 = shift(ring, 1, 0), shift(ring, -1, 0)
     z3, z4 = shift(z1, 1, 0), shift(z2, -1, 0)
-    low = jnp.concatenate([ring, z1, z2, z3], axis=0)
-    x1_low, x2_low = shift(low, 0, 1), shift(low, 0, -1)
+    groups = [jnp.concatenate([ring, z1], axis=0), jnp.concatenate([z2, z3], axis=0)]
     z5, z6 = shift(z3, 1, 0), shift(z4, -1, 0)
     half = BLOCKS // 2
     z7, z8 = shift(z5[:half], 1, 0), shift(z6[half:], -1, 0)
-    high = jnp.concatenate([z4, z5, z6, z7, z8], axis=0)
-    x1_high, x2_high = shift(high, 0, 1), shift(high, 0, -1)
-    x3_low, x3_high = shift(x1_low, 0, 1), shift(x2_high, 0, -1)
-    ring_arrays = [low, high, x1_low, x1_high, x2_low, x2_high, x3_low, x3_high]
+    groups += [jnp.concatenate([z4, z5], axis=0), jnp.concatenate([z6, z7, z8], axis=0)]
+    from_below = [shift(group, 0, 1) for group in groups]
+    from_above = [shift(group, 0, -1) for group in groups]
+    farthest = [shift(group, 0, 1) for group in from_below[:2]]
+    farthest += [shift(group, 0, -1) for group in from_above[2:]]
+    ring_arrays = groups + from_below + from_above + farthest
 
     core, chip = head % 2, head // 2
-    queries_core = swap(after(queries, low), 1)
-    near_queries = after([queries, queries_core], *ring_arrays[2:6])
+    queries_core = swap(after(queries, groups[3]), 1)
+    near_queries = after([queries, queries_core], *from_below, *from_above)
     near_state = near(
         jnp.stack([kv, core]).astype(jnp.int32), near_queries, span_keys, span_values
     )
-    picks_chip = swap(after(block_picks, x1_low, x2_low), 2)
-    queries_early, weight_early = after((queries, out_weight), x3_low, picks_chip)
+    picks_chip = swap(after(block_picks, from_below[1], from_above[1]), 2)
+    queries_early, weight_early = after(
+        (queries, out_weight), *from_below, *from_above, *farthest[:3], picks_chip
+    )
     queries_chip = swap(queries_early, 2)
     picks_pair = jnp.stack([block_picks, picks_chip])
     weights = [out_weight] + [None] * (heads - 1)
@@ -407,9 +410,10 @@
     dx = (owner % NX - ctx % NX) % NX
     order_x = jnp.where(dx == 0, 0, jnp.where(dx == 3, 1, jnp.where(dx == 1, 2, 3)))
     order_z = jnp.where(dz == 0, 0, jnp.where(dz > NZ // 2, 2 * (NZ - dz) - 1, 2 * dz))
-    place = jnp.where(dz == NZ // 2, NZ - 1, order_z) * BLOCKS + local
-    upper = (place >= low.shape[0]).astype(jnp.int32)
-    where = jnp.stack([2 * order_x + upper, place - low.shape[0] * upper], axis=-1)
+    order_z = jnp.where(dz == NZ // 2, NZ - 1, order_z)
+    where = jnp.stack(
+        [len(groups) * order_x + order_z // 2, order_z % 2 * BLOCKS + local], axis=-1
+    )
     early = collect(where.astype(jnp.int32), ring_arrays)
 
     picks, group_queries, weights, near_state, early = lax.optimization_barrier(

time: 194 us -> 196 us (1.010)
  starting transfers between devices: 53.2 us -> 80.7 us
  waiting for transfers between devices: 82.9 us -> 57.3 us
    all_gather x1, waiting for transfers between devices: 33.6 us -> 5.68 us  [body(): whole = lax.all_gather(cut(0, share - RING_ROWS), 'ctx', axis=0, tiled=True)]
    ppermute x20, starting transfers between devices: 30.7 us -> 46 us  [swap(): lax.ppermute(array, 'head', [(h, h ^ bits) for h in range(lax.axis_size('...]
    ppermute x14 -> x20, waiting for transfers between devices: 21.7 us -> 36 us  [shift(): return lax.ppermute(array, 'ctx', pairs)]
    ppermute x14 -> x20, starting transfers between devices: 22.5 us -> 34.7 us  [shift(): return lax.ppermute(array, 'ctx', pairs)]
    ppermute x20, waiting for transfers between devices: 27.5 us -> 15.5 us  [swap(): lax.ppermute(array, 'head', [(h, h ^ bits) for h in range(lax.axis_size('...]
  transfers between devices with their start and end apart: 35 -> 41, of which waited for: 14 -> 15; matrix products, arithmetic and copies ran while one was open for 2% -> 2% of each run, Pallas kernels for 10% -> 10%
where the time goes in v12:
time: 196 us
  starting transfers between devices  80.7 us (41%)
  waiting for transfers between devices  57.3 us (29%)
  Pallas kernels  35.9 us (18%)
  between operations  14.5 us (7%)
  local copies, waits for them, and re-layouts  4.58 us (2%)
  other arithmetic  2.78 us (1%)
    ppermute x20, starting transfers between devices, swap(): lax.ppermute(array, 'head', [(h, h ^ bits) for h in range(lax.axis_size('...  46 us
    ppermute x20, waiting for transfers between devices, shift(): return lax.ppermute(array, 'ctx', pairs)  36 us
    ppermute x20, starting transfers between devices, shift(): return lax.ppermute(array, 'ctx', pairs)  34.7 us
    ppermute x20, waiting for transfers between devices, swap(): lax.ppermute(array, 'head', [(h, h ^ bits) for h in range(lax.axis_size('...  15.5 us
    pallas_call x2, Pallas kernels, far(): pl.pallas_call(functools.partial(far_kernel, half=half), in_specs=[pl.Blo...  13 us
    pallas_call x1, Pallas kernels, near(): pl.pallas_call(near_kernel, grid_spec=grid_spec, out_shape=[jax.ShapeDtyp...  6.66 us
    all_gather x1, waiting for transfers between devices, body(): whole = lax.all_gather(cut(0, share - RING_ROWS), 'ctx', axis=0, tiled=True)  5.68 us
    pallas_call x1, Pallas kernels, collect(): pl.pallas_call(collect_kernel, in_specs=[pl.BlockSpec(memory_space=pltpu....  4.7 us
  transfers between devices with their start and end apart: 41, of which 15 were waited for; matrix products, arithmetic and copies ran while one was open for 2% of the time, Pallas kernels for 10%

profile of v12, /device:TPU:1, one launch (start us, length us, event | category | flops | bytes accessed | tf_op | source)
XLA Modules:
  0.0 195.7 jit_solution(12579137654195491889)
XLA Ops:
  12.7 4.0 %collective-permute-start.2 = (bf16[8,2,48,128]{3,2,1,0:T(8,128)(2,1)S(1)}, bf16[8,2,48,128]{3,2,1,0:T(8,128)(2,1)S(1)}, u32[]{:S(2)}, u32[]{:S(2)}) collective-permute-start(bf16[8,2,48,128]{3,2,1,0:T(8,128)(2,1)S(1)} %pad_maximum_fusion.2), channel_id=1, source_target_pairs={{0,224},{8,232},{16,240},{24,248},{32,0},{40,8},{48,16},{56,24},{6... | collective-permute-start | bytes 589832 | tf_op jit(solution)/shard_map/ppermute | solution.py:338
  16.8 4.5 %collective-permute-done = bf16[8,2,48,128]{3,2,1,0:T(8,128)(2,1)S(1)} collective-permute-done((bf16[8,2,48,128]{3,2,1,0:T(8,128)(2,1)S(1)}, bf16[8,2,48,128]{3,2,1,0:T(8,128)(2,1)S(1)}, u32[]{:S(2)}, u32[]{:S(2)}) %collective-permute-start) | collective-permute-done | bytes 196640 | tf_op jit(solution)/shard_map/ppermute | solution.py:338
  22.7 2.7 %collective-permute-start.5 = (bf16[8,2,48,128]{3,2,1,0:T(8,128)(2,1)S(1)}, bf16[8,2,48,128]{3,2,1,0:T(8,128)(2,1)S(1)}, u32[]{:S(2)}, u32[]{:S(2)}) collective-permute-start(bf16[8,2,48,128]{3,2,1,0:T(8,128)(2,1)S(1)} %collective-permute-done.2), channel_id=1, source_target_pairs={{0,224},{8,232},{16,240},{24,248},{32,0},{40,8},{48,16},{56,24},{6... | collective-permute-start | bytes 589832 | tf_op jit(solution)/shard_map/ppermute | solution.py:338
  29.0 2.7 %collective-permute-start.8 = (bf16[8,2,48,128]{3,2,1,0:T(8,128)(2,1)S(1)}, bf16[8,2,48,128]{3,2,1,0:T(8,128)(2,1)S(1)}, u32[]{:S(2)}, u32[]{:S(2)}) collective-permute-start(bf16[8,2,48,128]{3,2,1,0:T(8,128)(2,1)S(1)} %collective-permute-done.5), channel_id=1, source_target_pairs={{0,224},{8,232},{16,240},{24,248},{32,0},{40,8},{48,16},{56,24},{6... | collective-permute-start | bytes 589832 | tf_op jit(solution)/shard_map/ppermute | solution.py:338
  35.8 4.5 %collective-permute-start.13 = (bf16[16,2,48,128]{3,2,1,0:T(8,128)(2,1)S(1)}, bf16[16,2,48,128]{3,2,1,0:T(8,128)(2,1)S(1)}, u32[]{:S(2)}, u32[]{:S(2)}) collective-permute-start(bf16[16,2,48,128]{3,2,1,0:T(8,128)(2,1)S(1)} %constant_dynamic-update-slice_fusion.refs_1_), channel_id=1, source_target_pairs={{0,24},{8,0},{16,8},{24,16},{32,56},{40,32},{48,40},{56,48},{64,88... | collective-permute-start | bytes 1179656 | tf_op jit(solution)/shard_map/ppermute | solution.py:338
  40.4 2.7 %collective-permute-start.10 = (bf16[4,2,48,128]{3,2,1,0:T(8,128)(2,1)S(1)}, bf16[4,2,48,128]{3,2,1,0:T(8,128)(2,1)S(1)}, u32[]{:S(2)}, u32[]{:S(2)}) collective-permute-start(bf16[4,2,48,128]{3,2,1,0:T(8,128)(2,1)S(1)} %slice.25), channel_id=1, source_target_pairs={{0,224},{8,232},{16,240},{24,248},{32,0},{40,8},{48,16},{56,24},{6... | collective-permute-start | bytes 294920 | tf_op jit(solution)/shard_map/ppermute | solution.py:338
  43.2 2.9 %collective-permute-done.9 = bf16[4,2,48,128]{3,2,1,0:T(8,128)(2,1)S(1)} collective-permute-done((bf16[4,2,48,128]{3,2,1,0:T(8,128)(2,1)S(1)}, bf16[4,2,48,128]{3,2,1,0:T(8,128)(2,1)S(1)}, u32[]{:S(2)}, u32[]{:S(2)}) %collective-permute-start.9) | collective-permute-done | bytes 98336 | tf_op jit(solution)/shard_map/ppermute | solution.py:338
  46.1 2.7 %collective-permute-start.14 = (bf16[16,2,48,128]{3,2,1,0:T(8,128)(2,1)S(1)}, bf16[16,2,48,128]{3,2,1,0:T(8,128)(2,1)S(1)}, u32[]{:S(2)}, u32[]{:S(2)}) collective-permute-start(bf16[16,2,48,128]{3,2,1,0:T(8,128)(2,1)S(1)} %constant_dynamic-update-slice_fusion.2.refs_2_), channel_id=1, source_target_pairs={{0,24},{8,0},{16,8},{24,16},{32,56},{40,32},{48,40},{56,48},{64,88... | collective-permute-start | bytes 1179656 | tf_op jit(solution)/shard_map/ppermute | solution.py:338
  53.8 3.1 %collective-permute-start.15 = (bf16[16,2,48,128]{3,2,1,0:T(8,128)(2,1)S(1)}, bf16[16,2,48,128]{3,2,1,0:T(8,128)(2,1)}, u32[]{:S(2)}, u32[]{:S(2)}) collective-permute-start(bf16[16,2,48,128]{3,2,1,0:T(8,128)(2,1)S(1)} %constant_dynamic-update-slice_fusion.4.refs_3_), channel_id=1, source_target_pairs={{0,24},{8,0},{16,8},{24,16},{32,56},{40,32},{48,40},{56,48},{64,88... | collective-permute-start | bytes 1179656 | tf_op jit(solution)/shard_map/ppermute | solution.py:338
  59.3 3.2 %collective-permute-start.18 = (bf16[16,2,48,128]{3,2,1,0:T(8,128)(2,1)S(1)}, bf16[16,2,48,128]{3,2,1,0:T(8,128)(2,1)S(1)}, u32[]{:S(2)}, u32[]{:S(2)}) collective-permute-start(bf16[16,2,48,128]{3,2,1,0:T(8,128)(2,1)S(1)} %collective-permute-done.14.refs_10_), channel_id=1, source_target_pairs={{0,24},{8,0},{16,8},{24,16},{32,56},{40,32},{48,40},{56,48},{64,88... | collective-permute-start | bytes 1179656 | tf_op jit(solution)/shard_map/ppermute | solution.py:338
  62.6 12.0 %collective-permute-start.26 = (bf16[2048,128]{1,0:T(8,128)(2,1)S(1)}, bf16[2048,128]{1,0:T(8,128)(2,1)S(1)}, u32[]{:S(2)}, u32[]{:S(2)}) collective-permute-start(bf16[2048,128]{1,0:T(8,128)(2,1)S(1)} %copy-done.6), channel_id=1, source_target_pairs={{0,1},{1,0},{2,3},{3,2},{4,5},{5,4},{6,7},{7,6},{8,9},{9,8},{10,11... | collective-permute-start | bytes 1572872 | tf_op jit(solution)/shard_map/ppermute | solution.py:342
  74.5 12.0 %collective-permute-done.17.refs_13_ = bf16[16,2,48,128]{3,2,1,0:T(8,128)(2,1)S(1)} collective-permute-done((bf16[16,2,48,128]{3,2,1,0:T(8,128)(2,1)S(1)}, bf16[16,2,48,128]{3,2,1,0:T(8,128)(2,1)S(1)}, u32[]{:S(2)}, u32[]{:S(2)}) %collective-permute-start.17) | collective-permute-done | bytes 393248 | tf_op jit(solution)/shard_map/ppermute | solution.py:338
  88.5 2.9 %collective-permute-start.22 = (bf16[128,2048]{1,0:T(8,128)(2,1)S(1)}, bf16[128,2048]{1,0:T(8,128)(2,1)S(1)}, u32[]{:S(2)}, u32[]{:S(2)}) collective-permute-start(bf16[128,2048]{1,0:T(8,128)(2,1)S(1)} %copy-done), channel_id=1, source_target_pairs={{0,4},{1,5},{2,6},{3,7},{4,0},{5,1},{6,2},{7,3},{8,12},{9,13},{10,... | collective-permute-start | bytes 1572872 | tf_op jit(solution)/shard_map/ppermute | solution.py:342
  94.3 6.7 %near.1 = (f32[4,2,128,256]{3,2,1,0:T(8,128)}, f32[4,2,1,256]{3,2,1,0:T(1,128)}, f32[4,2,1,256]{3,2,1,0:T(1,128)}) custom-call(s32[2]{0:T(128)} %pad_add_fusion.2.place_ref, bf16[2048,128]{1,0:T(8,128)(2,1)} %refs_0_.1, bf16[2048,128]{1,0:T(8,128)(2,1)} %copy-done.7, bf16[2048,256]{1,0:T(8,128)(2,1)} %refs_2_.1, bf16[2048,256]{1,0:T(8,128)(2,1)} %refs_3_.1), custom_call_target="tpu_custom_call" | custom-call | flops 536870912 | bytes 4194304 | tf_op jit(solution)/shard_map/near/pallas_call | solution.py:66
  100.9 7.2 %collective-permute-done.24.refs_15_ = bf16[16,2,48,128]{3,2,1,0:T(8,128)(2,1)} collective-permute-done((bf16[16,2,48,128]{3,2,1,0:T(8,128)(2,1)}, bf16[16,2,48,128]{3,2,1,0:T(8,128)(2,1)}, u32[]{:S(2)}, u32[]{:S(2)}) %collective-permute-start.24) | collective-permute-done | bytes 393248 | tf_op jit(solution)/shard_map/ppermute | solution.py:338
  108.8 17.5 %collective-permute-start.25 = (s32[2,4,1,4]{3,1,2,0:T(4,128)S(1)}, s32[2,4,1,4]{3,1,2,0:T(4,128)S(1)}, u32[]{:S(2)}, u32[]{:S(2)}) collective-permute-start(s32[2,4,1,4]{3,1,2,0:T(4,128)S(1)} %pad_add_fusion), channel_id=1, source_target_pairs={{0,1},{1,0},{2,3},{3,2},{4,5},{5,4},{6,7},{7,6},{8,9},{9,8},{10,11... | collective-permute-start | bytes 392 | tf_op jit(solution)/shard_map/ppermute | solution.py:342
  129.0 4.7 %collect.1.refs_3_ = bf16[64,2,48,128]{3,2,1,0:T(8,128)(2,1)} custom-call(s32[64,2]{1,0:T(8,128)} %copy.15.where_ref, bf16[16,2,48,128]{3,2,1,0:T(8,128)(2,1)} %copy-done.2, bf16[16,2,48,128]{3,2,1,0:T(8,128)(2,1)} %copy-done.4, bf16[16,2,48,128]{3,2,1,0:T(8,128)(2,1)} %copy-done.3, bf16[16,2,48,128]{3,2,1,0:T(8,128)(2,1)} %copy-done.5, ...), custom_call_target="tpu_custom_call" | custom-call | tf_op jit(solution)/shard_map/collect/pallas_call | solution.py:204
  134.3 5.7 %all-gather.2.cloned.1.call-done.refs_2_ = bf16[256,2,80,128]{3,2,1,0:T(8,128)(2,1)} async-done(((bf16[8,2,80,128]{3,2,1,0:T(8,128)(2,1)}), bf16[256,2,80,128]{3,2,1,0:T(8,128)(2,1)}) %all-gather.2.cloned.1.call-update) | async-done | bytes 10485776 | tf_op jit(solution)/shard_map/all_gather | solution.py:365
  140.0 6.5 %far.2 = (bf16[8,144,256]{2,1,0:T(8,128)(2,1)}, bf16[8,144,256]{2,1,0:T(8,128)(2,1)}) custom-call(s32[33]{0:T(128)} %add_add_fusion.1.picks_ref, bf16[2048,128]{1,0:T(8,128)(2,1)} %collective-permute-done.20.refs_0_, bf16[2048,128]{1,0:T(8,128)(2,1)} %collective-permute-done.27.refs_1_, bf16[256,2,80,128]{3,2,1,0:T(8,128)(2,1)} %all-gather.2.cloned.1.call-done.refs_2_, ...), custom_call_target="tpu_custom_call" | custom-call | flops 8589934592 | bytes 5242880 | tf_op jit(solution)/shard_map/far/pallas_call | solution.py:163
  153.0 6.5 %far.3 = (bf16[8,144,256]{2,1,0:T(8,128)(2,1)}, bf16[8,144,256]{2,1,0:T(8,128)(2,1)}) custom-call(s32[33]{0:T(128)} %add_add_fusion.picks_ref, bf16[2048,128]{1,0:T(8,128)(2,1)} %refs_0_.1, bf16[2048,128]{1,0:T(8,128)(2,1)} %copy-done.7, bf16[256,2,80,128]{3,2,1,0:T(8,128)(2,1)} %all-gather.2.cloned.1.call-done.refs_2_, bf16[64,2,48,128]{3,2,1,0:T(8,128)(2,1)} %collect.1.refs_3_), custom_call_target="tpu_custom_call" | custom-call | flops 8589934592 | bytes 5242880 | tf_op jit(solution)/shard_map/far/pallas_call | solution.py:163
  160.6 5.8 %collective-permute-done.35.refs_1_ = bf16[4,144,256]{2,1,0:T(8,128)(2,1)} collective-permute-done((bf16[4,144,256]{2,1,0:T(8,128)(2,1)}, bf16[4,144,256]{2,1,0:T(8,128)(2,1)}, u32[]{:S(2)}, u32[]{:S(2)}) %collective-permute-start.35) | collective-permute-done | bytes 294944 | tf_op jit(solution)/shard_map/ppermute | solution.py:342
  166.4 4.0 %merge_last.1 = (bf16[4,256,128]{2,1,0:T(8,128)(2,1)}, bf16[4,256,128]{2,1,0:T(8,128)(2,1)}, bf16[2,256,128]{2,1,0:T(8,128)(2,1)}, bf16[2,256,128]{2,1,0:T(8,128...) custom-call(s32[1]{0:T(128)} %bitcast.1.chip_ref, bf16[8,144,256]{2,1,0:T(8,128)(2,1)} %get-tuple-element.85.a_ref, ...), custom_call_target="tpu_custom_call" | custom-call | tf_op jit(solution)/shard_map/merge_last/pallas_call | solution.py:281
  177.4 4.6 %collective-permute-done.38.refs_2_ = bf16[2,256,128]{2,1,0:T(8,128)(2,1)S(1)} collective-permute-done((bf16[2,256,128]{2,1,0:T(8,128)(2,1)}, bf16[2,256,128]{2,1,0:T(8,128)(2,1)S(1)}, u32[]{:S(2)}, u32[]{:S(2)}) %collective-permute-start.38) | collective-permute-done | bytes 131104 | tf_op jit(solution)/shard_map/ppermute | solution.py:342
  185.4 3.4 %project.1 = bf16[256,2048]{1,0:T(8,128)(2,1)} custom-call(bf16[2,256,128]{2,1,0:T(8,128)(2,1)S(1)} %copy-done.1, bf16[2,256,128]{2,1,0:T(8,128)(2,1)S(1)} %collective-permute-done.37.refs_1_, bf16[2,256,128]{2,1,0:T(8,128)(2,1)S(1)} %collective-permute-done.38.refs_2_, bf16[2,256,128]{2,1,0:T(8,128)(2,1)S(1)} %collective-permute-done.39.refs_3_, ...), custom_call_target="tpu_custom_call" | custom-call | tf_op jit(solution)/shard_map/project/pallas_call | solution.py:323
  (141 shorter events, 48.8 us)
Async XLA Ops:
  7.2 132.8 %all-gather.2.cloned.1.call-start = ((), (), s32[]{:S(2)}) async-start(), calls=%async_computation | async-start | bytes 10813440 | tf_op jit(solution)/shard_map/all_gather | solution.py:365
  10.2 11.1 %collective-permute-start = (bf16[8,2,48,128]{3,2,1,0:T(8,128)(2,1)S(1)}, bf16[8,2,48,128]{3,2,1,0:T(8,128)(2,1)S(1)}, u32[]{:S(2)}, u32[]{:S(2)}) collective-permute-start(bf16[8,2,48,128]{3,2,1,0:T(8,128)(2,1)S(1)} %pad_maximum_fusion.2), channel_id=1, source_target_pairs={{0,32},{8,40},{16,48},{24,56},{32,64},{40,72},{48,80},{56,88},{64,... | collective-permute-start | bytes 589832 | tf_op jit(solution)/shard_map/ppermute | solution.py:338
  12.7 9.9 %collective-permute-start.2 = (bf16[8,2,48,128]{3,2,1,0:T(8,128)(2,1)S(1)}, bf16[8,2,48,128]{3,2,1,0:T(8,128)(2,1)S(1)}, u32[]{:S(2)}, u32[]{:S(2)}) collective-permute-start(bf16[8,2,48,128]{3,2,1,0:T(8,128)(2,1)S(1)} %pad_maximum_fusion.2), channel_id=1, source_target_pairs={{0,224},{8,232},{16,240},{24,248},{32,0},{40,8},{48,16},{56,24},{6... | collective-permute-start | bytes 589832 | tf_op jit(solution)/shard_map/ppermute | solution.py:338
  21.4 19.1 %collective-permute-start.1 = (bf16[16,2,48,128]{3,2,1,0:T(8,128)(2,1)S(1)}, bf16[16,2,48,128]{3,2,1,0:T(8,128)(2,1)S(1)}, u32[]{:S(2)}, u32[]{:S(2)}) collective-permute-start(bf16[16,2,48,128]{3,2,1,0:T(8,128)(2,1)S(1)} %pad_maximum_fusion.refs_0_), channel_id=1, source_target_pairs={{0,8},{8,16},{16,24},{24,0},{32,40},{40,48},{48,56},{56,32},{64,72... | collective-permute-start | bytes 1179656 | tf_op jit(solution)/shard_map/ppermute | solution.py:338
  27.7 21.0 %collective-permute-start.4 = (bf16[16,2,48,128]{3,2,1,0:T(8,128)(2,1)S(1)}, bf16[16,2,48,128]{3,2,1,0:T(8,128)(2,1)S(1)}, u32[]{:S(2)}, u32[]{:S(2)}) collective-permute-start(bf16[16,2,48,128]{3,2,1,0:T(8,128)(2,1)S(1)} %constant_dynamic-update-slice_fusion.refs_1_), channel_id=1, source_target_pairs={{0,8},{8,16},{16,24},{24,0},{32,40},{40,48},{48,56},{56,32},{64,72... | collective-permute-start | bytes 1179656 | tf_op jit(solution)/shard_map/ppermute | solution.py:338
  29.0 11.3 %collective-permute-start.8 = (bf16[8,2,48,128]{3,2,1,0:T(8,128)(2,1)S(1)}, bf16[8,2,48,128]{3,2,1,0:T(8,128)(2,1)S(1)}, u32[]{:S(2)}, u32[]{:S(2)}) collective-permute-start(bf16[8,2,48,128]{3,2,1,0:T(8,128)(2,1)S(1)} %collective-permute-done.5), channel_id=1, source_target_pairs={{0,224},{8,232},{16,240},{24,248},{32,0},{40,8},{48,16},{56,24},{6... | collective-permute-start | bytes 589832 | tf_op jit(solution)/shard_map/ppermute | solution.py:338
  31.7 20.5 %collective-permute-start.12 = (bf16[16,2,48,128]{3,2,1,0:T(8,128)(2,1)S(1)}, bf16[16,2,48,128]{3,2,1,0:T(8,128)(2,1)S(1)}, u32[]{:S(2)}, u32[]{:S(2)}) collective-permute-start(bf16[16,2,48,128]{3,2,1,0:T(8,128)(2,1)S(1)} %pad_maximum_fusion.refs_0_), channel_id=1, source_target_pairs={{0,24},{8,0},{16,8},{24,16},{32,56},{40,32},{48,40},{56,48},{64,88... | collective-permute-start | bytes 1179656 | tf_op jit(solution)/shard_map/ppermute | solution.py:338
  35.8 15.2 %collective-permute-start.13 = (bf16[16,2,48,128]{3,2,1,0:T(8,128)(2,1)S(1)}, bf16[16,2,48,128]{3,2,1,0:T(8,128)(2,1)S(1)}, u32[]{:S(2)}, u32[]{:S(2)}) collective-permute-start(bf16[16,2,48,128]{3,2,1,0:T(8,128)(2,1)S(1)} %constant_dynamic-update-slice_fusion.refs_1_), channel_id=1, source_target_pairs={{0,24},{8,0},{16,8},{24,16},{32,56},{40,32},{48,40},{56,48},{64,88... | collective-permute-start | bytes 1179656 | tf_op jit(solution)/shard_map/ppermute | solution.py:338
  46.1 10.9 %collective-permute-start.7 = (bf16[16,2,48,128]{3,2,1,0:T(8,128)(2,1)S(1)}, bf16[16,2,48,128]{3,2,1,0:T(8,128)(2,1)S(1)}, u32[]{:S(2)}, u32[]{:S(2)}) collective-permute-start(bf16[16,2,48,128]{3,2,1,0:T(8,128)(2,1)S(1)} %constant_dynamic-update-slice_fusion.2.refs_2_), channel_id=1, source_target_pairs={{0,8},{8,16},{16,24},{24,0},{32,40},{40,48},{48,56},{56,32},{64,72... | collective-permute-start | bytes 1179656 | tf_op jit(solution)/shard_map/ppermute | solution.py:338
  46.1 13.2 %collective-permute-start.14 = (bf16[16,2,48,128]{3,2,1,0:T(8,128)(2,1)S(1)}, bf16[16,2,48,128]{3,2,1,0:T(8,128)(2,1)S(1)}, u32[]{:S(2)}, u32[]{:S(2)}) collective-permute-start(bf16[16,2,48,128]{3,2,1,0:T(8,128)(2,1)S(1)} %constant_dynamic-update-slice_fusion.2.refs_2_), channel_id=1, source_target_pairs={{0,24},{8,0},{16,8},{24,16},{32,56},{40,32},{48,40},{56,48},{64,88... | collective-permute-start | bytes 1179656 | tf_op jit(solution)/shard_map/ppermute | solution.py:338
  48.8 13.8 %collective-permute-start.16 = (bf16[16,2,48,128]{3,2,1,0:T(8,128)(2,1)S(1)}, bf16[16,2,48,128]{3,2,1,0:T(8,128)(2,1)S(1)}, u32[]{:S(2)}, u32[]{:S(2)}) collective-permute-start(bf16[16,2,48,128]{3,2,1,0:T(8,128)(2,1)S(1)} %collective-permute-done.1.refs_4_), channel_id=1, source_target_pairs={{0,8},{8,16},{16,24},{24,0},{32,40},{40,48},{48,56},{56,32},{64,72... | collective-permute-start | bytes 1179656 | tf_op jit(solution)/shard_map/ppermute | solution.py:338
  52.2 22.3 %collective-permute-start.11 = (bf16[16,2,48,128]{3,2,1,0:T(8,128)(2,1)S(1)}, bf16[16,2,48,128]{3,2,1,0:T(8,128)(2,1)S(1)}, u32[]{:S(2)}, u32[]{:S(2)}) collective-permute-start(bf16[16,2,48,128]{3,2,1,0:T(8,128)(2,1)S(1)} %constant_dynamic-update-slice_fusion.4.refs_3_), channel_id=1, source_target_pairs={{0,8},{8,16},{16,24},{24,0},{32,40},{40,48},{48,56},{56,32},{64,72... | collective-permute-start | bytes 1179656 | tf_op jit(solution)/shard_map/ppermute | solution.py:338
  53.8 20.7 %collective-permute-start.15 = (bf16[16,2,48,128]{3,2,1,0:T(8,128)(2,1)S(1)}, bf16[16,2,48,128]{3,2,1,0:T(8,128)(2,1)}, u32[]{:S(2)}, u32[]{:S(2)}) collective-permute-start(bf16[16,2,48,128]{3,2,1,0:T(8,128)(2,1)S(1)} %constant_dynamic-update-slice_fusion.4.refs_3_), channel_id=1, source_target_pairs={{0,24},{8,0},{16,8},{24,16},{32,56},{40,32},{48,40},{56,48},{64,88... | collective-permute-start | bytes 1179656 | tf_op jit(solution)/shard_map/ppermute | solution.py:338
  57.0 29.5 %collective-permute-start.17 = (bf16[16,2,48,128]{3,2,1,0:T(8,128)(2,1)S(1)}, bf16[16,2,48,128]{3,2,1,0:T(8,128)(2,1)S(1)}, u32[]{:S(2)}, u32[]{:S(2)}) collective-permute-start(bf16[16,2,48,128]{3,2,1,0:T(8,128)(2,1)S(1)} %collective-permute-done.4.refs_5_), channel_id=1, source_target_pairs={{0,8},{8,16},{16,24},{24,0},{32,40},{40,48},{48,56},{56,32},{64,72... | collective-permute-start | bytes 1179656 | tf_op jit(solution)/shard_map/ppermute | solution.py:338
  59.3 27.2 %collective-permute-start.18 = (bf16[16,2,48,128]{3,2,1,0:T(8,128)(2,1)S(1)}, bf16[16,2,48,128]{3,2,1,0:T(8,128)(2,1)S(1)}, u32[]{:S(2)}, u32[]{:S(2)}) collective-permute-start(bf16[16,2,48,128]{3,2,1,0:T(8,128)(2,1)S(1)} %collective-permute-done.14.refs_10_), channel_id=1, source_target_pairs={{0,24},{8,0},{16,8},{24,16},{32,56},{40,32},{48,40},{56,48},{64,88... | collective-permute-start | bytes 1179656 | tf_op jit(solution)/shard_map/ppermute | solution.py:338
  62.6 29.7 %collective-permute-start.26 = (bf16[2048,128]{1,0:T(8,128)(2,1)S(1)}, bf16[2048,128]{1,0:T(8,128)(2,1)S(1)}, u32[]{:S(2)}, u32[]{:S(2)}) collective-permute-start(bf16[2048,128]{1,0:T(8,128)(2,1)S(1)} %copy-done.6), channel_id=1, source_target_pairs={{0,1},{1,0},{2,3},{3,2},{4,5},{5,4},{6,7},{7,6},{8,9},{9,8},{10,11... | collective-permute-start | bytes 1572872 | tf_op jit(solution)/shard_map/ppermute | solution.py:342
  86.5 21.5 %collective-permute-start.20 = (bf16[2048,128]{1,0:T(8,128)(2,1)S(1)}, bf16[2048,128]{1,0:T(8,128)(2,1)}, u32[]{:S(2)}, u32[]{:S(2)}) collective-permute-start(bf16[2048,128]{1,0:T(8,128)(2,1)S(1)} %copy-done.6), channel_id=1, source_target_pairs={{0,2},{1,3},{2,0},{3,1},{4,6},{5,7},{6,4},{7,5},{8,10},{9,11},{10,... | collective-permute-start | bytes 1572872 | tf_op jit(solution)/shard_map/ppermute | solution.py:342
  88.4 19.7 %collective-permute-start.21 = (bf16[128,2048]{1,0:T(8,128)(2,1)S(1)}, bf16[128,2048]{1,0:T(8,128)(2,1)S(1)}, u32[]{:S(2)}, u32[]{:S(2)}) collective-permute-start(bf16[128,2048]{1,0:T(8,128)(2,1)S(1)} %copy-done), channel_id=1, source_target_pairs={{0,2},{1,3},{2,0},{3,1},{4,6},{5,7},{6,4},{7,5},{8,10},{9,11},{10,... | collective-permute-start | bytes 1572872 | tf_op jit(solution)/shard_map/ppermute | solution.py:342
  88.5 20.2 %collective-permute-start.22 = (bf16[128,2048]{1,0:T(8,128)(2,1)S(1)}, bf16[128,2048]{1,0:T(8,128)(2,1)S(1)}, u32[]{:S(2)}, u32[]{:S(2)}) collective-permute-start(bf16[128,2048]{1,0:T(8,128)(2,1)S(1)} %copy-done), channel_id=1, source_target_pairs={{0,4},{1,5},{2,6},{3,7},{4,0},{5,1},{6,2},{7,3},{8,12},{9,13},{10,... | collective-permute-start | bytes 1572872 | tf_op jit(solution)/shard_map/ppermute | solution.py:342
  91.4 17.4 %collective-permute-start.23 = (bf16[128,2048]{1,0:T(8,128)(2,1)S(1)}, bf16[128,2048]{1,0:T(8,128)(2,1)S(1)}, u32[]{:S(2)}, u32[]{:S(2)}) collective-permute-start(bf16[128,2048]{1,0:T(8,128)(2,1)S(1)} %copy-done), channel_id=1, source_target_pairs={{0,6},{1,7},{2,4},{3,5},{4,2},{5,3},{6,0},{7,1},{8,14},{9,15},{10,... | collective-permute-start | bytes 1572872 | tf_op jit(solution)/shard_map/ppermute | solution.py:342
  92.4 15.7 %collective-permute-start.24 = (bf16[16,2,48,128]{3,2,1,0:T(8,128)(2,1)}, bf16[16,2,48,128]{3,2,1,0:T(8,128)(2,1)}, u32[]{:S(2)}, u32[]{:S(2)}) collective-permute-start(bf16[16,2,48,128]{3,2,1,0:T(8,128)(2,1)} %collective-permute-done.15.refs_11_), channel_id=1, source_target_pairs={{0,24},{8,0},{16,8},{24,16},{32,56},{40,32},{48,40},{56,48},{64,88... | collective-permute-start | bytes 1179656 | tf_op jit(solution)/shard_map/ppermute | solution.py:338
  108.8 18.9 %collective-permute-start.25 = (s32[2,4,1,4]{3,1,2,0:T(4,128)S(1)}, s32[2,4,1,4]{3,1,2,0:T(4,128)S(1)}, u32[]{:S(2)}, u32[]{:S(2)}) collective-permute-start(s32[2,4,1,4]{3,1,2,0:T(4,128)S(1)} %pad_add_fusion), channel_id=1, source_target_pairs={{0,1},{1,0},{2,3},{3,2},{4,5},{5,4},{6,7},{7,6},{8,9},{9,8},{10,11... | collective-permute-start | bytes 392 | tf_op jit(solution)/shard_map/ppermute | solution.py:342
  152.8 13.6 %collective-permute-start.35 = (bf16[4,144,256]{2,1,0:T(8,128)(2,1)}, bf16[4,144,256]{2,1,0:T(8,128)(2,1)}, u32[]{:S(2)}, u32[]{:S(2)}) collective-permute-start(bf16[4,144,256]{2,1,0:T(8,128)(2,1)} %get-tuple-element.81), channel_id=1, source_target_pairs={{0,2},{1,3},{2,0},{3,1},{4,6},{5,7},{6,4},{7,5},{8,10},{9,11},{10,... | collective-permute-start | bytes 884744 | tf_op jit(solution)/shard_map/ppermute | solution.py:342
  175.3 9.2 %collective-permute-start.39 = (bf16[2,256,128]{2,1,0:T(8,128)(2,1)}, bf16[2,256,128]{2,1,0:T(8,128)(2,1)S(1)}, u32[]{:S(2)}, u32[]{:S(2)}) collective-permute-start(bf16[2,256,128]{2,1,0:T(8,128)(2,1)} %get-tuple-element.97), channel_id=1, source_target_pairs={{0,6},{1,7},{2,4},{3,5},{4,2},{5,3},{6,0},{7,1},{8,14},{9,15},{10,... | collective-permute-start | bytes 393224 | tf_op jit(solution)/shard_map/ppermute | solution.py:342
  (37 other events, 781.0 us)
Sparse Core Ops, SparseCore 0:
  10.6 129.3 all-gather.1

commit v13 on v12

--- a/solution.py
+++ b/solution.py
@@ -22,7 +22,7 @@
 BF16 = jnp.bfloat16
 NX = 4
 NZ = 8
-RING_ROWS = 48
+RING_ROWS = 32
 VMEM_BYTES = 56 << 20
 
 
@@ -386,7 +386,7 @@
     )
     picks_chip = swap(after(block_picks, from_below[1], from_above[1]), 2)
     queries_early, weight_early = after(
-        (queries, out_weight), *from_below, *from_above, *farthest[:3], picks_chip
+        (queries, out_weight), *from_below, *from_above, *farthest, picks_chip
     )
     queries_chip = swap(queries_early, 2)
     picks_pair = jnp.stack([block_picks, picks_chip])

time: 196 us -> 193 us (0.985)
  starting transfers between devices: 80.7 us -> 72.1 us
  waiting for transfers between devices: 57.3 us -> 62.1 us
    ppermute x20, waiting for transfers between devices: 36 us -> 15.5 us  [shift(): return lax.ppermute(array, 'ctx', pairs)]
    all_gather x1, waiting for transfers between devices: 5.68 us -> 22 us  [body(): whole = lax.all_gather(cut(0, share - RING_ROWS), 'ctx', axis=0, tiled=True)]
    ppermute x20, waiting for transfers between devices: 15.5 us -> 24.6 us  [swap(): lax.ppermute(array, 'head', [(h, h ^ bits) for h in range(lax.axis_size('...]
    ppermute x20, starting transfers between devices: 34.7 us -> 28.8 us  [shift(): return lax.ppermute(array, 'ctx', pairs)]
    ppermute x20, starting transfers between devices: 46 us -> 43.3 us  [swap(): lax.ppermute(array, 'head', [(h, h ^ bits) for h in range(lax.axis_size('...]
  transfers between devices with their start and end apart: 41 -> 41, of which waited for: 15 -> 14; matrix products, arithmetic and copies ran while one was open for 2% -> 2% of each run, Pallas kernels for 10% -> 10%
where the time goes in v13:
time: 193 us; the launch traced here: 192 us
  starting transfers between devices  72.1 us (37%)
  waiting for transfers between devices  62.1 us (32%)
  Pallas kernels  35.4 us (18%)
  between operations  14.6 us (8%)
  local copies, waits for them, and re-layouts  5.2 us (3%)
  other arithmetic  2.91 us (2%)
    ppermute x20, starting transfers between devices, swap(): lax.ppermute(array, 'head', [(h, h ^ bits) for h in range(lax.axis_size('...  43.3 us
    ppermute x20, starting transfers between devices, shift(): return lax.ppermute(array, 'ctx', pairs)  28.8 us
    ppermute x20, waiting for transfers between devices, swap(): lax.ppermute(array, 'head', [(h, h ^ bits) for h in range(lax.axis_size('...  24.6 us
    all_gather x1, waiting for transfers between devices, body(): whole = lax.all_gather(cut(0, share - RING_ROWS), 'ctx', axis=0, tiled=True)  22 us
    ppermute x20, waiting for transfers between devices, shift(): return lax.ppermute(array, 'ctx', pairs)  15.5 us
    pallas_call x2, Pallas kernels, far(): pl.pallas_call(functools.partial(far_kernel, half=half), in_specs=[pl.Blo...  12.7 us
    pallas_call x1, Pallas kernels, near(): pl.pallas_call(near_kernel, grid_spec=grid_spec, out_shape=[jax.ShapeDtyp...  6.67 us
    pallas_call x1, Pallas kernels, collect(): pl.pallas_call(collect_kernel, in_specs=[pl.BlockSpec(memory_space=pltpu....  4.49 us
  transfers between devices with their start and end apart: 41, of which 14 were waited for; matrix products, arithmetic and copies ran while one was open for 2% of the time, Pallas kernels for 10%

profile of v13, /device:TPU:1, one launch (start us, length us, event | category | flops | bytes accessed | tf_op | source)
XLA Modules:
  0.0 192.2 jit_solution(11768660982267270279)
XLA Ops:
  10.1 6.5 %collective-permute-start.2 = (bf16[8,2,32,128]{3,2,1,0:T(8,128)(2,1)S(1)}, bf16[8,2,32,128]{3,2,1,0:T(8,128)(2,1)S(1)}, u32[]{:S(2)}, u32[]{:S(2)}) collective-permute-start(bf16[8,2,32,128]{3,2,1,0:T(8,128)(2,1)S(1)} %pad_maximum_fusion.2), channel_id=1, source_target_pairs={{0,224},{8,232},{16,240},{24,248},{32,0},{40,8},{48,16},{56,24},{6... | collective-permute-start | bytes 393224 | tf_op jit(solution)/shard_map/ppermute | solution.py:338
  18.7 3.4 %collective-permute-start.5 = (bf16[8,2,32,128]{3,2,1,0:T(8,128)(2,1)S(1)}, bf16[8,2,32,128]{3,2,1,0:T(8,128)(2,1)S(1)}, u32[]{:S(2)}, u32[]{:S(2)}) collective-permute-start(bf16[8,2,32,128]{3,2,1,0:T(8,128)(2,1)S(1)} %collective-permute-done.2), channel_id=1, source_target_pairs={{0,224},{8,232},{16,240},{24,248},{32,0},{40,8},{48,16},{56,24},{6... | collective-permute-start | bytes 393224 | tf_op jit(solution)/shard_map/ppermute | solution.py:338
  22.2 2.6 %collective-permute-start.12 = (bf16[16,2,32,128]{3,2,1,0:T(8,128)(2,1)S(1)}, bf16[16,2,32,128]{3,2,1,0:T(8,128)(2,1)S(1)}, u32[]{:S(2)}, u32[]{:S(2)}) collective-permute-start(bf16[16,2,32,128]{3,2,1,0:T(8,128)(2,1)S(1)} %pad_maximum_fusion.1.refs_0_), channel_id=1, source_target_pairs={{0,24},{8,0},{16,8},{24,16},{32,56},{40,32},{48,40},{56,48},{64,88... | collective-permute-start | bytes 786440 | tf_op jit(solution)/shard_map/ppermute | solution.py:338
  24.8 2.7 %collective-permute-start.8 = (bf16[8,2,32,128]{3,2,1,0:T(8,128)(2,1)S(1)}, bf16[8,2,32,128]{3,2,1,0:T(8,128)(2,1)S(1)}, u32[]{:S(2)}, u32[]{:S(2)}) collective-permute-start(bf16[8,2,32,128]{3,2,1,0:T(8,128)(2,1)S(1)} %collective-permute-done.5), channel_id=1, source_target_pairs={{0,224},{8,232},{16,240},{24,248},{32,0},{40,8},{48,16},{56,24},{6... | collective-permute-start | bytes 393224 | tf_op jit(solution)/shard_map/ppermute | solution.py:338
  27.6 2.8 %collective-permute-start.13 = (bf16[16,2,32,128]{3,2,1,0:T(8,128)(2,1)S(1)}, bf16[16,2,32,128]{3,2,1,0:T(8,128)(2,1)S(1)}, u32[]{:S(2)}, u32[]{:S(2)}) collective-permute-start(bf16[16,2,32,128]{3,2,1,0:T(8,128)(2,1)S(1)} %constant_dynamic-update-slice_fusion.refs_1_), channel_id=1, source_target_pairs={{0,24},{8,0},{16,8},{24,16},{32,56},{40,32},{48,40},{56,48},{64,88... | collective-permute-start | bytes 786440 | tf_op jit(solution)/shard_map/ppermute | solution.py:338
  30.3 4.5 %collective-permute-done.6 = bf16[8,2,32,128]{3,2,1,0:T(8,128)(2,1)S(1)} collective-permute-done((bf16[8,2,32,128]{3,2,1,0:T(8,128)(2,1)S(1)}, bf16[8,2,32,128]{3,2,1,0:T(8,128)(2,1)S(1)}, u32[]{:S(2)}, u32[]{:S(2)}) %collective-permute-start.6) | collective-permute-done | bytes 131104 | tf_op jit(solution)/shard_map/ppermute | solution.py:338
  35.1 5.2 %collective-permute-done.9 = bf16[4,2,32,128]{3,2,1,0:T(8,128)(2,1)S(1)} collective-permute-done((bf16[4,2,32,128]{3,2,1,0:T(8,128)(2,1)S(1)}, bf16[4,2,32,128]{3,2,1,0:T(8,128)(2,1)S(1)}, u32[]{:S(2)}, u32[]{:S(2)}) %collective-permute-start.9) | collective-permute-done | bytes 65568 | tf_op jit(solution)/shard_map/ppermute | solution.py:338
  40.3 3.5 %collective-permute-done.10 = bf16[4,2,32,128]{3,2,1,0:T(8,128)(2,1)S(1)} collective-permute-done((bf16[4,2,32,128]{3,2,1,0:T(8,128)(2,1)S(1)}, bf16[4,2,32,128]{3,2,1,0:T(8,128)(2,1)S(1)}, u32[]{:S(2)}, u32[]{:S(2)}) %collective-permute-start.10) | collective-permute-done | bytes 65568 | tf_op jit(solution)/shard_map/ppermute | solution.py:338
  43.8 3.8 %collective-permute-start.14 = (bf16[16,2,32,128]{3,2,1,0:T(8,128)(2,1)S(1)}, bf16[16,2,32,128]{3,2,1,0:T(8,128)(2,1)S(1)}, u32[]{:S(2)}, u32[]{:S(2)}) collective-permute-start(bf16[16,2,32,128]{3,2,1,0:T(8,128)(2,1)S(1)} %constant_dynamic-update-slice_fusion.2.refs_2_), channel_id=1, source_target_pairs={{0,24},{8,0},{16,8},{24,16},{32,56},{40,32},{48,40},{56,48},{64,88... | collective-permute-start | bytes 786440 | tf_op jit(solution)/shard_map/ppermute | solution.py:338
  47.7 2.6 %collective-permute-start.15 = (bf16[16,2,32,128]{3,2,1,0:T(8,128)(2,1)S(1)}, bf16[16,2,32,128]{3,2,1,0:T(8,128)(2,1)S(1)}, u32[]{:S(2)}, u32[]{:S(2)}) collective-permute-start(bf16[16,2,32,128]{3,2,1,0:T(8,128)(2,1)S(1)} %constant_dynamic-update-slice_fusion.4.refs_3_), channel_id=1, source_target_pairs={{0,24},{8,0},{16,8},{24,16},{32,56},{40,32},{48,40},{56,48},{64,88... | collective-permute-start | bytes 786440 | tf_op jit(solution)/shard_map/ppermute | solution.py:338
  57.6 11.3 %collective-permute-start.26 = (bf16[2048,128]{1,0:T(8,128)(2,1)S(1)}, bf16[2048,128]{1,0:T(8,128)(2,1)S(1)}, u32[]{:S(2)}, u32[]{:S(2)}) collective-permute-start(bf16[2048,128]{1,0:T(8,128)(2,1)S(1)} %copy-done.6), channel_id=1, source_target_pairs={{0,1},{1,0},{2,3},{3,2},{4,5},{5,4},{6,7},{7,6},{8,9},{9,8},{10,11... | collective-permute-start | bytes 1572872 | tf_op jit(solution)/shard_map/ppermute | solution.py:342
  70.3 3.2 %collective-permute-start.24 = (bf16[128,2048]{1,0:T(8,128)(2,1)S(1)}, bf16[128,2048]{1,0:T(8,128)(2,1)S(1)}, u32[]{:S(2)}, u32[]{:S(2)}) collective-permute-start(bf16[128,2048]{1,0:T(8,128)(2,1)S(1)} %copy-done), channel_id=1, source_target_pairs={{0,6},{1,7},{2,4},{3,5},{4,2},{5,3},{6,0},{7,1},{8,14},{9,15},{10,... | collective-permute-start | bytes 1572872 | tf_op jit(solution)/shard_map/ppermute | solution.py:342
  76.3 6.7 %near.1 = (f32[4,2,128,256]{3,2,1,0:T(8,128)}, f32[4,2,1,256]{3,2,1,0:T(1,128)}, f32[4,2,1,256]{3,2,1,0:T(1,128)}) custom-call(s32[2]{0:T(128)} %pad_add_fusion.2.place_ref, bf16[2048,128]{1,0:T(8,128)(2,1)} %refs_0_.1, bf16[2048,128]{1,0:T(8,128)(2,1)} %copy-done.7, bf16[2048,256]{1,0:T(8,128)(2,1)} %refs_2_.1, bf16[2048,256]{1,0:T(8,128)(2,1)} %refs_3_.1), custom_call_target="tpu_custom_call" | custom-call | flops 536870912 | bytes 4194304 | tf_op jit(solution)/shard_map/near/pallas_call | solution.py:66
  86.8 4.5 %collective-permute-done.22.refs_6_ = bf16[128,2048]{1,0:T(8,128)(2,1)S(1)} collective-permute-done((bf16[128,2048]{1,0:T(8,128)(2,1)S(1)}, bf16[128,2048]{1,0:T(8,128)(2,1)S(1)}, u32[]{:S(2)}, u32[]{:S(2)}) %collective-permute-start.22) | collective-permute-done | bytes 524320 | tf_op jit(solution)/shard_map/ppermute | solution.py:342
  91.6 14.7 %collective-permute-start.25 = (s32[2,4,1,4]{3,1,2,0:T(4,128)S(1)}, s32[2,4,1,4]{3,1,2,0:T(4,128)S(1)}, u32[]{:S(2)}, u32[]{:S(2)}) collective-permute-start(s32[2,4,1,4]{3,1,2,0:T(4,128)S(1)} %pad_add_fusion), channel_id=1, source_target_pairs={{0,1},{1,0},{2,3},{3,2},{4,5},{5,4},{6,7},{7,6},{8,9},{9,8},{10,11... | collective-permute-start | bytes 392 | tf_op jit(solution)/shard_map/ppermute | solution.py:342
  108.7 4.5 %collect.1.refs_3_ = bf16[64,2,32,128]{3,2,1,0:T(8,128)(2,1)} custom-call(s32[64,2]{1,0:T(8,128)} %copy.15.where_ref, bf16[16,2,32,128]{3,2,1,0:T(8,128)(2,1)} %copy-done.2, bf16[16,2,32,128]{3,2,1,0:T(8,128)(2,1)} %copy-done.4, bf16[16,2,32,128]{3,2,1,0:T(8,128)(2,1)} %copy-done.3, bf16[16,2,32,128]{3,2,1,0:T(8,128)(2,1)} %copy-done.5, ...), custom_call_target="tpu_custom_call" | custom-call | tf_op jit(solution)/shard_map/collect/pallas_call | solution.py:204
  113.9 22.0 %all-gather.2.cloned.1.call-done.refs_2_ = bf16[256,2,96,128]{3,2,1,0:T(8,128)(2,1)} async-done(((bf16[8,2,96,128]{3,2,1,0:T(8,128)(2,1)}), bf16[256,2,96,128]{3,2,1,0:T(8,128)(2,1)}) %all-gather.2.cloned.1.call-update) | async-done | bytes 12582928 | tf_op jit(solution)/shard_map/all_gather | solution.py:365
  135.9 6.4 %far.2 = (bf16[8,144,256]{2,1,0:T(8,128)(2,1)}, bf16[8,144,256]{2,1,0:T(8,128)(2,1)}) custom-call(s32[33]{0:T(128)} %add_add_fusion.1.picks_ref, bf16[2048,128]{1,0:T(8,128)(2,1)} %collective-permute-done.21.refs_0_, bf16[2048,128]{1,0:T(8,128)(2,1)} %collective-permute-done.27.refs_1_, bf16[256,2,96,128]{3,2,1,0:T(8,128)(2,1)} %all-gather.2.cloned.1.call-done.refs_2_, ...), custom_call_target="tpu_custom_call" | custom-call | flops 8589934592 | bytes 5242880 | tf_op jit(solution)/shard_map/far/pallas_call | solution.py:163
  148.9 6.3 %far.3 = (bf16[8,144,256]{2,1,0:T(8,128)(2,1)}, bf16[8,144,256]{2,1,0:T(8,128)(2,1)}) custom-call(s32[33]{0:T(128)} %add_add_fusion.picks_ref, bf16[2048,128]{1,0:T(8,128)(2,1)} %refs_0_.1, bf16[2048,128]{1,0:T(8,128)(2,1)} %copy-done.7, bf16[256,2,96,128]{3,2,1,0:T(8,128)(2,1)} %all-gather.2.cloned.1.call-done.refs_2_, bf16[64,2,32,128]{3,2,1,0:T(8,128)(2,1)} %collect.1.refs_3_), custom_call_target="tpu_custom_call" | custom-call | flops 8589934592 | bytes 5242880 | tf_op jit(solution)/shard_map/far/pallas_call | solution.py:163
  156.3 6.0 %collective-permute-done.35.refs_1_ = bf16[4,144,256]{2,1,0:T(8,128)(2,1)} collective-permute-done((bf16[4,144,256]{2,1,0:T(8,128)(2,1)}, bf16[4,144,256]{2,1,0:T(8,128)(2,1)}, u32[]{:S(2)}, u32[]{:S(2)}) %collective-permute-start.35) | collective-permute-done | bytes 294944 | tf_op jit(solution)/shard_map/ppermute | solution.py:342
  162.3 4.0 %merge_last.1 = (bf16[4,256,128]{2,1,0:T(8,128)(2,1)}, bf16[4,256,128]{2,1,0:T(8,128)(2,1)}, bf16[2,256,128]{2,1,0:T(8,128)(2,1)}, bf16[2,256,128]{2,1,0:T(8,128...) custom-call(s32[1]{0:T(128)} %bitcast.1.chip_ref, bf16[8,144,256]{2,1,0:T(8,128)(2,1)} %get-tuple-element.85.a_ref, ...), custom_call_target="tpu_custom_call" | custom-call | tf_op jit(solution)/shard_map/merge_last/pallas_call | solution.py:281
  168.8 3.0 %collective-permute-start.38 = (bf16[2,256,128]{2,1,0:T(8,128)(2,1)}, bf16[2,256,128]{2,1,0:T(8,128)(2,1)S(1)}, u32[]{:S(2)}, u32[]{:S(2)}) collective-permute-start(bf16[2,256,128]{2,1,0:T(8,128)(2,1)} %get-tuple-element.96), channel_id=1, source_target_pairs={{0,4},{1,5},{2,6},{3,7},{4,0},{5,1},{6,2},{7,3},{8,12},{9,13},{10,... | collective-permute-start | bytes 393224 | tf_op jit(solution)/shard_map/ppermute | solution.py:342
  173.7 4.8 %collective-permute-done.38.refs_2_ = bf16[2,256,128]{2,1,0:T(8,128)(2,1)S(1)} collective-permute-done((bf16[2,256,128]{2,1,0:T(8,128)(2,1)}, bf16[2,256,128]{2,1,0:T(8,128)(2,1)S(1)}, u32[]{:S(2)}, u32[]{:S(2)}) %collective-permute-start.38) | collective-permute-done | bytes 131104 | tf_op jit(solution)/shard_map/ppermute | solution.py:342
  182.0 3.4 %project.1 = bf16[256,2048]{1,0:T(8,128)(2,1)} custom-call(bf16[2,256,128]{2,1,0:T(8,128)(2,1)S(1)} %copy-done.1, bf16[2,256,128]{2,1,0:T(8,128)(2,1)S(1)} %collective-permute-done.37.refs_1_, bf16[2,256,128]{2,1,0:T(8,128)(2,1)S(1)} %collective-permute-done.38.refs_2_, bf16[2,256,128]{2,1,0:T(8,128)(2,1)S(1)} %collective-permute-done.39.refs_3_, ...), custom_call_target="tpu_custom_call" | custom-call | tf_op jit(solution)/shard_map/project/pallas_call | solution.py:323
  (145 shorter events, 39.2 us)
Async XLA Ops:
  7.2 128.8 %all-gather.2.cloned.1.call-start = ((), (), s32[]{:S(2)}) async-start(), calls=%async_computation | async-start | bytes 12976128 | tf_op jit(solution)/shard_map/all_gather | solution.py:365
  10.1 8.6 %collective-permute-start.2 = (bf16[8,2,32,128]{3,2,1,0:T(8,128)(2,1)S(1)}, bf16[8,2,32,128]{3,2,1,0:T(8,128)(2,1)S(1)}, u32[]{:S(2)}, u32[]{:S(2)}) collective-permute-start(bf16[8,2,32,128]{3,2,1,0:T(8,128)(2,1)S(1)} %pad_maximum_fusion.2), channel_id=1, source_target_pairs={{0,224},{8,232},{16,240},{24,248},{32,0},{40,8},{48,16},{56,24},{6... | collective-permute-start | bytes 393224 | tf_op jit(solution)/shard_map/ppermute | solution.py:338
  22.2 28.2 %collective-permute-start.12 = (bf16[16,2,32,128]{3,2,1,0:T(8,128)(2,1)S(1)}, bf16[16,2,32,128]{3,2,1,0:T(8,128)(2,1)S(1)}, u32[]{:S(2)}, u32[]{:S(2)}) collective-permute-start(bf16[16,2,32,128]{3,2,1,0:T(8,128)(2,1)S(1)} %pad_maximum_fusion.1.refs_0_), channel_id=1, source_target_pairs={{0,24},{8,0},{16,8},{24,16},{32,56},{40,32},{48,40},{56,48},{64,88... | collective-permute-start | bytes 786440 | tf_op jit(solution)/shard_map/ppermute | solution.py:338
  24.8 22.9 %collective-permute-start.1 = (bf16[16,2,32,128]{3,2,1,0:T(8,128)(2,1)S(1)}, bf16[16,2,32,128]{3,2,1,0:T(8,128)(2,1)S(1)}, u32[]{:S(2)}, u32[]{:S(2)}) collective-permute-start(bf16[16,2,32,128]{3,2,1,0:T(8,128)(2,1)S(1)} %pad_maximum_fusion.1.refs_0_), channel_id=1, source_target_pairs={{0,8},{8,16},{16,24},{24,0},{32,40},{40,48},{48,56},{56,32},{64,72... | collective-permute-start | bytes 786440 | tf_op jit(solution)/shard_map/ppermute | solution.py:338
  24.8 10.2 %collective-permute-start.8 = (bf16[8,2,32,128]{3,2,1,0:T(8,128)(2,1)S(1)}, bf16[8,2,32,128]{3,2,1,0:T(8,128)(2,1)S(1)}, u32[]{:S(2)}, u32[]{:S(2)}) collective-permute-start(bf16[8,2,32,128]{3,2,1,0:T(8,128)(2,1)S(1)} %collective-permute-done.5), channel_id=1, source_target_pairs={{0,224},{8,232},{16,240},{24,248},{32,0},{40,8},{48,16},{56,24},{6... | collective-permute-start | bytes 393224 | tf_op jit(solution)/shard_map/ppermute | solution.py:338
  27.5 7.3 %collective-permute-start.6 = (bf16[8,2,32,128]{3,2,1,0:T(8,128)(2,1)S(1)}, bf16[8,2,32,128]{3,2,1,0:T(8,128)(2,1)S(1)}, u32[]{:S(2)}, u32[]{:S(2)}) collective-permute-start(bf16[8,2,32,128]{3,2,1,0:T(8,128)(2,1)S(1)} %collective-permute-done.3), channel_id=1, source_target_pairs={{0,32},{8,40},{16,48},{24,56},{32,64},{40,72},{48,80},{56,88},{64,... | collective-permute-start | bytes 393224 | tf_op jit(solution)/shard_map/ppermute | solution.py:338
  27.6 20.2 %collective-permute-start.13 = (bf16[16,2,32,128]{3,2,1,0:T(8,128)(2,1)S(1)}, bf16[16,2,32,128]{3,2,1,0:T(8,128)(2,1)S(1)}, u32[]{:S(2)}, u32[]{:S(2)}) collective-permute-start(bf16[16,2,32,128]{3,2,1,0:T(8,128)(2,1)S(1)} %constant_dynamic-update-slice_fusion.refs_1_), channel_id=1, source_target_pairs={{0,24},{8,0},{16,8},{24,16},{32,56},{40,32},{48,40},{56,48},{64,88... | collective-permute-start | bytes 786440 | tf_op jit(solution)/shard_map/ppermute | solution.py:338
  34.8 15.5 %collective-permute-start.4 = (bf16[16,2,32,128]{3,2,1,0:T(8,128)(2,1)S(1)}, bf16[16,2,32,128]{3,2,1,0:T(8,128)(2,1)S(1)}, u32[]{:S(2)}, u32[]{:S(2)}) collective-permute-start(bf16[16,2,32,128]{3,2,1,0:T(8,128)(2,1)S(1)} %constant_dynamic-update-slice_fusion.refs_1_), channel_id=1, source_target_pairs={{0,8},{8,16},{16,24},{24,0},{32,40},{40,48},{48,56},{56,32},{64,72... | collective-permute-start | bytes 786440 | tf_op jit(solution)/shard_map/ppermute | solution.py:338
  43.8 9.6 %collective-permute-start.14 = (bf16[16,2,32,128]{3,2,1,0:T(8,128)(2,1)S(1)}, bf16[16,2,32,128]{3,2,1,0:T(8,128)(2,1)S(1)}, u32[]{:S(2)}, u32[]{:S(2)}) collective-permute-start(bf16[16,2,32,128]{3,2,1,0:T(8,128)(2,1)S(1)} %constant_dynamic-update-slice_fusion.2.refs_2_), channel_id=1, source_target_pairs={{0,24},{8,0},{16,8},{24,16},{32,56},{40,32},{48,40},{56,48},{64,88... | collective-permute-start | bytes 786440 | tf_op jit(solution)/shard_map/ppermute | solution.py:338
  47.7 8.5 %collective-permute-start.15 = (bf16[16,2,32,128]{3,2,1,0:T(8,128)(2,1)S(1)}, bf16[16,2,32,128]{3,2,1,0:T(8,128)(2,1)S(1)}, u32[]{:S(2)}, u32[]{:S(2)}) collective-permute-start(bf16[16,2,32,128]{3,2,1,0:T(8,128)(2,1)S(1)} %constant_dynamic-update-slice_fusion.4.refs_3_), channel_id=1, source_target_pairs={{0,24},{8,0},{16,8},{24,16},{32,56},{40,32},{48,40},{56,48},{64,88... | collective-permute-start | bytes 786440 | tf_op jit(solution)/shard_map/ppermute | solution.py:338
  53.4 15.6 %collective-permute-start.11 = (bf16[16,2,32,128]{3,2,1,0:T(8,128)(2,1)S(1)}, bf16[16,2,32,128]{3,2,1,0:T(8,128)(2,1)S(1)}, u32[]{:S(2)}, u32[]{:S(2)}) collective-permute-start(bf16[16,2,32,128]{3,2,1,0:T(8,128)(2,1)S(1)} %constant_dynamic-update-slice_fusion.4.refs_3_), channel_id=1, source_target_pairs={{0,8},{8,16},{16,24},{24,0},{32,40},{40,48},{48,56},{56,32},{64,72... | collective-permute-start | bytes 786440 | tf_op jit(solution)/shard_map/ppermute | solution.py:338
  53.4 15.6 %collective-permute-start.17 = (bf16[16,2,32,128]{3,2,1,0:T(8,128)(2,1)S(1)}, bf16[16,2,32,128]{3,2,1,0:T(8,128)(2,1)S(1)}, u32[]{:S(2)}, u32[]{:S(2)}) collective-permute-start(bf16[16,2,32,128]{3,2,1,0:T(8,128)(2,1)S(1)} %collective-permute-done.4.refs_5_), channel_id=1, source_target_pairs={{0,8},{8,16},{16,24},{24,0},{32,40},{40,48},{48,56},{56,32},{64,72... | collective-permute-start | bytes 786440 | tf_op jit(solution)/shard_map/ppermute | solution.py:338
  54.5 14.4 %collective-permute-start.18 = (bf16[16,2,32,128]{3,2,1,0:T(8,128)(2,1)S(1)}, bf16[16,2,32,128]{3,2,1,0:T(8,128)(2,1)S(1)}, u32[]{:S(2)}, u32[]{:S(2)}) collective-permute-start(bf16[16,2,32,128]{3,2,1,0:T(8,128)(2,1)S(1)} %collective-permute-done.14.refs_10_), channel_id=1, source_target_pairs={{0,24},{8,0},{16,8},{24,16},{32,56},{40,32},{48,40},{56,48},{64,88... | collective-permute-start | bytes 786440 | tf_op jit(solution)/shard_map/ppermute | solution.py:338
  56.2 12.8 %collective-permute-start.19 = (bf16[16,2,32,128]{3,2,1,0:T(8,128)(2,1)S(1)}, bf16[16,2,32,128]{3,2,1,0:T(8,128)(2,1)S(1)}, u32[]{:S(2)}, u32[]{:S(2)}) collective-permute-start(bf16[16,2,32,128]{3,2,1,0:T(8,128)(2,1)S(1)} %collective-permute-done.15.refs_11_), channel_id=1, source_target_pairs={{0,24},{8,0},{16,8},{24,16},{32,56},{40,32},{48,40},{56,48},{64,88... | collective-permute-start | bytes 786440 | tf_op jit(solution)/shard_map/ppermute | solution.py:338
  57.6 17.9 %collective-permute-start.26 = (bf16[2048,128]{1,0:T(8,128)(2,1)S(1)}, bf16[2048,128]{1,0:T(8,128)(2,1)S(1)}, u32[]{:S(2)}, u32[]{:S(2)}) collective-permute-start(bf16[2048,128]{1,0:T(8,128)(2,1)S(1)} %copy-done.6), channel_id=1, source_target_pairs={{0,1},{1,0},{2,3},{3,2},{4,5},{5,4},{6,7},{7,6},{8,9},{9,8},{10,11... | collective-permute-start | bytes 1572872 | tf_op jit(solution)/shard_map/ppermute | solution.py:342
  69.0 14.0 %collective-permute-start.21 = (bf16[2048,128]{1,0:T(8,128)(2,1)S(1)}, bf16[2048,128]{1,0:T(8,128)(2,1)}, u32[]{:S(2)}, u32[]{:S(2)}) collective-permute-start(bf16[2048,128]{1,0:T(8,128)(2,1)S(1)} %copy-done.6), channel_id=1, source_target_pairs={{0,2},{1,3},{2,0},{3,1},{4,6},{5,7},{6,4},{7,5},{8,10},{9,11},{10,... | collective-permute-start | bytes 1572872 | tf_op jit(solution)/shard_map/ppermute | solution.py:342
  70.3 15.0 %collective-permute-start.24 = (bf16[128,2048]{1,0:T(8,128)(2,1)S(1)}, bf16[128,2048]{1,0:T(8,128)(2,1)S(1)}, u32[]{:S(2)}, u32[]{:S(2)}) collective-permute-start(bf16[128,2048]{1,0:T(8,128)(2,1)S(1)} %copy-done), channel_id=1, source_target_pairs={{0,6},{1,7},{2,4},{3,5},{4,2},{5,3},{6,0},{7,1},{8,14},{9,15},{10,... | collective-permute-start | bytes 1572872 | tf_op jit(solution)/shard_map/ppermute | solution.py:342
  73.5 13.3 %collective-permute-start.23 = (bf16[128,2048]{1,0:T(8,128)(2,1)S(1)}, bf16[128,2048]{1,0:T(8,128)(2,1)S(1)}, u32[]{:S(2)}, u32[]{:S(2)}) collective-permute-start(bf16[128,2048]{1,0:T(8,128)(2,1)S(1)} %copy-done), channel_id=1, source_target_pairs={{0,4},{1,5},{2,6},{3,7},{4,0},{5,1},{6,2},{7,3},{8,12},{9,13},{10,... | collective-permute-start | bytes 1572872 | tf_op jit(solution)/shard_map/ppermute | solution.py:342
  74.8 16.5 %collective-permute-start.22 = (bf16[128,2048]{1,0:T(8,128)(2,1)S(1)}, bf16[128,2048]{1,0:T(8,128)(2,1)S(1)}, u32[]{:S(2)}, u32[]{:S(2)}) collective-permute-start(bf16[128,2048]{1,0:T(8,128)(2,1)S(1)} %copy-done), channel_id=1, source_target_pairs={{0,2},{1,3},{2,0},{3,1},{4,6},{5,7},{6,4},{7,5},{8,10},{9,11},{10,... | collective-permute-start | bytes 1572872 | tf_op jit(solution)/shard_map/ppermute | solution.py:342
  91.6 15.7 %collective-permute-start.25 = (s32[2,4,1,4]{3,1,2,0:T(4,128)S(1)}, s32[2,4,1,4]{3,1,2,0:T(4,128)S(1)}, u32[]{:S(2)}, u32[]{:S(2)}) collective-permute-start(s32[2,4,1,4]{3,1,2,0:T(4,128)S(1)} %pad_add_fusion), channel_id=1, source_target_pairs={{0,1},{1,0},{2,3},{3,2},{4,5},{5,4},{6,7},{7,6},{8,9},{9,8},{10,11... | collective-permute-start | bytes 392 | tf_op jit(solution)/shard_map/ppermute | solution.py:342
  147.4 8.8 %collective-permute-start.34 = (bf16[4,144,256]{2,1,0:T(8,128)(2,1)}, bf16[4,144,256]{2,1,0:T(8,128)(2,1)S(1)}, u32[]{:S(2)}, u32[]{:S(2)}) collective-permute-start(bf16[4,144,256]{2,1,0:T(8,128)(2,1)} %get-tuple-element.80), channel_id=1, source_target_pairs={{0,2},{1,3},{2,0},{3,1},{4,6},{5,7},{6,4},{7,5},{8,10},{9,11},{10,... | collective-permute-start | bytes 884744 | tf_op jit(solution)/shard_map/ppermute | solution.py:342
  148.8 13.5 %collective-permute-start.35 = (bf16[4,144,256]{2,1,0:T(8,128)(2,1)}, bf16[4,144,256]{2,1,0:T(8,128)(2,1)}, u32[]{:S(2)}, u32[]{:S(2)}) collective-permute-start(bf16[4,144,256]{2,1,0:T(8,128)(2,1)} %get-tuple-element.81), channel_id=1, source_target_pairs={{0,2},{1,3},{2,0},{3,1},{4,6},{5,7},{6,4},{7,5},{8,10},{9,11},{10,... | collective-permute-start | bytes 884744 | tf_op jit(solution)/shard_map/ppermute | solution.py:342
  168.8 9.7 %collective-permute-start.38 = (bf16[2,256,128]{2,1,0:T(8,128)(2,1)}, bf16[2,256,128]{2,1,0:T(8,128)(2,1)S(1)}, u32[]{:S(2)}, u32[]{:S(2)}) collective-permute-start(bf16[2,256,128]{2,1,0:T(8,128)(2,1)} %get-tuple-element.96), channel_id=1, source_target_pairs={{0,4},{1,5},{2,6},{3,7},{4,0},{5,1},{6,2},{7,3},{8,12},{9,13},{10,... | collective-permute-start | bytes 393224 | tf_op jit(solution)/shard_map/ppermute | solution.py:342
  171.9 9.2 %collective-permute-start.39 = (bf16[2,256,128]{2,1,0:T(8,128)(2,1)}, bf16[2,256,128]{2,1,0:T(8,128)(2,1)S(1)}, u32[]{:S(2)}, u32[]{:S(2)}) collective-permute-start(bf16[2,256,128]{2,1,0:T(8,128)(2,1)} %get-tuple-element.97), channel_id=1, source_target_pairs={{0,6},{1,7},{2,4},{3,5},{4,2},{5,3},{6,0},{7,1},{8,14},{9,15},{10,... | collective-permute-start | bytes 393224 | tf_op jit(solution)/shard_map/ppermute | solution.py:342
  (39 other events, 579.0 us)
Sparse Core Ops, SparseCore 0:
  10.6 125.3 all-gather.1
